TPU v7x, 256 devices: a whole 4x4x8 slice. The times are simulated.
256 devices in a mesh: gx: 8 (over y_lo, x), row: 16 (over z, y_hi), rep: 2 (over core).
Axes of the slice: x: 4, y: 4 (y_hi: 2, y_lo: 2; y = y_hi * 2 + y_lo), z: 8, core: 2. Of those that a mesh axis runs over, the one named last changes fastest.
Arguments:
- samples: bfloat16 [2, 64, 32, 64, 128], P('rep', None, 'gx', 'row'), may hold values from -6 to 6
- cotangent: bfloat16 [2, 64, 32, 64, 128], P('rep', None, 'gx', 'row'), may hold values from -6 to 6
- kernel_0: bfloat16 [16, 27, 64], replicated, may hold values from -0.15625 to 0.15625
- kernel_1: bfloat16 [16, 27, 80], replicated, may hold values from -0.125 to 0.125
- kernel_2: bfloat16 [16, 27, 96], replicated, may hold values from -0.125 to 0.125
- kernel_3: bfloat16 [16, 27, 112], replicated, may hold values from -0.109375 to 0.109375
- layer_bias: bfloat16 [4, 16], replicated, may hold values from -3 to 3
- merging_weight: bfloat16 [64, 128], replicated, may hold values from -0.5 to 0.5
- merging_bias: bfloat16 [64], replicated, may hold values from -3 to 3
Outputs:
- output: float32 [2, 64, 32, 64, 128], P('rep', None, 'gx', 'row')
- grad_input: float32 [2, 64, 32, 64, 128], P('rep', None, 'gx', 'row')
- grad_kernel_0: float32 [16, 27, 64], replicated
- grad_kernel_1: float32 [16, 27, 80], replicated
- grad_kernel_2: float32 [16, 27, 96], replicated
- grad_kernel_3: float32 [16, 27, 112], replicated
- grad_layer_bias: float32 [4, 16], replicated
- grad_merging_weight: float32 [64, 128], replicated
- grad_merging_bias: float32 [64], replicated
All inputs are finite; a program needn't handle non-finite values.
Results may differ from a plain program's by a relative error of at most 0.009.
Values may be sent and summed in bfloat16 or wider, within the bound.
No kernel may reach another device: no remote copies, remote signals or barrier semaphores. Data moves between devices by JAX's collectives and lax.ppermute only.
A program may use at most 256 MiB of HBM per device.

v0:
```python
import math

import jax
import jax.numpy as jnp
from jax import lax
from jax.sharding import PartitionSpec as P

BETA = 0.2


def extended(x, sides, width):
    for axis, dim in sides:
        size, length = (lax.axis_size(axis), x.shape[dim])
        up = [(i, (i + 1) % size) for i in range(size - 1)]
        down = [(j, i) for i, j in up]
        last = lax.slice_in_dim(x, length - width, length, axis=dim)
        first = lax.slice_in_dim(x, 0, width, axis=dim)
        before = lax.ppermute(last, axis, up)
        after = lax.ppermute(first, axis, down)
        x = jnp.concatenate([before, x, after], axis=dim)
    return x


def activate(value):
    return 0.2 * value + 0.8 * value * jax.nn.sigmoid(value)


def slope_of(value):
    sigmoid_v = jax.nn.sigmoid(value)
    return 0.2 + 0.8 * (sigmoid_v + value * sigmoid_v * (1.0 - sigmoid_v))


def pad_depth(features):
    return jnp.pad(features, ((0, 0), (0, 0), (0, 0), (1, 1)))


def patches_of(padded, span_x, span_y, span_z):
    pieces = [
        padded[:, step_x : step_x + span_x, step_y : step_y + span_y, step_z : step_z + span_z]
        for step_x in range(3)
        for step_y in range(3)
        for step_z in range(3)
    ]
    stacked = jnp.stack(pieces, axis=0)
    return stacked.reshape(27 * padded.shape[0], span_x * span_y * span_z)


def back_patches(padded, span_x, span_y, span_z):
    pieces = [
        padded[
            :,
            2 - step_x : 2 - step_x + span_x,
            2 - step_y : 2 - step_y + span_y,
            2 - step_z : 2 - step_z + span_z,
        ]
        for step_x in range(3)
        for step_y in range(3)
        for step_z in range(3)
    ]
    stacked = jnp.stack(pieces, axis=0)
    return stacked.reshape(27 * padded.shape[0], span_x * span_y * span_z)


def feature_rim(features):
    rimmed = extended(features, (("gx", 1), ("row", 2)), 1)
    return pad_depth(rimmed)


def cotangent_rim(features):
    rimmed = extended(features, (("gx", 1), ("row", 2)), 1)
    return pad_depth(rimmed)


def body(
    samples,
    cotangent,
    kernel_0,
    kernel_1,
    kernel_2,
    kernel_3,
    layer_bias,
    merging_weight,
    merging_bias,
):
    kernels = (kernel_0, kernel_1, kernel_2, kernel_3)
    samples_local = samples[0]
    channels, span_x, span_y, span_z = samples_local.shape
    growth = layer_bias.shape[1]
    cell_count = span_x * span_y * span_z
    cell_total = (
        samples.shape[0]
        * lax.axis_size("rep")
        * span_x
        * lax.axis_size("gx")
        * span_y
        * lax.axis_size("row")
        * span_z
    )
    norm_scale = 1.0 / math.sqrt(cell_total)
    biases = layer_bias.astype(jnp.float32)
    padded_feats = []
    hidden_list = []
    pre_acts = []
    padded_feats.append(feature_rim(samples_local))
    for layer_num in range(4):
        stacked = jnp.concatenate(padded_feats, axis=0)
        patches = patches_of(stacked, span_x, span_y, span_z)
        pre_act = jnp.dot(
            kernels[layer_num].reshape(growth, -1), patches, preferred_element_type=jnp.float32
        )
        pre_act = (pre_act + biases[layer_num][:, None]).reshape(growth, span_x, span_y, span_z)
        hidden = activate(pre_act).astype(jnp.bfloat16)
        pre_acts.append(pre_act)
        hidden_list.append(hidden)
        if layer_num < 3:
            padded_feats.append(feature_rim(hidden))
    joined = jnp.concatenate([samples_local] + hidden_list, axis=0).reshape(-1, cell_count)
    merged = jnp.dot(merging_weight, joined, preferred_element_type=jnp.float32)
    merged = merged + merging_bias.astype(jnp.float32)[:, None]
    output = samples_local.reshape(channels, cell_count).astype(jnp.float32) + BETA * merged
    grad_out = cotangent[0].reshape(channels, cell_count).astype(jnp.float32)
    merge_grad = (BETA * grad_out).astype(jnp.bfloat16)
    grad_merging_weight = (
        lax.dot_general(
            merge_grad, joined, (((1,), (1,)), ((), ())), preferred_element_type=jnp.float32
        )
        * norm_scale
    )
    grad_merging_bias = jnp.sum(merge_grad.astype(jnp.float32), axis=1) * norm_scale
    carried = lax.dot_general(
        merging_weight, merge_grad, (((0,), (0,)), ((), ())), preferred_element_type=jnp.float32
    )
    grad_acc = grad_out + carried[:channels]
    hidden_grads = [carried[channels + k * growth : channels + (k + 1) * growth] for k in range(4)]
    grad_kernels = [None, None, None, None]
    grad_biases = [None, None, None, None]
    for layer_num in (3, 2, 1, 0):
        in_chans = channels + layer_num * growth
        slopes = slope_of(pre_acts[layer_num].reshape(growth, cell_count))
        pre_grad = (hidden_grads[layer_num] * slopes).astype(jnp.bfloat16)
        patches = patches_of(
            jnp.concatenate(padded_feats[: layer_num + 1], axis=0), span_x, span_y, span_z
        )
        kernel_grad = (
            lax.dot_general(
                pre_grad, patches, (((1,), (1,)), ((), ())), preferred_element_type=jnp.float32
            )
            * norm_scale
        )
        kernel_grad = kernel_grad.reshape(growth, 27, in_chans)
        bias_grad = jnp.sum(pre_grad.astype(jnp.float32), axis=1) * norm_scale
        grad_kernels[layer_num] = kernel_grad
        grad_biases[layer_num] = bias_grad
        rimmed = cotangent_rim(pre_grad.reshape(growth, span_x, span_y, span_z))
        grad_patches = back_patches(rimmed, span_x, span_y, span_z)
        flipped = kernels[layer_num].transpose(2, 1, 0).reshape(in_chans, 27 * growth)
        pulled = jnp.dot(flipped, grad_patches, preferred_element_type=jnp.float32)
        grad_acc = grad_acc + pulled[:channels]
        for other in range(layer_num):
            hidden_grads[other] = (
                hidden_grads[other]
                + pulled[channels + other * growth : channels + (other + 1) * growth]
            )
    grad_layer_bias = jnp.stack(grad_biases, axis=0)
    grad_k0, grad_k1, grad_k2, grad_k3 = grad_kernels
    grad_k0, grad_k1, grad_k2, grad_k3, grad_layer_bias, grad_merging_weight, grad_merging_bias = (
        lax.psum(
            (
                grad_k0,
                grad_k1,
                grad_k2,
                grad_k3,
                grad_layer_bias,
                grad_merging_weight,
                grad_merging_bias,
            ),
            ("gx", "row", "rep"),
        )
    )
    out_shape = (1, channels, span_x, span_y, span_z)
    return (
        output.reshape(out_shape),
        grad_acc.reshape(out_shape),
        grad_k0,
        grad_k1,
        grad_k2,
        grad_k3,
        grad_layer_bias,
        grad_merging_weight,
        grad_merging_bias,
    )


def solution(mesh):
    placed = (
        P("rep", None, "gx", "row", None),
        P("rep", None, "gx", "row", None),
        P(),
        P(),
        P(),
        P(),
        P(),
        P(),
        P(),
    )
    return jax.shard_map(
        body,
        mesh=mesh,
        in_specs=placed,
        out_specs=(
            P("rep", None, "gx", "row", None),
            P("rep", None, "gx", "row", None),
            P(),
            P(),
            P(),
            P(),
            P(),
            P(),
            P(),
        ),
        check_vma=False,
    )
```

profile of v0, /device:TPU:1, one launch (start us, length us, event | category | flops | bytes accessed | tf_op | source)
XLA Modules:
  0.0 855.7 jit_solution(3796646113841497538)
XLA Ops:
  25.8 5.3 collective-permute-done.3
  55.9 16.1 %copy.74 = bf16[27,64,4,4,128]{4,3,2,1,0:T(4,128)(2,1)} copy(bf16[27,64,4,4,128]{1,4,3,2,0:T(8,128)(2,1)} %fusion.99) | data formatting | bytes 14155776 | tf_op jit(solution)/shard_map/stack | solution.py:44
  72.0 12.4 %reshape.189 = bf16[1728,2048]{1,0:T(8,128)(2,1)} reshape(bf16[27,64,4,4,128]{4,3,2,1,0:T(4,128)(2,1)} %copy.74) | data formatting | bytes 14155776 | tf_op jit(solution)/shard_map/reshape | solution.py:45
  143.0 19.6 %copy.80 = bf16[27,80,4,4,128]{4,3,2,1,0:T(4,128)(2,1)} copy(bf16[27,80,4,4,128]{1,4,3,2,0:T(8,128)(2,1)} %fusion.72) | data formatting | bytes 17694720 | tf_op jit(solution)/shard_map/stack | solution.py:44
  162.6 15.4 %reshape.191 = bf16[2160,2048]{1,0:T(8,128)(2,1)} reshape(bf16[27,80,4,4,128]{4,3,2,1,0:T(4,128)(2,1)} %copy.80) | data formatting | bytes 17694720 | tf_op jit(solution)/shard_map/reshape | solution.py:45
  178.0 5.4 constant_dynamic-update-slice_fusion.12
  184.2 4.9 collective-permute-start.8
  196.0 5.7 collective-permute-start.10
  238.4 22.2 %copy.87 = bf16[27,96,4,4,128]{4,3,2,1,0:T(4,128)(2,1)} copy(bf16[27,96,4,4,128]{1,4,3,2,0:T(8,128)(2,1)} %fusion.44) | data formatting | bytes 21233664 | tf_op jit(solution)/shard_map/stack | solution.py:44
  260.6 18.1 %reshape.193 = bf16[2592,2048]{1,0:T(8,128)(2,1)} reshape(bf16[27,96,4,4,128]{4,3,2,1,0:T(4,128)(2,1)} %copy.87) | data formatting | bytes 21233664 | tf_op jit(solution)/shard_map/reshape | solution.py:45
  278.7 6.2 constant_dynamic-update-slice_fusion.11
  337.0 23.1 %copy.95 = bf16[27,112,4,4,128]{4,3,2,1,0:T(4,128)(2,1)} copy(bf16[27,112,4,4,128]{1,4,3,2,0:T(8,128)(2,1)} %fusion.17) | data formatting | bytes 24772608 | tf_op jit(solution)/shard_map/stack | solution.py:44
  360.1 20.9 %reshape.195 = bf16[3024,2048]{1,0:T(8,128)(2,1)} reshape(bf16[27,112,4,4,128]{4,3,2,1,0:T(4,128)(2,1)} %copy.95) | data formatting | bytes 24772608 | tf_op jit(solution)/shard_map/reshape | solution.py:45
  381.0 6.2 constant_dynamic-update-slice_fusion.10
  392.8 7.8 convolution_multiply_fusion.2
  405.3 5.0 collective-permute-start.18
  452.5 5.4 collective-permute-start.22
  459.2 6.9 convolution_multiply_fusion.1
  500.5 5.9 collective-permute-start.26
  507.9 5.9 convolution_multiply_fusion
  539.2 4.9 convolution_multiply_fusion.3
  552.9 6.6 collective-permute-start.30
  561.6 100.8 %all-reduce.8 = (f32[4,16]{1,0:T(4,128)}, f32[64,128]{1,0:T(8,128)}, f32[64]{0:T(128)}) all-reduce(f32[4,16]{1,0:T(4,128)S(1)} %pad_maximum_fusion.27, f32[64,128]{1,0:T(8,128)S(1)} %convolution_multiply_fusion.4, f32[64]{0:T(128)S(1)} %copy-done.22), channel_id=1, replica_groups=mesh['gx'=8,'row'=16,'rep'=2] {'gx','row','rep'}, use_global_device_ids=true, to_apply=%region_8.9 | all-reduce | flops 8320 | bytes 66560 | tf_op jit(solution)/shard_map/psum | solution.py:167
  689.6 151.7 %all-reduce.12.cloned.1.call-done = (f32[16,27,64]{2,1,0:T(8,128)}, f32[16,27,80]{2,1,0:T(8,128)}, f32[16,27,96]{2,1,0:T(8,128)}, f32[16,27,112]{2,1,0:T(8,128)}) async-done(((f32[16,27,64]{2,1,0:T(8,128)}, f32[16,27,80]{2,1,0:T(8,128)}, f32[16,27,96]{2,1,0:T(8,128)}, f32[16,27,112]{2,1,0:T(8,128)}), (f32[16,27,64]{2,1,0:T(8,128)}, f32[16,27,80]{2,1,0:T(8,128)}, f32[16,27,96]{2,1,0:T(8,128)}, ...) | async-done | bytes 608272 | tf_op jit(solution)/shard_map/psum | solution.py:167
  (439 shorter events, 357.5 us)
Async XLA Ops:
  7.2 834.1 %all-reduce.12.cloned.1.call-start = ((), (), s32[]{:S(2)}) async-start(), calls=%async_computation | async-start | bytes 2097152 | tf_op jit(solution)/shard_map/psum | solution.py:167
  8.6 6.4 collective-permute-start
  12.5 5.7 collective-permute-start.1
  18.3 7.4 collective-permute-start.2
  23.2 7.9 collective-permute-start.3
  96.8 6.1 collective-permute-start.6
  101.1 6.1 collective-permute-start.7
  184.2 7.3 collective-permute-start.8
  196.0 9.5 %collective-permute-start.10 = (bf16[16,6,1,128]{3,0,2,1:T(8,128)(2,1)}, bf16[16,6,1,128]{3,0,2,1:T(8,128)(2,1)S(1)}, u32[]{:S(2)}, u32[]{:S(2)}) collective-permute-start(bf16[16,6,1,128]{3,0,2,1:T(8,128)(2,1)} %get-tuple-element.82), channel_id=1, source_target_pairs={{0,2},{2,4},{4,6},{6,8},{8,10},{10,12},{12,14},{14,16},{16,18},{18... | collective-permute-start | bytes 73736 | tf_op jit(solution)/shard_map/ppermute | solution.py:18
  201.8 6.4 collective-permute-start.11
  285.0 6.8 collective-permute-start.12
  295.7 7.6 collective-permute-start.14
  299.8 6.4 collective-permute-start.15
  388.4 13.5 %collective-permute-start.16 = (bf16[16,1,4,128]{3,2,1,0:T(4,128)(2,1)S(1)}, bf16[16,1,4,128]{3,2,1,0:T(4,128)(2,1)S(1)}, u32[]{:S(2)}, u32[]{:S(2)}) collective-permute-start(bf16[16,1,4,128]{3,2,1,0:T(4,128)(2,1)S(1)} %get-tuple-element.93), channel_id=1, source_target_pairs={{0,32},{32,64},{64,96},{96,128},{128,160},{160,192},{192,224},{1,3... | collective-permute-start | bytes 49160 | tf_op jit(solution)/shard_map/ppermute | solution.py:18
  405.3 7.6 collective-permute-start.18
  410.3 6.3 collective-permute-start.19
  441.5 7.7 collective-permute-start.20
  452.5 13.6 %collective-permute-start.22 = (bf16[16,6,1,128]{3,2,1,0:T(2,128)(2,1)S(1)}, bf16[16,6,1,128]{3,2,1,0:T(2,128)(2,1)S(1)}, u32[]{:S(2)}, u32[]{:S(2)}) collective-permute-start(bf16[16,6,1,128]{3,2,1,0:T(2,128)(2,1)S(1)} %get-tuple-element.76), channel_id=1, source_target_pairs={{0,2},{2,4},{4,6},{6,8},{8,10},{10,12},{12,14},{14,16},{16,18},{18... | collective-permute-start | bytes 73736 | tf_op jit(solution)/shard_map/ppermute | solution.py:18
  457.9 8.2 collective-permute-start.23
  491.0 6.2 collective-permute-start.24
  500.5 14.3 %collective-permute-start.26 = (bf16[16,6,1,128]{3,2,1,0:T(2,128)(2,1)S(1)}, bf16[16,6,1,128]{3,2,1,0:T(2,128)(2,1)S(1)}, u32[]{:S(2)}, u32[]{:S(2)}) collective-permute-start(bf16[16,6,1,128]{3,2,1,0:T(2,128)(2,1)S(1)} %get-tuple-element.74), channel_id=1, source_target_pairs={{0,2},{2,4},{4,6},{6,8},{8,10},{10,12},{12,14},{14,16},{16,18},{18... | collective-permute-start | bytes 73736 | tf_op jit(solution)/shard_map/ppermute | solution.py:18
  506.4 8.4 collective-permute-start.27
  552.9 109.6 %collective-permute-start.30 = (bf16[16,6,1,128]{3,2,1,0:T(2,128)(2,1)S(1)}, bf16[16,6,1,128]{3,2,1,0:T(2,128)(2,1)S(1)}, u32[]{:S(2)}, u32[]{:S(2)}) collective-permute-start(bf16[16,6,1,128]{3,2,1,0:T(2,128)(2,1)S(1)} %get-tuple-element.72), channel_id=1, source_target_pairs={{0,2},{2,4},{4,6},{6,8},{8,10},{10,12},{12,14},{14,16},{16,18},{18... | collective-permute-start | bytes 73736 | tf_op jit(solution)/shard_map/ppermute | solution.py:18
  559.4 103.0 %collective-permute-start.31 = (bf16[16,6,1,128]{3,2,1,0:T(2,128)(2,1)S(1)}, bf16[16,6,1,128]{3,2,1,0:T(2,128)(2,1)S(1)}, u32[]{:S(2)}, u32[]{:S(2)}) collective-permute-start(bf16[16,6,1,128]{3,2,1,0:T(2,128)(2,1)S(1)} %get-tuple-element.73), channel_id=1, source_target_pairs={{2,0},{4,2},{6,4},{8,6},{10,8},{12,10},{14,12},{16,14},{18,16},{20... | collective-permute-start | bytes 73736 | tf_op jit(solution)/shard_map/ppermute | solution.py:19
  (33 other events, 422.7 us)
Sparse Core Ops, SparseCore 0:
  561.7 279.4 all-reduce.11
where the time goes:
time: 867 us; the launch traced here: 856 us
  local copies, waits for them, and re-layouts  320 us (37%)
  waiting for transfers between devices  196 us (23%)
  blocking collectives  101 us (12%)
  starting transfers between devices  95.7 us (11%)
  other arithmetic  73.1 us (8%)
  matrix products  54.8 us (6%)
  between operations  15.7 us (2%)
    psum x1, waiting for transfers between devices, body(): lax.psum((grad_k0, grad_k1, grad_k2, grad_k3, grad_layer_bias, grad_mergi...  152 us
    unnamed x229, local copies, waits for them, and re-layouts  139 us
    psum x1, blocking collectives, body(): lax.psum((grad_k0, grad_k1, grad_k2, grad_k3, grad_layer_bias, grad_mergi...  101 us
    another operation x7, local copies, waits for them, and re-layouts, patches_of(): stacked = jnp.stack(pieces, axis=0)  83.9 us
    ppermute x16, starting transfers between devices, extended(): before = lax.ppermute(last, axis, up)  74.1 us
    reshape x4, local copies, waits for them, and re-layouts, patches_of(): return stacked.reshape(27 * padded.shape[0], span_x * span_y * span_z)  66.8 us
    unnamed x60, other arithmetic  54.8 us
    ppermute x16, waiting for transfers between devices, extended(): after = lax.ppermute(first, axis, down)  43.3 us
  transfers between devices with their start and end apart: 33, of which 15 were waited for; matrix products, arithmetic and copies ran while one was open for 7% of the time, Pallas kernels for 0%

commit v1 on v0

v1 whole, which is shorter than its diff:
```python
import functools
import math

import jax
import jax.numpy as jnp
from jax import lax
from jax.experimental import pallas as pl
from jax.experimental.pallas import tpu as pltpu
from jax.sharding import PartitionSpec as P

BETA = 0.2
BF16, F32 = jnp.bfloat16, jnp.float32
Z = 128
B = 4
H = 2
N = B + 2 * H
MID = slice(H * Z, (H + B) * Z)
RING = slice((H - 1) * Z, (H + B + 1) * Z)
DEVICES = 256
ROWS = 8
VMEM_LIMIT = 24 * 2**20


def shape(dims, dtype):
    return jax.ShapeDtypeStruct(dims, dtype)


def call(kernel, outs, args, scratch=(), flops=1_000_000, name=None):
    moved = sum(math.prod(a.shape) * a.dtype.itemsize for a in list(args) + list(outs))
    return pl.pallas_call(
        kernel,
        out_shape=list(outs),
        in_specs=[pl.BlockSpec(memory_space=pltpu.VMEM)] * len(args),
        out_specs=[pl.BlockSpec(memory_space=pltpu.VMEM)] * len(outs),
        scratch_shapes=list(scratch),
        compiler_params=pltpu.CompilerParams(vmem_limit_bytes=VMEM_LIMIT),
        cost_estimate=pl.CostEstimate(flops=flops, bytes_accessed=moved, transcendentals=0),
        name=name,
    )(*args)


def lane_moves(rows, width):
    lane = lax.broadcasted_iota(jnp.int32, (rows, width), 1) % Z
    return lane != 0, lane != Z - 1


def from_left(v, keep):
    return jnp.where(keep, pltpu.roll(v, 1, 1), 0.0)


def from_right(v, keep):
    return jnp.where(keep, pltpu.roll(v, v.shape[1] - 1, 1), 0.0)


def spread(v):
    not_first, not_last = lane_moves(*v.shape)
    return jnp.concatenate([from_right(v, not_last), v, from_left(v, not_first)], axis=0).astype(BF16)


def conv_row(kernel_ref, sources, i, lanes):
    n = lanes.stop - lanes.start
    acc = jnp.zeros((48, n), F32)
    for a in range(3):
        for b in range(3):
            cut = pl.ds(lanes.start + (b - 1) * Z, n)
            rhs = [s[i + a - 1, :, cut] for s in sources]
            rhs = rhs[0] if len(rhs) == 1 else jnp.concatenate(rhs, axis=0)
            acc = acc + jnp.dot(kernel_ref[3 * a + b], rhs, preferred_element_type=F32)
    not_first, not_last = lane_moves(16, n)
    return from_left(acc[:16], not_first) + acc[16:32] + from_right(acc[32:], not_last)


def back_row(weights, spread_ref, i, lanes):
    n = lanes.stop - lanes.start
    pieces = [
        spread_ref[i + 1 - a, :, pl.ds(lanes.start + (1 - b) * Z, n)]
        for a in range(3)
        for b in range(3)
    ]
    return jnp.dot(weights, jnp.concatenate(pieces, axis=0), preferred_element_type=F32)


def kernel_gradient(out_ref, own, sources):
    for a in range(3):
        for b in range(3):
            cut = pl.ds((H + b - 1) * Z, B * Z)
            rhs = jnp.concatenate(
                [jnp.concatenate([s[H + i + a - 1, :, cut] for s in sources], axis=0) for i in range(B)],
                axis=1,
            )
            got = lax.dot_general(own, rhs, (((1,), (1,)), ((), ())), preferred_element_type=F32)
            t = 48 * (3 * a + b)
            out_ref[t : t + 48, : got.shape[1]] = got.astype(BF16)
            if got.shape[1] < Z:
                out_ref[t : t + 48, got.shape[1] :] = jnp.zeros((48, Z - got.shape[1]), BF16)


def own_cells(spread_ref):
    return jnp.concatenate([spread_ref[H + i, :, MID] for i in range(B)], axis=1)


def activate(value):
    sigmoid = jax.nn.sigmoid(value)
    return 0.2 * value + 0.8 * value * sigmoid, 0.2 + 0.8 * (
        sigmoid + value * sigmoid * (1.0 - sigmoid)
    )


def assemble(parts, frame):
    before, top, bottom, after, left, right = parts
    frame[0:2, :, MID] = before[...]
    frame[2:4, :, MID] = top[...]
    frame[4:6, :, MID] = bottom[...]
    frame[6:8, :, MID] = after[...]
    frame[:, :, : H * Z] = left[...]
    frame[:, :, (H + B) * Z :] = right[...]


def wide_sum(v):
    return jnp.broadcast_to(jnp.sum(v, axis=1, keepdims=True), (v.shape[0], Z))


def pack_kernel(x_ref, top_ref, bottom_ref, wide):
    wide[...] = x_ref[...].astype(F32)
    for i in range(B):
        out = top_ref if i < 2 else bottom_ref
        for j in range(B):
            got = wide[pl.ds(B * i + j, 64, stride=B * B), :]
            out[i % 2, :, j * Z : (j + 1) * Z] = got.astype(BF16)


def columns_kernel(before, top, bottom, after, left, right):
    for r, ref in enumerate((before, top, bottom, after)):
        left[2 * r : 2 * r + 2] = ref[:, :, : H * Z]
        right[2 * r : 2 * r + 2] = ref[:, :, (B - H) * Z :]


def prepare_kernel(cot_ref, merge_t, k0, k1, k2, k3, base, carried, merge_grad, w0, w1, w2, w3, wide):
    for k_ref, w_ref in ((k0, w0), (k1, w1), (k2, w2), (k3, w3)):
        w_ref[...] = jnp.transpose(k_ref[...].astype(F32)).astype(BF16)
    wide[...] = cot_ref[...].astype(F32)
    for i in range(B):
        cot = jnp.concatenate(
            [wide[pl.ds(B * i + j, 64, stride=B * B), :] for j in range(B)], axis=1
        )
        grad = (BETA * cot).astype(BF16)
        merge_grad[i] = grad
        back = jnp.dot(merge_t[...], grad, preferred_element_type=F32)
        base[i] = cot + back[:64]
        carried[i] = back[64:]


def first_kernel(
    before, top, bottom, after, left, right, k0, k1, bias, mask,
    frame, hidden_0, slope_0, slope_1, send_top, send_bottom,
):
    assemble((before, top, bottom, after, left, right), frame)

    def ring(i, carry):
        pre = conv_row(k0, [frame], i, RING) + bias[0:16, 0:1]
        value, slope = activate(pre)
        slope_0[i] = slope
        hidden_0[i, :, RING] = (value * mask[pl.ds(i, 1), RING]).astype(BF16)
        return carry

    lax.fori_loop(H - 1, H + B + 1, ring, 0)
    for i in range(B):
        pre = conv_row(k1, [frame, hidden_0], H + i, MID) + bias[16:32, 0:1]
        value, slope = activate(pre)
        slope_1[i] = slope
        send = send_top if i < 2 else send_bottom
        send[i % 2, 0:16] = hidden_0[H + i, :, MID]
        send[i % 2, 16:32] = value.astype(BF16)


def second_kernel(
    before, top, bottom, after, left, right, frame, k2, k3, bias, mask, carried,
    hidden_01, hidden_2, hidden_3, slope_2, own_3, send_top, send_bottom,
):
    assemble((before, top, bottom, after, left, right), hidden_01)

    def ring(i, carry):
        pre = conv_row(k2, [frame, hidden_01], i, RING) + bias[32:48, 0:1]
        value, slope = activate(pre)
        slope_2[i] = slope
        hidden_2[i, :, RING] = (value * mask[pl.ds(i, 1), RING]).astype(BF16)
        return carry

    lax.fori_loop(H - 1, H + B + 1, ring, 0)
    for i in range(B):
        pre = conv_row(k3, [frame, hidden_01, hidden_2], H + i, MID) + bias[48:64, 0:1]
        value, slope = activate(pre)
        hidden_3[i] = value.astype(BF16)
        grad = (carried[i, 48:64] * slope).astype(BF16)
        own_3[i] = spread(grad.astype(F32))
        send = send_top if i < 2 else send_bottom
        send[i % 2, 0:16] = grad
        send[i % 2, 16:32] = carried[i, 32:48].astype(BF16)


def merge_kernel(
    frame, hidden_01, hidden_2, hidden_3, own_3, merge, merge_bias, merge_grad,
    out_ref, grad_3, grad_merge,
):
    total = jnp.zeros((64, 128), F32)
    total_bias = jnp.zeros((64, B * Z), F32)
    for i in range(B):
        base = frame[H + i, :, MID]
        joined = jnp.concatenate(
            [base, hidden_01[H + i, :, MID], hidden_2[H + i, :, MID], hidden_3[i]], axis=0
        )
        merged = jnp.dot(merge[...], joined, preferred_element_type=F32) + merge_bias[:, 0:1]
        out = base.astype(F32) + BETA * merged
        for j in range(B):
            out_ref[pl.ds(B * i + j, 64, stride=B * B), :] = out[:, j * Z : (j + 1) * Z]
        grad = merge_grad[i]
        total = total + lax.dot_general(
            grad, joined, (((1,), (1,)), ((), ())), preferred_element_type=F32
        )
        total_bias = total_bias + grad.astype(F32)
    grad_merge[0:64] = total.astype(BF16)
    grad_merge[64:128] = wide_sum(total_bias).astype(BF16)
    own = jnp.concatenate([own_3[i] for i in range(B)], axis=1)
    grad_merge[128:144] = wide_sum(own[16:32].astype(F32)).astype(BF16)
    kernel_gradient(grad_3, own, [frame, hidden_01, hidden_2])


def third_kernel(
    before, top, bottom, after, left, right, w2, w3, slope_1, slope_2, mask, carried,
    spread_3, spread_2, own_1, send_top, send_bottom, pieces, held,
):
    assemble((before, top, bottom, after, left, right), pieces)
    held[...] = pieces[:, 16:32, :].astype(F32)
    for i in range(B):
        held[H + i, :, MID] = carried[i, 32:48]

    def move(i, carry):
        spread_3[i] = spread(pieces[i, 0:16].astype(F32))
        return carry

    lax.fori_loop(0, N, move, 0)

    def ring(i, carry):
        got = held[i, :, RING] + back_row(w3[96:112], spread_3, i, RING)
        grad = (got * slope_2[i] * mask[pl.ds(i, 1), RING]).astype(BF16)
        spread_2[i, :, RING] = spread(grad.astype(F32))
        return carry

    lax.fori_loop(H - 1, H + B + 1, ring, 0)
    for i in range(B):
        got = (
            carried[i, 16:32]
            + back_row(w3[80:96], spread_3, H + i, MID)
            + back_row(w2[80:96], spread_2, H + i, MID)
        )
        grad = (got * slope_1[i]).astype(BF16)
        own_1[i] = spread(grad.astype(F32))
        send = send_top if i < 2 else send_bottom
        send[i % 2, 0:16] = spread_2[H + i, 16:32, MID]
        send[i % 2, 16:32] = grad
        send[i % 2, 32:48] = carried[i, 0:16].astype(BF16)


def beside_kernel(
    frame, hidden_01, spread_3, spread_2, own_1, w3, base,
    grad_2, grad_1, grad_bias, part_0, part_base,
):
    own = jnp.concatenate([own_1[i] for i in range(B)], axis=1)
    grad_bias[0:16] = wide_sum(own[16:32].astype(F32)).astype(BF16)
    kernel_gradient(grad_1, own, [frame, hidden_01.at[:, 0:16, :]])
    own = own_cells(spread_2)
    grad_bias[16:32] = wide_sum(own[16:32].astype(F32)).astype(BF16)
    kernel_gradient(grad_2, own, [frame, hidden_01])

    def ring(i, carry):
        part_0[i] = back_row(w3[64:80], spread_3, i, RING)
        return carry

    lax.fori_loop(H - 1, H + B + 1, ring, 0)
    for i in range(B):
        part_base[i] = base[i] + back_row(w3[0:64], spread_3, H + i, MID)


def fourth_kernel(
    before, top, bottom, after, left, right, w1, w2, slope_0, mask, carried, part_0, frame,
    grad_1, grad_2, grad_3, grad_merge, grad_bias,
    spread_2, spread_1, spread_0, sums, pieces, held,
):
    assemble((before, top, bottom, after, left, right), pieces)
    held[...] = pieces[:, 32:48, :].astype(F32)
    for i in range(B):
        held[H + i, :, MID] = carried[i, 0:16]

    def move(i, carry):
        spread_2[i] = spread(pieces[i, 0:16].astype(F32))
        spread_1[i] = spread(pieces[i, 16:32].astype(F32))
        return carry

    lax.fori_loop(0, N, move, 0)

    def ring(i, carry):
        got = (
            held[i, :, RING]
            + part_0[i]
            + back_row(w2[64:80], spread_2, i, RING)
            + back_row(w1[64:80], spread_1, i, RING)
        )
        grad = (got * slope_0[i] * mask[pl.ds(i, 1), RING]).astype(BF16)
        spread_0[i, :, RING] = spread(grad.astype(F32))
        return carry

    lax.fori_loop(H - 1, H + B + 1, ring, 0)
    own = own_cells(spread_0)
    kernel_gradient(sums.at[0:432], own, [frame])
    sums[432:864] = grad_1[...]
    sums[864:1296] = grad_2[...]
    sums[1296:1728] = grad_3[...]
    sums[1728:1856] = grad_merge[0:128]
    sums[1856:1872] = wide_sum(own[16:32].astype(F32)).astype(BF16)
    sums[1872:1904] = grad_bias[...]
    sums[1904:1920] = grad_merge[128:144]
    sums[1920:2048] = jnp.zeros((128, Z), BF16)


def last_kernel(spread_2, spread_1, spread_0, w0, w1, w2, part_base, out_ref):
    for i in range(B):
        out = (
            part_base[i]
            + back_row(w2[0:64], spread_2, H + i, MID)
            + back_row(w1[0:64], spread_1, H + i, MID)
            + back_row(w0[...], spread_0, H + i, MID)
        )
        for j in range(B):
            out_ref[pl.ds(B * i + j, 64, stride=B * B), :] = out[:, j * Z : (j + 1) * Z]


def add_kernel(x_ref, out_ref):
    def step(k, acc):
        block = x_ref[pl.ds(pl.multiple_of(k * 128, 128), 128), :].astype(F32)
        return acc + block

    acc = lax.fori_loop(0, DEVICES * ROWS // 128, step, jnp.zeros((128, Z), F32))
    total = acc[0:ROWS]
    for k in range(1, 128 // ROWS):
        total = total + acc[k * ROWS : (k + 1) * ROWS]
    block = jnp.concatenate([total] * (128 // ROWS), axis=0).astype(BF16)

    def put(k, carry):
        out_ref[pl.ds(pl.multiple_of(k * 128, 128), 128), :] = block
        return carry

    lax.fori_loop(0, DEVICES * ROWS // 128, put, 0)


def turned(block, scale):
    rows = lax.broadcasted_iota(jnp.int32, block.shape, 0)
    lanes = lax.broadcasted_iota(jnp.int32, block.shape, 1)
    return jnp.sum(jnp.where(rows == lanes, block, 0.0), axis=0, keepdims=True) * scale


def unpack_kernel(scale, x_ref, g0, g1, g2, g3, bias, weight, weight_bias):
    for k, g in enumerate((g0, g1, g2, g3)):
        g[...] = x_ref[432 * k : 432 * (k + 1), : g.shape[1]].astype(F32) * scale
    weight[...] = x_ref[1728:1792].astype(F32) * scale
    weight_bias[...] = turned(x_ref[1792:1856].astype(F32), scale)[:, :64]
    for k in range(4):
        block = x_ref[1856 + 16 * k : 1872 + 16 * k].astype(F32)
        bias[k : k + 1] = turned(block, scale)[:, :16]


def exchange(top, bottom):
    channels = top.shape[1]
    up = [(i, i + 1) for i in range(lax.axis_size("gx") - 1)]
    before = lax.ppermute(bottom, "gx", up)
    after = lax.ppermute(top, "gx", [(j, i) for i, j in up])
    side = shape((N, channels, H * Z), BF16)
    left, right = call(
        columns_kernel, [side, side], [before, top, bottom, after], name="columns"
    )
    up = [(i, i + 1) for i in range(lax.axis_size("row") - 1)]
    from_before = lax.ppermute(right, "row", up)
    from_after = lax.ppermute(left, "row", [(j, i) for i, j in up])
    return [before, top, bottom, after, from_before, from_after]


def grid_mask():
    steps = jnp.arange(N) - H
    gx = lax.axis_index("gx") * B + steps
    gy = lax.axis_index("row") * B + steps
    inside_x = (gx >= 0) & (gx < lax.axis_size("gx") * B)
    inside_y = (gy >= 0) & (gy < lax.axis_size("row") * B)
    inside = (inside_x[:, None] & inside_y[None, :]).astype(F32)
    return jnp.repeat(inside, Z, axis=1)


def body(samples, cotangent, kernel_0, kernel_1, kernel_2, kernel_3, layer_bias, merging_weight, merging_bias):
    kernels = (kernel_0, kernel_1, kernel_2, kernel_3)
    cells = B * B * Z * lax.axis_size("gx") * lax.axis_size("row") * lax.axis_size("rep")
    scale = 1.0 / math.sqrt(cells)
    taps = [k.transpose(1, 0, 2).reshape(9, 48, k.shape[2]) for k in kernels]
    flat = [k.transpose(1, 0, 2).reshape(432, k.shape[2]) for k in kernels]
    bias = jnp.broadcast_to(layer_bias.astype(F32).reshape(64, 1), (64, Z))
    merge_bias = jnp.broadcast_to(merging_bias.astype(F32)[:, None], (64, Z))
    mask = grid_mask()
    half = shape((2, 64, B * Z), BF16)
    wide = pltpu.VMEM((1024, Z), F32)
    top, bottom = call(
        pack_kernel, [half, half], [samples.reshape(1024, Z)], [wide], name="pack"
    )
    base, carried, merge_grad, w0, w1, w2, w3 = call(
        prepare_kernel,
        [shape((B, 64, B * Z), F32)] * 2
        + [shape((B, 64, B * Z), BF16)]
        + [shape((k.shape[2], 432), BF16) for k in kernels],
        [cotangent.reshape(1024, Z), merging_weight.T] + flat,
        [wide],
        flops=40_000_000,
        name="prepare",
    )
    parts = exchange(top, bottom)
    ring = shape((N, 16, (B + 2) * Z), F32)
    send = shape((2, 32, B * Z), BF16)
    frame, hidden_0, slope_0, slope_1, top, bottom = call(
        first_kernel,
        [shape((N, 64, N * Z), BF16), shape((N, 16, N * Z), BF16), ring, shape((B, 16, B * Z), F32), send, send],
        parts + [taps[0], taps[1], bias, mask],
        name="layers_0_1",
    )
    parts = exchange(top, bottom)
    hidden_01, hidden_2, hidden_3, slope_2, own_3, top, bottom = call(
        second_kernel,
        [
            shape((N, 32, N * Z), BF16),
            shape((N, 16, N * Z), BF16),
            shape((B, 16, B * Z), BF16),
            ring,
            shape((B, 48, B * Z), BF16),
            send,
            send,
        ],
        parts + [frame, taps[2], taps[3], bias, mask, carried],
        name="layers_2_3",
    )
    parts = exchange(top, bottom)
    grads = shape((432, Z), BF16)
    output, grad_3, grad_merge = call(
        merge_kernel,
        [shape((1024, Z), F32), grads, shape((144, Z), BF16)],
        [frame, hidden_01, hidden_2, hidden_3, own_3, merging_weight, merge_bias, merge_grad],
        flops=100_000_000,
        name="merge",
    )
    send = shape((2, 48, B * Z), BF16)
    spreads = shape((N, 48, N * Z), BF16)
    spread_3, spread_2, own_1, top, bottom = call(
        third_kernel,
        [spreads, spreads, shape((B, 48, B * Z), BF16), send, send],
        parts + [w2, w3, slope_1, slope_2, mask, carried],
        [pltpu.VMEM((N, 32, N * Z), BF16), pltpu.VMEM((N, 16, N * Z), F32)],
        name="gradients_2_1",
    )
    parts = exchange(top, bottom)
    grad_2, grad_1, grad_bias, part_0, part_base = call(
        beside_kernel,
        [grads, grads, shape((32, Z), BF16), ring, shape((B, 64, B * Z), F32)],
        [frame, hidden_01, spread_3, spread_2, own_1, w3, base],
        flops=200_000_000,
        name="kernel_gradients_2_1",
    )
    spread_2, spread_1, spread_0, sums = call(
        fourth_kernel,
        [spreads, spreads, spreads, shape((DEVICES * ROWS, Z), BF16)],
        parts
        + [w1, w2, slope_0, mask, carried, part_0, frame]
        + [grad_1, grad_2, grad_3, grad_merge, grad_bias],
        [pltpu.VMEM((N, 48, N * Z), BF16), pltpu.VMEM((N, 16, N * Z), F32)],
        name="gradient_0",
    )
    axes = ("gx", "row", "rep")
    spread_sums = lax.all_to_all(sums.reshape(DEVICES, ROWS, Z), axes, 0, 0, tiled=True)
    (added,) = call(
        add_kernel,
        [shape((DEVICES * ROWS, Z), BF16)],
        [spread_sums.reshape(DEVICES * ROWS, Z)],
        name="add",
    )
    totals = lax.all_to_all(added.reshape(DEVICES, ROWS, Z), axes, 0, 0, tiled=True)
    (grad_input,) = call(
        last_kernel,
        [shape((1024, Z), F32)],
        [spread_2, spread_1, spread_0, w0, w1, w2, part_base],
        flops=300_000_000,
        name="input_gradient",
    )
    unpacked = call(
        functools.partial(unpack_kernel, scale),
        [shape((432, k.shape[2]), F32) for k in kernels]
        + [shape((4, 16), F32), shape((64, 128), F32), shape((1, 64), F32)],
        [totals.reshape(DEVICES * ROWS, Z)],
        name="unpack",
    )
    grad_kernels = [g.reshape(27, 16, g.shape[1]).transpose(1, 0, 2) for g in unpacked[:4]]
    out_shape = (1, 64, B, B, Z)
    return (
        output.reshape(out_shape),
        grad_input.reshape(out_shape),
        *grad_kernels,
        unpacked[4],
        unpacked[5],
        unpacked[6].reshape(64),
    )


def solution(mesh):
    split = P("rep", None, "gx", "row", None)
    return jax.shard_map(
        body,
        mesh=mesh,
        in_specs=(split, split) + (P(),) * 7,
        out_specs=(split, split) + (P(),) * 7,
        check_vma=False,
    )
```

time: 867 us -> 183 us (0.21); the launches traced: 856 us -> 182 us
  local copies, waits for them, and re-layouts: 320 us -> 4.48 us
  waiting for transfers between devices: 196 us -> 53.9 us
  other arithmetic: 73.1 us -> 0.08 us
  blocking collectives: 101 us -> 44.4 us
  matrix products: 54.8 us -> 0 us
  starting transfers between devices: 95.7 us -> 53.6 us
  Pallas kernels: 0 us -> 24.6 us
  between operations: 15.7 us -> 1.05 us
    psum x1 -> x0, waiting for transfers between devices: 152 us -> none  [body(): lax.psum((grad_k0, grad_k1, grad_k2, grad_k3, grad_layer_bias, grad_mergi...]
    unnamed x229 -> x35, local copies, waits for them, and re-layouts: 139 us -> 4.18 us
    psum x1 -> x0, blocking collectives: 101 us -> none  [body(): lax.psum((grad_k0, grad_k1, grad_k2, grad_k3, grad_layer_bias, grad_mergi...]
    another operation x16 -> x0, local copies, waits for them, and re-layouts: 87.8 us -> none  [the longest x7 83.9 us: patches_of(): stacked = jnp.stack(pieces, axis=0)]
    reshape x22 -> x1, local copies, waits for them, and re-layouts: 86.6 us -> 0.07 us  [grid_mask(): return jnp.repeat(inside, Z, axis=1)]
    unnamed x60 -> x0, other arithmetic: 54.8 us -> none
    dot_general x15 -> x0, matrix products: 54.8 us -> none  [the longest x4 25.5 us: body(): lax.dot_general(pre_grad, patches, (((1,), (1,)), ((), ())), preferred_el...]
    ppermute x32 -> x16, starting transfers between devices: 95.6 us -> 46.7 us  [the longest x4 19.5 us: exchange(): from_before = lax.ppermute(right, 'row', up)]
  transfers between devices with their start and end apart: 33 -> 17, of which waited for: 15 -> 13; matrix products, arithmetic and copies ran while one was open for 7% -> 0% of each run, Pallas kernels for 0% -> 4%
where the time goes in v1:
time: 183 us; the launch traced here: 182 us
  waiting for transfers between devices  53.9 us (29%)
  starting transfers between devices  53.6 us (29%)
  blocking collectives  44.4 us (24%)
  Pallas kernels  24.6 us (13%)
  local copies, waits for them, and re-layouts  4.48 us (2%)
    all_to_all x1, blocking collectives, body(): lax.all_to_all(sums.reshape(DEVICES, ROWS, Z), axes, 0, 0, tiled=True)  44.4 us
    pallas_call x15, Pallas kernels, call(): pl.pallas_call(kernel, out_shape=list(outs), in_specs=[pl.BlockSpec(memor...  24.6 us
    ppermute x4, waiting for transfers between devices, exchange(): from_after = lax.ppermute(left, 'row', [(j, i) for i, j in up])  19.7 us
    ppermute x4, starting transfers between devices, exchange(): from_before = lax.ppermute(right, 'row', up)  19.5 us
    ppermute x4, starting transfers between devices, exchange(): before = lax.ppermute(bottom, 'gx', up)  16.7 us
    all_to_all x1, waiting for transfers between devices, body(): lax.all_to_all(added.reshape(DEVICES, ROWS, Z), axes, 0, 0, tiled=True)  16.4 us
    ppermute x4, waiting for transfers between devices, exchange(): after = lax.ppermute(top, 'gx', [(j, i) for i, j in up])  14.9 us
    all_to_all x1, starting transfers between devices, body(): lax.all_to_all(added.reshape(DEVICES, ROWS, Z), axes, 0, 0, tiled=True)  6.97 us
  transfers between devices with their start and end apart: 17, of which 13 were waited for; matrix products, arithmetic and copies ran while one was open for 0% of the time, Pallas kernels for 4%

profile of v1, /device:TPU:1, one launch (start us, length us, event | category | flops | bytes accessed | tf_op | source)
XLA Modules:
  0.0 182.2 jit_solution(6682929813285155817)
XLA Ops:
  1.8 4.0 %collective-permute-start = (bf16[2,64,512]{2,1,0:T(8,128)(2,1)S(1)}, bf16[2,64,512]{2,1,0:T(8,128)(2,1)S(1)}, u32[]{:S(2)}, u32[]{:S(2)}) collective-permute-start(bf16[2,64,512]{2,1,0:T(8,128)(2,1)S(1)} %get-tuple-element.62.bottom), channel_id=1, source_target_pairs={{0,32},{32,64},{64,96},{96,128},{128,160},{160,192},{192,224},{1,3... | collective-permute-start | bytes 393224 | tf_op jit(solution)/shard_map/ppermute | solution.py:374
  7.9 3.6 %collective-permute-done.1.after = bf16[2,64,512]{2,1,0:T(8,128)(2,1)S(1)} collective-permute-done((bf16[2,64,512]{2,1,0:T(8,128)(2,1)S(1)}, bf16[2,64,512]{2,1,0:T(8,128)(2,1)S(1)}, u32[]{:S(2)}, u32[]{:S(2)}) %collective-permute-start.1) | collective-permute-done | bytes 131104 | tf_op jit(solution)/shard_map/ppermute | solution.py:375
  11.5 5.0 %collective-permute-start.2 = (bf16[8,64,256]{2,1,0:T(8,128)(2,1)S(1)}, bf16[8,64,256]{2,1,0:T(8,128)(2,1)S(1)}, u32[]{:S(2)}, u32[]{:S(2)}) collective-permute-start(bf16[8,64,256]{2,1,0:T(8,128)(2,1)S(1)} %get-tuple-element.64), channel_id=1, source_target_pairs={{0,2},{2,4},{4,6},{6,8},{8,10},{10,12},{12,14},{14,16},{16,18},{18... | collective-permute-start | bytes 786440 | tf_op jit(solution)/shard_map/ppermute | solution.py:381
  19.8 5.3 %collective-permute-done.3.right = bf16[8,64,256]{2,1,0:T(8,128)(2,1)S(1)} collective-permute-done((bf16[8,64,256]{2,1,0:T(8,128)(2,1)S(1)}, bf16[8,64,256]{2,1,0:T(8,128)(2,1)S(1)}, u32[]{:S(2)}, u32[]{:S(2)}) %collective-permute-start.3) | collective-permute-done | bytes 262176 | tf_op jit(solution)/shard_map/ppermute | solution.py:382
  25.2 3.8 %layers_0_1.1 = (bf16[8,64,1024]{2,1,0:T(8,128)(2,1)S(1)}, bf16[8,16,1024]{2,1,0:T(8,128)(2,1)}, f32[8,16,768]{2,1,0:T(8,128)S(1)}, f32[4,16,512]{2,1,0:T(8,128)...) custom-call(bf16[2,64,512]{2,1,0:T(8,128)(2,1)S(1)} %collective-permute-done.before, ...), custom_call_target="tpu_custom_call" | custom-call | flops 1000000 | bytes 3204608 | tf_op jit(solution)/shard_map/layers_0_1/pallas_call | solution.py:30
  29.8 3.1 %collective-permute-start.4 = (bf16[2,32,512]{2,1,0:T(8,128)(2,1)S(1)}, bf16[2,32,512]{2,1,0:T(8,128)(2,1)S(1)}, u32[]{:S(2)}, u32[]{:S(2)}) collective-permute-start(bf16[2,32,512]{2,1,0:T(8,128)(2,1)S(1)} %get-tuple-element.67.bottom), channel_id=1, source_target_pairs={{0,32},{32,64},{64,96},{96,128},{128,160},{160,192},{192,224},{1,3... | collective-permute-start | bytes 196616 | tf_op jit(solution)/shard_map/ppermute | solution.py:374
  34.4 3.7 %collective-permute-done.5.after = bf16[2,32,512]{2,1,0:T(8,128)(2,1)S(1)} collective-permute-done((bf16[2,32,512]{2,1,0:T(8,128)(2,1)S(1)}, bf16[2,32,512]{2,1,0:T(8,128)(2,1)S(1)}, u32[]{:S(2)}, u32[]{:S(2)}) %collective-permute-start.5) | collective-permute-done | bytes 65568 | tf_op jit(solution)/shard_map/ppermute | solution.py:375
  38.1 4.3 %collective-permute-start.6 = (bf16[8,32,256]{2,1,0:T(8,128)(2,1)S(1)}, bf16[8,32,256]{2,1,0:T(8,128)(2,1)S(1)}, u32[]{:S(2)}, u32[]{:S(2)}) collective-permute-start(bf16[8,32,256]{2,1,0:T(8,128)(2,1)S(1)} %get-tuple-element.69), channel_id=1, source_target_pairs={{0,2},{2,4},{4,6},{6,8},{8,10},{10,12},{12,14},{14,16},{16,18},{18... | collective-permute-start | bytes 393224 | tf_op jit(solution)/shard_map/ppermute | solution.py:381
  44.3 7.8 %collective-permute-done.7.right = bf16[8,32,256]{2,1,0:T(8,128)(2,1)S(1)} collective-permute-done((bf16[8,32,256]{2,1,0:T(8,128)(2,1)S(1)}, bf16[8,32,256]{2,1,0:T(8,128)(2,1)S(1)}, u32[]{:S(2)}, u32[]{:S(2)}) %collective-permute-start.7) | collective-permute-done | bytes 131104 | tf_op jit(solution)/shard_map/ppermute | solution.py:382
  52.1 3.5 %layers_2_3.1 = (bf16[8,32,1024]{2,1,0:T(8,128)(2,1)S(1)}, bf16[8,16,1024]{2,1,0:T(8,128)(2,1)S(1)}, bf16[4,16,512]{2,1,0:T(8,128)(2,1)S(1)}, f32[8,16,768]{2,1,...) custom-call(bf16[2,32,512]{2,1,0:T(8,128)(2,1)S(1)} %collective-perm, ...), custom_call_target="tpu_custom_call" | custom-call | flops 1000000 | bytes 3915264 | tf_op jit(solution)/shard_map/layers_2_3/pallas_call | solution.py:30
  55.7 5.0 %collective-permute-start.8 = (bf16[2,32,512]{2,1,0:T(8,128)(2,1)S(1)}, bf16[2,32,512]{2,1,0:T(8,128)(2,1)S(1)}, u32[]{:S(2)}, u32[]{:S(2)}) collective-permute-start(bf16[2,32,512]{2,1,0:T(8,128)(2,1)S(1)} %get-tuple-element.78.bottom), channel_id=1, source_target_pairs={{0,32},{32,64},{64,96},{96,128},{128,160},{160,192},{192,224},{1,3... | collective-permute-start | bytes 196616 | tf_op jit(solution)/shard_map/ppermute | solution.py:374
  62.0 3.7 %collective-permute-done.9.after = bf16[2,32,512]{2,1,0:T(8,128)(2,1)S(1)} collective-permute-done((bf16[2,32,512]{2,1,0:T(8,128)(2,1)S(1)}, bf16[2,32,512]{2,1,0:T(8,128)(2,1)S(1)}, u32[]{:S(2)}, u32[]{:S(2)}) %collective-permute-start.9) | collective-permute-done | bytes 65568 | tf_op jit(solution)/shard_map/ppermute | solution.py:375
  65.7 5.8 %collective-permute-start.10 = (bf16[8,32,256]{2,1,0:T(8,128)(2,1)S(1)}, bf16[8,32,256]{2,1,0:T(8,128)(2,1)S(1)}, u32[]{:S(2)}, u32[]{:S(2)}) collective-permute-start(bf16[8,32,256]{2,1,0:T(8,128)(2,1)S(1)} %get-tuple-element.80), channel_id=1, source_target_pairs={{0,2},{2,4},{4,6},{6,8},{8,10},{10,12},{12,14},{14,16},{16,18},{18... | collective-permute-start | bytes 393224 | tf_op jit(solution)/shard_map/ppermute | solution.py:381
  73.4 5.3 %collective-permute-done.11.right = bf16[8,32,256]{2,1,0:T(8,128)(2,1)S(1)} collective-permute-done((bf16[8,32,256]{2,1,0:T(8,128)(2,1)S(1)}, bf16[8,32,256]{2,1,0:T(8,128)(2,1)S(1)}, u32[]{:S(2)}, u32[]{:S(2)}) %collective-permute-start.11) | collective-permute-done | bytes 131104 | tf_op jit(solution)/shard_map/ppermute | solution.py:382
  78.7 3.2 %gradients_2_1.1 = (bf16[8,48,1024]{2,1,0:T(8,128)(2,1)S(1)}, bf16[8,48,1024]{2,1,0:T(8,128)(2,1)S(1)}, bf16[4,48,512]{2,1,0:T(8,128)(2,1)S(1)}, bf16[2,48,512]{2,1,0:T(8,128)(2,1)S(1)}, bf16[2,48,512]{2,1,0:T(8,128)(2,1)S(1)}) custom-call(bf16[2,32,512]{2,1,0:T(8,128)(2,1)S(1)} %collective-permute-done.8.before, ...), custom_call_target="tpu_custom_call" | custom-call | flops 1000000 | bytes 3751424 | tf_op jit(solution)/shard_map/gradients_2_1/pallas_call | solution.py:30
  81.9 4.6 %collective-permute-start.12 = (bf16[2,48,512]{2,1,0:T(8,128)(2,1)S(1)}, bf16[2,48,512]{2,1,0:T(8,128)(2,1)S(1)}, u32[]{:S(2)}, u32[]{:S(2)}) collective-permute-start(bf16[2,48,512]{2,1,0:T(8,128)(2,1)S(1)} %get-tuple-element.86.bottom), channel_id=1, source_target_pairs={{0,32},{32,64},{64,96},{96,128},{128,160},{160,192},{192,224},{1,3... | collective-permute-start | bytes 294920 | tf_op jit(solution)/shard_map/ppermute | solution.py:374
  88.2 3.9 %collective-permute-done.13.after = bf16[2,48,512]{2,1,0:T(8,128)(2,1)S(1)} collective-permute-done((bf16[2,48,512]{2,1,0:T(8,128)(2,1)S(1)}, bf16[2,48,512]{2,1,0:T(8,128)(2,1)S(1)}, u32[]{:S(2)}, u32[]{:S(2)}) %collective-permute-start.13) | collective-permute-done | bytes 98336 | tf_op jit(solution)/shard_map/ppermute | solution.py:375
  92.2 4.5 %collective-permute-start.14 = (bf16[8,48,256]{2,1,0:T(8,128)(2,1)S(1)}, bf16[8,48,256]{2,1,0:T(8,128)(2,1)S(1)}, u32[]{:S(2)}, u32[]{:S(2)}) collective-permute-start(bf16[8,48,256]{2,1,0:T(8,128)(2,1)S(1)} %get-tuple-element.88), channel_id=1, source_target_pairs={{0,2},{2,4},{4,6},{6,8},{8,10},{10,12},{12,14},{14,16},{16,18},{18... | collective-permute-start | bytes 589832 | tf_op jit(solution)/shard_map/ppermute | solution.py:381
  98.1 1.9 %merge.2 = (f32[1024,128]{1,0:T(8,128)}, bf16[432,128]{1,0:T(8,128)(2,1)S(1)}, bf16[144,128]{1,0:T(8,128)(2,1)S(1)}) custom-call(bf16[8,64,1024]{2,1,0:T(8,128)(2,1)S(1)} %get-tuple-element.66.frame, bf16[8,32,1024]{2,1,0:T(8,128)(2,1)S(1)} %get-tuple-element.72.hidden_01, bf16[8,16,1024]{2,1,0:T(8,128)(2,1)S(1)} %get-tuple-element.73.hidden_2, ...), custom_call_target="tpu_custom_call" | custom-call | flops 100000000 | bytes 3080192 | tf_op jit(solution)/shard_map/merge/pallas_call | solution.py:30
  100.0 3.5 %kernel_gradients_2_1.1 = (bf16[432,128]{1,0:T(8,128)(2,1)S(1)}, bf16[432,128]{1,0:T(8,128)(2,1)S(1)}, bf16[32,128]{1,0:T(8,128)(2,1)S(1)}, f32[8,16,768]{2,1,0:T(8,128)S(1)}, f32[4,64,512]{2,1,0:T(8,128)S(1)}) custom-call(bf16[8,64,1024]{2,1,0:T(8,128)(2,1)S(1)} %get-tuple-element.66.frame, bf16[8,32,1024]{2,1,0:T(8,128)(2,1)S(1)} %get-tuple-element.72.hidden_01, ...), custom_call_target="tpu_custom_call" | custom-call | flops 200000000 | bytes 5110272 | tf_op jit(solution)/shard_map/kernel_gradients_2_1/pallas_call | solution.py:30
  104.8 4.0 %gradient_0.1 = (bf16[8,48,1024]{2,1,0:T(8,128)(2,1)S(1)}, bf16[8,48,1024]{2,1,0:T(8,128)(2,1)S(1)}, bf16[8,48,1024]{2,1,0:T(8,128)(2,1)S(1)}, bf16[2048,128]{1,0:T(8,128)(2,1)S(1)}) custom-call(bf16[2,48,512]{2,1,0:T(8,128)(2,1)S(1)} %collective-permute-done.12.before, bf16[2,48,512]{2,1,0:T(8,128)(2,1)S(1)} %get-tuple-element.87.top, ...), custom_call_target="tpu_custom_call" | custom-call | flops 1000000 | bytes 6590976 | tf_op jit(solution)/shard_map/gradient_0/pallas_call | solution.py:30
  108.8 44.4 %all_to_all.10 = bf16[256,8,128]{2,1,0:T(8,128)(2,1)S(1)} all-to-all(bf16[256,8,128]{2,1,0:T(8,128)(2,1)S(1)} %bitcast.46), channel_id=1, replica_groups=mesh['gx'=8,'row'=16,'rep'=2] {'gx','row','rep'}, dimensions={0} | all-to-all | bytes 1048576 | tf_op jit(solution)/shard_map/all_to_all | solution.py:480
  154.3 7.0 %all-to-all-start.1 = ((bf16[256,8,128]{2,1,0:T(8,128)(2,1)}), bf16[256,8,128]{2,1,0:T(8,128)(2,1)S(1)}, u32[]{:S(2)}, u32[]{:S(2)}) async-start(bf16[256,8,128]{2,1,0:T(8,128)(2,1)} %bitcast.20), calls=%async_computation.1 | async-start | bytes 1048576 | tf_op jit(solution)/shard_map/all_to_all | solution.py:487
  164.9 16.4 %all-to-all-done.1 = bf16[256,8,128]{2,1,0:T(8,128)(2,1)S(1)} async-done(((bf16[256,8,128]{2,1,0:T(8,128)(2,1)}), bf16[256,8,128]{2,1,0:T(8,128)(2,1)S(1)}, u32[]{:S(2)}, u32[]{:S(2)}) %all-to-all-start.1) | async-done | bytes 524320 | tf_op jit(solution)/shard_map/all_to_all | solution.py:487
  (67 shorter events, 23.9 us)
Async XLA Ops:
  1.8 6.1 %collective-permute-start = (bf16[2,64,512]{2,1,0:T(8,128)(2,1)S(1)}, bf16[2,64,512]{2,1,0:T(8,128)(2,1)S(1)}, u32[]{:S(2)}, u32[]{:S(2)}) collective-permute-start(bf16[2,64,512]{2,1,0:T(8,128)(2,1)S(1)} %get-tuple-element.62.bottom), channel_id=1, source_target_pairs={{0,32},{32,64},{64,96},{96,128},{128,160},{160,192},{192,224},{1,3... | collective-permute-start | bytes 393224 | tf_op jit(solution)/shard_map/ppermute | solution.py:374
  5.8 5.7 %collective-permute-start.1 = (bf16[2,64,512]{2,1,0:T(8,128)(2,1)S(1)}, bf16[2,64,512]{2,1,0:T(8,128)(2,1)S(1)}, u32[]{:S(2)}, u32[]{:S(2)}) collective-permute-start(bf16[2,64,512]{2,1,0:T(8,128)(2,1)S(1)} %get-tuple-element.63.top), channel_id=1, source_target_pairs={{32,0},{64,32},{96,64},{128,96},{160,128},{192,160},{224,192},{33,... | collective-permute-start | bytes 393224 | tf_op jit(solution)/shard_map/ppermute | solution.py:375
  11.5 13.7 %copy-start.2 = (bf16[16,27,64]{2,0,1:T(8,128)(2,1)S(1)}, bf16[16,27,64]{2,0,1:T(8,128)(2,1)}, u32[]{:S(2)}) copy-start(bf16[16,27,64]{2,0,1:T(8,128)(2,1)} %param.11) | copy-start | bytes 165892
  11.5 13.7 %copy-start.3 = (bf16[16,27,80]{2,0,1:T(8,128)(2,1)S(1)}, bf16[16,27,80]{2,0,1:T(8,128)(2,1)}, u32[]{:S(2)}) copy-start(bf16[16,27,80]{2,0,1:T(8,128)(2,1)} %param.12) | copy-start | bytes 207364
  11.5 8.3 %collective-permute-start.2 = (bf16[8,64,256]{2,1,0:T(8,128)(2,1)S(1)}, bf16[8,64,256]{2,1,0:T(8,128)(2,1)S(1)}, u32[]{:S(2)}, u32[]{:S(2)}) collective-permute-start(bf16[8,64,256]{2,1,0:T(8,128)(2,1)S(1)} %get-tuple-element.64), channel_id=1, source_target_pairs={{0,2},{2,4},{4,6},{6,8},{8,10},{10,12},{12,14},{14,16},{16,18},{18... | collective-permute-start | bytes 786440 | tf_op jit(solution)/shard_map/ppermute | solution.py:381
  16.5 8.6 %collective-permute-start.3 = (bf16[8,64,256]{2,1,0:T(8,128)(2,1)S(1)}, bf16[8,64,256]{2,1,0:T(8,128)(2,1)S(1)}, u32[]{:S(2)}, u32[]{:S(2)}) collective-permute-start(bf16[8,64,256]{2,1,0:T(8,128)(2,1)S(1)} %get-tuple-element.65), channel_id=1, source_target_pairs={{2,0},{4,2},{6,4},{8,6},{10,8},{12,10},{14,12},{16,14},{18,16},{20... | collective-permute-start | bytes 786440 | tf_op jit(solution)/shard_map/ppermute | solution.py:382
  25.2 18.6 %copy-start.10 = (bf16[1,64,4,4,128]{4,3,2,1,0:T(4,128)(2,1)S(1)}, bf16[1,64,4,4,128]{4,3,2,1,0:T(4,128)(2,1)}, u32[]{:S(2)}) copy-start(bf16[1,64,4,4,128]{4,3,2,1,0:T(4,128)(2,1)} %param.10) | copy-start | bytes 786436
  29.8 4.6 %collective-permute-start.4 = (bf16[2,32,512]{2,1,0:T(8,128)(2,1)S(1)}, bf16[2,32,512]{2,1,0:T(8,128)(2,1)S(1)}, u32[]{:S(2)}, u32[]{:S(2)}) collective-permute-start(bf16[2,32,512]{2,1,0:T(8,128)(2,1)S(1)} %get-tuple-element.67.bottom), channel_id=1, source_target_pairs={{0,32},{32,64},{64,96},{96,128},{128,160},{160,192},{192,224},{1,3... | collective-permute-start | bytes 196616 | tf_op jit(solution)/shard_map/ppermute | solution.py:374
  32.9 10.9 %copy-start.4 = (bf16[16,27,96]{2,0,1:T(8,128)(2,1)S(1)}, bf16[16,27,96]{2,0,1:T(8,128)(2,1)}, u32[]{:S(2)}) copy-start(bf16[16,27,96]{2,0,1:T(8,128)(2,1)} %param.13) | copy-start | bytes 248836
  32.9 10.9 %copy-start.5 = (bf16[16,27,112]{2,0,1:T(8,128)(2,1)S(1)}, bf16[16,27,112]{2,0,1:T(8,128)(2,1)}, u32[]{:S(2)}) copy-start(bf16[16,27,112]{2,0,1:T(8,128)(2,1)} %param.14) | copy-start | bytes 290308
  32.9 5.1 %collective-permute-start.5 = (bf16[2,32,512]{2,1,0:T(8,128)(2,1)S(1)}, bf16[2,32,512]{2,1,0:T(8,128)(2,1)S(1)}, u32[]{:S(2)}, u32[]{:S(2)}) collective-permute-start(bf16[2,32,512]{2,1,0:T(8,128)(2,1)S(1)} %get-tuple-element.68.top), channel_id=1, source_target_pairs={{32,0},{64,32},{96,64},{128,96},{160,128},{192,160},{224,192},{33,... | collective-permute-start | bytes 196616 | tf_op jit(solution)/shard_map/ppermute | solution.py:375
  38.1 6.2 %collective-permute-start.6 = (bf16[8,32,256]{2,1,0:T(8,128)(2,1)S(1)}, bf16[8,32,256]{2,1,0:T(8,128)(2,1)S(1)}, u32[]{:S(2)}, u32[]{:S(2)}) collective-permute-start(bf16[8,32,256]{2,1,0:T(8,128)(2,1)S(1)} %get-tuple-element.69), channel_id=1, source_target_pairs={{0,2},{2,4},{4,6},{6,8},{8,10},{10,12},{12,14},{14,16},{16,18},{18... | collective-permute-start | bytes 393224 | tf_op jit(solution)/shard_map/ppermute | solution.py:381
  42.4 9.8 %collective-permute-start.7 = (bf16[8,32,256]{2,1,0:T(8,128)(2,1)S(1)}, bf16[8,32,256]{2,1,0:T(8,128)(2,1)S(1)}, u32[]{:S(2)}, u32[]{:S(2)}) collective-permute-start(bf16[8,32,256]{2,1,0:T(8,128)(2,1)S(1)} %get-tuple-element.70), channel_id=1, source_target_pairs={{2,0},{4,2},{6,4},{8,6},{10,8},{12,10},{14,12},{16,14},{18,16},{20... | collective-permute-start | bytes 393224 | tf_op jit(solution)/shard_map/ppermute | solution.py:382
  44.3 11.4 %copy-start.12 = (bf16[64,432]{1,0:T(8,128)(2,1)}, bf16[64,432]{1,0:T(8,128)(2,1)S(1)}, u32[]{:S(2)}) copy-start(bf16[64,432]{1,0:T(8,128)(2,1)S(1)} %get-tuple-element.105.w0) | copy-start | bytes 165892
  44.3 60.5 %copy-start.8 = (bf16[80,432]{1,0:T(8,128)(2,1)}, bf16[80,432]{1,0:T(8,128)(2,1)S(1)}, u32[]{:S(2)}) copy-start(bf16[80,432]{1,0:T(8,128)(2,1)S(1)} %get-tuple-element.90.w1) | copy-start | bytes 207364
  55.7 6.3 %collective-permute-start.8 = (bf16[2,32,512]{2,1,0:T(8,128)(2,1)S(1)}, bf16[2,32,512]{2,1,0:T(8,128)(2,1)S(1)}, u32[]{:S(2)}, u32[]{:S(2)}) collective-permute-start(bf16[2,32,512]{2,1,0:T(8,128)(2,1)S(1)} %get-tuple-element.78.bottom), channel_id=1, source_target_pairs={{0,32},{32,64},{64,96},{96,128},{128,160},{160,192},{192,224},{1,3... | collective-permute-start | bytes 196616 | tf_op jit(solution)/shard_map/ppermute | solution.py:374
  60.7 5.0 %collective-permute-start.9 = (bf16[2,32,512]{2,1,0:T(8,128)(2,1)S(1)}, bf16[2,32,512]{2,1,0:T(8,128)(2,1)S(1)}, u32[]{:S(2)}, u32[]{:S(2)}) collective-permute-start(bf16[2,32,512]{2,1,0:T(8,128)(2,1)S(1)} %get-tuple-element.79.top), channel_id=1, source_target_pairs={{32,0},{64,32},{96,64},{128,96},{160,128},{192,160},{224,192},{33,... | collective-permute-start | bytes 196616 | tf_op jit(solution)/shard_map/ppermute | solution.py:375
  65.7 7.7 %collective-permute-start.10 = (bf16[8,32,256]{2,1,0:T(8,128)(2,1)S(1)}, bf16[8,32,256]{2,1,0:T(8,128)(2,1)S(1)}, u32[]{:S(2)}, u32[]{:S(2)}) collective-permute-start(bf16[8,32,256]{2,1,0:T(8,128)(2,1)S(1)} %get-tuple-element.80), channel_id=1, source_target_pairs={{0,2},{2,4},{4,6},{6,8},{8,10},{10,12},{12,14},{14,16},{16,18},{18... | collective-permute-start | bytes 393224 | tf_op jit(solution)/shard_map/ppermute | solution.py:381
  71.5 7.2 %collective-permute-start.11 = (bf16[8,32,256]{2,1,0:T(8,128)(2,1)S(1)}, bf16[8,32,256]{2,1,0:T(8,128)(2,1)S(1)}, u32[]{:S(2)}, u32[]{:S(2)}) collective-permute-start(bf16[8,32,256]{2,1,0:T(8,128)(2,1)S(1)} %get-tuple-element.81), channel_id=1, source_target_pairs={{2,0},{4,2},{6,4},{8,6},{10,8},{12,10},{14,12},{16,14},{18,16},{20... | collective-permute-start | bytes 393224 | tf_op jit(solution)/shard_map/ppermute | solution.py:382
  81.9 6.3 %collective-permute-start.12 = (bf16[2,48,512]{2,1,0:T(8,128)(2,1)S(1)}, bf16[2,48,512]{2,1,0:T(8,128)(2,1)S(1)}, u32[]{:S(2)}, u32[]{:S(2)}) collective-permute-start(bf16[2,48,512]{2,1,0:T(8,128)(2,1)S(1)} %get-tuple-element.86.bottom), channel_id=1, source_target_pairs={{0,32},{32,64},{64,96},{96,128},{128,160},{160,192},{192,224},{1,3... | collective-permute-start | bytes 294920 | tf_op jit(solution)/shard_map/ppermute | solution.py:374
  86.6 5.5 %collective-permute-start.13 = (bf16[2,48,512]{2,1,0:T(8,128)(2,1)S(1)}, bf16[2,48,512]{2,1,0:T(8,128)(2,1)S(1)}, u32[]{:S(2)}, u32[]{:S(2)}) collective-permute-start(bf16[2,48,512]{2,1,0:T(8,128)(2,1)S(1)} %get-tuple-element.87.top), channel_id=1, source_target_pairs={{32,0},{64,32},{96,64},{128,96},{160,128},{192,160},{224,192},{33,... | collective-permute-start | bytes 294920 | tf_op jit(solution)/shard_map/ppermute | solution.py:375
  92.2 11.3 %collective-permute-start.14 = (bf16[8,48,256]{2,1,0:T(8,128)(2,1)S(1)}, bf16[8,48,256]{2,1,0:T(8,128)(2,1)S(1)}, u32[]{:S(2)}, u32[]{:S(2)}) collective-permute-start(bf16[8,48,256]{2,1,0:T(8,128)(2,1)S(1)} %get-tuple-element.88), channel_id=1, source_target_pairs={{0,2},{2,4},{4,6},{6,8},{8,10},{10,12},{12,14},{14,16},{16,18},{18... | collective-permute-start | bytes 589832 | tf_op jit(solution)/shard_map/ppermute | solution.py:381
  96.7 8.1 %collective-permute-start.15 = (bf16[8,48,256]{2,1,0:T(8,128)(2,1)S(1)}, bf16[8,48,256]{2,1,0:T(8,128)(2,1)S(1)}, u32[]{:S(2)}, u32[]{:S(2)}) collective-permute-start(bf16[8,48,256]{2,1,0:T(8,128)(2,1)S(1)} %get-tuple-element.89), channel_id=1, source_target_pairs={{2,0},{4,2},{6,4},{8,6},{10,8},{12,10},{14,12},{16,14},{18,16},{20... | collective-permute-start | bytes 589832 | tf_op jit(solution)/shard_map/ppermute | solution.py:382
  154.3 27.0 %all-to-all-start.1 = ((bf16[256,8,128]{2,1,0:T(8,128)(2,1)}), bf16[256,8,128]{2,1,0:T(8,128)(2,1)S(1)}, u32[]{:S(2)}, u32[]{:S(2)}) async-start(bf16[256,8,128]{2,1,0:T(8,128)(2,1)} %bitcast.20), calls=%async_computation.1 | async-start | bytes 1048576 | tf_op jit(solution)/shard_map/all_to_all | solution.py:487
  (10 other events, 37.8 us)

commit v2 on v1

--- a/solution.py
+++ b/solution.py
@@ -16,8 +16,9 @@
 N = B + 2 * H
 MID = slice(H * Z, (H + B) * Z)
 RING = slice((H - 1) * Z, (H + B + 1) * Z)
-DEVICES = 256
+GROUP = 128
 ROWS = 8
+HALF = GROUP * ROWS
 VMEM_LIMIT = 24 * 2**20
 
 
@@ -30,7 +31,9 @@
     return pl.pallas_call(
         kernel,
         out_shape=list(outs),
-        in_specs=[pl.BlockSpec(memory_space=pltpu.VMEM)] * len(args),
+        in_specs=[
+            pl.BlockSpec(memory_space=pltpu.SMEM if a.dtype == jnp.int32 else pltpu.VMEM) for a in args
+        ],
         out_specs=[pl.BlockSpec(memory_space=pltpu.VMEM)] * len(outs),
         scratch_shapes=list(scratch),
         compiler_params=pltpu.CompilerParams(vmem_limit_bytes=VMEM_LIMIT),
@@ -59,44 +62,52 @@
 
 def conv_row(kernel_ref, sources, i, lanes):
     n = lanes.stop - lanes.start
-    acc = jnp.zeros((48, n), F32)
-    for a in range(3):
-        for b in range(3):
-            cut = pl.ds(lanes.start + (b - 1) * Z, n)
-            rhs = [s[i + a - 1, :, cut] for s in sources]
-            rhs = rhs[0] if len(rhs) == 1 else jnp.concatenate(rhs, axis=0)
-            acc = acc + jnp.dot(kernel_ref[3 * a + b], rhs, preferred_element_type=F32)
+    cut = slice(lanes.start - Z, lanes.stop + Z)
+    rhs = jnp.concatenate([s[i + a - 1, :, cut] for a in range(3) for s in sources], axis=0)
+    got = jnp.dot(kernel_ref[...], rhs, preferred_element_type=F32)
+    acc = got[:48, :n] + got[48:96, Z : Z + n] + got[96:, 2 * Z :]
     not_first, not_last = lane_moves(16, n)
     return from_left(acc[:16], not_first) + acc[16:32] + from_right(acc[32:], not_last)
 
 
-def back_row(weights, spread_ref, i, lanes):
-    n = lanes.stop - lanes.start
-    pieces = [
-        spread_ref[i + 1 - a, :, pl.ds(lanes.start + (1 - b) * Z, n)]
-        for a in range(3)
-        for b in range(3)
-    ]
-    return jnp.dot(weights, jnp.concatenate(pieces, axis=0), preferred_element_type=F32)
+def back_row(turned_ref, channels, spread_ref, i, lanes):
+    n, q = lanes.stop - lanes.start, channels.stop - channels.start
+    cut = slice(lanes.start - Z, lanes.stop + Z)
+    lhs = jnp.concatenate([turned_ref[b, channels] for b in range(3)], axis=0)
+    rhs = jnp.concatenate([spread_ref[i + 1 - a, :, cut] for a in range(3)], axis=0)
+    got = jnp.dot(lhs, rhs, preferred_element_type=F32)
+    return got[:q, 2 * Z :] + got[q : 2 * q, Z : Z + n] + got[2 * q :, :n]
 
 
 def kernel_gradient(out_ref, own, sources):
+    gap = jnp.zeros((48, Z), BF16)
+    lhs = jnp.concatenate(
+        [
+            jnp.concatenate(
+                [
+                    jnp.concatenate([gap] * b + [rows] + [gap] * (2 - b), axis=1)
+                    for b in range(3)
+                ],
+                axis=0,
+            )
+            for rows in own
+        ],
+        axis=1,
+    )
     for a in range(3):
-        for b in range(3):
-            cut = pl.ds((H + b - 1) * Z, B * Z)
-            rhs = jnp.concatenate(
-                [jnp.concatenate([s[H + i + a - 1, :, cut] for s in sources], axis=0) for i in range(B)],
-                axis=1,
-            )
-            got = lax.dot_general(own, rhs, (((1,), (1,)), ((), ())), preferred_element_type=F32)
-            t = 48 * (3 * a + b)
-            out_ref[t : t + 48, : got.shape[1]] = got.astype(BF16)
-            if got.shape[1] < Z:
-                out_ref[t : t + 48, got.shape[1] :] = jnp.zeros((48, Z - got.shape[1]), BF16)
+        rhs = jnp.concatenate(
+            [jnp.concatenate([s[H + i + a - 1, :, RING] for s in sources], axis=0) for i in range(B)],
+            axis=1,
+        )
+        got = lax.dot_general(lhs, rhs, (((1,), (1,)), ((), ())), preferred_element_type=F32)
+        rows = slice(144 * a, 144 * (a + 1))
+        out_ref[rows, : got.shape[1]] = got.astype(out_ref.dtype)
+        if got.shape[1] < Z:
+            out_ref[rows, got.shape[1] :] = jnp.zeros((144, Z - got.shape[1]), out_ref.dtype)
 
 
 def own_cells(spread_ref):
-    return jnp.concatenate([spread_ref[H + i, :, MID] for i in range(B)], axis=1)
+    return [spread_ref[H + i, :, MID] for i in range(B)]
 
 
 def activate(value):
@@ -116,8 +127,13 @@
     frame[:, :, (H + B) * Z :] = right[...]
 
 
-def wide_sum(v):
-    return jnp.broadcast_to(jnp.sum(v, axis=1, keepdims=True), (v.shape[0], Z))
+def wide_sum(blocks):
+    total = sum(block.astype(F32) for block in blocks)
+    return jnp.broadcast_to(jnp.sum(total, axis=1, keepdims=True), (total.shape[0], Z))
+
+
+def cell_sum(own):
+    return wide_sum([rows[16:32] for rows in own])
 
 
 def pack_kernel(x_ref, top_ref, bottom_ref, wide):
@@ -135,9 +151,12 @@
         right[2 * r : 2 * r + 2] = ref[:, :, (B - H) * Z :]
 
 
-def prepare_kernel(cot_ref, merge_t, k0, k1, k2, k3, base, carried, merge_grad, w0, w1, w2, w3, wide):
-    for k_ref, w_ref in ((k0, w0), (k1, w1), (k2, w2), (k3, w3)):
-        w_ref[...] = jnp.transpose(k_ref[...].astype(F32)).astype(BF16)
+def prepare_kernel(cot_ref, merge_t, k0, k1, k2, k3, base, carried, merge_grad, w0, w1, w2, w3, t0, t1, t2, t3, wide):
+    for k_ref, w_ref, t_ref in ((k0, w0, t0), (k1, w1, t1), (k2, w2, t2), (k3, w3, t3)):
+        w_ref[...] = jnp.concatenate([k_ref[144 * a : 144 * (a + 1)] for a in range(3)], axis=1)
+        for b in range(3):
+            rows = [k_ref[48 * t : 48 * (t + 1)] for t in (b, 3 + b, 6 + b)]
+            t_ref[b] = jnp.transpose(jnp.concatenate(rows, axis=0).astype(F32)).astype(BF16)
     wide[...] = cot_ref[...].astype(F32)
     for i in range(B):
         cot = jnp.concatenate(
@@ -203,7 +222,6 @@
     out_ref, grad_3, grad_merge,
 ):
     total = jnp.zeros((64, 128), F32)
-    total_bias = jnp.zeros((64, B * Z), F32)
     for i in range(B):
         base = frame[H + i, :, MID]
         joined = jnp.concatenate(
@@ -217,16 +235,15 @@
         total = total + lax.dot_general(
             grad, joined, (((1,), (1,)), ((), ())), preferred_element_type=F32
         )
-        total_bias = total_bias + grad.astype(F32)
-    grad_merge[0:64] = total.astype(BF16)
-    grad_merge[64:128] = wide_sum(total_bias).astype(BF16)
-    own = jnp.concatenate([own_3[i] for i in range(B)], axis=1)
-    grad_merge[128:144] = wide_sum(own[16:32].astype(F32)).astype(BF16)
+    grad_merge[0:64] = total
+    grad_merge[64:128] = wide_sum([merge_grad[i] for i in range(B)])
+    own = [own_3[i] for i in range(B)]
+    grad_merge[128:144] = cell_sum(own)
     kernel_gradient(grad_3, own, [frame, hidden_01, hidden_2])
 
 
 def third_kernel(
-    before, top, bottom, after, left, right, w2, w3, slope_1, slope_2, mask, carried,
+    before, top, bottom, after, left, right, t2, t3, slope_1, slope_2, mask, carried,
     spread_3, spread_2, own_1, send_top, send_bottom, pieces, held,
 ):
     assemble((before, top, bottom, after, left, right), pieces)
@@ -241,7 +258,7 @@
     lax.fori_loop(0, N, move, 0)
 
     def ring(i, carry):
-        got = held[i, :, RING] + back_row(w3[96:112], spread_3, i, RING)
+        got = held[i, :, RING] + back_row(t3, slice(96, 112), spread_3, i, RING)
         grad = (got * slope_2[i] * mask[pl.ds(i, 1), RING]).astype(BF16)
         spread_2[i, :, RING] = spread(grad.astype(F32))
         return carry
@@ -250,8 +267,8 @@
     for i in range(B):
         got = (
             carried[i, 16:32]
-            + back_row(w3[80:96], spread_3, H + i, MID)
-            + back_row(w2[80:96], spread_2, H + i, MID)
+            + back_row(t3, slice(80, 96), spread_3, H + i, MID)
+            + back_row(t2, slice(80, 96), spread_2, H + i, MID)
         )
         grad = (got * slope_1[i]).astype(BF16)
         own_1[i] = spread(grad.astype(F32))
@@ -262,29 +279,29 @@
 
 
 def beside_kernel(
-    frame, hidden_01, spread_3, spread_2, own_1, w3, base,
+    frame, hidden_01, spread_3, spread_2, own_1, t3, base,
     grad_2, grad_1, grad_bias, part_0, part_base,
 ):
-    own = jnp.concatenate([own_1[i] for i in range(B)], axis=1)
-    grad_bias[0:16] = wide_sum(own[16:32].astype(F32)).astype(BF16)
+    own = [own_1[i] for i in range(B)]
+    grad_bias[0:16] = cell_sum(own)
     kernel_gradient(grad_1, own, [frame, hidden_01.at[:, 0:16, :]])
     own = own_cells(spread_2)
-    grad_bias[16:32] = wide_sum(own[16:32].astype(F32)).astype(BF16)
+    grad_bias[16:32] = cell_sum(own)
     kernel_gradient(grad_2, own, [frame, hidden_01])
 
     def ring(i, carry):
-        part_0[i] = back_row(w3[64:80], spread_3, i, RING)
+        part_0[i] = back_row(t3, slice(64, 80), spread_3, i, RING)
         return carry
 
     lax.fori_loop(H - 1, H + B + 1, ring, 0)
     for i in range(B):
-        part_base[i] = base[i] + back_row(w3[0:64], spread_3, H + i, MID)
+        part_base[i] = base[i] + back_row(t3, slice(0, 64), spread_3, H + i, MID)
 
 
 def fourth_kernel(
-    before, top, bottom, after, left, right, w1, w2, slope_0, mask, carried, part_0, frame,
+    before, top, bottom, after, left, right, t1, t2, slope_0, mask, carried, part_0, frame,
     grad_1, grad_2, grad_3, grad_merge, grad_bias,
-    spread_2, spread_1, spread_0, sums, pieces, held,
+    place, spread_2, spread_1, spread_0, kept, sent, sums, pieces, held,
 ):
     assemble((before, top, bottom, after, left, right), pieces)
     held[...] = pieces[:, 32:48, :].astype(F32)
@@ -302,8 +319,8 @@
         got = (
             held[i, :, RING]
             + part_0[i]
-            + back_row(w2[64:80], spread_2, i, RING)
-            + back_row(w1[64:80], spread_1, i, RING)
+            + back_row(t2, slice(64, 80), spread_2, i, RING)
+            + back_row(t1, slice(64, 80), spread_1, i, RING)
         )
         grad = (got * slope_0[i] * mask[pl.ds(i, 1), RING]).astype(BF16)
         spread_0[i, :, RING] = spread(grad.astype(F32))
@@ -316,30 +333,37 @@
     sums[864:1296] = grad_2[...]
     sums[1296:1728] = grad_3[...]
     sums[1728:1856] = grad_merge[0:128]
-    sums[1856:1872] = wide_sum(own[16:32].astype(F32)).astype(BF16)
+    sums[1856:1872] = cell_sum(own)
     sums[1872:1904] = grad_bias[...]
     sums[1904:1920] = grad_merge[128:144]
-    sums[1920:2048] = jnp.zeros((128, Z), BF16)
-
-
-def last_kernel(spread_2, spread_1, spread_0, w0, w1, w2, part_base, out_ref):
+    sums[1920:] = jnp.zeros((2 * HALF - 1920, Z), F32)
+    mine = pl.multiple_of(place[0] * HALF, HALF)
+    other = pl.multiple_of(HALF - place[0] * HALF, HALF)
+    kept[...] = sums[pl.ds(mine, HALF), :]
+    sent[...] = sums[pl.ds(other, HALF), :].astype(BF16)
+
+
+def last_kernel(spread_2, spread_1, spread_0, t0, t1, t2, part_base, out_ref):
     for i in range(B):
         out = (
             part_base[i]
-            + back_row(w2[0:64], spread_2, H + i, MID)
-            + back_row(w1[0:64], spread_1, H + i, MID)
-            + back_row(w0[...], spread_0, H + i, MID)
+            + back_row(t2, slice(0, 64), spread_2, H + i, MID)
+            + back_row(t1, slice(0, 64), spread_1, H + i, MID)
+            + back_row(t0, slice(0, 64), spread_0, H + i, MID)
         )
         for j in range(B):
             out_ref[pl.ds(B * i + j, 64, stride=B * B), :] = out[:, j * Z : (j + 1) * Z]
 
 
+def pair_kernel(kept, came, out_ref):
+    out_ref[...] = (kept[...] + came[...].astype(F32)).astype(BF16)
+
+
 def add_kernel(x_ref, out_ref):
     def step(k, acc):
-        block = x_ref[pl.ds(pl.multiple_of(k * 128, 128), 128), :].astype(F32)
-        return acc + block
-
-    acc = lax.fori_loop(0, DEVICES * ROWS // 128, step, jnp.zeros((128, Z), F32))
+        return acc + x_ref[pl.ds(pl.multiple_of(k * 128, 128), 128), :].astype(F32)
+
+    acc = lax.fori_loop(0, HALF // 128, step, jnp.zeros((128, Z), F32))
     total = acc[0:ROWS]
     for k in range(1, 128 // ROWS):
         total = total + acc[k * ROWS : (k + 1) * ROWS]
@@ -349,23 +373,26 @@
         out_ref[pl.ds(pl.multiple_of(k * 128, 128), 128), :] = block
         return carry
 
-    lax.fori_loop(0, DEVICES * ROWS // 128, put, 0)
-
-
-def turned(block, scale):
+    lax.fori_loop(0, HALF // 128, put, 0)
+
+
+def turned(block):
     rows = lax.broadcasted_iota(jnp.int32, block.shape, 0)
     lanes = lax.broadcasted_iota(jnp.int32, block.shape, 1)
-    return jnp.sum(jnp.where(rows == lanes, block, 0.0), axis=0, keepdims=True) * scale
-
-
-def unpack_kernel(scale, x_ref, g0, g1, g2, g3, bias, weight, weight_bias):
+    return jnp.sum(jnp.where(rows == lanes, block, 0.0), axis=0, keepdims=True)
+
+
+def unpack_kernel(scale, mine, other, place, g0, g1, g2, g3, bias, weight, weight_bias, sums):
+    sums[pl.ds(pl.multiple_of(place[0] * HALF, HALF), HALF), :] = mine[...].astype(F32) * scale
+    sums[pl.ds(pl.multiple_of(HALF - place[0] * HALF, HALF), HALF), :] = (
+        other[...].astype(F32) * scale
+    )
     for k, g in enumerate((g0, g1, g2, g3)):
-        g[...] = x_ref[432 * k : 432 * (k + 1), : g.shape[1]].astype(F32) * scale
-    weight[...] = x_ref[1728:1792].astype(F32) * scale
-    weight_bias[...] = turned(x_ref[1792:1856].astype(F32), scale)[:, :64]
+        g[...] = sums[432 * k : 432 * (k + 1), : g.shape[1]]
+    weight[...] = sums[1728:1792]
+    weight_bias[...] = turned(sums[1792:1856])[:, :64]
     for k in range(4):
-        block = x_ref[1856 + 16 * k : 1872 + 16 * k].astype(F32)
-        bias[k : k + 1] = turned(block, scale)[:, :16]
+        bias[k : k + 1] = turned(sums[1856 + 16 * k : 1872 + 16 * k])[:, :16]
 
 
 def exchange(top, bottom):
@@ -397,7 +424,6 @@
     kernels = (kernel_0, kernel_1, kernel_2, kernel_3)
     cells = B * B * Z * lax.axis_size("gx") * lax.axis_size("row") * lax.axis_size("rep")
     scale = 1.0 / math.sqrt(cells)
-    taps = [k.transpose(1, 0, 2).reshape(9, 48, k.shape[2]) for k in kernels]
     flat = [k.transpose(1, 0, 2).reshape(432, k.shape[2]) for k in kernels]
     bias = jnp.broadcast_to(layer_bias.astype(F32).reshape(64, 1), (64, Z))
     merge_bias = jnp.broadcast_to(merging_bias.astype(F32)[:, None], (64, Z))
@@ -407,11 +433,13 @@
     top, bottom = call(
         pack_kernel, [half, half], [samples.reshape(1024, Z)], [wide], name="pack"
     )
-    base, carried, merge_grad, w0, w1, w2, w3 = call(
+    place = lax.axis_index("rep").astype(jnp.int32).reshape(1)
+    base, carried, merge_grad, w0, w1, w2, w3, t0, t1, t2, t3 = call(
         prepare_kernel,
         [shape((B, 64, B * Z), F32)] * 2
         + [shape((B, 64, B * Z), BF16)]
-        + [shape((k.shape[2], 432), BF16) for k in kernels],
+        + [shape((144, 3 * k.shape[2]), BF16) for k in kernels]
+        + [shape((3, k.shape[2], 144), BF16) for k in kernels],
         [cotangent.reshape(1024, Z), merging_weight.T] + flat,
         [wide],
         flops=40_000_000,
@@ -423,7 +451,7 @@
     frame, hidden_0, slope_0, slope_1, top, bottom = call(
         first_kernel,
         [shape((N, 64, N * Z), BF16), shape((N, 16, N * Z), BF16), ring, shape((B, 16, B * Z), F32), send, send],
-        parts + [taps[0], taps[1], bias, mask],
+        parts + [w0, w1, bias, mask],
         name="layers_0_1",
     )
     parts = exchange(top, bottom)
@@ -438,14 +466,14 @@
             send,
             send,
         ],
-        parts + [frame, taps[2], taps[3], bias, mask, carried],
+        parts + [frame, w2, w3, bias, mask, carried],
         name="layers_2_3",
     )
     parts = exchange(top, bottom)
-    grads = shape((432, Z), BF16)
+    grads = shape((432, Z), F32)
     output, grad_3, grad_merge = call(
         merge_kernel,
-        [shape((1024, Z), F32), grads, shape((144, Z), BF16)],
+        [shape((1024, Z), F32), grads, shape((144, Z), F32)],
         [frame, hidden_01, hidden_2, hidden_3, own_3, merging_weight, merge_bias, merge_grad],
         flops=100_000_000,
         name="merge",
@@ -455,40 +483,40 @@
     spread_3, spread_2, own_1, top, bottom = call(
         third_kernel,
         [spreads, spreads, shape((B, 48, B * Z), BF16), send, send],
-        parts + [w2, w3, slope_1, slope_2, mask, carried],
+        parts + [t2, t3, slope_1, slope_2, mask, carried],
         [pltpu.VMEM((N, 32, N * Z), BF16), pltpu.VMEM((N, 16, N * Z), F32)],
         name="gradients_2_1",
     )
     parts = exchange(top, bottom)
     grad_2, grad_1, grad_bias, part_0, part_base = call(
         beside_kernel,
-        [grads, grads, shape((32, Z), BF16), ring, shape((B, 64, B * Z), F32)],
-        [frame, hidden_01, spread_3, spread_2, own_1, w3, base],
+        [grads, grads, shape((32, Z), F32), ring, shape((B, 64, B * Z), F32)],
+        [frame, hidden_01, spread_3, spread_2, own_1, t3, base],
         flops=200_000_000,
         name="kernel_gradients_2_1",
     )
-    spread_2, spread_1, spread_0, sums = call(
+    spread_2, spread_1, spread_0, kept, sent = call(
         fourth_kernel,
-        [spreads, spreads, spreads, shape((DEVICES * ROWS, Z), BF16)],
+        [spreads, spreads, spreads, shape((HALF, Z), F32), shape((HALF, Z), BF16)],
         parts
-        + [w1, w2, slope_0, mask, carried, part_0, frame]
-        + [grad_1, grad_2, grad_3, grad_merge, grad_bias],
-        [pltpu.VMEM((N, 48, N * Z), BF16), pltpu.VMEM((N, 16, N * Z), F32)],
+        + [t1, t2, slope_0, mask, carried, part_0, frame]
+        + [grad_1, grad_2, grad_3, grad_merge, grad_bias, place],
+        [pltpu.VMEM((2 * HALF, Z), F32), pltpu.VMEM((N, 48, N * Z), BF16), pltpu.VMEM((N, 16, N * Z), F32)],
         name="gradient_0",
     )
-    axes = ("gx", "row", "rep")
-    spread_sums = lax.all_to_all(sums.reshape(DEVICES, ROWS, Z), axes, 0, 0, tiled=True)
-    (added,) = call(
-        add_kernel,
-        [shape((DEVICES * ROWS, Z), BF16)],
-        [spread_sums.reshape(DEVICES * ROWS, Z)],
-        name="add",
-    )
-    totals = lax.all_to_all(added.reshape(DEVICES, ROWS, Z), axes, 0, 0, tiled=True)
+    axes = ("gx", "row")
+    swap = [(0, 1), (1, 0)]
+    half_sum = shape((HALF, Z), BF16)
+    (paired,) = call(pair_kernel, [half_sum], [kept, lax.ppermute(sent, "rep", swap)], name="pair")
+    spread_sums = lax.all_to_all(paired.reshape(GROUP, ROWS, Z), axes, 0, 0, tiled=True)
+    (added,) = call(add_kernel, [half_sum], [spread_sums.reshape(HALF, Z)], name="add")
+    totals = lax.all_to_all(added.reshape(GROUP, ROWS, Z), axes, 0, 0, tiled=True)
+    totals = totals.reshape(HALF, Z)
+    others = lax.ppermute(totals, "rep", swap)
     (grad_input,) = call(
         last_kernel,
         [shape((1024, Z), F32)],
-        [spread_2, spread_1, spread_0, w0, w1, w2, part_base],
+        [spread_2, spread_1, spread_0, t0, t1, t2, part_base],
         flops=300_000_000,
         name="input_gradient",
     )
@@ -496,7 +524,8 @@
         functools.partial(unpack_kernel, scale),
         [shape((432, k.shape[2]), F32) for k in kernels]
         + [shape((4, 16), F32), shape((64, 128), F32), shape((1, 64), F32)],
-        [totals.reshape(DEVICES * ROWS, Z)],
+        [totals, others, place],
+        [pltpu.VMEM((2 * HALF, Z), F32)],
         name="unpack",
     )
     grad_kernels = [g.reshape(27, 16, g.shape[1]).transpose(1, 0, 2) for g in unpacked[:4]]

time: 183 us -> 185 us (1.011)
  waiting for transfers between devices: 53.9 us -> 36.8 us
  local copies, waits for them, and re-layouts: 4.48 us -> 13.6 us
  blocking collectives: 44.4 us -> 50.2 us
  starting transfers between devices: 53.6 us -> 58.6 us
    all_to_all x1 -> x0, waiting for transfers between devices: 16.4 us -> none  [body(): lax.all_to_all(added.reshape(DEVICES, ROWS, Z), axes, 0, 0, tiled=True)]
    ppermute x0 -> x2, starting transfers between devices: none -> 11.4 us  [the longest x1 7.96 us: body(): lax.ppermute(sent, 'rep', swap)]
    unnamed x35 -> x71, local copies, waits for them, and re-layouts: 4.18 us -> 12.6 us
    all_to_all x1 -> x0, starting transfers between devices: 6.97 us -> none  [body(): lax.all_to_all(added.reshape(DEVICES, ROWS, Z), axes, 0, 0, tiled=True)]
    all_to_all x1 -> x2, blocking collectives: 44.4 us -> 50.2 us  [the longest x1 30 us: body(): lax.all_to_all(paired.reshape(GROUP, ROWS, Z), axes, 0, 0, tiled=True)]
    ppermute x4, waiting for transfers between devices: 19.7 us -> 17.5 us  [exchange(): from_after = lax.ppermute(left, 'row', [(j, i) for i, j in up])]
    pallas_call x15 -> x16, Pallas kernels: 24.6 us -> 23.5 us  [call(): pl.pallas_call(kernel, out_shape=list(outs), in_specs=[pl.BlockSpec(memor...]
  transfers between devices with their start and end apart: 17 -> 18, of which waited for: 13 -> 13; matrix products, arithmetic and copies ran while one was open for 0% -> 1% of each run, Pallas kernels for 4% -> 4%
where the time goes in v2:
time: 185 us; the launch traced here: 184 us
  starting transfers between devices  58.6 us (32%)
  blocking collectives  50.2 us (27%)
  waiting for transfers between devices  36.8 us (20%)
  Pallas kernels  23.5 us (13%)
  local copies, waits for them, and re-layouts  13.6 us (7%)
    all_to_all x1, blocking collectives, body(): lax.all_to_all(paired.reshape(GROUP, ROWS, Z), axes, 0, 0, tiled=True)  30 us
    pallas_call x16, Pallas kernels, call(): pl.pallas_call(kernel, out_shape=list(outs), in_specs=[pl.BlockSpec(memor...  23.5 us
    all_to_all x1, blocking collectives, body(): lax.all_to_all(added.reshape(GROUP, ROWS, Z), axes, 0, 0, tiled=True)  20.2 us
    ppermute x4, starting transfers between devices, exchange(): from_before = lax.ppermute(right, 'row', up)  20.1 us
    ppermute x4, waiting for transfers between devices, exchange(): from_after = lax.ppermute(left, 'row', [(j, i) for i, j in up])  17.5 us
    ppermute x4, starting transfers between devices, exchange(): before = lax.ppermute(bottom, 'gx', up)  16.7 us
    ppermute x4, waiting for transfers between devices, exchange(): after = lax.ppermute(top, 'gx', [(j, i) for i, j in up])  14.9 us
    unnamed x71, local copies, waits for them, and re-layouts  12.6 us
  transfers between devices with their start and end apart: 18, of which 13 were waited for; matrix products, arithmetic and copies ran while one was open for 1% of the time, Pallas kernels for 4%

profile of v2, /device:TPU:1, one launch (start us, length us, event | category | flops | bytes accessed | tf_op | source)
XLA Modules:
  0.0 183.8 jit_solution(3445980568859950334)
XLA Ops:
  1.8 4.0 %collective-permute-start = (bf16[2,64,512]{2,1,0:T(8,128)(2,1)S(1)}, bf16[2,64,512]{2,1,0:T(8,128)(2,1)S(1)}, u32[]{:S(2)}, u32[]{:S(2)}) collective-permute-start(bf16[2,64,512]{2,1,0:T(8,128)(2,1)S(1)} %get-tuple-element.67.bottom), channel_id=1, source_target_pairs={{0,32},{32,64},{64,96},{96,128},{128,160},{160,192},{192,224},{1,3... | collective-permute-start | bytes 393224 | tf_op jit(solution)/shard_map/ppermute | solution.py:401
  7.9 3.6 %collective-permute-done.1.after = bf16[2,64,512]{2,1,0:T(8,128)(2,1)S(1)} collective-permute-done((bf16[2,64,512]{2,1,0:T(8,128)(2,1)S(1)}, bf16[2,64,512]{2,1,0:T(8,128)(2,1)S(1)}, u32[]{:S(2)}, u32[]{:S(2)}) %collective-permute-start.1) | collective-permute-done | bytes 131104 | tf_op jit(solution)/shard_map/ppermute | solution.py:402
  12.3 4.8 %collective-permute-start.2 = (bf16[8,64,256]{2,1,0:T(8,128)(2,1)}, bf16[8,64,256]{2,1,0:T(8,128)(2,1)S(1)}, u32[]{:S(2)}, u32[]{:S(2)}) collective-permute-start(bf16[8,64,256]{2,1,0:T(8,128)(2,1)} %get-tuple-element.69), channel_id=1, source_target_pairs={{0,2},{2,4},{4,6},{6,8},{8,10},{10,12},{12,14},{14,16},{16,18},{18... | collective-permute-start | bytes 786440 | tf_op jit(solution)/shard_map/ppermute | solution.py:408
  21.6 4.4 %collective-permute-done.3.right = bf16[8,64,256]{2,1,0:T(8,128)(2,1)S(1)} collective-permute-done((bf16[8,64,256]{2,1,0:T(8,128)(2,1)}, bf16[8,64,256]{2,1,0:T(8,128)(2,1)S(1)}, u32[]{:S(2)}, u32[]{:S(2)}) %collective-permute-start.3) | collective-permute-done | bytes 262176 | tf_op jit(solution)/shard_map/ppermute | solution.py:409
  28.6 2.8 %layers_0_1.1 = (bf16[8,64,1024]{2,1,0:T(8,128)(2,1)S(1)}, bf16[8,16,1024]{2,1,0:T(8,128)(2,1)}, f32[8,16,768]{2,1,0:T(8,128)S(1)}, f32[4,16,512]{2,1,0:T(8,128)...) custom-call(bf16[2,64,512]{2,1,0:T(8,128)(2,1)S(1)} %collective-permute-done.before, ...), custom_call_target="tpu_custom_call" | custom-call | flops 1000000 | bytes 3204608 | tf_op jit(solution)/shard_map/layers_0_1/pallas_call | solution.py:31
  32.3 3.1 %collective-permute-start.4 = (bf16[2,32,512]{2,1,0:T(8,128)(2,1)S(1)}, bf16[2,32,512]{2,1,0:T(8,128)(2,1)S(1)}, u32[]{:S(2)}, u32[]{:S(2)}) collective-permute-start(bf16[2,32,512]{2,1,0:T(8,128)(2,1)S(1)} %get-tuple-element.74.bottom), channel_id=1, source_target_pairs={{0,32},{32,64},{64,96},{96,128},{128,160},{160,192},{192,224},{1,3... | collective-permute-start | bytes 196616 | tf_op jit(solution)/shard_map/ppermute | solution.py:401
  36.7 3.7 %collective-permute-done.5.after = bf16[2,32,512]{2,1,0:T(8,128)(2,1)S(1)} collective-permute-done((bf16[2,32,512]{2,1,0:T(8,128)(2,1)S(1)}, bf16[2,32,512]{2,1,0:T(8,128)(2,1)S(1)}, u32[]{:S(2)}, u32[]{:S(2)}) %collective-permute-start.5) | collective-permute-done | bytes 65568 | tf_op jit(solution)/shard_map/ppermute | solution.py:402
  40.4 4.3 %collective-permute-start.6 = (bf16[8,32,256]{2,1,0:T(8,128)(2,1)S(1)}, bf16[8,32,256]{2,1,0:T(8,128)(2,1)S(1)}, u32[]{:S(2)}, u32[]{:S(2)}) collective-permute-start(bf16[8,32,256]{2,1,0:T(8,128)(2,1)S(1)} %get-tuple-element.76), channel_id=1, source_target_pairs={{0,2},{2,4},{4,6},{6,8},{8,10},{10,12},{12,14},{14,16},{16,18},{18... | collective-permute-start | bytes 393224 | tf_op jit(solution)/shard_map/ppermute | solution.py:408
  46.6 7.8 %collective-permute-done.7.right = bf16[8,32,256]{2,1,0:T(8,128)(2,1)S(1)} collective-permute-done((bf16[8,32,256]{2,1,0:T(8,128)(2,1)S(1)}, bf16[8,32,256]{2,1,0:T(8,128)(2,1)S(1)}, u32[]{:S(2)}, u32[]{:S(2)}) %collective-permute-start.7) | collective-permute-done | bytes 131104 | tf_op jit(solution)/shard_map/ppermute | solution.py:409
  54.4 3.4 %layers_2_3.1 = (bf16[8,32,1024]{2,1,0:T(8,128)(2,1)S(1)}, bf16[8,16,1024]{2,1,0:T(8,128)(2,1)S(1)}, bf16[4,16,512]{2,1,0:T(8,128)(2,1)S(1)}, f32[8,16,768]{2,1,...) custom-call(bf16[2,32,512]{2,1,0:T(8,128)(2,1)S(1)} %collective-perm, ...), custom_call_target="tpu_custom_call" | custom-call | flops 1000000 | bytes 3915264 | tf_op jit(solution)/shard_map/layers_2_3/pallas_call | solution.py:31
  59.2 5.0 %collective-permute-start.8 = (bf16[2,32,512]{2,1,0:T(8,128)(2,1)S(1)}, bf16[2,32,512]{2,1,0:T(8,128)(2,1)S(1)}, u32[]{:S(2)}, u32[]{:S(2)}) collective-permute-start(bf16[2,32,512]{2,1,0:T(8,128)(2,1)S(1)} %get-tuple-element.87.bottom), channel_id=1, source_target_pairs={{0,32},{32,64},{64,96},{96,128},{128,160},{160,192},{192,224},{1,3... | collective-permute-start | bytes 196616 | tf_op jit(solution)/shard_map/ppermute | solution.py:401
  65.5 3.7 %collective-permute-done.9.after = bf16[2,32,512]{2,1,0:T(8,128)(2,1)S(1)} collective-permute-done((bf16[2,32,512]{2,1,0:T(8,128)(2,1)S(1)}, bf16[2,32,512]{2,1,0:T(8,128)(2,1)S(1)}, u32[]{:S(2)}, u32[]{:S(2)}) %collective-permute-start.9) | collective-permute-done | bytes 65568 | tf_op jit(solution)/shard_map/ppermute | solution.py:402
  69.2 5.7 %collective-permute-start.10 = (bf16[8,32,256]{2,1,0:T(8,128)(2,1)S(1)}, bf16[8,32,256]{2,1,0:T(8,128)(2,1)S(1)}, u32[]{:S(2)}, u32[]{:S(2)}) collective-permute-start(bf16[8,32,256]{2,1,0:T(8,128)(2,1)S(1)} %get-tuple-element.89), channel_id=1, source_target_pairs={{0,2},{2,4},{4,6},{6,8},{8,10},{10,12},{12,14},{14,16},{16,18},{18... | collective-permute-start | bytes 393224 | tf_op jit(solution)/shard_map/ppermute | solution.py:408
  76.9 5.3 %collective-permute-done.11.right = bf16[8,32,256]{2,1,0:T(8,128)(2,1)S(1)} collective-permute-done((bf16[8,32,256]{2,1,0:T(8,128)(2,1)S(1)}, bf16[8,32,256]{2,1,0:T(8,128)(2,1)S(1)}, u32[]{:S(2)}, u32[]{:S(2)}) %collective-permute-start.11) | collective-permute-done | bytes 131104 | tf_op jit(solution)/shard_map/ppermute | solution.py:409
  82.2 2.8 %gradients_2_1.1 = (bf16[8,48,1024]{2,1,0:T(8,128)(2,1)S(1)}, bf16[8,48,1024]{2,1,0:T(8,128)(2,1)S(1)}, bf16[4,48,512]{2,1,0:T(8,128)(2,1)S(1)}, bf16[2,48,512]{2,1,0:T(8,128)(2,1)S(1)}, bf16[2,48,512]{2,1,0:T(8,128)(2,1)S(1)}) custom-call(bf16[2,32,512]{2,1,0:T(8,128)(2,1)S(1)} %collective-permute-done.8.before, ...), custom_call_target="tpu_custom_call" | custom-call | flops 1000000 | bytes 3751424 | tf_op jit(solution)/shard_map/gradients_2_1/pallas_call | solution.py:31
  86.6 4.6 %collective-permute-start.12 = (bf16[2,48,512]{2,1,0:T(8,128)(2,1)S(1)}, bf16[2,48,512]{2,1,0:T(8,128)(2,1)S(1)}, u32[]{:S(2)}, u32[]{:S(2)}) collective-permute-start(bf16[2,48,512]{2,1,0:T(8,128)(2,1)S(1)} %get-tuple-element.95.bottom), channel_id=1, source_target_pairs={{0,32},{32,64},{64,96},{96,128},{128,160},{160,192},{192,224},{1,3... | collective-permute-start | bytes 294920 | tf_op jit(solution)/shard_map/ppermute | solution.py:401
  92.9 3.9 %collective-permute-done.13.after = bf16[2,48,512]{2,1,0:T(8,128)(2,1)S(1)} collective-permute-done((bf16[2,48,512]{2,1,0:T(8,128)(2,1)S(1)}, bf16[2,48,512]{2,1,0:T(8,128)(2,1)S(1)}, u32[]{:S(2)}, u32[]{:S(2)}) %collective-permute-start.13) | collective-permute-done | bytes 98336 | tf_op jit(solution)/shard_map/ppermute | solution.py:402
  97.6 5.3 %collective-permute-start.14 = (bf16[8,48,256]{2,1,0:T(8,128)(2,1)}, bf16[8,48,256]{2,1,0:T(8,128)(2,1)}, u32[]{:S(2)}, u32[]{:S(2)}) collective-permute-start(bf16[8,48,256]{2,1,0:T(8,128)(2,1)} %get-tuple-element.97), channel_id=1, source_target_pairs={{0,2},{2,4},{4,6},{6,8},{8,10},{10,12},{12,14},{14,16},{16,18},{18... | collective-permute-start | bytes 589832 | tf_op jit(solution)/shard_map/ppermute | solution.py:408
  110.0 3.0 %kernel_gradients_2_1.1 = (f32[432,128]{1,0:T(8,128)S(1)}, f32[432,128]{1,0:T(8,128)S(1)}, f32[32,128]{1,0:T(8,128)S(1)}, f32[8,16,768]{2,1,0:T(8,128)S(1)}, f32[4,64,512]{2,1,0:T(8,128)S(1)}) custom-call(bf16[8,64,1024]{2,1,0:T(8,128)(2,1)S(1)} %get-tuple-element.73.frame, bf16[8,32,1024]{2,1,0:T(8,128)(2,1)S(1)} %get-tuple-element.81.hidden_01, ...), custom_call_target="tpu_custom_call" | custom-call | flops 200000000 | bytes 5339648 | tf_op jit(solution)/shard_map/kernel_gradients_2_1/pallas_call | solution.py:31
  113.1 4.7 %gradient_0.1 = (bf16[8,48,1024]{2,1,0:T(8,128)(2,1)S(1)}, bf16[8,48,1024]{2,1,0:T(8,128)(2,1)S(1)}, bf16[8,48,1024]{2,1,0:T(8,128)(2,1)S(1)}, f32[1024,128]{1,0:T(8,128)S(1)}, bf16[1024,128]{1,0:T(8,128)(2,1)S(1)}) custom-call(bf16[2,48,512]{2,1,0:T(8,128)(2,1)S(1)} %copy-done.7, bf16[2,48,512]{2,1,0:T(8,128)(2,1)S(1)} %get-tuple-element.96.top, ...), custom_call_target="tpu_custom_call" | custom-call | flops 1000000 | bytes 7229956 | tf_op jit(solution)/shard_map/gradient_0/pallas_call | solution.py:31
  117.9 8.0 %collective-permute-start.16 = (bf16[1024,128]{1,0:T(8,128)(2,1)S(1)}, bf16[1024,128]{1,0:T(8,128)(2,1)S(1)}, u32[]{:S(2)}, u32[]{:S(2)}) collective-permute-start(bf16[1024,128]{1,0:T(8,128)(2,1)S(1)} %get-tuple-element.117), channel_id=1, source_target_pairs={{0,1},{1,0},{2,3},{3,2},{4,5},{5,4},{6,7},{7,6},{8,9},{9,8},{10,11... | collective-permute-start | bytes 786440 | tf_op jit(solution)/shard_map/ppermute | solution.py:510
  127.0 30.0 %all_to_all.10 = bf16[128,8,128]{2,1,0:T(8,128)(2,1)S(1)} all-to-all(bf16[128,8,128]{2,1,0:T(8,128)(2,1)S(1)} %bitcast.41), channel_id=1, replica_groups=mesh['gx'=8,'row'=16,'rep'=2] {'gx','row'}, dimensions={0} | all-to-all | bytes 524288 | tf_op jit(solution)/shard_map/all_to_all | solution.py:511
  157.1 20.2 %all_to_all.11 = bf16[128,8,128]{2,1,0:T(8,128)(2,1)S(1)} all-to-all(bf16[128,8,128]{2,1,0:T(8,128)(2,1)S(1)} %bitcast.40), channel_id=1, replica_groups=mesh['gx'=8,'row'=16,'rep'=2] {'gx','row'}, dimensions={0} | all-to-all | bytes 524288 | tf_op jit(solution)/shard_map/all_to_all | solution.py:513
  177.3 3.5 %collective-permute-start.17 = (bf16[1024,128]{1,0:T(8,128)(2,1)S(1)}, bf16[1024,128]{1,0:T(8,128)(2,1)S(1)}, u32[]{:S(2)}, u32[]{:S(2)}) collective-permute-start(bf16[1024,128]{1,0:T(8,128)(2,1)S(1)} %bitcast.37), channel_id=1, source_target_pairs={{0,1},{1,0},{2,3},{3,2},{4,5},{5,4},{6,7},{7,6},{8,9},{9,8},{10,11... | collective-permute-start | bytes 786440 | tf_op jit(solution)/shard_map/ppermute | solution.py:515
  (107 shorter events, 35.1 us)
Async XLA Ops:
  1.6 17.1 %copy-start.27 = (bf16[16,27,112]{2,0,1:T(8,128)(2,1)S(1)}, bf16[16,27,112]{2,0,1:T(8,128)(2,1)}, u32[]{:S(2)}) copy-start(bf16[16,27,112]{2,0,1:T(8,128)(2,1)} %param.14) | copy-start | bytes 290308
  1.8 6.1 %collective-permute-start = (bf16[2,64,512]{2,1,0:T(8,128)(2,1)S(1)}, bf16[2,64,512]{2,1,0:T(8,128)(2,1)S(1)}, u32[]{:S(2)}, u32[]{:S(2)}) collective-permute-start(bf16[2,64,512]{2,1,0:T(8,128)(2,1)S(1)} %get-tuple-element.67.bottom), channel_id=1, source_target_pairs={{0,32},{32,64},{64,96},{96,128},{128,160},{160,192},{192,224},{1,3... | collective-permute-start | bytes 393224 | tf_op jit(solution)/shard_map/ppermute | solution.py:401
  5.8 5.7 %collective-permute-start.1 = (bf16[2,64,512]{2,1,0:T(8,128)(2,1)S(1)}, bf16[2,64,512]{2,1,0:T(8,128)(2,1)S(1)}, u32[]{:S(2)}, u32[]{:S(2)}) collective-permute-start(bf16[2,64,512]{2,1,0:T(8,128)(2,1)S(1)} %get-tuple-element.68.top), channel_id=1, source_target_pairs={{32,0},{64,32},{96,64},{128,96},{160,128},{192,160},{224,192},{33,... | collective-permute-start | bytes 393224 | tf_op jit(solution)/shard_map/ppermute | solution.py:402
  7.1 11.6 %copy-start.10 = (bf16[1,64,4,4,128]{4,3,2,1,0:T(4,128)(2,1)S(1)}, bf16[1,64,4,4,128]{4,3,2,1,0:T(4,128)(2,1)}, u32[]{:S(2)}) copy-start(bf16[1,64,4,4,128]{4,3,2,1,0:T(4,128)(2,1)} %param.10) | copy-start | bytes 786436
  12.3 8.6 %collective-permute-start.2 = (bf16[8,64,256]{2,1,0:T(8,128)(2,1)}, bf16[8,64,256]{2,1,0:T(8,128)(2,1)S(1)}, u32[]{:S(2)}, u32[]{:S(2)}) collective-permute-start(bf16[8,64,256]{2,1,0:T(8,128)(2,1)} %get-tuple-element.69), channel_id=1, source_target_pairs={{0,2},{2,4},{4,6},{6,8},{8,10},{10,12},{12,14},{14,16},{16,18},{18... | collective-permute-start | bytes 786440 | tf_op jit(solution)/shard_map/ppermute | solution.py:408
  17.1 8.8 %collective-permute-start.3 = (bf16[8,64,256]{2,1,0:T(8,128)(2,1)}, bf16[8,64,256]{2,1,0:T(8,128)(2,1)S(1)}, u32[]{:S(2)}, u32[]{:S(2)}) collective-permute-start(bf16[8,64,256]{2,1,0:T(8,128)(2,1)} %get-tuple-element.70), channel_id=1, source_target_pairs={{2,0},{4,2},{6,4},{8,6},{10,8},{12,10},{14,12},{16,14},{18,16},{20... | collective-permute-start | bytes 786440 | tf_op jit(solution)/shard_map/ppermute | solution.py:409
  19.9 11.5 %copy-start.2 = (f32[4,64,512]{2,1,0:T(8,128)}, f32[4,64,512]{2,1,0:T(8,128)S(1)}, u32[]{:S(2)}) copy-start(f32[4,64,512]{2,1,0:T(8,128)S(1)} %get-tuple-element.104.base) | copy-start | bytes 1572868
  19.9 11.6 %copy-start.11 = (bf16[4,64,512]{2,1,0:T(8,128)(2,1)}, bf16[4,64,512]{2,1,0:T(8,128)(2,1)S(1)}, u32[]{:S(2)}) copy-start(bf16[4,64,512]{2,1,0:T(8,128)(2,1)S(1)} %get-tuple-element.85.merge_grad) | copy-start | bytes 786436
  32.3 4.4 %collective-permute-start.4 = (bf16[2,32,512]{2,1,0:T(8,128)(2,1)S(1)}, bf16[2,32,512]{2,1,0:T(8,128)(2,1)S(1)}, u32[]{:S(2)}, u32[]{:S(2)}) collective-permute-start(bf16[2,32,512]{2,1,0:T(8,128)(2,1)S(1)} %get-tuple-element.74.bottom), channel_id=1, source_target_pairs={{0,32},{32,64},{64,96},{96,128},{128,160},{160,192},{192,224},{1,3... | collective-permute-start | bytes 196616 | tf_op jit(solution)/shard_map/ppermute | solution.py:401
  35.4 5.0 %collective-permute-start.5 = (bf16[2,32,512]{2,1,0:T(8,128)(2,1)S(1)}, bf16[2,32,512]{2,1,0:T(8,128)(2,1)S(1)}, u32[]{:S(2)}, u32[]{:S(2)}) collective-permute-start(bf16[2,32,512]{2,1,0:T(8,128)(2,1)S(1)} %get-tuple-element.75.top), channel_id=1, source_target_pairs={{32,0},{64,32},{96,64},{128,96},{160,128},{192,160},{224,192},{33,... | collective-permute-start | bytes 196616 | tf_op jit(solution)/shard_map/ppermute | solution.py:402
  40.4 6.2 %collective-permute-start.6 = (bf16[8,32,256]{2,1,0:T(8,128)(2,1)S(1)}, bf16[8,32,256]{2,1,0:T(8,128)(2,1)S(1)}, u32[]{:S(2)}, u32[]{:S(2)}) collective-permute-start(bf16[8,32,256]{2,1,0:T(8,128)(2,1)S(1)} %get-tuple-element.76), channel_id=1, source_target_pairs={{0,2},{2,4},{4,6},{6,8},{8,10},{10,12},{12,14},{14,16},{16,18},{18... | collective-permute-start | bytes 393224 | tf_op jit(solution)/shard_map/ppermute | solution.py:408
  44.7 9.7 %collective-permute-start.7 = (bf16[8,32,256]{2,1,0:T(8,128)(2,1)S(1)}, bf16[8,32,256]{2,1,0:T(8,128)(2,1)S(1)}, u32[]{:S(2)}, u32[]{:S(2)}) collective-permute-start(bf16[8,32,256]{2,1,0:T(8,128)(2,1)S(1)} %get-tuple-element.77), channel_id=1, source_target_pairs={{2,0},{4,2},{6,4},{8,6},{10,8},{12,10},{14,12},{16,14},{18,16},{20... | collective-permute-start | bytes 393224 | tf_op jit(solution)/shard_map/ppermute | solution.py:409
  59.2 23.0 %copy-start.13 = (bf16[8,16,1024]{2,1,0:T(8,128)(2,1)}, bf16[8,16,1024]{2,1,0:T(8,128)(2,1)S(1)}, u32[]{:S(2)}) copy-start(bf16[8,16,1024]{2,1,0:T(8,128)(2,1)S(1)} %get-tuple-element.82.hidden_2) | copy-start | bytes 786436
  59.2 6.4 %collective-permute-start.8 = (bf16[2,32,512]{2,1,0:T(8,128)(2,1)S(1)}, bf16[2,32,512]{2,1,0:T(8,128)(2,1)S(1)}, u32[]{:S(2)}, u32[]{:S(2)}) collective-permute-start(bf16[2,32,512]{2,1,0:T(8,128)(2,1)S(1)} %get-tuple-element.87.bottom), channel_id=1, source_target_pairs={{0,32},{32,64},{64,96},{96,128},{128,160},{160,192},{192,224},{1,3... | collective-permute-start | bytes 196616 | tf_op jit(solution)/shard_map/ppermute | solution.py:401
  64.2 5.0 %collective-permute-start.9 = (bf16[2,32,512]{2,1,0:T(8,128)(2,1)S(1)}, bf16[2,32,512]{2,1,0:T(8,128)(2,1)S(1)}, u32[]{:S(2)}, u32[]{:S(2)}) collective-permute-start(bf16[2,32,512]{2,1,0:T(8,128)(2,1)S(1)} %get-tuple-element.88.top), channel_id=1, source_target_pairs={{32,0},{64,32},{96,64},{128,96},{160,128},{192,160},{224,192},{33,... | collective-permute-start | bytes 196616 | tf_op jit(solution)/shard_map/ppermute | solution.py:402
  69.2 7.6 %collective-permute-start.10 = (bf16[8,32,256]{2,1,0:T(8,128)(2,1)S(1)}, bf16[8,32,256]{2,1,0:T(8,128)(2,1)S(1)}, u32[]{:S(2)}, u32[]{:S(2)}) collective-permute-start(bf16[8,32,256]{2,1,0:T(8,128)(2,1)S(1)} %get-tuple-element.89), channel_id=1, source_target_pairs={{0,2},{2,4},{4,6},{6,8},{8,10},{10,12},{12,14},{14,16},{16,18},{18... | collective-permute-start | bytes 393224 | tf_op jit(solution)/shard_map/ppermute | solution.py:408
  75.0 7.2 %collective-permute-start.11 = (bf16[8,32,256]{2,1,0:T(8,128)(2,1)S(1)}, bf16[8,32,256]{2,1,0:T(8,128)(2,1)S(1)}, u32[]{:S(2)}, u32[]{:S(2)}) collective-permute-start(bf16[8,32,256]{2,1,0:T(8,128)(2,1)S(1)} %get-tuple-element.90), channel_id=1, source_target_pairs={{2,0},{4,2},{6,4},{8,6},{10,8},{12,10},{14,12},{16,14},{18,16},{20... | collective-permute-start | bytes 393224 | tf_op jit(solution)/shard_map/ppermute | solution.py:409
  86.6 6.3 %collective-permute-start.12 = (bf16[2,48,512]{2,1,0:T(8,128)(2,1)S(1)}, bf16[2,48,512]{2,1,0:T(8,128)(2,1)S(1)}, u32[]{:S(2)}, u32[]{:S(2)}) collective-permute-start(bf16[2,48,512]{2,1,0:T(8,128)(2,1)S(1)} %get-tuple-element.95.bottom), channel_id=1, source_target_pairs={{0,32},{32,64},{64,96},{96,128},{128,160},{160,192},{192,224},{1,3... | collective-permute-start | bytes 294920 | tf_op jit(solution)/shard_map/ppermute | solution.py:401
  91.3 5.5 %collective-permute-start.13 = (bf16[2,48,512]{2,1,0:T(8,128)(2,1)S(1)}, bf16[2,48,512]{2,1,0:T(8,128)(2,1)S(1)}, u32[]{:S(2)}, u32[]{:S(2)}) collective-permute-start(bf16[2,48,512]{2,1,0:T(8,128)(2,1)S(1)} %get-tuple-element.96.top), channel_id=1, source_target_pairs={{32,0},{64,32},{96,64},{128,96},{160,128},{192,160},{224,192},{33,... | collective-permute-start | bytes 294920 | tf_op jit(solution)/shard_map/ppermute | solution.py:402
  97.6 15.5 %collective-permute-start.14 = (bf16[8,48,256]{2,1,0:T(8,128)(2,1)}, bf16[8,48,256]{2,1,0:T(8,128)(2,1)}, u32[]{:S(2)}, u32[]{:S(2)}) collective-permute-start(bf16[8,48,256]{2,1,0:T(8,128)(2,1)} %get-tuple-element.97), channel_id=1, source_target_pairs={{0,2},{2,4},{4,6},{6,8},{8,10},{10,12},{12,14},{14,16},{16,18},{18... | collective-permute-start | bytes 589832 | tf_op jit(solution)/shard_map/ppermute | solution.py:408
  102.8 10.2 %collective-permute-start.15 = (bf16[8,48,256]{2,1,0:T(8,128)(2,1)}, bf16[8,48,256]{2,1,0:T(8,128)(2,1)}, u32[]{:S(2)}, u32[]{:S(2)}) collective-permute-start(bf16[8,48,256]{2,1,0:T(8,128)(2,1)} %get-tuple-element.98), channel_id=1, source_target_pairs={{2,0},{4,2},{6,4},{8,6},{10,8},{12,10},{14,12},{16,14},{18,16},{20... | collective-permute-start | bytes 589832 | tf_op jit(solution)/shard_map/ppermute | solution.py:409
  117.9 9.1 %collective-permute-start.16 = (bf16[1024,128]{1,0:T(8,128)(2,1)S(1)}, bf16[1024,128]{1,0:T(8,128)(2,1)S(1)}, u32[]{:S(2)}, u32[]{:S(2)}) collective-permute-start(bf16[1024,128]{1,0:T(8,128)(2,1)S(1)} %get-tuple-element.117), channel_id=1, source_target_pairs={{0,1},{1,0},{2,3},{3,2},{4,5},{5,4},{6,7},{7,6},{8,9},{9,8},{10,11... | collective-permute-start | bytes 786440 | tf_op jit(solution)/shard_map/ppermute | solution.py:510
  157.1 23.7 %copy-start.29 = (bf16[3,64,144]{2,1,0:T(8,128)(2,1)S(1)}, bf16[3,64,144]{2,1,0:T(8,128)(2,1)}, u32[]{:S(2)}) copy-start(bf16[3,64,144]{2,1,0:T(8,128)(2,1)} %copy-done.28) | copy-start | bytes 165892
  177.3 5.4 %collective-permute-start.17 = (bf16[1024,128]{1,0:T(8,128)(2,1)S(1)}, bf16[1024,128]{1,0:T(8,128)(2,1)S(1)}, u32[]{:S(2)}, u32[]{:S(2)}) collective-permute-start(bf16[1024,128]{1,0:T(8,128)(2,1)S(1)} %bitcast.37), channel_id=1, source_target_pairs={{0,1},{1,0},{2,3},{3,2},{4,5},{5,4},{6,7},{7,6},{8,9},{9,8},{10,11... | collective-permute-start | bytes 786440 | tf_op jit(solution)/shard_map/ppermute | solution.py:515
  (29 other events, 76.4 us)

commit v3 on v2

--- a/solution.py
+++ b/solution.py
@@ -31,9 +31,7 @@
     return pl.pallas_call(
         kernel,
         out_shape=list(outs),
-        in_specs=[
-            pl.BlockSpec(memory_space=pltpu.SMEM if a.dtype == jnp.int32 else pltpu.VMEM) for a in args
-        ],
+        in_specs=[pl.BlockSpec(memory_space=pltpu.VMEM)] * len(args),
         out_specs=[pl.BlockSpec(memory_space=pltpu.VMEM)] * len(outs),
         scratch_shapes=list(scratch),
         compiler_params=pltpu.CompilerParams(vmem_limit_bytes=VMEM_LIMIT),
@@ -55,9 +53,37 @@
     return jnp.where(keep, pltpu.roll(v, v.shape[1] - 1, 1), 0.0)
 
 
-def spread(v):
-    not_first, not_last = lane_moves(*v.shape)
-    return jnp.concatenate([from_right(v, not_last), v, from_left(v, not_first)], axis=0).astype(BF16)
+def one_cell_moves():
+    row = lax.broadcasted_iota(jnp.int32, (Z, 2 * Z), 0)
+    lane = lax.broadcasted_iota(jnp.int32, (Z, 2 * Z), 1)
+    return jnp.where((row == lane + 1) | (row == lane - Z - 1), 1.0, 0.0).astype(BF16)
+
+
+def spread(v, moves):
+    blocks = v.shape[1] // Z
+    tall = jnp.concatenate([v[:, k * Z : (k + 1) * Z] for k in range(blocks)], axis=0)
+    got = jnp.dot(tall, moves, preferred_element_type=F32).astype(BF16)
+    later, earlier = (
+        jnp.concatenate([half[16 * k : 16 * (k + 1)] for k in range(blocks)], axis=1)
+        for half in (got[:, :Z], got[:, Z:])
+    )
+    return jnp.concatenate([later, v, earlier], axis=0)
+
+
+def inside(i):
+    x = lax.axis_index("gx") * B + i - H
+    block = lax.broadcasted_iota(jnp.int32, (1, (B + 2) * Z), 1) // Z
+    y = lax.axis_index("row") * B + block + 1 - H
+    in_x = (x >= 0) & (x < lax.axis_size("gx") * B)
+    in_y = (y >= 0) & (y < lax.axis_size("row") * B)
+    return jnp.where(in_y, 1.0, 0.0) * jnp.where(in_x, 1.0, 0.0)
+
+
+def as_column(row):
+    n = row.shape[1]
+    rows = lax.broadcasted_iota(jnp.int32, (n, n), 0)
+    lanes = lax.broadcasted_iota(jnp.int32, (n, n), 1)
+    return jnp.sum(jnp.where(rows == lanes, row, 0.0), axis=1, keepdims=True)
 
 
 def conv_row(kernel_ref, sources, i, lanes):
@@ -118,13 +144,20 @@
 
 
 def assemble(parts, frame):
-    before, top, bottom, after, left, right = parts
-    frame[0:2, :, MID] = before[...]
-    frame[2:4, :, MID] = top[...]
-    frame[4:6, :, MID] = bottom[...]
-    frame[6:8, :, MID] = after[...]
-    frame[:, :, : H * Z] = left[...]
-    frame[:, :, (H + B) * Z :] = right[...]
+    before, left, right, after, above, below = parts
+    own = slice(H, H + B)
+    frame[own, :, : H * Z] = before[...]
+    frame[own, :, H * Z : 2 * H * Z] = left[...]
+    frame[own, :, 2 * H * Z : 3 * H * Z] = right[...]
+    frame[own, :, 3 * H * Z :] = after[...]
+    frame[:H] = above[...]
+    frame[H + B :] = below[...]
+
+
+def put(pair, i, rows, value):
+    left, right = pair
+    left[i, rows] = value[:, : H * Z]
+    right[i, rows] = value[:, H * Z :]
 
 
 def wide_sum(blocks):
@@ -136,50 +169,54 @@
     return wide_sum([rows[16:32] for rows in own])
 
 
-def pack_kernel(x_ref, top_ref, bottom_ref, wide):
+def pack_kernel(x_ref, layer_bias, merging_bias, left, right, bias, merge_bias, wide):
     wide[...] = x_ref[...].astype(F32)
     for i in range(B):
-        out = top_ref if i < 2 else bottom_ref
-        for j in range(B):
-            got = wide[pl.ds(B * i + j, 64, stride=B * B), :]
-            out[i % 2, :, j * Z : (j + 1) * Z] = got.astype(BF16)
-
-
-def columns_kernel(before, top, bottom, after, left, right):
-    for r, ref in enumerate((before, top, bottom, after)):
-        left[2 * r : 2 * r + 2] = ref[:, :, : H * Z]
-        right[2 * r : 2 * r + 2] = ref[:, :, (B - H) * Z :]
-
-
-def prepare_kernel(cot_ref, merge_t, k0, k1, k2, k3, base, carried, merge_grad, w0, w1, w2, w3, t0, t1, t2, t3, wide):
+        row = [wide[pl.ds(B * i + j, 64, stride=B * B), :].astype(BF16) for j in range(B)]
+        put((left, right), i, slice(0, 64), jnp.concatenate(row, axis=1))
+    for k in range(4):
+        column = as_column(layer_bias[k : k + 1].astype(F32))
+        bias[16 * k : 16 * (k + 1)] = jnp.broadcast_to(column, (16, Z))
+    merge_bias[...] = jnp.broadcast_to(as_column(merging_bias[...].astype(F32)), (64, Z))
+
+
+def rows_kernel(before, left, right, after, top, bottom):
+    for k, ref in enumerate((before, left, right, after)):
+        lanes = slice(k * H * Z, (k + 1) * H * Z)
+        top[:, :, lanes] = ref[:H]
+        bottom[:, :, lanes] = ref[B - H :]
+
+
+def prepare_kernel(cot_ref, merge, k0, k1, k2, k3, base, carried, merge_grad, w0, w1, w2, w3, t0, t1, t2, t3, wide):
     for k_ref, w_ref, t_ref in ((k0, w0, t0), (k1, w1, t1), (k2, w2, t2), (k3, w3, t3)):
         w_ref[...] = jnp.concatenate([k_ref[144 * a : 144 * (a + 1)] for a in range(3)], axis=1)
         for b in range(3):
             rows = [k_ref[48 * t : 48 * (t + 1)] for t in (b, 3 + b, 6 + b)]
             t_ref[b] = jnp.transpose(jnp.concatenate(rows, axis=0).astype(F32)).astype(BF16)
     wide[...] = cot_ref[...].astype(F32)
+    merge_t = jnp.transpose(merge[...].astype(F32)).astype(BF16)
     for i in range(B):
         cot = jnp.concatenate(
             [wide[pl.ds(B * i + j, 64, stride=B * B), :] for j in range(B)], axis=1
         )
         grad = (BETA * cot).astype(BF16)
         merge_grad[i] = grad
-        back = jnp.dot(merge_t[...], grad, preferred_element_type=F32)
+        back = jnp.dot(merge_t, grad, preferred_element_type=F32)
         base[i] = cot + back[:64]
         carried[i] = back[64:]
 
 
 def first_kernel(
-    before, top, bottom, after, left, right, k0, k1, bias, mask,
-    frame, hidden_0, slope_0, slope_1, send_top, send_bottom,
+    before, left, right, after, above, below, k0, k1, bias,
+    frame, hidden_0, slope_0, slope_1, send_left, send_right,
 ):
-    assemble((before, top, bottom, after, left, right), frame)
+    assemble((before, left, right, after, above, below), frame)
 
     def ring(i, carry):
         pre = conv_row(k0, [frame], i, RING) + bias[0:16, 0:1]
         value, slope = activate(pre)
         slope_0[i] = slope
-        hidden_0[i, :, RING] = (value * mask[pl.ds(i, 1), RING]).astype(BF16)
+        hidden_0[i, :, RING] = (value * inside(i)).astype(BF16)
         return carry
 
     lax.fori_loop(H - 1, H + B + 1, ring, 0)
@@ -187,22 +224,22 @@
         pre = conv_row(k1, [frame, hidden_0], H + i, MID) + bias[16:32, 0:1]
         value, slope = activate(pre)
         slope_1[i] = slope
-        send = send_top if i < 2 else send_bottom
-        send[i % 2, 0:16] = hidden_0[H + i, :, MID]
-        send[i % 2, 16:32] = value.astype(BF16)
+        put((send_left, send_right), i, slice(0, 16), hidden_0[H + i, :, MID])
+        put((send_left, send_right), i, slice(16, 32), value.astype(BF16))
 
 
 def second_kernel(
-    before, top, bottom, after, left, right, frame, k2, k3, bias, mask, carried,
-    hidden_01, hidden_2, hidden_3, slope_2, own_3, send_top, send_bottom,
+    before, left, right, after, above, below, frame, k2, k3, bias, carried,
+    hidden_01, hidden_2, hidden_3, slope_2, own_3, send_left, send_right,
 ):
-    assemble((before, top, bottom, after, left, right), hidden_01)
+    assemble((before, left, right, after, above, below), hidden_01)
+    moves = one_cell_moves()
 
     def ring(i, carry):
         pre = conv_row(k2, [frame, hidden_01], i, RING) + bias[32:48, 0:1]
         value, slope = activate(pre)
         slope_2[i] = slope
-        hidden_2[i, :, RING] = (value * mask[pl.ds(i, 1), RING]).astype(BF16)
+        hidden_2[i, :, RING] = (value * inside(i)).astype(BF16)
         return carry
 
     lax.fori_loop(H - 1, H + B + 1, ring, 0)
@@ -211,10 +248,9 @@
         value, slope = activate(pre)
         hidden_3[i] = value.astype(BF16)
         grad = (carried[i, 48:64] * slope).astype(BF16)
-        own_3[i] = spread(grad.astype(F32))
-        send = send_top if i < 2 else send_bottom
-        send[i % 2, 0:16] = grad
-        send[i % 2, 16:32] = carried[i, 32:48].astype(BF16)
+        own_3[i] = spread(grad, moves)
+        put((send_left, send_right), i, slice(0, 16), grad)
+        put((send_left, send_right), i, slice(16, 32), carried[i, 32:48].astype(BF16))
 
 
 def merge_kernel(
@@ -243,24 +279,25 @@
 
 
 def third_kernel(
-    before, top, bottom, after, left, right, t2, t3, slope_1, slope_2, mask, carried,
-    spread_3, spread_2, own_1, send_top, send_bottom, pieces, held,
+    before, left, right, after, above, below, t2, t3, slope_1, slope_2, carried,
+    spread_3, spread_2, own_1, send_left, send_right, pieces, held,
 ):
-    assemble((before, top, bottom, after, left, right), pieces)
+    assemble((before, left, right, after, above, below), pieces)
+    moves = one_cell_moves()
     held[...] = pieces[:, 16:32, :].astype(F32)
     for i in range(B):
         held[H + i, :, MID] = carried[i, 32:48]
 
     def move(i, carry):
-        spread_3[i] = spread(pieces[i, 0:16].astype(F32))
+        spread_3[i] = spread(pieces[i, 0:16], moves)
         return carry
 
     lax.fori_loop(0, N, move, 0)
 
     def ring(i, carry):
         got = held[i, :, RING] + back_row(t3, slice(96, 112), spread_3, i, RING)
-        grad = (got * slope_2[i] * mask[pl.ds(i, 1), RING]).astype(BF16)
-        spread_2[i, :, RING] = spread(grad.astype(F32))
+        grad = (got * slope_2[i] * inside(i)).astype(BF16)
+        spread_2[i, :, RING] = spread(grad, moves)
         return carry
 
     lax.fori_loop(H - 1, H + B + 1, ring, 0)
@@ -271,11 +308,10 @@
             + back_row(t2, slice(80, 96), spread_2, H + i, MID)
         )
         grad = (got * slope_1[i]).astype(BF16)
-        own_1[i] = spread(grad.astype(F32))
-        send = send_top if i < 2 else send_bottom
-        send[i % 2, 0:16] = spread_2[H + i, 16:32, MID]
-        send[i % 2, 16:32] = grad
-        send[i % 2, 32:48] = carried[i, 0:16].astype(BF16)
+        own_1[i] = spread(grad, moves)
+        put((send_left, send_right), i, slice(0, 16), spread_2[H + i, 16:32, MID])
+        put((send_left, send_right), i, slice(16, 32), grad)
+        put((send_left, send_right), i, slice(32, 48), carried[i, 0:16].astype(BF16))
 
 
 def beside_kernel(
@@ -299,18 +335,19 @@
 
 
 def fourth_kernel(
-    before, top, bottom, after, left, right, t1, t2, slope_0, mask, carried, part_0, frame,
+    before, left, right, after, above, below, t1, t2, slope_0, carried, part_0, frame,
     grad_1, grad_2, grad_3, grad_merge, grad_bias,
-    place, spread_2, spread_1, spread_0, kept, sent, sums, pieces, held,
+    spread_2, spread_1, spread_0, kept, sent, sums, pieces, held,
 ):
-    assemble((before, top, bottom, after, left, right), pieces)
+    assemble((before, left, right, after, above, below), pieces)
+    moves = one_cell_moves()
     held[...] = pieces[:, 32:48, :].astype(F32)
     for i in range(B):
         held[H + i, :, MID] = carried[i, 0:16]
 
     def move(i, carry):
-        spread_2[i] = spread(pieces[i, 0:16].astype(F32))
-        spread_1[i] = spread(pieces[i, 16:32].astype(F32))
+        spread_2[i] = spread(pieces[i, 0:16], moves)
+        spread_1[i] = spread(pieces[i, 16:32], moves)
         return carry
 
     lax.fori_loop(0, N, move, 0)
@@ -322,8 +359,8 @@
             + back_row(t2, slice(64, 80), spread_2, i, RING)
             + back_row(t1, slice(64, 80), spread_1, i, RING)
         )
-        grad = (got * slope_0[i] * mask[pl.ds(i, 1), RING]).astype(BF16)
-        spread_0[i, :, RING] = spread(grad.astype(F32))
+        grad = (got * slope_0[i] * inside(i)).astype(BF16)
+        spread_0[i, :, RING] = spread(grad, moves)
         return carry
 
     lax.fori_loop(H - 1, H + B + 1, ring, 0)
@@ -337,8 +374,7 @@
     sums[1872:1904] = grad_bias[...]
     sums[1904:1920] = grad_merge[128:144]
     sums[1920:] = jnp.zeros((2 * HALF - 1920, Z), F32)
-    mine = pl.multiple_of(place[0] * HALF, HALF)
-    other = pl.multiple_of(HALF - place[0] * HALF, HALF)
+    mine, other = halves()
     kept[...] = sums[pl.ds(mine, HALF), :]
     sent[...] = sums[pl.ds(other, HALF), :].astype(BF16)
 
@@ -355,6 +391,11 @@
             out_ref[pl.ds(B * i + j, 64, stride=B * B), :] = out[:, j * Z : (j + 1) * Z]
 
 
+def halves():
+    first = lax.axis_index("rep") * HALF
+    return pl.multiple_of(first, HALF), pl.multiple_of(HALF - first, HALF)
+
+
 def pair_kernel(kept, came, out_ref):
     out_ref[...] = (kept[...] + came[...].astype(F32)).astype(BF16)
 
@@ -382,11 +423,10 @@
     return jnp.sum(jnp.where(rows == lanes, block, 0.0), axis=0, keepdims=True)
 
 
-def unpack_kernel(scale, mine, other, place, g0, g1, g2, g3, bias, weight, weight_bias, sums):
-    sums[pl.ds(pl.multiple_of(place[0] * HALF, HALF), HALF), :] = mine[...].astype(F32) * scale
-    sums[pl.ds(pl.multiple_of(HALF - place[0] * HALF, HALF), HALF), :] = (
-        other[...].astype(F32) * scale
-    )
+def unpack_kernel(scale, mine_ref, other_ref, g0, g1, g2, g3, bias, weight, weight_bias, sums):
+    mine, other = halves()
+    sums[pl.ds(mine, HALF), :] = mine_ref[...].astype(F32) * scale
+    sums[pl.ds(other, HALF), :] = other_ref[...].astype(F32) * scale
     for k, g in enumerate((g0, g1, g2, g3)):
         g[...] = sums[432 * k : 432 * (k + 1), : g.shape[1]]
     weight[...] = sums[1728:1792]
@@ -395,29 +435,17 @@
         bias[k : k + 1] = turned(sums[1856 + 16 * k : 1872 + 16 * k])[:, :16]
 
 
-def exchange(top, bottom):
-    channels = top.shape[1]
+def exchange(left, right):
+    channels = left.shape[1]
+    up = [(i, i + 1) for i in range(lax.axis_size("row") - 1)]
+    before = lax.ppermute(right, "row", up)
+    after = lax.ppermute(left, "row", [(j, i) for i, j in up])
+    edge = shape((H, channels, N * Z), BF16)
+    top, bottom = call(rows_kernel, [edge, edge], [before, left, right, after], name="rows")
     up = [(i, i + 1) for i in range(lax.axis_size("gx") - 1)]
-    before = lax.ppermute(bottom, "gx", up)
-    after = lax.ppermute(top, "gx", [(j, i) for i, j in up])
-    side = shape((N, channels, H * Z), BF16)
-    left, right = call(
-        columns_kernel, [side, side], [before, top, bottom, after], name="columns"
-    )
-    up = [(i, i + 1) for i in range(lax.axis_size("row") - 1)]
-    from_before = lax.ppermute(right, "row", up)
-    from_after = lax.ppermute(left, "row", [(j, i) for i, j in up])
-    return [before, top, bottom, after, from_before, from_after]
-
-
-def grid_mask():
-    steps = jnp.arange(N) - H
-    gx = lax.axis_index("gx") * B + steps
-    gy = lax.axis_index("row") * B + steps
-    inside_x = (gx >= 0) & (gx < lax.axis_size("gx") * B)
-    inside_y = (gy >= 0) & (gy < lax.axis_size("row") * B)
-    inside = (inside_x[:, None] & inside_y[None, :]).astype(F32)
-    return jnp.repeat(inside, Z, axis=1)
+    above = lax.ppermute(bottom, "gx", up)
+    below = lax.ppermute(top, "gx", [(j, i) for i, j in up])
+    return [before, left, right, after, above, below]
 
 
 def body(samples, cotangent, kernel_0, kernel_1, kernel_2, kernel_3, layer_bias, merging_weight, merging_bias):
@@ -425,37 +453,38 @@
     cells = B * B * Z * lax.axis_size("gx") * lax.axis_size("row") * lax.axis_size("rep")
     scale = 1.0 / math.sqrt(cells)
     flat = [k.transpose(1, 0, 2).reshape(432, k.shape[2]) for k in kernels]
-    bias = jnp.broadcast_to(layer_bias.astype(F32).reshape(64, 1), (64, Z))
-    merge_bias = jnp.broadcast_to(merging_bias.astype(F32)[:, None], (64, Z))
-    mask = grid_mask()
-    half = shape((2, 64, B * Z), BF16)
+    half = shape((B, 64, H * Z), BF16)
+    columns = shape((64, Z), F32)
     wide = pltpu.VMEM((1024, Z), F32)
-    top, bottom = call(
-        pack_kernel, [half, half], [samples.reshape(1024, Z)], [wide], name="pack"
-    )
-    place = lax.axis_index("rep").astype(jnp.int32).reshape(1)
+    left, right, bias, merge_bias = call(
+        pack_kernel,
+        [half, half, columns, columns],
+        [samples.reshape(1024, Z), layer_bias, merging_bias.reshape(1, 64)],
+        [wide],
+        name="pack",
+    )
     base, carried, merge_grad, w0, w1, w2, w3, t0, t1, t2, t3 = call(
         prepare_kernel,
         [shape((B, 64, B * Z), F32)] * 2
         + [shape((B, 64, B * Z), BF16)]
         + [shape((144, 3 * k.shape[2]), BF16) for k in kernels]
         + [shape((3, k.shape[2], 144), BF16) for k in kernels],
-        [cotangent.reshape(1024, Z), merging_weight.T] + flat,
+        [cotangent.reshape(1024, Z), merging_weight] + flat,
         [wide],
         flops=40_000_000,
         name="prepare",
     )
-    parts = exchange(top, bottom)
+    parts = exchange(left, right)
     ring = shape((N, 16, (B + 2) * Z), F32)
-    send = shape((2, 32, B * Z), BF16)
-    frame, hidden_0, slope_0, slope_1, top, bottom = call(
+    send = shape((B, 32, H * Z), BF16)
+    frame, hidden_0, slope_0, slope_1, left, right = call(
         first_kernel,
         [shape((N, 64, N * Z), BF16), shape((N, 16, N * Z), BF16), ring, shape((B, 16, B * Z), F32), send, send],
-        parts + [w0, w1, bias, mask],
+        parts + [w0, w1, bias],
         name="layers_0_1",
     )
-    parts = exchange(top, bottom)
-    hidden_01, hidden_2, hidden_3, slope_2, own_3, top, bottom = call(
+    parts = exchange(left, right)
+    hidden_01, hidden_2, hidden_3, slope_2, own_3, left, right = call(
         second_kernel,
         [
             shape((N, 32, N * Z), BF16),
@@ -466,10 +495,10 @@
             send,
             send,
         ],
-        parts + [frame, w2, w3, bias, mask, carried],
+        parts + [frame, w2, w3, bias, carried],
         name="layers_2_3",
     )
-    parts = exchange(top, bottom)
+    parts = exchange(left, right)
     grads = shape((432, Z), F32)
     output, grad_3, grad_merge = call(
         merge_kernel,
@@ -478,16 +507,16 @@
         flops=100_000_000,
         name="merge",
     )
-    send = shape((2, 48, B * Z), BF16)
+    send = shape((B, 48, H * Z), BF16)
     spreads = shape((N, 48, N * Z), BF16)
-    spread_3, spread_2, own_1, top, bottom = call(
+    spread_3, spread_2, own_1, left, right = call(
         third_kernel,
         [spreads, spreads, shape((B, 48, B * Z), BF16), send, send],
-        parts + [t2, t3, slope_1, slope_2, mask, carried],
+        parts + [t2, t3, slope_1, slope_2, carried],
         [pltpu.VMEM((N, 32, N * Z), BF16), pltpu.VMEM((N, 16, N * Z), F32)],
         name="gradients_2_1",
     )
-    parts = exchange(top, bottom)
+    parts = exchange(left, right)
     grad_2, grad_1, grad_bias, part_0, part_base = call(
         beside_kernel,
         [grads, grads, shape((32, Z), F32), ring, shape((B, 64, B * Z), F32)],
@@ -499,8 +528,8 @@
         fourth_kernel,
         [spreads, spreads, spreads, shape((HALF, Z), F32), shape((HALF, Z), BF16)],
         parts
-        + [t1, t2, slope_0, mask, carried, part_0, frame]
-        + [grad_1, grad_2, grad_3, grad_merge, grad_bias, place],
+        + [t1, t2, slope_0, carried, part_0, frame]
+        + [grad_1, grad_2, grad_3, grad_merge, grad_bias],
         [pltpu.VMEM((2 * HALF, Z), F32), pltpu.VMEM((N, 48, N * Z), BF16), pltpu.VMEM((N, 16, N * Z), F32)],
         name="gradient_0",
     )
@@ -524,7 +553,7 @@
         functools.partial(unpack_kernel, scale),
         [shape((432, k.shape[2]), F32) for k in kernels]
         + [shape((4, 16), F32), shape((64, 128), F32), shape((1, 64), F32)],
-        [totals, others, place],
+        [totals, others],
         [pltpu.VMEM((2 * HALF, Z), F32)],
         name="unpack",
     )

time: 185 us -> 173 us (0.935)
  local copies, waits for them, and re-layouts: 13.6 us -> 1.65 us
  blocking collectives: 50.2 us -> 47.9 us
    unnamed x71 -> x18, local copies, waits for them, and re-layouts: 12.6 us -> 1.65 us
    ppermute x1, starting transfers between devices: 7.96 us -> 11.4 us  [body(): lax.ppermute(sent, 'rep', swap)]
    ppermute x16, starting transfers between devices: 47.2 us -> 44.6 us  [the longest x4 20.1 us: exchange(): before = lax.ppermute(right, 'row', up)]
    all_to_all x1, blocking collectives: 30 us -> 27.9 us  [body(): lax.all_to_all(paired.reshape(GROUP, ROWS, Z), axes, 0, 0, tiled=True)]
  transfers between devices with their start and end apart: 18 -> 18, of which waited for: 13 -> 14; matrix products, arithmetic and copies ran while one was open for 1% -> 0% of each run, Pallas kernels for 4% -> 4%
where the time goes in v3:
time: 173 us; the launch traced here: 172 us
  starting transfers between devices  59.5 us (34%)
  blocking collectives  47.9 us (28%)
  waiting for transfers between devices  38.6 us (22%)
  Pallas kernels  23.8 us (14%)
    all_to_all x1, blocking collectives, body(): lax.all_to_all(paired.reshape(GROUP, ROWS, Z), axes, 0, 0, tiled=True)  27.9 us
    pallas_call x16, Pallas kernels, call(): pl.pallas_call(kernel, out_shape=list(outs), in_specs=[pl.BlockSpec(memor...  23.8 us
    ppermute x4, waiting for transfers between devices, exchange(): after = lax.ppermute(left, 'row', [(j, i) for i, j in up])  20.9 us
    ppermute x4, starting transfers between devices, exchange(): before = lax.ppermute(right, 'row', up)  20.1 us
    all_to_all x1, blocking collectives, body(): lax.all_to_all(added.reshape(GROUP, ROWS, Z), axes, 0, 0, tiled=True)  20.1 us
    ppermute x4, starting transfers between devices, exchange(): above = lax.ppermute(bottom, 'gx', up)  14 us
    ppermute x4, waiting for transfers between devices, exchange(): below = lax.ppermute(top, 'gx', [(j, i) for i, j in up])  12.9 us
    ppermute x1, starting transfers between devices, body(): lax.ppermute(sent, 'rep', swap)  11.4 us
  transfers between devices with their start and end apart: 18, of which 14 were waited for; matrix products, arithmetic and copies ran while one was open for 0% of the time, Pallas kernels for 4%

profile of v3, /device:TPU:1, one launch (start us, length us, event | category | flops | bytes accessed | tf_op | source)
XLA Modules:
  0.0 172.5 jit_solution(8049774612768498588)
XLA Ops:
  2.5 5.7 %collective-permute-start = (bf16[4,64,256]{2,1,0:T(8,128)(2,1)S(1)}, bf16[4,64,256]{2,1,0:T(8,128)(2,1)S(1)}, u32[]{:S(2)}, u32[]{:S(2)}) collective-permute-start(bf16[4,64,256]{2,1,0:T(8,128)(2,1)S(1)} %get-tuple-element.69.right), channel_id=1, source_target_pairs={{0,2},{2,4},{4,6},{6,8},{8,10},{10,12},{12,14},{14,16},{16,18},{18... | collective-permute-start | bytes 393224 | tf_op jit(solution)/shard_map/ppermute | solution.py:441
  10.3 5.2 %collective-permute-done.1.after = bf16[4,64,256]{2,1,0:T(8,128)(2,1)S(1)} collective-permute-done((bf16[4,64,256]{2,1,0:T(8,128)(2,1)S(1)}, bf16[4,64,256]{2,1,0:T(8,128)(2,1)S(1)}, u32[]{:S(2)}, u32[]{:S(2)}) %collective-permute-start.1) | collective-permute-done | bytes 131104 | tf_op jit(solution)/shard_map/ppermute | solution.py:442
  15.6 3.1 %collective-permute-start.2 = (bf16[2,64,1024]{2,1,0:T(8,128)(2,1)S(1)}, bf16[2,64,1024]{2,1,0:T(8,128)(2,1)S(1)}, u32[]{:S(2)}, u32[]{:S(2)}) collective-permute-start(bf16[2,64,1024]{2,1,0:T(8,128)(2,1)S(1)} %get-tuple-element.71), channel_id=1, source_target_pairs={{0,32},{32,64},{64,96},{96,128},{128,160},{160,192},{192,224},{1,3... | collective-permute-start | bytes 786440 | tf_op jit(solution)/shard_map/ppermute | solution.py:446
  22.0 3.8 %collective-permute-done.3.below = bf16[2,64,1024]{2,1,0:T(8,128)(2,1)S(1)} collective-permute-done((bf16[2,64,1024]{2,1,0:T(8,128)(2,1)S(1)}, bf16[2,64,1024]{2,1,0:T(8,128)(2,1)S(1)}, u32[]{:S(2)}, u32[]{:S(2)}) %collective-permute-start.3) | collective-permute-done | bytes 262176 | tf_op jit(solution)/shard_map/ppermute | solution.py:447
  25.8 2.8 %layers_0_1.1 = (bf16[8,64,1024]{2,1,0:T(8,128)(2,1)S(1)}, bf16[8,16,1024]{2,1,0:T(8,128)(2,1)}, f32[8,16,768]{2,1,0:T(8,128)S(1)}, f32[4,16,512]{2,1,0:T(8,128)...) custom-call(bf16[4,64,256]{2,1,0:T(8,128)(2,1)S(1)} %collective-permute-done.before, ...), custom_call_target="tpu_custom_call" | custom-call | flops 1000000 | bytes 3171840 | tf_op jit(solution)/shard_map/layers_0_1/pallas_call | solution.py:31
  28.7 4.2 %collective-permute-start.4 = (bf16[4,32,256]{2,1,0:T(8,128)(2,1)S(1)}, bf16[4,32,256]{2,1,0:T(8,128)(2,1)S(1)}, u32[]{:S(2)}, u32[]{:S(2)}) collective-permute-start(bf16[4,32,256]{2,1,0:T(8,128)(2,1)S(1)} %get-tuple-element.77.right), channel_id=1, source_target_pairs={{0,2},{2,4},{4,6},{6,8},{8,10},{10,12},{12,14},{14,16},{16,18},{18... | collective-permute-start | bytes 196616 | tf_op jit(solution)/shard_map/ppermute | solution.py:441
  34.2 5.2 %collective-permute-done.5.after = bf16[4,32,256]{2,1,0:T(8,128)(2,1)S(1)} collective-permute-done((bf16[4,32,256]{2,1,0:T(8,128)(2,1)S(1)}, bf16[4,32,256]{2,1,0:T(8,128)(2,1)S(1)}, u32[]{:S(2)}, u32[]{:S(2)}) %collective-permute-start.5) | collective-permute-done | bytes 65568 | tf_op jit(solution)/shard_map/ppermute | solution.py:442
  39.4 3.1 %collective-permute-start.6 = (bf16[2,32,1024]{2,1,0:T(8,128)(2,1)S(1)}, bf16[2,32,1024]{2,1,0:T(8,128)(2,1)S(1)}, u32[]{:S(2)}, u32[]{:S(2)}) collective-permute-start(bf16[2,32,1024]{2,1,0:T(8,128)(2,1)S(1)} %get-tuple-element.79), channel_id=1, source_target_pairs={{0,32},{32,64},{64,96},{96,128},{128,160},{160,192},{192,224},{1,3... | collective-permute-start | bytes 393224 | tf_op jit(solution)/shard_map/ppermute | solution.py:446
  44.5 4.1 %collective-permute-done.7.below = bf16[2,32,1024]{2,1,0:T(8,128)(2,1)S(1)} collective-permute-done((bf16[2,32,1024]{2,1,0:T(8,128)(2,1)S(1)}, bf16[2,32,1024]{2,1,0:T(8,128)(2,1)S(1)}, u32[]{:S(2)}, u32[]{:S(2)}) %collective-permute-start.7) | collective-permute-done | bytes 131104 | tf_op jit(solution)/shard_map/ppermute | solution.py:447
  48.5 4.3 %layers_2_3.1 = (bf16[8,32,1024]{2,1,0:T(8,128)(2,1)S(1)}, bf16[8,16,1024]{2,1,0:T(8,128)(2,1)S(1)}, bf16[4,16,512]{2,1,0:T(8,128)(2,1)S(1)}, f32[8,16,768]{2,1,...) custom-call(bf16[4,32,256]{2,1,0:T(8,128)(2,1)S(1)} %collective-perm, ...), custom_call_target="tpu_custom_call" | custom-call | flops 1000000 | bytes 3882496 | tf_op jit(solution)/shard_map/layers_2_3/pallas_call | solution.py:31
  52.8 4.5 %collective-permute-start.8 = (bf16[4,32,256]{2,1,0:T(8,128)(2,1)S(1)}, bf16[4,32,256]{2,1,0:T(8,128)(2,1)S(1)}, u32[]{:S(2)}, u32[]{:S(2)}) collective-permute-start(bf16[4,32,256]{2,1,0:T(8,128)(2,1)S(1)} %get-tuple-element.91.right), channel_id=1, source_target_pairs={{0,2},{2,4},{4,6},{6,8},{8,10},{10,12},{12,14},{14,16},{16,18},{18... | collective-permute-start | bytes 196616 | tf_op jit(solution)/shard_map/ppermute | solution.py:441
  58.7 5.2 %collective-permute-done.9.after = bf16[4,32,256]{2,1,0:T(8,128)(2,1)S(1)} collective-permute-done((bf16[4,32,256]{2,1,0:T(8,128)(2,1)S(1)}, bf16[4,32,256]{2,1,0:T(8,128)(2,1)S(1)}, u32[]{:S(2)}, u32[]{:S(2)}) %collective-permute-start.9) | collective-permute-done | bytes 65568 | tf_op jit(solution)/shard_map/ppermute | solution.py:442
  63.9 4.1 %collective-permute-start.10 = (bf16[2,32,1024]{2,1,0:T(8,128)(2,1)S(1)}, bf16[2,32,1024]{2,1,0:T(8,128)(2,1)S(1)}, u32[]{:S(2)}, u32[]{:S(2)}) collective-permute-start(bf16[2,32,1024]{2,1,0:T(8,128)(2,1)S(1)} %get-tuple-element.93), channel_id=1, source_target_pairs={{0,32},{32,64},{64,96},{96,128},{128,160},{160,192},{192,224},{1,3... | collective-permute-start | bytes 393224 | tf_op jit(solution)/shard_map/ppermute | solution.py:446
  69.9 3.8 %collective-permute-done.11.below = bf16[2,32,1024]{2,1,0:T(8,128)(2,1)S(1)} collective-permute-done((bf16[2,32,1024]{2,1,0:T(8,128)(2,1)S(1)}, bf16[2,32,1024]{2,1,0:T(8,128)(2,1)S(1)}, u32[]{:S(2)}, u32[]{:S(2)}) %collective-permute-start.11) | collective-permute-done | bytes 131104 | tf_op jit(solution)/shard_map/ppermute | solution.py:447
  73.7 3.9 %gradients_2_1.1 = (bf16[8,48,1024]{2,1,0:T(8,128)(2,1)S(1)}, bf16[8,48,1024]{2,1,0:T(8,128)(2,1)S(1)}, bf16[4,48,512]{2,1,0:T(8,128)(2,1)S(1)}, bf16[4,48,256]{2,1,0:T(8,128)(2,1)S(1)}, bf16[4,48,256]{2,1,0:T(8,128)(2,1)S(1)}) custom-call(bf16[4,32,256]{2,1,0:T(8,128)(2,1)S(1)} %collective-permute-done.8.before, ...), custom_call_target="tpu_custom_call" | custom-call | flops 1000000 | bytes 3718656 | tf_op jit(solution)/shard_map/gradients_2_1/pallas_call | solution.py:31
  77.7 5.8 %collective-permute-start.12 = (bf16[4,48,256]{2,1,0:T(8,128)(2,1)S(1)}, bf16[4,48,256]{2,1,0:T(8,128)(2,1)S(1)}, u32[]{:S(2)}, u32[]{:S(2)}) collective-permute-start(bf16[4,48,256]{2,1,0:T(8,128)(2,1)S(1)} %get-tuple-element.99.right), channel_id=1, source_target_pairs={{0,2},{2,4},{4,6},{6,8},{8,10},{10,12},{12,14},{14,16},{16,18},{18... | collective-permute-start | bytes 294920 | tf_op jit(solution)/shard_map/ppermute | solution.py:441
  85.0 5.2 %collective-permute-done.13.after = bf16[4,48,256]{2,1,0:T(8,128)(2,1)S(1)} collective-permute-done((bf16[4,48,256]{2,1,0:T(8,128)(2,1)S(1)}, bf16[4,48,256]{2,1,0:T(8,128)(2,1)S(1)}, u32[]{:S(2)}, u32[]{:S(2)}) %collective-permute-start.13) | collective-permute-done | bytes 98336 | tf_op jit(solution)/shard_map/ppermute | solution.py:442
  90.3 3.7 %collective-permute-start.14 = (bf16[2,48,1024]{2,1,0:T(8,128)(2,1)S(1)}, bf16[2,48,1024]{2,1,0:T(8,128)(2,1)S(1)}, u32[]{:S(2)}, u32[]{:S(2)}) collective-permute-start(bf16[2,48,1024]{2,1,0:T(8,128)(2,1)S(1)} %get-tuple-element.101), channel_id=1, source_target_pairs={{0,32},{32,64},{64,96},{96,128},{128,160},{160,192},{192,224},{1,3... | collective-permute-start | bytes 589832 | tf_op jit(solution)/shard_map/ppermute | solution.py:446
  96.5 3.0 %kernel_gradients_2_1.1 = (f32[432,128]{1,0:T(8,128)S(1)}, f32[432,128]{1,0:T(8,128)S(1)}, f32[32,128]{1,0:T(8,128)S(1)}, f32[8,16,768]{2,1,0:T(8,128)S(1)}, f32[4,64,512]{2,1,0:T(8,128)S(1)}) custom-call(bf16[8,64,1024]{2,1,0:T(8,128)(2,1)S(1)} %get-tuple-element.76.frame, bf16[8,32,1024]{2,1,0:T(8,128)(2,1)S(1)} %get-tuple-element.84.hidden_01, ...), custom_call_target="tpu_custom_call" | custom-call | flops 200000000 | bytes 5339648 | tf_op jit(solution)/shard_map/kernel_gradients_2_1/pallas_call | solution.py:31
  100.7 4.5 %gradient_0.1 = (bf16[8,48,1024]{2,1,0:T(8,128)(2,1)S(1)}, bf16[8,48,1024]{2,1,0:T(8,128)(2,1)S(1)}, bf16[8,48,1024]{2,1,0:T(8,128)(2,1)S(1)}, f32[1024,128]{1,0:T(8,128)S(1)}, bf16[1024,128]{1,0:T(8,128)(2,1)S(1)}) custom-call(bf16[4,48,256]{2,1,0:T(8,128)(2,1)S(1)} %collective-permute-done.12.before, bf16[4,48,256]{2,1,0:T(8,128)(2,1)S(1)} %get-tuple-element.100.left, ...), custom_call_target="tpu_custom_call" | custom-call | flops 1000000 | bytes 7197184 | tf_op jit(solution)/shard_map/gradient_0/pallas_call | solution.py:31
  105.3 11.4 %collective-permute-start.16 = (bf16[1024,128]{1,0:T(8,128)(2,1)S(1)}, bf16[1024,128]{1,0:T(8,128)(2,1)S(1)}, u32[]{:S(2)}, u32[]{:S(2)}) collective-permute-start(bf16[1024,128]{1,0:T(8,128)(2,1)S(1)} %get-tuple-element.121), channel_id=1, source_target_pairs={{0,1},{1,0},{2,3},{3,2},{4,5},{5,4},{6,7},{7,6},{8,9},{9,8},{10,11... | collective-permute-start | bytes 786440 | tf_op jit(solution)/shard_map/ppermute | solution.py:539
  118.0 27.9 %all_to_all.10 = bf16[128,8,128]{2,1,0:T(8,128)(2,1)S(1)} all-to-all(bf16[128,8,128]{2,1,0:T(8,128)(2,1)S(1)} %bitcast.38), channel_id=1, replica_groups=mesh['gx'=8,'row'=16,'rep'=2] {'gx','row'}, dimensions={0} | all-to-all | bytes 524288 | tf_op jit(solution)/shard_map/all_to_all | solution.py:540
  146.0 20.1 %all_to_all.11 = bf16[128,8,128]{2,1,0:T(8,128)(2,1)S(1)} all-to-all(bf16[128,8,128]{2,1,0:T(8,128)(2,1)S(1)} %bitcast.37), channel_id=1, replica_groups=mesh['gx'=8,'row'=16,'rep'=2] {'gx','row'}, dimensions={0} | all-to-all | bytes 524288 | tf_op jit(solution)/shard_map/all_to_all | solution.py:542
  166.1 3.5 %collective-permute-start.17 = (bf16[1024,128]{1,0:T(8,128)(2,1)S(1)}, bf16[1024,128]{1,0:T(8,128)(2,1)S(1)}, u32[]{:S(2)}, u32[]{:S(2)}) collective-permute-start(bf16[1024,128]{1,0:T(8,128)(2,1)S(1)} %bitcast.34), channel_id=1, source_target_pairs={{0,1},{1,0},{2,3},{3,2},{4,5},{5,4},{6,7},{7,6},{8,9},{9,8},{10,11... | collective-permute-start | bytes 786440 | tf_op jit(solution)/shard_map/ppermute | solution.py:544
  (48 shorter events, 23.3 us)
Async XLA Ops:
  2.3 17.8 %copy-start.4 = (bf16[16,27,96]{2,0,1:T(8,128)(2,1)S(1)}, bf16[16,27,96]{2,0,1:T(8,128)(2,1)}, u32[]{:S(2)}) copy-start(bf16[16,27,96]{2,0,1:T(8,128)(2,1)} %param.13) | copy-start | bytes 248836
  2.3 17.8 %copy-start.5 = (bf16[16,27,112]{2,0,1:T(8,128)(2,1)S(1)}, bf16[16,27,112]{2,0,1:T(8,128)(2,1)}, u32[]{:S(2)}) copy-start(bf16[16,27,112]{2,0,1:T(8,128)(2,1)} %param.14) | copy-start | bytes 290308
  2.5 7.8 %collective-permute-start = (bf16[4,64,256]{2,1,0:T(8,128)(2,1)S(1)}, bf16[4,64,256]{2,1,0:T(8,128)(2,1)S(1)}, u32[]{:S(2)}, u32[]{:S(2)}) collective-permute-start(bf16[4,64,256]{2,1,0:T(8,128)(2,1)S(1)} %get-tuple-element.69.right), channel_id=1, source_target_pairs={{0,2},{2,4},{4,6},{6,8},{8,10},{10,12},{12,14},{14,16},{16,18},{18... | collective-permute-start | bytes 393224 | tf_op jit(solution)/shard_map/ppermute | solution.py:441
  8.1 11.9 %copy-start.1 = (bf16[1,64,4,4,128]{4,3,2,1,0:T(4,128)(2,1)S(1)}, bf16[1,64,4,4,128]{4,3,2,1,0:T(4,128)(2,1)}, u32[]{:S(2)}) copy-start(bf16[1,64,4,4,128]{4,3,2,1,0:T(4,128)(2,1)} %param.10) | copy-start | bytes 786436
  8.2 11.9 %copy-start.2 = (bf16[16,27,64]{2,0,1:T(8,128)(2,1)S(1)}, bf16[16,27,64]{2,0,1:T(8,128)(2,1)}, u32[]{:S(2)}) copy-start(bf16[16,27,64]{2,0,1:T(8,128)(2,1)} %param.11) | copy-start | bytes 165892
  8.2 11.9 %copy-start.3 = (bf16[16,27,80]{2,0,1:T(8,128)(2,1)S(1)}, bf16[16,27,80]{2,0,1:T(8,128)(2,1)}, u32[]{:S(2)}) copy-start(bf16[16,27,80]{2,0,1:T(8,128)(2,1)} %param.12) | copy-start | bytes 207364
  8.2 7.3 %collective-permute-start.1 = (bf16[4,64,256]{2,1,0:T(8,128)(2,1)S(1)}, bf16[4,64,256]{2,1,0:T(8,128)(2,1)S(1)}, u32[]{:S(2)}, u32[]{:S(2)}) collective-permute-start(bf16[4,64,256]{2,1,0:T(8,128)(2,1)S(1)} %get-tuple-element.70.left), channel_id=1, source_target_pairs={{2,0},{4,2},{6,4},{8,6},{10,8},{12,10},{14,12},{16,14},{18,16},{20... | collective-permute-start | bytes 393224 | tf_op jit(solution)/shard_map/ppermute | solution.py:442
  15.5 4.6 %copy-start.6 = (bf16[64,128]{1,0:T(8,128)(2,1)S(1)}, bf16[64,128]{1,0:T(8,128)(2,1)}, u32[]{:S(2)}) copy-start(bf16[64,128]{1,0:T(8,128)(2,1)} %merge.5) | copy-start | bytes 49156
  15.6 6.4 %collective-permute-start.2 = (bf16[2,64,1024]{2,1,0:T(8,128)(2,1)S(1)}, bf16[2,64,1024]{2,1,0:T(8,128)(2,1)S(1)}, u32[]{:S(2)}, u32[]{:S(2)}) collective-permute-start(bf16[2,64,1024]{2,1,0:T(8,128)(2,1)S(1)} %get-tuple-element.71), channel_id=1, source_target_pairs={{0,32},{32,64},{64,96},{96,128},{128,160},{160,192},{192,224},{1,3... | collective-permute-start | bytes 786440 | tf_op jit(solution)/shard_map/ppermute | solution.py:446
  18.7 7.1 %collective-permute-start.3 = (bf16[2,64,1024]{2,1,0:T(8,128)(2,1)S(1)}, bf16[2,64,1024]{2,1,0:T(8,128)(2,1)S(1)}, u32[]{:S(2)}, u32[]{:S(2)}) collective-permute-start(bf16[2,64,1024]{2,1,0:T(8,128)(2,1)S(1)} %get-tuple-element.72), channel_id=1, source_target_pairs={{32,0},{64,32},{96,64},{128,96},{160,128},{192,160},{224,192},{33,... | collective-permute-start | bytes 786440 | tf_op jit(solution)/shard_map/ppermute | solution.py:447
  28.7 5.5 %collective-permute-start.4 = (bf16[4,32,256]{2,1,0:T(8,128)(2,1)S(1)}, bf16[4,32,256]{2,1,0:T(8,128)(2,1)S(1)}, u32[]{:S(2)}, u32[]{:S(2)}) collective-permute-start(bf16[4,32,256]{2,1,0:T(8,128)(2,1)S(1)} %get-tuple-element.77.right), channel_id=1, source_target_pairs={{0,2},{2,4},{4,6},{6,8},{8,10},{10,12},{12,14},{14,16},{16,18},{18... | collective-permute-start | bytes 196616 | tf_op jit(solution)/shard_map/ppermute | solution.py:441
  32.9 6.5 %collective-permute-start.5 = (bf16[4,32,256]{2,1,0:T(8,128)(2,1)S(1)}, bf16[4,32,256]{2,1,0:T(8,128)(2,1)S(1)}, u32[]{:S(2)}, u32[]{:S(2)}) collective-permute-start(bf16[4,32,256]{2,1,0:T(8,128)(2,1)S(1)} %get-tuple-element.78.left), channel_id=1, source_target_pairs={{2,0},{4,2},{6,4},{8,6},{10,8},{12,10},{14,12},{16,14},{18,16},{20... | collective-permute-start | bytes 196616 | tf_op jit(solution)/shard_map/ppermute | solution.py:442
  39.4 5.0 %collective-permute-start.6 = (bf16[2,32,1024]{2,1,0:T(8,128)(2,1)S(1)}, bf16[2,32,1024]{2,1,0:T(8,128)(2,1)S(1)}, u32[]{:S(2)}, u32[]{:S(2)}) collective-permute-start(bf16[2,32,1024]{2,1,0:T(8,128)(2,1)S(1)} %get-tuple-element.79), channel_id=1, source_target_pairs={{0,32},{32,64},{64,96},{96,128},{128,160},{160,192},{192,224},{1,3... | collective-permute-start | bytes 393224 | tf_op jit(solution)/shard_map/ppermute | solution.py:446
  42.5 6.0 %collective-permute-start.7 = (bf16[2,32,1024]{2,1,0:T(8,128)(2,1)S(1)}, bf16[2,32,1024]{2,1,0:T(8,128)(2,1)S(1)}, u32[]{:S(2)}, u32[]{:S(2)}) collective-permute-start(bf16[2,32,1024]{2,1,0:T(8,128)(2,1)S(1)} %get-tuple-element.80), channel_id=1, source_target_pairs={{32,0},{64,32},{96,64},{128,96},{160,128},{192,160},{224,192},{33,... | collective-permute-start | bytes 393224 | tf_op jit(solution)/shard_map/ppermute | solution.py:447
  52.8 5.8 %collective-permute-start.8 = (bf16[4,32,256]{2,1,0:T(8,128)(2,1)S(1)}, bf16[4,32,256]{2,1,0:T(8,128)(2,1)S(1)}, u32[]{:S(2)}, u32[]{:S(2)}) collective-permute-start(bf16[4,32,256]{2,1,0:T(8,128)(2,1)S(1)} %get-tuple-element.91.right), channel_id=1, source_target_pairs={{0,2},{2,4},{4,6},{6,8},{8,10},{10,12},{12,14},{14,16},{16,18},{18... | collective-permute-start | bytes 196616 | tf_op jit(solution)/shard_map/ppermute | solution.py:441
  57.4 6.5 %collective-permute-start.9 = (bf16[4,32,256]{2,1,0:T(8,128)(2,1)S(1)}, bf16[4,32,256]{2,1,0:T(8,128)(2,1)S(1)}, u32[]{:S(2)}, u32[]{:S(2)}) collective-permute-start(bf16[4,32,256]{2,1,0:T(8,128)(2,1)S(1)} %get-tuple-element.92.left), channel_id=1, source_target_pairs={{2,0},{4,2},{6,4},{8,6},{10,8},{12,10},{14,12},{16,14},{18,16},{20... | collective-permute-start | bytes 196616 | tf_op jit(solution)/shard_map/ppermute | solution.py:442
  63.9 6.0 %collective-permute-start.10 = (bf16[2,32,1024]{2,1,0:T(8,128)(2,1)S(1)}, bf16[2,32,1024]{2,1,0:T(8,128)(2,1)S(1)}, u32[]{:S(2)}, u32[]{:S(2)}) collective-permute-start(bf16[2,32,1024]{2,1,0:T(8,128)(2,1)S(1)} %get-tuple-element.93), channel_id=1, source_target_pairs={{0,32},{32,64},{64,96},{96,128},{128,160},{160,192},{192,224},{1,3... | collective-permute-start | bytes 393224 | tf_op jit(solution)/shard_map/ppermute | solution.py:446
  68.0 5.7 %collective-permute-start.11 = (bf16[2,32,1024]{2,1,0:T(8,128)(2,1)S(1)}, bf16[2,32,1024]{2,1,0:T(8,128)(2,1)S(1)}, u32[]{:S(2)}, u32[]{:S(2)}) collective-permute-start(bf16[2,32,1024]{2,1,0:T(8,128)(2,1)S(1)} %get-tuple-element.94), channel_id=1, source_target_pairs={{32,0},{64,32},{96,64},{128,96},{160,128},{192,160},{224,192},{33,... | collective-permute-start | bytes 393224 | tf_op jit(solution)/shard_map/ppermute | solution.py:447
  77.7 7.4 %collective-permute-start.12 = (bf16[4,48,256]{2,1,0:T(8,128)(2,1)S(1)}, bf16[4,48,256]{2,1,0:T(8,128)(2,1)S(1)}, u32[]{:S(2)}, u32[]{:S(2)}) collective-permute-start(bf16[4,48,256]{2,1,0:T(8,128)(2,1)S(1)} %get-tuple-element.99.right), channel_id=1, source_target_pairs={{0,2},{2,4},{4,6},{6,8},{8,10},{10,12},{12,14},{14,16},{16,18},{18... | collective-permute-start | bytes 294920 | tf_op jit(solution)/shard_map/ppermute | solution.py:441
  83.4 6.9 %collective-permute-start.13 = (bf16[4,48,256]{2,1,0:T(8,128)(2,1)S(1)}, bf16[4,48,256]{2,1,0:T(8,128)(2,1)S(1)}, u32[]{:S(2)}, u32[]{:S(2)}) collective-permute-start(bf16[4,48,256]{2,1,0:T(8,128)(2,1)S(1)} %get-tuple-element.100.left), channel_id=1, source_target_pairs={{2,0},{4,2},{6,4},{8,6},{10,8},{12,10},{14,12},{16,14},{18,16},{20... | collective-permute-start | bytes 294920 | tf_op jit(solution)/shard_map/ppermute | solution.py:442
  90.3 9.2 %collective-permute-start.14 = (bf16[2,48,1024]{2,1,0:T(8,128)(2,1)S(1)}, bf16[2,48,1024]{2,1,0:T(8,128)(2,1)S(1)}, u32[]{:S(2)}, u32[]{:S(2)}) collective-permute-start(bf16[2,48,1024]{2,1,0:T(8,128)(2,1)S(1)} %get-tuple-element.101), channel_id=1, source_target_pairs={{0,32},{32,64},{64,96},{96,128},{128,160},{160,192},{192,224},{1,3... | collective-permute-start | bytes 589832 | tf_op jit(solution)/shard_map/ppermute | solution.py:446
  94.0 6.7 %collective-permute-start.15 = (bf16[2,48,1024]{2,1,0:T(8,128)(2,1)S(1)}, bf16[2,48,1024]{2,1,0:T(8,128)(2,1)S(1)}, u32[]{:S(2)}, u32[]{:S(2)}) collective-permute-start(bf16[2,48,1024]{2,1,0:T(8,128)(2,1)S(1)} %get-tuple-element.102), channel_id=1, source_target_pairs={{32,0},{64,32},{96,64},{128,96},{160,128},{192,160},{224,192},{33,... | collective-permute-start | bytes 589832 | tf_op jit(solution)/shard_map/ppermute | solution.py:447
  105.3 12.6 %collective-permute-start.16 = (bf16[1024,128]{1,0:T(8,128)(2,1)S(1)}, bf16[1024,128]{1,0:T(8,128)(2,1)S(1)}, u32[]{:S(2)}, u32[]{:S(2)}) collective-permute-start(bf16[1024,128]{1,0:T(8,128)(2,1)S(1)} %get-tuple-element.121), channel_id=1, source_target_pairs={{0,1},{1,0},{2,3},{3,2},{4,5},{5,4},{6,7},{7,6},{8,9},{9,8},{10,11... | collective-permute-start | bytes 786440 | tf_op jit(solution)/shard_map/ppermute | solution.py:539
  166.1 5.4 %collective-permute-start.17 = (bf16[1024,128]{1,0:T(8,128)(2,1)S(1)}, bf16[1024,128]{1,0:T(8,128)(2,1)S(1)}, u32[]{:S(2)}, u32[]{:S(2)}) collective-permute-start(bf16[1024,128]{1,0:T(8,128)(2,1)S(1)} %bitcast.34), channel_id=1, source_target_pairs={{0,1},{1,0},{2,3},{3,2},{4,5},{5,4},{6,7},{7,6},{8,9},{9,8},{10,11... | collective-permute-start | bytes 786440 | tf_op jit(solution)/shard_map/ppermute | solution.py:544
  (3 other events, 2.3 us)

commit v4 on v3

--- a/solution.py
+++ b/solution.py
@@ -53,21 +53,9 @@
     return jnp.where(keep, pltpu.roll(v, v.shape[1] - 1, 1), 0.0)
 
 
-def one_cell_moves():
-    row = lax.broadcasted_iota(jnp.int32, (Z, 2 * Z), 0)
-    lane = lax.broadcasted_iota(jnp.int32, (Z, 2 * Z), 1)
-    return jnp.where((row == lane + 1) | (row == lane - Z - 1), 1.0, 0.0).astype(BF16)
-
-
-def spread(v, moves):
-    blocks = v.shape[1] // Z
-    tall = jnp.concatenate([v[:, k * Z : (k + 1) * Z] for k in range(blocks)], axis=0)
-    got = jnp.dot(tall, moves, preferred_element_type=F32).astype(BF16)
-    later, earlier = (
-        jnp.concatenate([half[16 * k : 16 * (k + 1)] for k in range(blocks)], axis=1)
-        for half in (got[:, :Z], got[:, Z:])
-    )
-    return jnp.concatenate([later, v, earlier], axis=0)
+def spread(v):
+    not_first, not_last = lane_moves(*v.shape)
+    return jnp.concatenate([from_right(v, not_last), v, from_left(v, not_first)], axis=0).astype(BF16)
 
 
 def inside(i):
@@ -169,15 +157,11 @@
     return wide_sum([rows[16:32] for rows in own])
 
 
-def pack_kernel(x_ref, layer_bias, merging_bias, left, right, bias, merge_bias, wide):
+def pack_kernel(x_ref, left, right, wide):
     wide[...] = x_ref[...].astype(F32)
     for i in range(B):
         row = [wide[pl.ds(B * i + j, 64, stride=B * B), :].astype(BF16) for j in range(B)]
         put((left, right), i, slice(0, 64), jnp.concatenate(row, axis=1))
-    for k in range(4):
-        column = as_column(layer_bias[k : k + 1].astype(F32))
-        bias[16 * k : 16 * (k + 1)] = jnp.broadcast_to(column, (16, Z))
-    merge_bias[...] = jnp.broadcast_to(as_column(merging_bias[...].astype(F32)), (64, Z))
 
 
 def rows_kernel(before, left, right, after, top, bottom):
@@ -187,7 +171,14 @@
         bottom[:, :, lanes] = ref[B - H :]
 
 
-def prepare_kernel(cot_ref, merge, k0, k1, k2, k3, base, carried, merge_grad, w0, w1, w2, w3, t0, t1, t2, t3, wide):
+def prepare_kernel(
+    cot_ref, merge, layer_bias, merging_bias, k0, k1, k2, k3,
+    base, carried, merge_grad, bias, merge_bias, w0, w1, w2, w3, t0, t1, t2, t3, wide,
+):
+    for k in range(4):
+        column = as_column(layer_bias[k : k + 1].astype(F32))
+        bias[16 * k : 16 * (k + 1)] = jnp.broadcast_to(column, (16, Z))
+    merge_bias[...] = jnp.broadcast_to(as_column(merging_bias[...].astype(F32)), (64, Z))
     for k_ref, w_ref, t_ref in ((k0, w0, t0), (k1, w1, t1), (k2, w2, t2), (k3, w3, t3)):
         w_ref[...] = jnp.concatenate([k_ref[144 * a : 144 * (a + 1)] for a in range(3)], axis=1)
         for b in range(3):
@@ -212,14 +203,11 @@
 ):
     assemble((before, left, right, after, above, below), frame)
 
-    def ring(i, carry):
+    for i in range(H - 1, H + B + 1):
         pre = conv_row(k0, [frame], i, RING) + bias[0:16, 0:1]
         value, slope = activate(pre)
         slope_0[i] = slope
         hidden_0[i, :, RING] = (value * inside(i)).astype(BF16)
-        return carry
-
-    lax.fori_loop(H - 1, H + B + 1, ring, 0)
     for i in range(B):
         pre = conv_row(k1, [frame, hidden_0], H + i, MID) + bias[16:32, 0:1]
         value, slope = activate(pre)
@@ -233,22 +221,18 @@
     hidden_01, hidden_2, hidden_3, slope_2, own_3, send_left, send_right,
 ):
     assemble((before, left, right, after, above, below), hidden_01)
-    moves = one_cell_moves()
-
-    def ring(i, carry):
+
+    for i in range(H - 1, H + B + 1):
         pre = conv_row(k2, [frame, hidden_01], i, RING) + bias[32:48, 0:1]
         value, slope = activate(pre)
         slope_2[i] = slope
         hidden_2[i, :, RING] = (value * inside(i)).astype(BF16)
-        return carry
-
-    lax.fori_loop(H - 1, H + B + 1, ring, 0)
     for i in range(B):
         pre = conv_row(k3, [frame, hidden_01, hidden_2], H + i, MID) + bias[48:64, 0:1]
         value, slope = activate(pre)
         hidden_3[i] = value.astype(BF16)
         grad = (carried[i, 48:64] * slope).astype(BF16)
-        own_3[i] = spread(grad, moves)
+        own_3[i] = spread(grad.astype(F32))
         put((send_left, send_right), i, slice(0, 16), grad)
         put((send_left, send_right), i, slice(16, 32), carried[i, 32:48].astype(BF16))
 
@@ -283,24 +267,17 @@
     spread_3, spread_2, own_1, send_left, send_right, pieces, held,
 ):
     assemble((before, left, right, after, above, below), pieces)
-    moves = one_cell_moves()
     held[...] = pieces[:, 16:32, :].astype(F32)
     for i in range(B):
         held[H + i, :, MID] = carried[i, 32:48]
 
-    def move(i, carry):
-        spread_3[i] = spread(pieces[i, 0:16], moves)
-        return carry
-
-    lax.fori_loop(0, N, move, 0)
-
-    def ring(i, carry):
+    for i in range(N):
+        spread_3[i] = spread(pieces[i, 0:16].astype(F32))
+
+    for i in range(H - 1, H + B + 1):
         got = held[i, :, RING] + back_row(t3, slice(96, 112), spread_3, i, RING)
         grad = (got * slope_2[i] * inside(i)).astype(BF16)
-        spread_2[i, :, RING] = spread(grad, moves)
-        return carry
-
-    lax.fori_loop(H - 1, H + B + 1, ring, 0)
+        spread_2[i, :, RING] = spread(grad.astype(F32))
     for i in range(B):
         got = (
             carried[i, 16:32]
@@ -308,7 +285,7 @@
             + back_row(t2, slice(80, 96), spread_2, H + i, MID)
         )
         grad = (got * slope_1[i]).astype(BF16)
-        own_1[i] = spread(grad, moves)
+        own_1[i] = spread(grad.astype(F32))
         put((send_left, send_right), i, slice(0, 16), spread_2[H + i, 16:32, MID])
         put((send_left, send_right), i, slice(16, 32), grad)
         put((send_left, send_right), i, slice(32, 48), carried[i, 0:16].astype(BF16))
@@ -325,11 +302,8 @@
     grad_bias[16:32] = cell_sum(own)
     kernel_gradient(grad_2, own, [frame, hidden_01])
 
-    def ring(i, carry):
+    for i in range(H - 1, H + B + 1):
         part_0[i] = back_row(t3, slice(64, 80), spread_3, i, RING)
-        return carry
-
-    lax.fori_loop(H - 1, H + B + 1, ring, 0)
     for i in range(B):
         part_base[i] = base[i] + back_row(t3, slice(0, 64), spread_3, H + i, MID)
 
@@ -340,19 +314,15 @@
     spread_2, spread_1, spread_0, kept, sent, sums, pieces, held,
 ):
     assemble((before, left, right, after, above, below), pieces)
-    moves = one_cell_moves()
     held[...] = pieces[:, 32:48, :].astype(F32)
     for i in range(B):
         held[H + i, :, MID] = carried[i, 0:16]
 
-    def move(i, carry):
-        spread_2[i] = spread(pieces[i, 0:16], moves)
-        spread_1[i] = spread(pieces[i, 16:32], moves)
-        return carry
-
-    lax.fori_loop(0, N, move, 0)
-
-    def ring(i, carry):
+    for i in range(N):
+        spread_2[i] = spread(pieces[i, 0:16].astype(F32))
+        spread_1[i] = spread(pieces[i, 16:32].astype(F32))
+
+    for i in range(H - 1, H + B + 1):
         got = (
             held[i, :, RING]
             + part_0[i]
@@ -360,10 +330,7 @@
             + back_row(t1, slice(64, 80), spread_1, i, RING)
         )
         grad = (got * slope_0[i] * inside(i)).astype(BF16)
-        spread_0[i, :, RING] = spread(grad, moves)
-        return carry
-
-    lax.fori_loop(H - 1, H + B + 1, ring, 0)
+        spread_0[i, :, RING] = spread(grad.astype(F32))
     own = own_cells(spread_0)
     kernel_gradient(sums.at[0:432], own, [frame])
     sums[432:864] = grad_1[...]
@@ -456,20 +423,14 @@
     half = shape((B, 64, H * Z), BF16)
     columns = shape((64, Z), F32)
     wide = pltpu.VMEM((1024, Z), F32)
-    left, right, bias, merge_bias = call(
-        pack_kernel,
-        [half, half, columns, columns],
-        [samples.reshape(1024, Z), layer_bias, merging_bias.reshape(1, 64)],
-        [wide],
-        name="pack",
-    )
-    base, carried, merge_grad, w0, w1, w2, w3, t0, t1, t2, t3 = call(
+    left, right = call(pack_kernel, [half, half], [samples.reshape(1024, Z)], [wide], name="pack")
+    base, carried, merge_grad, bias, merge_bias, w0, w1, w2, w3, t0, t1, t2, t3 = call(
         prepare_kernel,
         [shape((B, 64, B * Z), F32)] * 2
-        + [shape((B, 64, B * Z), BF16)]
+        + [shape((B, 64, B * Z), BF16), columns, columns]
         + [shape((144, 3 * k.shape[2]), BF16) for k in kernels]
         + [shape((3, k.shape[2], 144), BF16) for k in kernels],
-        [cotangent.reshape(1024, Z), merging_weight] + flat,
+        [cotangent.reshape(1024, Z), merging_weight, layer_bias, merging_bias.reshape(1, 64)] + flat,
         [wide],
         flops=40_000_000,
         name="prepare",

time: 173 us -> 163 us (0.942)
  Pallas kernels: 23.8 us -> 13.6 us
    pallas_call x16, Pallas kernels: 23.8 us -> 13.6 us  [call(): pl.pallas_call(kernel, out_shape=list(outs), in_specs=[pl.BlockSpec(memor...]
where the time goes in v4:
time: 163 us; the launch traced here: 162 us
  starting transfers between devices  59.6 us (37%)
  blocking collectives  47.3 us (29%)
  waiting for transfers between devices  38.9 us (24%)
  Pallas kernels  13.6 us (8%)
    all_to_all x1, blocking collectives, body(): lax.all_to_all(paired.reshape(GROUP, ROWS, Z), axes, 0, 0, tiled=True)  27.2 us
    ppermute x4, waiting for transfers between devices, exchange(): after = lax.ppermute(left, 'row', [(j, i) for i, j in up])  20.9 us
    ppermute x4, starting transfers between devices, exchange(): before = lax.ppermute(right, 'row', up)  20.1 us
    all_to_all x1, blocking collectives, body(): lax.all_to_all(added.reshape(GROUP, ROWS, Z), axes, 0, 0, tiled=True)  20.1 us
    ppermute x4, starting transfers between devices, exchange(): above = lax.ppermute(bottom, 'gx', up)  14 us
    ppermute x4, waiting for transfers between devices, exchange(): below = lax.ppermute(top, 'gx', [(j, i) for i, j in up])  13.9 us
    pallas_call x16, Pallas kernels, call(): pl.pallas_call(kernel, out_shape=list(outs), in_specs=[pl.BlockSpec(memor...  13.6 us
    ppermute x1, starting transfers between devices, body(): lax.ppermute(sent, 'rep', swap)  11.6 us
  transfers between devices with their start and end apart: 18, of which 14 were waited for; matrix products, arithmetic and copies ran while one was open for 0% of the time, Pallas kernels for 4%

profile of v4, /device:TPU:1, one launch (start us, length us, event | category | flops | bytes accessed | tf_op | source)
XLA Modules:
  0.0 162.0 jit_solution(14213522734532043723)
XLA Ops:
  1.8 5.7 %collective-permute-start = (bf16[4,64,256]{2,1,0:T(8,128)(2,1)S(1)}, bf16[4,64,256]{2,1,0:T(8,128)(2,1)S(1)}, u32[]{:S(2)}, u32[]{:S(2)}) collective-permute-start(bf16[4,64,256]{2,1,0:T(8,128)(2,1)S(1)} %get-tuple-element.69.right), channel_id=1, source_target_pairs={{0,2},{2,4},{4,6},{6,8},{8,10},{10,12},{12,14},{14,16},{16,18},{18... | collective-permute-start | bytes 393224 | tf_op jit(solution)/shard_map/ppermute | solution.py:408
  9.6 5.2 %collective-permute-done.1.after = bf16[4,64,256]{2,1,0:T(8,128)(2,1)S(1)} collective-permute-done((bf16[4,64,256]{2,1,0:T(8,128)(2,1)S(1)}, bf16[4,64,256]{2,1,0:T(8,128)(2,1)S(1)}, u32[]{:S(2)}, u32[]{:S(2)}) %collective-permute-start.1) | collective-permute-done | bytes 131104 | tf_op jit(solution)/shard_map/ppermute | solution.py:409
  14.9 3.1 %collective-permute-start.2 = (bf16[2,64,1024]{2,1,0:T(8,128)(2,1)S(1)}, bf16[2,64,1024]{2,1,0:T(8,128)(2,1)S(1)}, u32[]{:S(2)}, u32[]{:S(2)}) collective-permute-start(bf16[2,64,1024]{2,1,0:T(8,128)(2,1)S(1)} %get-tuple-element.71), channel_id=1, source_target_pairs={{0,32},{32,64},{64,96},{96,128},{128,160},{160,192},{192,224},{1,3... | collective-permute-start | bytes 786440 | tf_op jit(solution)/shard_map/ppermute | solution.py:413
  21.3 3.8 %collective-permute-done.3.below = bf16[2,64,1024]{2,1,0:T(8,128)(2,1)S(1)} collective-permute-done((bf16[2,64,1024]{2,1,0:T(8,128)(2,1)S(1)}, bf16[2,64,1024]{2,1,0:T(8,128)(2,1)S(1)}, u32[]{:S(2)}, u32[]{:S(2)}) %collective-permute-start.3) | collective-permute-done | bytes 262176 | tf_op jit(solution)/shard_map/ppermute | solution.py:414
  26.7 4.2 %collective-permute-start.4 = (bf16[4,32,256]{2,1,0:T(8,128)(2,1)S(1)}, bf16[4,32,256]{2,1,0:T(8,128)(2,1)S(1)}, u32[]{:S(2)}, u32[]{:S(2)}) collective-permute-start(bf16[4,32,256]{2,1,0:T(8,128)(2,1)S(1)} %get-tuple-element.77.right), channel_id=1, source_target_pairs={{0,2},{2,4},{4,6},{6,8},{8,10},{10,12},{12,14},{14,16},{16,18},{18... | collective-permute-start | bytes 196616 | tf_op jit(solution)/shard_map/ppermute | solution.py:408
  32.3 5.2 %collective-permute-done.5.after = bf16[4,32,256]{2,1,0:T(8,128)(2,1)S(1)} collective-permute-done((bf16[4,32,256]{2,1,0:T(8,128)(2,1)S(1)}, bf16[4,32,256]{2,1,0:T(8,128)(2,1)S(1)}, u32[]{:S(2)}, u32[]{:S(2)}) %collective-permute-start.5) | collective-permute-done | bytes 65568 | tf_op jit(solution)/shard_map/ppermute | solution.py:409
  37.5 3.1 %collective-permute-start.6 = (bf16[2,32,1024]{2,1,0:T(8,128)(2,1)S(1)}, bf16[2,32,1024]{2,1,0:T(8,128)(2,1)S(1)}, u32[]{:S(2)}, u32[]{:S(2)}) collective-permute-start(bf16[2,32,1024]{2,1,0:T(8,128)(2,1)S(1)} %get-tuple-element.79), channel_id=1, source_target_pairs={{0,32},{32,64},{64,96},{96,128},{128,160},{160,192},{192,224},{1,3... | collective-permute-start | bytes 393224 | tf_op jit(solution)/shard_map/ppermute | solution.py:413
  42.5 4.1 %collective-permute-done.7.below = bf16[2,32,1024]{2,1,0:T(8,128)(2,1)S(1)} collective-permute-done((bf16[2,32,1024]{2,1,0:T(8,128)(2,1)S(1)}, bf16[2,32,1024]{2,1,0:T(8,128)(2,1)S(1)}, u32[]{:S(2)}, u32[]{:S(2)}) %collective-permute-start.7) | collective-permute-done | bytes 131104 | tf_op jit(solution)/shard_map/ppermute | solution.py:414
  46.6 1.8 %layers_2_3.1 = (bf16[8,32,1024]{2,1,0:T(8,128)(2,1)S(1)}, bf16[8,16,1024]{2,1,0:T(8,128)(2,1)S(1)}, bf16[4,16,512]{2,1,0:T(8,128)(2,1)S(1)}, f32[8,16,768]{2,1,...) custom-call(bf16[4,32,256]{2,1,0:T(8,128)(2,1)S(1)} %collective-perm, ...), custom_call_target="tpu_custom_call" | custom-call | flops 1000000 | bytes 3882496 | tf_op jit(solution)/shard_map/layers_2_3/pallas_call | solution.py:31
  48.4 4.5 %collective-permute-start.8 = (bf16[4,32,256]{2,1,0:T(8,128)(2,1)S(1)}, bf16[4,32,256]{2,1,0:T(8,128)(2,1)S(1)}, u32[]{:S(2)}, u32[]{:S(2)}) collective-permute-start(bf16[4,32,256]{2,1,0:T(8,128)(2,1)S(1)} %get-tuple-element.91.right), channel_id=1, source_target_pairs={{0,2},{2,4},{4,6},{6,8},{8,10},{10,12},{12,14},{14,16},{16,18},{18... | collective-permute-start | bytes 196616 | tf_op jit(solution)/shard_map/ppermute | solution.py:408
  54.3 5.2 %collective-permute-done.9.after = bf16[4,32,256]{2,1,0:T(8,128)(2,1)S(1)} collective-permute-done((bf16[4,32,256]{2,1,0:T(8,128)(2,1)S(1)}, bf16[4,32,256]{2,1,0:T(8,128)(2,1)S(1)}, u32[]{:S(2)}, u32[]{:S(2)}) %collective-permute-start.9) | collective-permute-done | bytes 65568 | tf_op jit(solution)/shard_map/ppermute | solution.py:409
  59.5 4.1 %collective-permute-start.10 = (bf16[2,32,1024]{2,1,0:T(8,128)(2,1)S(1)}, bf16[2,32,1024]{2,1,0:T(8,128)(2,1)S(1)}, u32[]{:S(2)}, u32[]{:S(2)}) collective-permute-start(bf16[2,32,1024]{2,1,0:T(8,128)(2,1)S(1)} %get-tuple-element.93), channel_id=1, source_target_pairs={{0,32},{32,64},{64,96},{96,128},{128,160},{160,192},{192,224},{1,3... | collective-permute-start | bytes 393224 | tf_op jit(solution)/shard_map/ppermute | solution.py:413
  65.5 3.8 %collective-permute-done.11.below = bf16[2,32,1024]{2,1,0:T(8,128)(2,1)S(1)} collective-permute-done((bf16[2,32,1024]{2,1,0:T(8,128)(2,1)S(1)}, bf16[2,32,1024]{2,1,0:T(8,128)(2,1)S(1)}, u32[]{:S(2)}, u32[]{:S(2)}) %collective-permute-start.11) | collective-permute-done | bytes 131104 | tf_op jit(solution)/shard_map/ppermute | solution.py:414
  70.3 5.7 %collective-permute-start.12 = (bf16[4,48,256]{2,1,0:T(8,128)(2,1)S(1)}, bf16[4,48,256]{2,1,0:T(8,128)(2,1)S(1)}, u32[]{:S(2)}, u32[]{:S(2)}) collective-permute-start(bf16[4,48,256]{2,1,0:T(8,128)(2,1)S(1)} %get-tuple-element.99.right), channel_id=1, source_target_pairs={{0,2},{2,4},{4,6},{6,8},{8,10},{10,12},{12,14},{14,16},{16,18},{18... | collective-permute-start | bytes 294920 | tf_op jit(solution)/shard_map/ppermute | solution.py:408
  77.7 5.2 %collective-permute-done.13.after = bf16[4,48,256]{2,1,0:T(8,128)(2,1)S(1)} collective-permute-done((bf16[4,48,256]{2,1,0:T(8,128)(2,1)S(1)}, bf16[4,48,256]{2,1,0:T(8,128)(2,1)S(1)}, u32[]{:S(2)}, u32[]{:S(2)}) %collective-permute-start.13) | collective-permute-done | bytes 98336 | tf_op jit(solution)/shard_map/ppermute | solution.py:409
  83.0 3.7 %collective-permute-start.14 = (bf16[2,48,1024]{2,1,0:T(8,128)(2,1)S(1)}, bf16[2,48,1024]{2,1,0:T(8,128)(2,1)S(1)}, u32[]{:S(2)}, u32[]{:S(2)}) collective-permute-start(bf16[2,48,1024]{2,1,0:T(8,128)(2,1)S(1)} %get-tuple-element.101), channel_id=1, source_target_pairs={{0,32},{32,64},{64,96},{96,128},{128,160},{160,192},{192,224},{1,3... | collective-permute-start | bytes 589832 | tf_op jit(solution)/shard_map/ppermute | solution.py:413
  89.2 2.1 %kernel_gradients_2_1.1 = (f32[432,128]{1,0:T(8,128)S(1)}, f32[432,128]{1,0:T(8,128)S(1)}, f32[32,128]{1,0:T(8,128)S(1)}, f32[8,16,768]{2,1,0:T(8,128)S(1)}, f32[4,64,512]{2,1,0:T(8,128)S(1)}) custom-call(bf16[8,64,1024]{2,1,0:T(8,128)(2,1)S(1)} %get-tuple-element.76.frame, bf16[8,32,1024]{2,1,0:T(8,128)(2,1)S(1)} %get-tuple-element.84.hidden_01, ...), custom_call_target="tpu_custom_call" | custom-call | flops 200000000 | bytes 5339648 | tf_op jit(solution)/shard_map/kernel_gradients_2_1/pallas_call | solution.py:31
  91.2 2.1 %collective-permute-done.15.below = bf16[2,48,1024]{2,1,0:T(8,128)(2,1)S(1)} collective-permute-done((bf16[2,48,1024]{2,1,0:T(8,128)(2,1)S(1)}, bf16[2,48,1024]{2,1,0:T(8,128)(2,1)S(1)}, u32[]{:S(2)}, u32[]{:S(2)}) %collective-permute-start.15) | collective-permute-done | bytes 196640 | tf_op jit(solution)/shard_map/ppermute | solution.py:414
  93.4 2.0 %gradient_0.1 = (bf16[8,48,1024]{2,1,0:T(8,128)(2,1)S(1)}, bf16[8,48,1024]{2,1,0:T(8,128)(2,1)S(1)}, bf16[8,48,1024]{2,1,0:T(8,128)(2,1)S(1)}, f32[1024,128]{1,0:T(8,128)S(1)}, bf16[1024,128]{1,0:T(8,128)(2,1)S(1)}) custom-call(bf16[4,48,256]{2,1,0:T(8,128)(2,1)S(1)} %collective-permute-done.12.before, bf16[4,48,256]{2,1,0:T(8,128)(2,1)S(1)} %get-tuple-element.100.left, ...), custom_call_target="tpu_custom_call" | custom-call | flops 1000000 | bytes 7197184 | tf_op jit(solution)/shard_map/gradient_0/pallas_call | solution.py:31
  95.3 11.6 %collective-permute-start.16 = (bf16[1024,128]{1,0:T(8,128)(2,1)S(1)}, bf16[1024,128]{1,0:T(8,128)(2,1)S(1)}, u32[]{:S(2)}, u32[]{:S(2)}) collective-permute-start(bf16[1024,128]{1,0:T(8,128)(2,1)S(1)} %get-tuple-element.121), channel_id=1, source_target_pairs={{0,1},{1,0},{2,3},{3,2},{4,5},{5,4},{6,7},{7,6},{8,9},{9,8},{10,11... | collective-permute-start | bytes 786440 | tf_op jit(solution)/shard_map/ppermute | solution.py:500
  108.1 27.2 %all_to_all.10 = bf16[128,8,128]{2,1,0:T(8,128)(2,1)S(1)} all-to-all(bf16[128,8,128]{2,1,0:T(8,128)(2,1)S(1)} %bitcast.38), channel_id=1, replica_groups=mesh['gx'=8,'row'=16,'rep'=2] {'gx','row'}, dimensions={0} | all-to-all | bytes 524288 | tf_op jit(solution)/shard_map/all_to_all | solution.py:501
  135.5 20.1 %all_to_all.11 = bf16[128,8,128]{2,1,0:T(8,128)(2,1)S(1)} all-to-all(bf16[128,8,128]{2,1,0:T(8,128)(2,1)S(1)} %bitcast.37), channel_id=1, replica_groups=mesh['gx'=8,'row'=16,'rep'=2] {'gx','row'}, dimensions={0} | all-to-all | bytes 524288 | tf_op jit(solution)/shard_map/all_to_all | solution.py:503
  155.6 3.5 %collective-permute-start.17 = (bf16[1024,128]{1,0:T(8,128)(2,1)S(1)}, bf16[1024,128]{1,0:T(8,128)(2,1)S(1)}, u32[]{:S(2)}, u32[]{:S(2)}) collective-permute-start(bf16[1024,128]{1,0:T(8,128)(2,1)S(1)} %bitcast.34), channel_id=1, source_target_pairs={{0,1},{1,0},{2,3},{3,2},{4,5},{5,4},{6,7},{7,6},{8,9},{9,8},{10,11... | collective-permute-start | bytes 786440 | tf_op jit(solution)/shard_map/ppermute | solution.py:505
  159.0 2.0 %input_gradient.1 = f32[1024,128]{1,0:T(8,128)} custom-call(bf16[8,48,1024]{2,1,0:T(8,128)(2,1)S(1)} %get-tuple-element.115.spread_2, bf16[8,48,1024]{2,1,0:T(8,128)(2,1)S(1)} %get-tuple-element.116.spread_1, bf16[8,48,1024]{2,1,0:T(8,128)(2,1)S(1)} %get-tuple-element.117.spread_0, bf16[3,64,144]{2,1,0:T(8,128)(2,1)S(1)} %get-tuple-element.118.t0, ...), custom_call_target="tpu_custom_call" | custom-call | flops 300000000 | bytes 3615232 | tf_op jit(solution)/shard_map/input_gradient/pallas_call | solution.py:31
  (48 shorter events, 22.0 us)
Async XLA Ops:
  1.6 17.8 %copy-start.4 = (bf16[16,27,96]{2,0,1:T(8,128)(2,1)S(1)}, bf16[16,27,96]{2,0,1:T(8,128)(2,1)}, u32[]{:S(2)}) copy-start(bf16[16,27,96]{2,0,1:T(8,128)(2,1)} %param.13) | copy-start | bytes 248836
  1.6 17.8 %copy-start.5 = (bf16[16,27,112]{2,0,1:T(8,128)(2,1)S(1)}, bf16[16,27,112]{2,0,1:T(8,128)(2,1)}, u32[]{:S(2)}) copy-start(bf16[16,27,112]{2,0,1:T(8,128)(2,1)} %param.14) | copy-start | bytes 290308
  1.8 7.8 %collective-permute-start = (bf16[4,64,256]{2,1,0:T(8,128)(2,1)S(1)}, bf16[4,64,256]{2,1,0:T(8,128)(2,1)S(1)}, u32[]{:S(2)}, u32[]{:S(2)}) collective-permute-start(bf16[4,64,256]{2,1,0:T(8,128)(2,1)S(1)} %get-tuple-element.69.right), channel_id=1, source_target_pairs={{0,2},{2,4},{4,6},{6,8},{8,10},{10,12},{12,14},{14,16},{16,18},{18... | collective-permute-start | bytes 393224 | tf_op jit(solution)/shard_map/ppermute | solution.py:408
  7.4 11.9 %copy-start = (bf16[1,64,4,4,128]{4,3,2,1,0:T(4,128)(2,1)S(1)}, bf16[1,64,4,4,128]{4,3,2,1,0:T(4,128)(2,1)}, u32[]{:S(2)}) copy-start(bf16[1,64,4,4,128]{4,3,2,1,0:T(4,128)(2,1)} %param.10) | copy-start | bytes 786436
  7.5 11.9 %copy-start.2 = (bf16[16,27,64]{2,0,1:T(8,128)(2,1)S(1)}, bf16[16,27,64]{2,0,1:T(8,128)(2,1)}, u32[]{:S(2)}) copy-start(bf16[16,27,64]{2,0,1:T(8,128)(2,1)} %param.11) | copy-start | bytes 165892
  7.5 11.9 %copy-start.3 = (bf16[16,27,80]{2,0,1:T(8,128)(2,1)S(1)}, bf16[16,27,80]{2,0,1:T(8,128)(2,1)}, u32[]{:S(2)}) copy-start(bf16[16,27,80]{2,0,1:T(8,128)(2,1)} %param.12) | copy-start | bytes 207364
  7.5 7.3 %collective-permute-start.1 = (bf16[4,64,256]{2,1,0:T(8,128)(2,1)S(1)}, bf16[4,64,256]{2,1,0:T(8,128)(2,1)S(1)}, u32[]{:S(2)}, u32[]{:S(2)}) collective-permute-start(bf16[4,64,256]{2,1,0:T(8,128)(2,1)S(1)} %get-tuple-element.70.left), channel_id=1, source_target_pairs={{2,0},{4,2},{6,4},{8,6},{10,8},{12,10},{14,12},{16,14},{18,16},{20... | collective-permute-start | bytes 393224 | tf_op jit(solution)/shard_map/ppermute | solution.py:409
  14.8 4.6 %copy-start.6 = (bf16[64,128]{1,0:T(8,128)(2,1)S(1)}, bf16[64,128]{1,0:T(8,128)(2,1)}, u32[]{:S(2)}) copy-start(bf16[64,128]{1,0:T(8,128)(2,1)} %merge.5) | copy-start | bytes 49156
  14.9 6.4 %collective-permute-start.2 = (bf16[2,64,1024]{2,1,0:T(8,128)(2,1)S(1)}, bf16[2,64,1024]{2,1,0:T(8,128)(2,1)S(1)}, u32[]{:S(2)}, u32[]{:S(2)}) collective-permute-start(bf16[2,64,1024]{2,1,0:T(8,128)(2,1)S(1)} %get-tuple-element.71), channel_id=1, source_target_pairs={{0,32},{32,64},{64,96},{96,128},{128,160},{160,192},{192,224},{1,3... | collective-permute-start | bytes 786440 | tf_op jit(solution)/shard_map/ppermute | solution.py:413
  18.0 7.1 %collective-permute-start.3 = (bf16[2,64,1024]{2,1,0:T(8,128)(2,1)S(1)}, bf16[2,64,1024]{2,1,0:T(8,128)(2,1)S(1)}, u32[]{:S(2)}, u32[]{:S(2)}) collective-permute-start(bf16[2,64,1024]{2,1,0:T(8,128)(2,1)S(1)} %get-tuple-element.72), channel_id=1, source_target_pairs={{32,0},{64,32},{96,64},{128,96},{160,128},{192,160},{224,192},{33,... | collective-permute-start | bytes 786440 | tf_op jit(solution)/shard_map/ppermute | solution.py:414
  26.7 5.5 %collective-permute-start.4 = (bf16[4,32,256]{2,1,0:T(8,128)(2,1)S(1)}, bf16[4,32,256]{2,1,0:T(8,128)(2,1)S(1)}, u32[]{:S(2)}, u32[]{:S(2)}) collective-permute-start(bf16[4,32,256]{2,1,0:T(8,128)(2,1)S(1)} %get-tuple-element.77.right), channel_id=1, source_target_pairs={{0,2},{2,4},{4,6},{6,8},{8,10},{10,12},{12,14},{14,16},{16,18},{18... | collective-permute-start | bytes 196616 | tf_op jit(solution)/shard_map/ppermute | solution.py:408
  31.0 6.5 %collective-permute-start.5 = (bf16[4,32,256]{2,1,0:T(8,128)(2,1)S(1)}, bf16[4,32,256]{2,1,0:T(8,128)(2,1)S(1)}, u32[]{:S(2)}, u32[]{:S(2)}) collective-permute-start(bf16[4,32,256]{2,1,0:T(8,128)(2,1)S(1)} %get-tuple-element.78.left), channel_id=1, source_target_pairs={{2,0},{4,2},{6,4},{8,6},{10,8},{12,10},{14,12},{16,14},{18,16},{20... | collective-permute-start | bytes 196616 | tf_op jit(solution)/shard_map/ppermute | solution.py:409
  37.5 5.0 %collective-permute-start.6 = (bf16[2,32,1024]{2,1,0:T(8,128)(2,1)S(1)}, bf16[2,32,1024]{2,1,0:T(8,128)(2,1)S(1)}, u32[]{:S(2)}, u32[]{:S(2)}) collective-permute-start(bf16[2,32,1024]{2,1,0:T(8,128)(2,1)S(1)} %get-tuple-element.79), channel_id=1, source_target_pairs={{0,32},{32,64},{64,96},{96,128},{128,160},{160,192},{192,224},{1,3... | collective-permute-start | bytes 393224 | tf_op jit(solution)/shard_map/ppermute | solution.py:413
  40.6 6.0 %collective-permute-start.7 = (bf16[2,32,1024]{2,1,0:T(8,128)(2,1)S(1)}, bf16[2,32,1024]{2,1,0:T(8,128)(2,1)S(1)}, u32[]{:S(2)}, u32[]{:S(2)}) collective-permute-start(bf16[2,32,1024]{2,1,0:T(8,128)(2,1)S(1)} %get-tuple-element.80), channel_id=1, source_target_pairs={{32,0},{64,32},{96,64},{128,96},{160,128},{192,160},{224,192},{33,... | collective-permute-start | bytes 393224 | tf_op jit(solution)/shard_map/ppermute | solution.py:414
  48.4 5.8 %collective-permute-start.8 = (bf16[4,32,256]{2,1,0:T(8,128)(2,1)S(1)}, bf16[4,32,256]{2,1,0:T(8,128)(2,1)S(1)}, u32[]{:S(2)}, u32[]{:S(2)}) collective-permute-start(bf16[4,32,256]{2,1,0:T(8,128)(2,1)S(1)} %get-tuple-element.91.right), channel_id=1, source_target_pairs={{0,2},{2,4},{4,6},{6,8},{8,10},{10,12},{12,14},{14,16},{16,18},{18... | collective-permute-start | bytes 196616 | tf_op jit(solution)/shard_map/ppermute | solution.py:408
  53.0 6.5 %collective-permute-start.9 = (bf16[4,32,256]{2,1,0:T(8,128)(2,1)S(1)}, bf16[4,32,256]{2,1,0:T(8,128)(2,1)S(1)}, u32[]{:S(2)}, u32[]{:S(2)}) collective-permute-start(bf16[4,32,256]{2,1,0:T(8,128)(2,1)S(1)} %get-tuple-element.92.left), channel_id=1, source_target_pairs={{2,0},{4,2},{6,4},{8,6},{10,8},{12,10},{14,12},{16,14},{18,16},{20... | collective-permute-start | bytes 196616 | tf_op jit(solution)/shard_map/ppermute | solution.py:409
  59.5 6.0 %collective-permute-start.10 = (bf16[2,32,1024]{2,1,0:T(8,128)(2,1)S(1)}, bf16[2,32,1024]{2,1,0:T(8,128)(2,1)S(1)}, u32[]{:S(2)}, u32[]{:S(2)}) collective-permute-start(bf16[2,32,1024]{2,1,0:T(8,128)(2,1)S(1)} %get-tuple-element.93), channel_id=1, source_target_pairs={{0,32},{32,64},{64,96},{96,128},{128,160},{160,192},{192,224},{1,3... | collective-permute-start | bytes 393224 | tf_op jit(solution)/shard_map/ppermute | solution.py:413
  63.5 5.8 %collective-permute-start.11 = (bf16[2,32,1024]{2,1,0:T(8,128)(2,1)S(1)}, bf16[2,32,1024]{2,1,0:T(8,128)(2,1)S(1)}, u32[]{:S(2)}, u32[]{:S(2)}) collective-permute-start(bf16[2,32,1024]{2,1,0:T(8,128)(2,1)S(1)} %get-tuple-element.94), channel_id=1, source_target_pairs={{32,0},{64,32},{96,64},{128,96},{160,128},{192,160},{224,192},{33,... | collective-permute-start | bytes 393224 | tf_op jit(solution)/shard_map/ppermute | solution.py:414
  70.3 7.4 %collective-permute-start.12 = (bf16[4,48,256]{2,1,0:T(8,128)(2,1)S(1)}, bf16[4,48,256]{2,1,0:T(8,128)(2,1)S(1)}, u32[]{:S(2)}, u32[]{:S(2)}) collective-permute-start(bf16[4,48,256]{2,1,0:T(8,128)(2,1)S(1)} %get-tuple-element.99.right), channel_id=1, source_target_pairs={{0,2},{2,4},{4,6},{6,8},{8,10},{10,12},{12,14},{14,16},{16,18},{18... | collective-permute-start | bytes 294920 | tf_op jit(solution)/shard_map/ppermute | solution.py:408
  76.0 6.9 %collective-permute-start.13 = (bf16[4,48,256]{2,1,0:T(8,128)(2,1)S(1)}, bf16[4,48,256]{2,1,0:T(8,128)(2,1)S(1)}, u32[]{:S(2)}, u32[]{:S(2)}) collective-permute-start(bf16[4,48,256]{2,1,0:T(8,128)(2,1)S(1)} %get-tuple-element.100.left), channel_id=1, source_target_pairs={{2,0},{4,2},{6,4},{8,6},{10,8},{12,10},{14,12},{16,14},{18,16},{20... | collective-permute-start | bytes 294920 | tf_op jit(solution)/shard_map/ppermute | solution.py:409
  83.0 8.3 %collective-permute-start.14 = (bf16[2,48,1024]{2,1,0:T(8,128)(2,1)S(1)}, bf16[2,48,1024]{2,1,0:T(8,128)(2,1)S(1)}, u32[]{:S(2)}, u32[]{:S(2)}) collective-permute-start(bf16[2,48,1024]{2,1,0:T(8,128)(2,1)S(1)} %get-tuple-element.101), channel_id=1, source_target_pairs={{0,32},{32,64},{64,96},{96,128},{128,160},{160,192},{192,224},{1,3... | collective-permute-start | bytes 589832 | tf_op jit(solution)/shard_map/ppermute | solution.py:413
  86.7 6.7 %collective-permute-start.15 = (bf16[2,48,1024]{2,1,0:T(8,128)(2,1)S(1)}, bf16[2,48,1024]{2,1,0:T(8,128)(2,1)S(1)}, u32[]{:S(2)}, u32[]{:S(2)}) collective-permute-start(bf16[2,48,1024]{2,1,0:T(8,128)(2,1)S(1)} %get-tuple-element.102), channel_id=1, source_target_pairs={{32,0},{64,32},{96,64},{128,96},{160,128},{192,160},{224,192},{33,... | collective-permute-start | bytes 589832 | tf_op jit(solution)/shard_map/ppermute | solution.py:414
  95.3 12.7 %collective-permute-start.16 = (bf16[1024,128]{1,0:T(8,128)(2,1)S(1)}, bf16[1024,128]{1,0:T(8,128)(2,1)S(1)}, u32[]{:S(2)}, u32[]{:S(2)}) collective-permute-start(bf16[1024,128]{1,0:T(8,128)(2,1)S(1)} %get-tuple-element.121), channel_id=1, source_target_pairs={{0,1},{1,0},{2,3},{3,2},{4,5},{5,4},{6,7},{7,6},{8,9},{9,8},{10,11... | collective-permute-start | bytes 786440 | tf_op jit(solution)/shard_map/ppermute | solution.py:500
  155.6 5.4 %collective-permute-start.17 = (bf16[1024,128]{1,0:T(8,128)(2,1)S(1)}, bf16[1024,128]{1,0:T(8,128)(2,1)S(1)}, u32[]{:S(2)}, u32[]{:S(2)}) collective-permute-start(bf16[1024,128]{1,0:T(8,128)(2,1)S(1)} %bitcast.34), channel_id=1, source_target_pairs={{0,1},{1,0},{2,3},{3,2},{4,5},{5,4},{6,7},{7,6},{8,9},{9,8},{10,11... | collective-permute-start | bytes 786440 | tf_op jit(solution)/shard_map/ppermute | solution.py:505
  (3 other events, 2.3 us)

commit v5 on v4

--- a/solution.py
+++ b/solution.py
@@ -58,10 +58,10 @@
     return jnp.concatenate([from_right(v, not_last), v, from_left(v, not_first)], axis=0).astype(BF16)
 
 
-def inside(i):
-    x = lax.axis_index("gx") * B + i - H
-    block = lax.broadcasted_iota(jnp.int32, (1, (B + 2) * Z), 1) // Z
-    y = lax.axis_index("row") * B + block + 1 - H
+def inside(x, y, blocks):
+    x = lax.axis_index("gx") * B + x
+    block = lax.broadcasted_iota(jnp.int32, (1, blocks * Z), 1) // Z
+    y = lax.axis_index("row") * B + block + y
     in_x = (x >= 0) & (x < lax.axis_size("gx") * B)
     in_y = (y >= 0) & (y < lax.axis_size("row") * B)
     return jnp.where(in_y, 1.0, 0.0) * jnp.where(in_x, 1.0, 0.0)
@@ -77,7 +77,7 @@
 def conv_row(kernel_ref, sources, i, lanes):
     n = lanes.stop - lanes.start
     cut = slice(lanes.start - Z, lanes.stop + Z)
-    rhs = jnp.concatenate([s[i + a - 1, :, cut] for a in range(3) for s in sources], axis=0)
+    rhs = jnp.concatenate([s(i + a - 1, cut) for a in range(3) for s in sources], axis=0)
     got = jnp.dot(kernel_ref[...], rhs, preferred_element_type=F32)
     acc = got[:48, :n] + got[48:96, Z : Z + n] + got[96:, 2 * Z :]
     not_first, not_last = lane_moves(16, n)
@@ -157,11 +157,16 @@
     return wide_sum([rows[16:32] for rows in own])
 
 
-def pack_kernel(x_ref, left, right, wide):
+def pack_kernel(x_ref, out_ref, wide):
     wide[...] = x_ref[...].astype(F32)
     for i in range(B):
         row = [wide[pl.ds(B * i + j, 64, stride=B * B), :].astype(BF16) for j in range(B)]
-        put((left, right), i, slice(0, 64), jnp.concatenate(row, axis=1))
+        out_ref[i] = jnp.concatenate(row, axis=1)
+
+
+def band_kernel(before, own, after, out_ref):
+    for k, ref in enumerate((before, own, after)):
+        out_ref[:, :, k * B * Z : (k + 1) * B * Z] = ref[...]
 
 
 def rows_kernel(before, left, right, after, top, bottom):
@@ -197,38 +202,37 @@
         carried[i] = back[64:]
 
 
-def first_kernel(
-    before, left, right, after, above, below, k0, k1, bias,
-    frame, hidden_0, slope_0, slope_1, send_left, send_right,
+def forward_kernel(
+    above, band, below, k0, k1, k2, k3, bias, carried,
+    frame, hidden_01, hidden_2, hidden_3, slope_0, slope_1, slope_2, own_3, send_left, send_right,
+    wide_0, wide_1, wide_2,
 ):
-    assemble((before, left, right, after, above, below), frame)
-
-    for i in range(H - 1, H + B + 1):
-        pre = conv_row(k0, [frame], i, RING) + bias[0:16, 0:1]
-        value, slope = activate(pre)
-        slope_0[i] = slope
-        hidden_0[i, :, RING] = (value * inside(i)).astype(BF16)
-    for i in range(B):
-        pre = conv_row(k1, [frame, hidden_0], H + i, MID) + bias[16:32, 0:1]
-        value, slope = activate(pre)
-        slope_1[i] = slope
-        put((send_left, send_right), i, slice(0, 16), hidden_0[H + i, :, MID])
-        put((send_left, send_right), i, slice(16, 32), value.astype(BF16))
-
-
-def second_kernel(
-    before, left, right, after, above, below, frame, k2, k3, bias, carried,
-    hidden_01, hidden_2, hidden_3, slope_2, own_3, send_left, send_right,
-):
-    assemble((before, left, right, after, above, below), hidden_01)
-
-    for i in range(H - 1, H + B + 1):
-        pre = conv_row(k2, [frame, hidden_01], i, RING) + bias[32:48, 0:1]
-        value, slope = activate(pre)
-        slope_2[i] = slope
-        hidden_2[i, :, RING] = (value * inside(i)).astype(BF16)
-    for i in range(B):
-        pre = conv_row(k3, [frame, hidden_01, hidden_2], H + i, MID) + bias[48:64, 0:1]
+    bands = (above, band, below)
+    near = slice((B - H) * Z, (2 * B + H) * Z)
+    sources = [lambda i, cut: bands[i // B][i % B, :, cut]]
+    for i in range(N):
+        frame[i] = sources[0](i + B - H, near)
+    slopes = (slope_0, slope_1, slope_2)
+    for k, (kernel_ref, wide) in enumerate(((k0, wide_0), (k1, wide_1), (k2, wide_2))):
+        reach = 3 - k
+        lanes = slice((B - reach) * Z, (2 * B + reach) * Z)
+        for i in range(B - reach, 2 * B + reach):
+            pre = conv_row(kernel_ref, sources, i, lanes) + bias[16 * k : 16 * (k + 1), 0:1]
+            value, slope = activate(pre)
+            value = value * inside(i - B, -reach, B + 2 * reach)
+            wide[i, :, lanes] = value.astype(BF16)
+            if k == 1 and B <= i < 2 * B:
+                slope_1[i - B] = slope[:, reach * Z : (reach + B) * Z]
+            if k != 1 and B - 1 <= i < 2 * B + 1:
+                slopes[k][i - B + H] = slope[:, (reach - 1) * Z : (reach + B + 1) * Z]
+        sources.append(lambda i, cut, wide=wide: wide[i, :, cut])
+    for i in range(N):
+        hidden_01[i, 0:16] = wide_0[i + B - H, :, near]
+        hidden_01[i, 16:32] = wide_1[i + B - H, :, near]
+        if 0 < i < N - 1:
+            hidden_2[i, :, RING] = wide_2[i + B - H, :, slice((B - 1) * Z, (2 * B + 1) * Z)]
+    for i in range(B):
+        pre = conv_row(k3, sources, B + i, slice(B * Z, 2 * B * Z)) + bias[48:64, 0:1]
         value, slope = activate(pre)
         hidden_3[i] = value.astype(BF16)
         grad = (carried[i, 48:64] * slope).astype(BF16)
@@ -276,7 +280,7 @@
 
     for i in range(H - 1, H + B + 1):
         got = held[i, :, RING] + back_row(t3, slice(96, 112), spread_3, i, RING)
-        grad = (got * slope_2[i] * inside(i)).astype(BF16)
+        grad = (got * slope_2[i] * inside(i - H, 1 - H, B + 2)).astype(BF16)
         spread_2[i, :, RING] = spread(grad.astype(F32))
     for i in range(B):
         got = (
@@ -329,7 +333,7 @@
             + back_row(t2, slice(64, 80), spread_2, i, RING)
             + back_row(t1, slice(64, 80), spread_1, i, RING)
         )
-        grad = (got * slope_0[i] * inside(i)).astype(BF16)
+        grad = (got * slope_0[i] * inside(i - H, 1 - H, B + 2)).astype(BF16)
         spread_0[i, :, RING] = spread(grad.astype(F32))
     own = own_cells(spread_0)
     kernel_gradient(sums.at[0:432], own, [frame])
@@ -402,16 +406,16 @@
         bias[k : k + 1] = turned(sums[1856 + 16 * k : 1872 + 16 * k])[:, :16]
 
 
+def neighbours(low, high, axis):
+    up = [(i, i + 1) for i in range(lax.axis_size(axis) - 1)]
+    return lax.ppermute(high, axis, up), lax.ppermute(low, axis, [(j, i) for i, j in up])
+
+
 def exchange(left, right):
-    channels = left.shape[1]
-    up = [(i, i + 1) for i in range(lax.axis_size("row") - 1)]
-    before = lax.ppermute(right, "row", up)
-    after = lax.ppermute(left, "row", [(j, i) for i, j in up])
-    edge = shape((H, channels, N * Z), BF16)
+    before, after = neighbours(left, right, "row")
+    edge = shape((H, left.shape[1], N * Z), BF16)
     top, bottom = call(rows_kernel, [edge, edge], [before, left, right, after], name="rows")
-    up = [(i, i + 1) for i in range(lax.axis_size("gx") - 1)]
-    above = lax.ppermute(bottom, "gx", up)
-    below = lax.ppermute(top, "gx", [(j, i) for i, j in up])
+    above, below = neighbours(top, bottom, "gx")
     return [before, left, right, after, above, below]
 
 
@@ -420,10 +424,15 @@
     cells = B * B * Z * lax.axis_size("gx") * lax.axis_size("row") * lax.axis_size("rep")
     scale = 1.0 / math.sqrt(cells)
     flat = [k.transpose(1, 0, 2).reshape(432, k.shape[2]) for k in kernels]
-    half = shape((B, 64, H * Z), BF16)
     columns = shape((64, Z), F32)
     wide = pltpu.VMEM((1024, Z), F32)
-    left, right = call(pack_kernel, [half, half], [samples.reshape(1024, Z)], [wide], name="pack")
+    (own,) = call(
+        pack_kernel,
+        [shape((B, 64, B * Z), BF16)],
+        [samples.reshape(1024, Z)],
+        [wide],
+        name="pack",
+    )
     base, carried, merge_grad, bias, merge_bias, w0, w1, w2, w3, t0, t1, t2, t3 = call(
         prepare_kernel,
         [shape((B, 64, B * Z), F32)] * 2
@@ -435,29 +444,31 @@
         flops=40_000_000,
         name="prepare",
     )
-    parts = exchange(left, right)
+    before, after = neighbours(own, own, "row")
+    (band,) = call(band_kernel, [shape((B, 64, 3 * B * Z), BF16)], [before, own, after], name="band")
+    above, below = neighbours(band, band, "gx")
     ring = shape((N, 16, (B + 2) * Z), F32)
     send = shape((B, 32, H * Z), BF16)
-    frame, hidden_0, slope_0, slope_1, left, right = call(
-        first_kernel,
-        [shape((N, 64, N * Z), BF16), shape((N, 16, N * Z), BF16), ring, shape((B, 16, B * Z), F32), send, send],
-        parts + [w0, w1, bias],
-        name="layers_0_1",
-    )
-    parts = exchange(left, right)
-    hidden_01, hidden_2, hidden_3, slope_2, own_3, left, right = call(
-        second_kernel,
+    (
+        frame, hidden_01, hidden_2, hidden_3,
+        slope_0, slope_1, slope_2, own_3, left, right,
+    ) = call(
+        forward_kernel,
         [
+            shape((N, 64, N * Z), BF16),
             shape((N, 32, N * Z), BF16),
             shape((N, 16, N * Z), BF16),
             shape((B, 16, B * Z), BF16),
+            ring,
+            shape((B, 16, B * Z), F32),
             ring,
             shape((B, 48, B * Z), BF16),
             send,
             send,
         ],
-        parts + [frame, w2, w3, bias, carried],
-        name="layers_2_3",
+        [above, band, below, w0, w1, w2, w3, bias, carried],
+        [pltpu.VMEM((3 * B, 16, 3 * B * Z), BF16)] * 3,
+        name="forward",
     )
     parts = exchange(left, right)
     grads = shape((432, Z), F32)

time: 163 us -> 160 us (0.982)
  starting transfers between devices: 59.6 us -> 45.6 us
  waiting for transfers between devices: 38.9 us -> 46.9 us
  blocking collectives: 47.3 us -> 50.5 us
    ppermute x16 -> x12, starting transfers between devices: 44.6 us -> 35.2 us  [the longest x6 27.3 us: neighbours(): lax.ppermute(high, axis, up)]
    ppermute x16 -> x12, waiting for transfers between devices: 37.8 us -> 45.7 us  [the longest x6 34.6 us: neighbours(): lax.ppermute(low, axis, [(j, i) for i, j in up])]
    ppermute x1, starting transfers between devices: 11.6 us -> 6.91 us  [body(): lax.ppermute(sent, 'rep', swap)]
    all_to_all x1, blocking collectives: 27.2 us -> 30.4 us  [body(): lax.all_to_all(paired.reshape(GROUP, ROWS, Z), axes, 0, 0, tiled=True)]
    pallas_call x16 -> x14, Pallas kernels: 13.6 us -> 14.1 us  [call(): pl.pallas_call(kernel, out_shape=list(outs), in_specs=[pl.BlockSpec(memor...]
  transfers between devices with their start and end apart: 18 -> 14, of which waited for: 14 -> 11; matrix products, arithmetic and copies ran while one was open for 0% -> 0% of each run, Pallas kernels for 4% -> 4%
where the time goes in v5:
time: 160 us
  blocking collectives  50.5 us (32%)
  waiting for transfers between devices  46.9 us (29%)
  starting transfers between devices  45.6 us (28%)
  Pallas kernels  14.1 us (9%)
    ppermute x6, waiting for transfers between devices, neighbours(): lax.ppermute(low, axis, [(j, i) for i, j in up])  34.6 us
    all_to_all x1, blocking collectives, body(): lax.all_to_all(paired.reshape(GROUP, ROWS, Z), axes, 0, 0, tiled=True)  30.4 us
    ppermute x6, starting transfers between devices, neighbours(): lax.ppermute(high, axis, up)  27.3 us
    all_to_all x1, blocking collectives, body(): lax.all_to_all(added.reshape(GROUP, ROWS, Z), axes, 0, 0, tiled=True)  20.1 us
    pallas_call x14, Pallas kernels, call(): pl.pallas_call(kernel, out_shape=list(outs), in_specs=[pl.BlockSpec(memor...  14.1 us
    ppermute x6, waiting for transfers between devices, neighbours(): lax.ppermute(high, axis, up)  11.1 us
    ppermute x6, starting transfers between devices, neighbours(): lax.ppermute(low, axis, [(j, i) for i, j in up])  7.88 us
    ppermute x1, starting transfers between devices, body(): lax.ppermute(sent, 'rep', swap)  6.91 us
  transfers between devices with their start and end apart: 14, of which 11 were waited for; matrix products, arithmetic and copies ran while one was open for 0% of the time, Pallas kernels for 4%

profile of v5, /device:TPU:1, one launch (start us, length us, event | category | flops | bytes accessed | tf_op | source)
XLA Modules:
  0.0 159.6 jit_solution(11644338667721833223)
XLA Ops:
  1.8 1.4 collective-permute-start.1
  3.3 6.3 %collective-permute-start = (bf16[4,64,512]{2,1,0:T(8,128)(2,1)S(1)}, bf16[4,64,512]{2,1,0:T(8,128)(2,1)S(1)}, u32[]{:S(2)}, u32[]{:S(2)}) collective-permute-start(bf16[4,64,512]{2,1,0:T(8,128)(2,1)S(1)} %pack.1.own), channel_id=1, source_target_pairs={{0,2},{2,4},{4,6},{6,8},{8,10},{10,12},{12,14},{14,16},{16,18},{18... | collective-permute-start | bytes 786440 | tf_op jit(solution)/shard_map/ppermute | solution.py:411
  9.6 1.8 %collective-permute-done.1.after = bf16[4,64,512]{2,1,0:T(8,128)(2,1)S(1)} collective-permute-done((bf16[4,64,512]{2,1,0:T(8,128)(2,1)S(1)}, bf16[4,64,512]{2,1,0:T(8,128)(2,1)S(1)}, u32[]{:S(2)}, u32[]{:S(2)}) %collective-permute-start.1) | collective-permute-done | bytes 262176 | tf_op jit(solution)/shard_map/ppermute | solution.py:411
  11.4 8.8 %collective-permute-done.before = bf16[4,64,512]{2,1,0:T(8,128)(2,1)S(1)} collective-permute-done((bf16[4,64,512]{2,1,0:T(8,128)(2,1)S(1)}, bf16[4,64,512]{2,1,0:T(8,128)(2,1)S(1)}, u32[]{:S(2)}, u32[]{:S(2)}) %collective-permute-start) | collective-permute-done | bytes 262176 | tf_op jit(solution)/shard_map/ppermute | solution.py:411
  20.2 1.3 collective-permute-start.3
  21.5 4.0 %collective-permute-start.2 = (bf16[4,64,1536]{2,1,0:T(8,128)(2,1)S(1)}, bf16[4,64,1536]{2,1,0:T(8,128)(2,1)S(1)}, u32[]{:S(2)}, u32[]{:S(2)}) collective-permute-start(bf16[4,64,1536]{2,1,0:T(8,128)(2,1)S(1)} %band.1), channel_id=1, source_target_pairs={{0,32},{32,64},{64,96},{96,128},{128,160},{160,192},{192,224},{1,3... | collective-permute-start | bytes 2359304 | tf_op jit(solution)/shard_map/ppermute | solution.py:411
  26.8 13.9 %collective-permute-done.3.below = bf16[4,64,1536]{2,1,0:T(8,128)(2,1)S(1)} collective-permute-done((bf16[4,64,1536]{2,1,0:T(8,128)(2,1)S(1)}, bf16[4,64,1536]{2,1,0:T(8,128)(2,1)S(1)}, u32[]{:S(2)}, u32[]{:S(2)}) %collective-permute-start.3) | collective-permute-done | bytes 786464 | tf_op jit(solution)/shard_map/ppermute | solution.py:411
  41.6 3.9 %forward.1 = (bf16[8,64,1024]{2,1,0:T(8,128)(2,1)S(1)}, bf16[8,32,1024]{2,1,0:T(8,128)(2,1)S(1)}, bf16[8,16,1024]{2,1,0:T(8,128)(2,1)S(1)}, bf16[4,16,512]{2,1,0...) custom-call(bf16[4,64,1536]{2,1,0:T(8,128)(2,1)S(1)} %collective-per, ...), custom_call_target="tpu_custom_call" | custom-call | flops 1000000 | bytes 6366208 | tf_op jit(solution)/shard_map/forward/pallas_call | solution.py:31
  45.5 5.6 %collective-permute-start.4 = (bf16[4,32,256]{2,1,0:T(8,128)(2,1)S(1)}, bf16[4,32,256]{2,1,0:T(8,128)(2,1)S(1)}, u32[]{:S(2)}, u32[]{:S(2)}) collective-permute-start(bf16[4,32,256]{2,1,0:T(8,128)(2,1)S(1)} %get-tuple-element.75.right), channel_id=1, source_target_pairs={{0,2},{2,4},{4,6},{6,8},{8,10},{10,12},{12,14},{14,16},{16,18},{18... | collective-permute-start | bytes 196616 | tf_op jit(solution)/shard_map/ppermute | solution.py:411
  52.4 5.2 %collective-permute-done.5.after = bf16[4,32,256]{2,1,0:T(8,128)(2,1)S(1)} collective-permute-done((bf16[4,32,256]{2,1,0:T(8,128)(2,1)S(1)}, bf16[4,32,256]{2,1,0:T(8,128)(2,1)S(1)}, u32[]{:S(2)}, u32[]{:S(2)}) %collective-permute-start.5) | collective-permute-done | bytes 65568 | tf_op jit(solution)/shard_map/ppermute | solution.py:411
  57.7 4.1 %collective-permute-start.6 = (bf16[2,32,1024]{2,1,0:T(8,128)(2,1)S(1)}, bf16[2,32,1024]{2,1,0:T(8,128)(2,1)S(1)}, u32[]{:S(2)}, u32[]{:S(2)}) collective-permute-start(bf16[2,32,1024]{2,1,0:T(8,128)(2,1)S(1)} %get-tuple-element.77), channel_id=1, source_target_pairs={{0,32},{32,64},{64,96},{96,128},{128,160},{160,192},{192,224},{1,3... | collective-permute-start | bytes 393224 | tf_op jit(solution)/shard_map/ppermute | solution.py:411
  61.8 1.3 collective-permute-start.7
  63.7 3.8 %collective-permute-done.7.below = bf16[2,32,1024]{2,1,0:T(8,128)(2,1)S(1)} collective-permute-done((bf16[2,32,1024]{2,1,0:T(8,128)(2,1)S(1)}, bf16[2,32,1024]{2,1,0:T(8,128)(2,1)S(1)}, u32[]{:S(2)}, u32[]{:S(2)}) %collective-permute-start.7) | collective-permute-done | bytes 131104 | tf_op jit(solution)/shard_map/ppermute | solution.py:411
  68.5 3.4 %collective-permute-start.8 = (bf16[4,48,256]{2,1,0:T(8,128)(2,1)S(1)}, bf16[4,48,256]{2,1,0:T(8,128)(2,1)S(1)}, u32[]{:S(2)}, u32[]{:S(2)}) collective-permute-start(bf16[4,48,256]{2,1,0:T(8,128)(2,1)S(1)} %get-tuple-element.83.right), channel_id=1, source_target_pairs={{0,2},{2,4},{4,6},{6,8},{8,10},{10,12},{12,14},{14,16},{16,18},{18... | collective-permute-start | bytes 294920 | tf_op jit(solution)/shard_map/ppermute | solution.py:411
  74.1 4.7 %collective-permute-done.9.after = bf16[4,48,256]{2,1,0:T(8,128)(2,1)S(1)} collective-permute-done((bf16[4,48,256]{2,1,0:T(8,128)(2,1)S(1)}, bf16[4,48,256]{2,1,0:T(8,128)(2,1)S(1)}, u32[]{:S(2)}, u32[]{:S(2)}) %collective-permute-start.9) | collective-permute-done | bytes 98336 | tf_op jit(solution)/shard_map/ppermute | solution.py:411
  78.8 3.9 %collective-permute-start.10 = (bf16[2,48,1024]{2,1,0:T(8,128)(2,1)S(1)}, bf16[2,48,1024]{2,1,0:T(8,128)(2,1)S(1)}, u32[]{:S(2)}, u32[]{:S(2)}) collective-permute-start(bf16[2,48,1024]{2,1,0:T(8,128)(2,1)S(1)} %get-tuple-element.85), channel_id=1, source_target_pairs={{0,32},{32,64},{64,96},{96,128},{128,160},{160,192},{192,224},{1,3... | collective-permute-start | bytes 589832 | tf_op jit(solution)/shard_map/ppermute | solution.py:411
  85.2 2.1 %kernel_gradients_2_1.1 = (f32[432,128]{1,0:T(8,128)S(1)}, f32[432,128]{1,0:T(8,128)S(1)}, f32[32,128]{1,0:T(8,128)S(1)}, f32[8,16,768]{2,1,0:T(8,128)S(1)}, f32[4,64,512]{2,1,0:T(8,128)S(1)}) custom-call(bf16[8,64,1024]{2,1,0:T(8,128)(2,1)S(1)} %get-tuple-element.67.frame, bf16[8,32,1024]{2,1,0:T(8,128)(2,1)S(1)} %get-tuple-element.68.hidden_01, ...), custom_call_target="tpu_custom_call" | custom-call | flops 200000000 | bytes 5339648 | tf_op jit(solution)/shard_map/kernel_gradients_2_1/pallas_call | solution.py:31
  87.3 5.1 %collective-permute-done.11.below = bf16[2,48,1024]{2,1,0:T(8,128)(2,1)S(1)} collective-permute-done((bf16[2,48,1024]{2,1,0:T(8,128)(2,1)S(1)}, bf16[2,48,1024]{2,1,0:T(8,128)(2,1)S(1)}, u32[]{:S(2)}, u32[]{:S(2)}) %collective-permute-start.11) | collective-permute-done | bytes 196640 | tf_op jit(solution)/shard_map/ppermute | solution.py:411
  92.4 2.0 %gradient_0.1 = (bf16[8,48,1024]{2,1,0:T(8,128)(2,1)S(1)}, bf16[8,48,1024]{2,1,0:T(8,128)(2,1)S(1)}, bf16[8,48,1024]{2,1,0:T(8,128)(2,1)S(1)}, f32[1024,128]{1,0:T(8,128)S(1)}, bf16[1024,128]{1,0:T(8,128)(2,1)S(1)}) custom-call(bf16[4,48,256]{2,1,0:T(8,128)(2,1)S(1)} %collective-permute-done.8.before, bf16[4,48,256]{2,1,0:T(8,128)(2,1)S(1)} %get-tuple-element.84.left, ...), custom_call_target="tpu_custom_call" | custom-call | flops 1000000 | bytes 7197184 | tf_op jit(solution)/shard_map/gradient_0/pallas_call | solution.py:31
  94.4 6.9 %collective-permute-start.12 = (bf16[1024,128]{1,0:T(8,128)(2,1)S(1)}, bf16[1024,128]{1,0:T(8,128)(2,1)S(1)}, u32[]{:S(2)}, u32[]{:S(2)}) collective-permute-start(bf16[1024,128]{1,0:T(8,128)(2,1)S(1)} %get-tuple-element.105), channel_id=1, source_target_pairs={{0,1},{1,0},{2,3},{3,2},{4,5},{5,4},{6,7},{7,6},{8,9},{9,8},{10,11... | collective-permute-start | bytes 786440 | tf_op jit(solution)/shard_map/ppermute | solution.py:511
  102.5 30.4 %all_to_all.10 = bf16[128,8,128]{2,1,0:T(8,128)(2,1)S(1)} all-to-all(bf16[128,8,128]{2,1,0:T(8,128)(2,1)S(1)} %bitcast.38), channel_id=1, replica_groups=mesh['gx'=8,'row'=16,'rep'=2] {'gx','row'}, dimensions={0} | all-to-all | bytes 524288 | tf_op jit(solution)/shard_map/all_to_all | solution.py:512
  133.1 20.1 %all_to_all.11 = bf16[128,8,128]{2,1,0:T(8,128)(2,1)S(1)} all-to-all(bf16[128,8,128]{2,1,0:T(8,128)(2,1)S(1)} %bitcast.37), channel_id=1, replica_groups=mesh['gx'=8,'row'=16,'rep'=2] {'gx','row'}, dimensions={0} | all-to-all | bytes 524288 | tf_op jit(solution)/shard_map/all_to_all | solution.py:514
  153.1 3.5 %collective-permute-start.13 = (bf16[1024,128]{1,0:T(8,128)(2,1)S(1)}, bf16[1024,128]{1,0:T(8,128)(2,1)S(1)}, u32[]{:S(2)}, u32[]{:S(2)}) collective-permute-start(bf16[1024,128]{1,0:T(8,128)(2,1)S(1)} %bitcast.34), channel_id=1, source_target_pairs={{0,1},{1,0},{2,3},{3,2},{4,5},{5,4},{6,7},{7,6},{8,9},{9,8},{10,11... | collective-permute-start | bytes 786440 | tf_op jit(solution)/shard_map/ppermute | solution.py:516
  156.6 2.0 %input_gradient.1 = f32[1024,128]{1,0:T(8,128)} custom-call(bf16[8,48,1024]{2,1,0:T(8,128)(2,1)S(1)} %get-tuple-element.99.spread_2, bf16[8,48,1024]{2,1,0:T(8,128)(2,1)S(1)} %get-tuple-element.100.spread_1, bf16[8,48,1024]{2,1,0:T(8,128)(2,1)S(1)} %get-tuple-element.101.spread_0, bf16[3,64,144]{2,1,0:T(8,128)(2,1)S(1)} %get-tuple-element.102.t0, ...), custom_call_target="tpu_custom_call" | custom-call | flops 300000000 | bytes 3615232 | tf_op jit(solution)/shard_map/input_gradient/pallas_call | solution.py:31
  (38 shorter events, 13.2 us)
Async XLA Ops:
  0.6 1.0 copy-start.1
  1.8 23.8 %copy-start = (bf16[1,64,4,4,128]{4,3,2,1,0:T(4,128)(2,1)S(1)}, bf16[1,64,4,4,128]{4,3,2,1,0:T(4,128)(2,1)}, u32[]{:S(2)}) copy-start(bf16[1,64,4,4,128]{4,3,2,1,0:T(4,128)(2,1)} %param.10) | copy-start | bytes 786436
  1.8 23.8 %copy-start.2 = (bf16[16,27,64]{2,0,1:T(8,128)(2,1)S(1)}, bf16[16,27,64]{2,0,1:T(8,128)(2,1)}, u32[]{:S(2)}) copy-start(bf16[16,27,64]{2,0,1:T(8,128)(2,1)} %param.11) | copy-start | bytes 165892
  1.8 23.8 %copy-start.3 = (bf16[16,27,80]{2,0,1:T(8,128)(2,1)S(1)}, bf16[16,27,80]{2,0,1:T(8,128)(2,1)}, u32[]{:S(2)}) copy-start(bf16[16,27,80]{2,0,1:T(8,128)(2,1)} %param.12) | copy-start | bytes 207364
  1.8 23.8 %copy-start.4 = (bf16[16,27,96]{2,0,1:T(8,128)(2,1)S(1)}, bf16[16,27,96]{2,0,1:T(8,128)(2,1)}, u32[]{:S(2)}) copy-start(bf16[16,27,96]{2,0,1:T(8,128)(2,1)} %param.13) | copy-start | bytes 248836
  1.8 23.8 %copy-start.5 = (bf16[16,27,112]{2,0,1:T(8,128)(2,1)S(1)}, bf16[16,27,112]{2,0,1:T(8,128)(2,1)}, u32[]{:S(2)}) copy-start(bf16[16,27,112]{2,0,1:T(8,128)(2,1)} %param.14) | copy-start | bytes 290308
  1.8 9.5 %collective-permute-start.1 = (bf16[4,64,512]{2,1,0:T(8,128)(2,1)S(1)}, bf16[4,64,512]{2,1,0:T(8,128)(2,1)S(1)}, u32[]{:S(2)}, u32[]{:S(2)}) collective-permute-start(bf16[4,64,512]{2,1,0:T(8,128)(2,1)S(1)} %pack.1.own), channel_id=1, source_target_pairs={{2,0},{4,2},{6,4},{8,6},{10,8},{12,10},{14,12},{16,14},{18,16},{20... | collective-permute-start | bytes 786440 | tf_op jit(solution)/shard_map/ppermute | solution.py:411
  3.3 16.9 %collective-permute-start = (bf16[4,64,512]{2,1,0:T(8,128)(2,1)S(1)}, bf16[4,64,512]{2,1,0:T(8,128)(2,1)S(1)}, u32[]{:S(2)}, u32[]{:S(2)}) collective-permute-start(bf16[4,64,512]{2,1,0:T(8,128)(2,1)S(1)} %pack.1.own), channel_id=1, source_target_pairs={{0,2},{2,4},{4,6},{6,8},{8,10},{10,12},{12,14},{14,16},{16,18},{18... | collective-permute-start | bytes 786440 | tf_op jit(solution)/shard_map/ppermute | solution.py:411
  20.2 5.5 %copy-start.6 = (bf16[64,128]{1,0:T(8,128)(2,1)S(1)}, bf16[64,128]{1,0:T(8,128)(2,1)}, u32[]{:S(2)}) copy-start(bf16[64,128]{1,0:T(8,128)(2,1)} %merge.5) | copy-start | bytes 49156
  20.2 20.5 %collective-permute-start.3 = (bf16[4,64,1536]{2,1,0:T(8,128)(2,1)S(1)}, bf16[4,64,1536]{2,1,0:T(8,128)(2,1)S(1)}, u32[]{:S(2)}, u32[]{:S(2)}) collective-permute-start(bf16[4,64,1536]{2,1,0:T(8,128)(2,1)S(1)} %band.1), channel_id=1, source_target_pairs={{32,0},{64,32},{96,64},{128,96},{160,128},{192,160},{224,192},{33,... | collective-permute-start | bytes 2359304 | tf_op jit(solution)/shard_map/ppermute | solution.py:411
  21.5 20.1 %collective-permute-start.2 = (bf16[4,64,1536]{2,1,0:T(8,128)(2,1)S(1)}, bf16[4,64,1536]{2,1,0:T(8,128)(2,1)S(1)}, u32[]{:S(2)}, u32[]{:S(2)}) collective-permute-start(bf16[4,64,1536]{2,1,0:T(8,128)(2,1)S(1)} %band.1), channel_id=1, source_target_pairs={{0,32},{32,64},{64,96},{96,128},{128,160},{160,192},{192,224},{1,3... | collective-permute-start | bytes 2359304 | tf_op jit(solution)/shard_map/ppermute | solution.py:411
  25.6 0.7 copy-start.7
  25.6 0.7 copy-start.8
  45.5 6.9 %collective-permute-start.4 = (bf16[4,32,256]{2,1,0:T(8,128)(2,1)S(1)}, bf16[4,32,256]{2,1,0:T(8,128)(2,1)S(1)}, u32[]{:S(2)}, u32[]{:S(2)}) collective-permute-start(bf16[4,32,256]{2,1,0:T(8,128)(2,1)S(1)} %get-tuple-element.75.right), channel_id=1, source_target_pairs={{0,2},{2,4},{4,6},{6,8},{8,10},{10,12},{12,14},{14,16},{16,18},{18... | collective-permute-start | bytes 196616 | tf_op jit(solution)/shard_map/ppermute | solution.py:411
  51.1 6.5 %collective-permute-start.5 = (bf16[4,32,256]{2,1,0:T(8,128)(2,1)S(1)}, bf16[4,32,256]{2,1,0:T(8,128)(2,1)S(1)}, u32[]{:S(2)}, u32[]{:S(2)}) collective-permute-start(bf16[4,32,256]{2,1,0:T(8,128)(2,1)S(1)} %get-tuple-element.76.left), channel_id=1, source_target_pairs={{2,0},{4,2},{6,4},{8,6},{10,8},{12,10},{14,12},{16,14},{18,16},{20... | collective-permute-start | bytes 196616 | tf_op jit(solution)/shard_map/ppermute | solution.py:411
  57.7 6.0 %collective-permute-start.6 = (bf16[2,32,1024]{2,1,0:T(8,128)(2,1)S(1)}, bf16[2,32,1024]{2,1,0:T(8,128)(2,1)S(1)}, u32[]{:S(2)}, u32[]{:S(2)}) collective-permute-start(bf16[2,32,1024]{2,1,0:T(8,128)(2,1)S(1)} %get-tuple-element.77), channel_id=1, source_target_pairs={{0,32},{32,64},{64,96},{96,128},{128,160},{160,192},{192,224},{1,3... | collective-permute-start | bytes 393224 | tf_op jit(solution)/shard_map/ppermute | solution.py:411
  61.8 5.7 %collective-permute-start.7 = (bf16[2,32,1024]{2,1,0:T(8,128)(2,1)S(1)}, bf16[2,32,1024]{2,1,0:T(8,128)(2,1)S(1)}, u32[]{:S(2)}, u32[]{:S(2)}) collective-permute-start(bf16[2,32,1024]{2,1,0:T(8,128)(2,1)S(1)} %get-tuple-element.78), channel_id=1, source_target_pairs={{32,0},{64,32},{96,64},{128,96},{160,128},{192,160},{224,192},{33,... | collective-permute-start | bytes 393224 | tf_op jit(solution)/shard_map/ppermute | solution.py:411
  68.5 5.6 %collective-permute-start.8 = (bf16[4,48,256]{2,1,0:T(8,128)(2,1)S(1)}, bf16[4,48,256]{2,1,0:T(8,128)(2,1)S(1)}, u32[]{:S(2)}, u32[]{:S(2)}) collective-permute-start(bf16[4,48,256]{2,1,0:T(8,128)(2,1)S(1)} %get-tuple-element.83.right), channel_id=1, source_target_pairs={{0,2},{2,4},{4,6},{6,8},{8,10},{10,12},{12,14},{14,16},{16,18},{18... | collective-permute-start | bytes 294920 | tf_op jit(solution)/shard_map/ppermute | solution.py:411
  71.9 6.9 %collective-permute-start.9 = (bf16[4,48,256]{2,1,0:T(8,128)(2,1)S(1)}, bf16[4,48,256]{2,1,0:T(8,128)(2,1)S(1)}, u32[]{:S(2)}, u32[]{:S(2)}) collective-permute-start(bf16[4,48,256]{2,1,0:T(8,128)(2,1)S(1)} %get-tuple-element.84.left), channel_id=1, source_target_pairs={{2,0},{4,2},{6,4},{8,6},{10,8},{12,10},{14,12},{16,14},{18,16},{20... | collective-permute-start | bytes 294920 | tf_op jit(solution)/shard_map/ppermute | solution.py:411
  78.8 8.4 %collective-permute-start.10 = (bf16[2,48,1024]{2,1,0:T(8,128)(2,1)S(1)}, bf16[2,48,1024]{2,1,0:T(8,128)(2,1)S(1)}, u32[]{:S(2)}, u32[]{:S(2)}) collective-permute-start(bf16[2,48,1024]{2,1,0:T(8,128)(2,1)S(1)} %get-tuple-element.85), channel_id=1, source_target_pairs={{0,32},{32,64},{64,96},{96,128},{128,160},{160,192},{192,224},{1,3... | collective-permute-start | bytes 589832 | tf_op jit(solution)/shard_map/ppermute | solution.py:411
  82.7 9.7 %collective-permute-start.11 = (bf16[2,48,1024]{2,1,0:T(8,128)(2,1)S(1)}, bf16[2,48,1024]{2,1,0:T(8,128)(2,1)S(1)}, u32[]{:S(2)}, u32[]{:S(2)}) collective-permute-start(bf16[2,48,1024]{2,1,0:T(8,128)(2,1)S(1)} %get-tuple-element.86), channel_id=1, source_target_pairs={{32,0},{64,32},{96,64},{128,96},{160,128},{192,160},{224,192},{33,... | collective-permute-start | bytes 589832 | tf_op jit(solution)/shard_map/ppermute | solution.py:411
  94.4 8.1 %collective-permute-start.12 = (bf16[1024,128]{1,0:T(8,128)(2,1)S(1)}, bf16[1024,128]{1,0:T(8,128)(2,1)S(1)}, u32[]{:S(2)}, u32[]{:S(2)}) collective-permute-start(bf16[1024,128]{1,0:T(8,128)(2,1)S(1)} %get-tuple-element.105), channel_id=1, source_target_pairs={{0,1},{1,0},{2,3},{3,2},{4,5},{5,4},{6,7},{7,6},{8,9},{9,8},{10,11... | collective-permute-start | bytes 786440 | tf_op jit(solution)/shard_map/ppermute | solution.py:511
  153.1 5.4 %collective-permute-start.13 = (bf16[1024,128]{1,0:T(8,128)(2,1)S(1)}, bf16[1024,128]{1,0:T(8,128)(2,1)S(1)}, u32[]{:S(2)}, u32[]{:S(2)}) collective-permute-start(bf16[1024,128]{1,0:T(8,128)(2,1)S(1)} %bitcast.34), channel_id=1, source_target_pairs={{0,1},{1,0},{2,3},{3,2},{4,5},{5,4},{6,7},{7,6},{8,9},{9,8},{10,11... | collective-permute-start | bytes 786440 | tf_op jit(solution)/shard_map/ppermute | solution.py:516

commit v6 on v5

--- a/solution.py
+++ b/solution.py
@@ -15,6 +15,9 @@
 H = 2
 N = B + 2 * H
 MID = slice(H * Z, (H + B) * Z)
+WIDTHS = (4, 3, 3, 2, 1)
+Y_AT = tuple(Z * sum(WIDTHS[:u]) for u in range(6))
+X_AT = tuple(Z * sum(w * (B + 2 * w) for w in WIDTHS[:u]) for u in range(6))
 RING = slice((H - 1) * Z, (H + B + 1) * Z)
 GROUP = 128
 ROWS = 8
@@ -93,18 +96,16 @@
     return got[:q, 2 * Z :] + got[q : 2 * q, Z : Z + n] + got[2 * q :, :n]
 
 
-def kernel_gradient(out_ref, own, sources):
+def kernel_gradient(own, sources):
     gap = jnp.zeros((48, Z), BF16)
+
+    def shifted(rows):
+        return [jnp.concatenate([gap] * b + [rows] + [gap] * (2 - b), axis=1) for b in range(3)]
+
     lhs = jnp.concatenate(
         [
-            jnp.concatenate(
-                [
-                    jnp.concatenate([gap] * b + [rows] + [gap] * (2 - b), axis=1)
-                    for b in range(3)
-                ],
-                axis=0,
-            )
-            for rows in own
+            jnp.concatenate([part for layer in own for part in shifted(layer[i])], axis=0)
+            for i in range(B)
         ],
         axis=1,
     )
@@ -114,14 +115,12 @@
             axis=1,
         )
         got = lax.dot_general(lhs, rhs, (((1,), (1,)), ((), ())), preferred_element_type=F32)
-        rows = slice(144 * a, 144 * (a + 1))
-        out_ref[rows, : got.shape[1]] = got.astype(out_ref.dtype)
-        if got.shape[1] < Z:
-            out_ref[rows, got.shape[1] :] = jnp.zeros((144, Z - got.shape[1]), out_ref.dtype)
+        gap_lanes = jnp.zeros((got.shape[0], Z - got.shape[1]), F32)
+        yield a, jnp.concatenate([got, gap_lanes], axis=1)
 
 
 def own_cells(spread_ref):
-    return [spread_ref[H + i, :, MID] for i in range(B)]
+    return [spread_ref[B + i, :, slice(B * Z, 2 * B * Z)] for i in range(B)]
 
 
 def activate(value):
@@ -131,21 +130,18 @@
     )
 
 
-def assemble(parts, frame):
-    before, left, right, after, above, below = parts
-    own = slice(H, H + B)
-    frame[own, :, : H * Z] = before[...]
-    frame[own, :, H * Z : 2 * H * Z] = left[...]
-    frame[own, :, 2 * H * Z : 3 * H * Z] = right[...]
-    frame[own, :, 3 * H * Z :] = after[...]
-    frame[:H] = above[...]
-    frame[H + B :] = below[...]
-
-
-def put(pair, i, rows, value):
-    left, right = pair
-    left[i, rows] = value[:, : H * Z]
-    right[i, rows] = value[:, H * Z :]
+def ring_row(parts, u, f):
+    above, below, before, own, after = parts
+    w = WIDTHS[u]
+    if B <= f < 2 * B:
+        side = slice(Y_AT[u], Y_AT[u + 1])
+        i = f - B
+        return jnp.concatenate(
+            [before[i, :, side], own[i, 16 * u : 16 * (u + 1)], after[i, :, side]], axis=1
+        )
+    ref, r = (above, f - B + w) if f < B else (below, f - 2 * B)
+    at = X_AT[u] + r * (B + 2 * w) * Z
+    return ref[:, at : at + (B + 2 * w) * Z]
 
 
 def wide_sum(blocks):
@@ -169,11 +165,14 @@
         out_ref[:, :, k * B * Z : (k + 1) * B * Z] = ref[...]
 
 
-def rows_kernel(before, left, right, after, top, bottom):
-    for k, ref in enumerate((before, left, right, after)):
-        lanes = slice(k * H * Z, (k + 1) * H * Z)
-        top[:, :, lanes] = ref[:H]
-        bottom[:, :, lanes] = ref[B - H :]
+def edges_kernel(before, own, after, top, bottom):
+    for u, w in enumerate(WIDTHS):
+        parts = (top, bottom, before, own, after)
+        for r in range(w):
+            at = X_AT[u] + r * (B + 2 * w) * Z
+            lanes = slice(at, at + (B + 2 * w) * Z)
+            top[:, lanes] = ring_row(parts, u, B + r)
+            bottom[:, lanes] = ring_row(parts, u, 2 * B - w + r)
 
 
 def prepare_kernel(
@@ -204,7 +203,7 @@
 
 def forward_kernel(
     above, band, below, k0, k1, k2, k3, bias, carried,
-    frame, hidden_01, hidden_2, hidden_3, slope_0, slope_1, slope_2, own_3, send_left, send_right,
+    frame, hidden_01, hidden_2, hidden_3, slope_0, slope_1, slope_2, own_3, own, left, right,
     wide_0, wide_1, wide_2,
 ):
     bands = (above, band, below)
@@ -212,19 +211,21 @@
     sources = [lambda i, cut: bands[i // B][i % B, :, cut]]
     for i in range(N):
         frame[i] = sources[0](i + B - H, near)
-    slopes = (slope_0, slope_1, slope_2)
     for k, (kernel_ref, wide) in enumerate(((k0, wide_0), (k1, wide_1), (k2, wide_2))):
         reach = 3 - k
         lanes = slice((B - reach) * Z, (2 * B + reach) * Z)
         for i in range(B - reach, 2 * B + reach):
             pre = conv_row(kernel_ref, sources, i, lanes) + bias[16 * k : 16 * (k + 1), 0:1]
             value, slope = activate(pre)
-            value = value * inside(i - B, -reach, B + 2 * reach)
-            wide[i, :, lanes] = value.astype(BF16)
-            if k == 1 and B <= i < 2 * B:
-                slope_1[i - B] = slope[:, reach * Z : (reach + B) * Z]
-            if k != 1 and B - 1 <= i < 2 * B + 1:
-                slopes[k][i - B + H] = slope[:, (reach - 1) * Z : (reach + B + 1) * Z]
+            present = inside(i - B, -reach, B + 2 * reach)
+            wide[i, :, lanes] = (value * present).astype(BF16)
+            slope = slope * present
+            if k == 0 and B - 1 <= i < 2 * B + 1:
+                slope_0[i - B + 1] = slope[:, 2 * Z : (B + 4) * Z]
+            if k == 1:
+                slope_1[i - B + 2] = slope
+            if k == 2 and B <= i < 2 * B:
+                slope_2[i - B] = slope[:, Z : (B + 1) * Z]
         sources.append(lambda i, cut, wide=wide: wide[i, :, cut])
     for i in range(N):
         hidden_01[i, 0:16] = wide_0[i + B - H, :, near]
@@ -237,8 +238,11 @@
         hidden_3[i] = value.astype(BF16)
         grad = (carried[i, 48:64] * slope).astype(BF16)
         own_3[i] = spread(grad.astype(F32))
-        put((send_left, send_right), i, slice(0, 16), grad)
-        put((send_left, send_right), i, slice(16, 32), carried[i, 32:48].astype(BF16))
+        rest = [slope_2[i]] + [carried[i, 16 * k : 16 * (k + 1)] for k in (2, 1, 0)]
+        ready = [grad] + [value.astype(BF16) for value in rest]
+        own[i] = jnp.concatenate(ready, axis=0)
+        left[i] = jnp.concatenate([v[:, : w * Z] for v, w in zip(ready, WIDTHS)], axis=1)
+        right[i] = jnp.concatenate([v[:, (B - w) * Z :] for v, w in zip(ready, WIDTHS)], axis=1)
 
 
 def merge_kernel(
@@ -263,86 +267,53 @@
     grad_merge[64:128] = wide_sum([merge_grad[i] for i in range(B)])
     own = [own_3[i] for i in range(B)]
     grad_merge[128:144] = cell_sum(own)
-    kernel_gradient(grad_3, own, [frame, hidden_01, hidden_2])
-
-
-def third_kernel(
-    before, left, right, after, above, below, t2, t3, slope_1, slope_2, carried,
-    spread_3, spread_2, own_1, send_left, send_right, pieces, held,
+    for a, got in kernel_gradient([own], [frame, hidden_01, hidden_2]):
+        grad_3[144 * a : 144 * (a + 1)] = got
+
+
+def backward_kernel(
+    above, below, before, own, after, t1, t2, t3, slope_0, slope_1, slope_2, carried,
+    frame, hidden_01, grad_3, grad_merge,
+    spread_0, spread_1, spread_2, spread_3, kept, sent, sums,
 ):
-    assemble((before, left, right, after, above, below), pieces)
-    held[...] = pieces[:, 16:32, :].astype(F32)
-    for i in range(B):
-        held[H + i, :, MID] = carried[i, 32:48]
-
-    for i in range(N):
-        spread_3[i] = spread(pieces[i, 0:16].astype(F32))
-
-    for i in range(H - 1, H + B + 1):
-        got = held[i, :, RING] + back_row(t3, slice(96, 112), spread_3, i, RING)
-        grad = (got * slope_2[i] * inside(i - H, 1 - H, B + 2)).astype(BF16)
-        spread_2[i, :, RING] = spread(grad.astype(F32))
-    for i in range(B):
-        got = (
-            carried[i, 16:32]
-            + back_row(t3, slice(80, 96), spread_3, H + i, MID)
-            + back_row(t2, slice(80, 96), spread_2, H + i, MID)
-        )
-        grad = (got * slope_1[i]).astype(BF16)
-        own_1[i] = spread(grad.astype(F32))
-        put((send_left, send_right), i, slice(0, 16), spread_2[H + i, 16:32, MID])
-        put((send_left, send_right), i, slice(16, 32), grad)
-        put((send_left, send_right), i, slice(32, 48), carried[i, 0:16].astype(BF16))
-
-
-def beside_kernel(
-    frame, hidden_01, spread_3, spread_2, own_1, t3, base,
-    grad_2, grad_1, grad_bias, part_0, part_base,
-):
-    own = [own_1[i] for i in range(B)]
-    grad_bias[0:16] = cell_sum(own)
-    kernel_gradient(grad_1, own, [frame, hidden_01.at[:, 0:16, :]])
-    own = own_cells(spread_2)
-    grad_bias[16:32] = cell_sum(own)
-    kernel_gradient(grad_2, own, [frame, hidden_01])
-
-    for i in range(H - 1, H + B + 1):
-        part_0[i] = back_row(t3, slice(64, 80), spread_3, i, RING)
-    for i in range(B):
-        part_base[i] = base[i] + back_row(t3, slice(0, 64), spread_3, H + i, MID)
-
-
-def fourth_kernel(
-    before, left, right, after, above, below, t1, t2, slope_0, carried, part_0, frame,
-    grad_1, grad_2, grad_3, grad_merge, grad_bias,
-    spread_2, spread_1, spread_0, kept, sent, sums, pieces, held,
-):
-    assemble((before, left, right, after, above, below), pieces)
-    held[...] = pieces[:, 32:48, :].astype(F32)
-    for i in range(B):
-        held[H + i, :, MID] = carried[i, 0:16]
-
-    for i in range(N):
-        spread_2[i] = spread(pieces[i, 0:16].astype(F32))
-        spread_1[i] = spread(pieces[i, 16:32].astype(F32))
-
-    for i in range(H - 1, H + B + 1):
-        got = (
-            held[i, :, RING]
-            + part_0[i]
-            + back_row(t2, slice(64, 80), spread_2, i, RING)
-            + back_row(t1, slice(64, 80), spread_1, i, RING)
-        )
-        grad = (got * slope_0[i] * inside(i - H, 1 - H, B + 2)).astype(BF16)
-        spread_0[i, :, RING] = spread(grad.astype(F32))
-    own = own_cells(spread_0)
-    kernel_gradient(sums.at[0:432], own, [frame])
-    sums[432:864] = grad_1[...]
-    sums[864:1296] = grad_2[...]
+    parts = (above, below, before, own, after)
+    spreads = (spread_0, spread_1, spread_2, spread_3)
+    turned_refs = (None, t1, t2, t3)
+    for f in range(3 * B):
+        spread_3[f] = spread(ring_row(parts, 0, f).astype(F32))
+    for k in (2, 1, 0):
+        reach = k + 1
+        lanes = slice((B - reach) * Z, (2 * B + reach) * Z)
+        middle = slice(reach * Z, (B + reach) * Z)
+        channels = slice(64 + 16 * k, 80 + 16 * k)
+        for f in range(B - reach, 2 * B + reach):
+            i = f - B
+            here = 0 <= i < B
+            got = ring_row(parts, 4 - k, f).astype(F32)
+            if here:
+                exact = carried[i, 16 * k : 16 * (k + 1)]
+                got = jnp.concatenate([got[:, : middle.start], exact, got[:, middle.stop :]], axis=1)
+            for m in range(k + 1, 4):
+                got = got + back_row(turned_refs[m], channels, spreads[m], f, lanes)
+            if k == 2:
+                slope = ring_row(parts, 1, f).astype(F32)
+                if here:
+                    slope = jnp.concatenate(
+                        [slope[:, : middle.start], slope_2[i], slope[:, middle.stop :]], axis=1
+                    )
+            else:
+                slope = (slope_0, slope_1)[k][i + reach]
+            grad = (got * slope).astype(BF16)
+            spreads[k][f, :, lanes] = spread(grad.astype(F32))
+    owns = [own_cells(ref) for ref in spreads[:3]]
+    for a, got in kernel_gradient(owns, [frame, hidden_01]):
+        for k in range(3):
+            at = 432 * k + 144 * a
+            sums[at : at + 144] = got[144 * k : 144 * (k + 1)]
     sums[1296:1728] = grad_3[...]
     sums[1728:1856] = grad_merge[0:128]
-    sums[1856:1872] = cell_sum(own)
-    sums[1872:1904] = grad_bias[...]
+    for k in range(3):
+        sums[1856 + 16 * k : 1872 + 16 * k] = cell_sum(owns[k])
     sums[1904:1920] = grad_merge[128:144]
     sums[1920:] = jnp.zeros((2 * HALF - 1920, Z), F32)
     mine, other = halves()
@@ -350,14 +321,11 @@
     sent[...] = sums[pl.ds(other, HALF), :].astype(BF16)
 
 
-def last_kernel(spread_2, spread_1, spread_0, t0, t1, t2, part_base, out_ref):
+def last_kernel(spread_0, spread_1, spread_2, spread_3, t0, t1, t2, t3, base, out_ref):
     for i in range(B):
-        out = (
-            part_base[i]
-            + back_row(t2, slice(0, 64), spread_2, H + i, MID)
-            + back_row(t1, slice(0, 64), spread_1, H + i, MID)
-            + back_row(t0, slice(0, 64), spread_0, H + i, MID)
-        )
+        out = base[i]
+        for ref, turned_ref in zip((spread_0, spread_1, spread_2, spread_3), (t0, t1, t2, t3)):
+            out = out + back_row(turned_ref, slice(0, 64), ref, B + i, slice(B * Z, 2 * B * Z))
         for j in range(B):
             out_ref[pl.ds(B * i + j, 64, stride=B * B), :] = out[:, j * Z : (j + 1) * Z]
 
@@ -409,14 +377,6 @@
 def neighbours(low, high, axis):
     up = [(i, i + 1) for i in range(lax.axis_size(axis) - 1)]
     return lax.ppermute(high, axis, up), lax.ppermute(low, axis, [(j, i) for i, j in up])
-
-
-def exchange(left, right):
-    before, after = neighbours(left, right, "row")
-    edge = shape((H, left.shape[1], N * Z), BF16)
-    top, bottom = call(rows_kernel, [edge, edge], [before, left, right, after], name="rows")
-    above, below = neighbours(top, bottom, "gx")
-    return [before, left, right, after, above, below]
 
 
 def body(samples, cotangent, kernel_0, kernel_1, kernel_2, kernel_3, layer_bias, merging_weight, merging_bias):
@@ -447,11 +407,10 @@
     before, after = neighbours(own, own, "row")
     (band,) = call(band_kernel, [shape((B, 64, 3 * B * Z), BF16)], [before, own, after], name="band")
     above, below = neighbours(band, band, "gx")
-    ring = shape((N, 16, (B + 2) * Z), F32)
-    send = shape((B, 32, H * Z), BF16)
+    side = shape((B, 16, Y_AT[5]), BF16)
     (
         frame, hidden_01, hidden_2, hidden_3,
-        slope_0, slope_1, slope_2, own_3, left, right,
+        slope_0, slope_1, slope_2, own_3, own, left, right,
     ) = call(
         forward_kernel,
         [
@@ -459,51 +418,37 @@
             shape((N, 32, N * Z), BF16),
             shape((N, 16, N * Z), BF16),
             shape((B, 16, B * Z), BF16),
-            ring,
+            shape((B + 2, 16, (B + 2) * Z), F32),
+            shape((B + 4, 16, (B + 4) * Z), F32),
             shape((B, 16, B * Z), F32),
-            ring,
             shape((B, 48, B * Z), BF16),
-            send,
-            send,
+            shape((B, 80, B * Z), BF16),
+            side,
+            side,
         ],
         [above, band, below, w0, w1, w2, w3, bias, carried],
         [pltpu.VMEM((3 * B, 16, 3 * B * Z), BF16)] * 3,
         name="forward",
     )
-    parts = exchange(left, right)
-    grads = shape((432, Z), F32)
+    before, after = neighbours(left, right, "row")
+    edge = shape((16, X_AT[5]), BF16)
+    top, bottom = call(edges_kernel, [edge, edge], [before, own, after], name="edges")
+    above, below = neighbours(top, bottom, "gx")
     output, grad_3, grad_merge = call(
         merge_kernel,
-        [shape((1024, Z), F32), grads, shape((144, Z), F32)],
+        [shape((1024, Z), F32), shape((432, Z), F32), shape((144, Z), F32)],
         [frame, hidden_01, hidden_2, hidden_3, own_3, merging_weight, merge_bias, merge_grad],
         flops=100_000_000,
         name="merge",
     )
-    send = shape((B, 48, H * Z), BF16)
-    spreads = shape((N, 48, N * Z), BF16)
-    spread_3, spread_2, own_1, left, right = call(
-        third_kernel,
-        [spreads, spreads, shape((B, 48, B * Z), BF16), send, send],
-        parts + [t2, t3, slope_1, slope_2, carried],
-        [pltpu.VMEM((N, 32, N * Z), BF16), pltpu.VMEM((N, 16, N * Z), F32)],
-        name="gradients_2_1",
-    )
-    parts = exchange(left, right)
-    grad_2, grad_1, grad_bias, part_0, part_base = call(
-        beside_kernel,
-        [grads, grads, shape((32, Z), F32), ring, shape((B, 64, B * Z), F32)],
-        [frame, hidden_01, spread_3, spread_2, own_1, t3, base],
-        flops=200_000_000,
-        name="kernel_gradients_2_1",
-    )
-    spread_2, spread_1, spread_0, kept, sent = call(
-        fourth_kernel,
-        [spreads, spreads, spreads, shape((HALF, Z), F32), shape((HALF, Z), BF16)],
-        parts
-        + [t1, t2, slope_0, carried, part_0, frame]
-        + [grad_1, grad_2, grad_3, grad_merge, grad_bias],
-        [pltpu.VMEM((2 * HALF, Z), F32), pltpu.VMEM((N, 48, N * Z), BF16), pltpu.VMEM((N, 16, N * Z), F32)],
-        name="gradient_0",
+    spreads = [shape((3 * B, 48, 3 * B * Z), BF16)] * 4
+    *spreads, kept, sent = call(
+        backward_kernel,
+        spreads + [shape((HALF, Z), F32), shape((HALF, Z), BF16)],
+        [above, below, before, own, after, t1, t2, t3, slope_0, slope_1, slope_2, carried]
+        + [frame, hidden_01, grad_3, grad_merge],
+        [pltpu.VMEM((2 * HALF, Z), F32)],
+        name="backward",
     )
     axes = ("gx", "row")
     swap = [(0, 1), (1, 0)]
@@ -517,7 +462,7 @@
     (grad_input,) = call(
         last_kernel,
         [shape((1024, Z), F32)],
-        [spread_2, spread_1, spread_0, t0, t1, t2, part_base],
+        spreads + [t0, t1, t2, t3, base],
         flops=300_000_000,
         name="input_gradient",
     )

time: 160 us -> 146 us (0.912)
  starting transfers between devices: 45.6 us -> 33.1 us
  waiting for transfers between devices: 46.9 us -> 43.5 us
  blocking collectives: 50.5 us -> 52.5 us
    ppermute x6 -> x4, waiting for transfers between devices: 34.6 us -> 25.5 us  [neighbours(): lax.ppermute(low, axis, [(j, i) for i, j in up])]
    ppermute x6 -> x4, starting transfers between devices: 27.3 us -> 20.1 us  [neighbours(): lax.ppermute(high, axis, up)]
    ppermute x6 -> x4, waiting for transfers between devices: 11.1 us -> 16.8 us  [neighbours(): lax.ppermute(high, axis, up)]
    ppermute x6 -> x4, starting transfers between devices: 7.88 us -> 5.17 us  [neighbours(): lax.ppermute(low, axis, [(j, i) for i, j in up])]
    ppermute x1, starting transfers between devices: 6.91 us -> 4.39 us  [body(): lax.ppermute(sent, 'rep', swap)]
    all_to_all x1, blocking collectives: 30.4 us -> 32.4 us  [body(): lax.all_to_all(paired.reshape(GROUP, ROWS, Z), axes, 0, 0, tiled=True)]
    pallas_call x14 -> x11, Pallas kernels: 14.1 us -> 14.4 us  [call(): pl.pallas_call(kernel, out_shape=list(outs), in_specs=[pl.BlockSpec(memor...]
  transfers between devices with their start and end apart: 14 -> 10, of which waited for: 11 -> 9; matrix products, arithmetic and copies ran while one was open for 0% -> 0% of each run, Pallas kernels for 4% -> 3%
where the time goes in v6:
time: 146 us; the launch traced here: 145 us
  blocking collectives  52.5 us (36%)
  waiting for transfers between devices  43.5 us (30%)
  starting transfers between devices  33.1 us (23%)
  Pallas kernels  14.4 us (10%)
    all_to_all x1, blocking collectives, body(): lax.all_to_all(paired.reshape(GROUP, ROWS, Z), axes, 0, 0, tiled=True)  32.4 us
    ppermute x4, waiting for transfers between devices, neighbours(): lax.ppermute(low, axis, [(j, i) for i, j in up])  25.5 us
    ppermute x4, starting transfers between devices, neighbours(): lax.ppermute(high, axis, up)  20.1 us
    all_to_all x1, blocking collectives, body(): lax.all_to_all(added.reshape(GROUP, ROWS, Z), axes, 0, 0, tiled=True)  20.1 us
    ppermute x4, waiting for transfers between devices, neighbours(): lax.ppermute(high, axis, up)  16.8 us
    pallas_call x11, Pallas kernels, call(): pl.pallas_call(kernel, out_shape=list(outs), in_specs=[pl.BlockSpec(memor...  14.4 us
    ppermute x4, starting transfers between devices, neighbours(): lax.ppermute(low, axis, [(j, i) for i, j in up])  5.17 us
    ppermute x1, starting transfers between devices, body(): lax.ppermute(sent, 'rep', swap)  4.39 us
  transfers between devices with their start and end apart: 10, of which 9 were waited for; matrix products, arithmetic and copies ran while one was open for 0% of the time, Pallas kernels for 3%

profile of v6, /device:TPU:1, one launch (start us, length us, event | category | flops | bytes accessed | tf_op | source)
XLA Modules:
  0.0 145.4 jit_solution(7158115199670316733)
XLA Ops:
  1.9 1.3 collective-permute-start.1
  3.2 6.3 %collective-permute-start = (bf16[4,64,512]{2,1,0:T(8,128)(2,1)S(1)}, bf16[4,64,512]{2,1,0:T(8,128)(2,1)S(1)}, u32[]{:S(2)}, u32[]{:S(2)}) collective-permute-start(bf16[4,64,512]{2,1,0:T(8,128)(2,1)S(1)} %pack.1.own), channel_id=1, source_target_pairs={{0,2},{2,4},{4,6},{6,8},{8,10},{10,12},{12,14},{14,16},{16,18},{18... | collective-permute-start | bytes 786440 | tf_op jit(solution)/shard_map/ppermute | solution.py:379
  9.5 1.8 %collective-permute-done.1.after = bf16[4,64,512]{2,1,0:T(8,128)(2,1)S(1)} collective-permute-done((bf16[4,64,512]{2,1,0:T(8,128)(2,1)S(1)}, bf16[4,64,512]{2,1,0:T(8,128)(2,1)S(1)}, u32[]{:S(2)}, u32[]{:S(2)}) %collective-permute-start.1) | collective-permute-done | bytes 262176 | tf_op jit(solution)/shard_map/ppermute | solution.py:379
  11.3 8.8 %collective-permute-done.before = bf16[4,64,512]{2,1,0:T(8,128)(2,1)S(1)} collective-permute-done((bf16[4,64,512]{2,1,0:T(8,128)(2,1)S(1)}, bf16[4,64,512]{2,1,0:T(8,128)(2,1)S(1)}, u32[]{:S(2)}, u32[]{:S(2)}) %collective-permute-start) | collective-permute-done | bytes 262176 | tf_op jit(solution)/shard_map/ppermute | solution.py:379
  20.1 1.3 collective-permute-start.3
  21.4 4.0 %collective-permute-start.2 = (bf16[4,64,1536]{2,1,0:T(8,128)(2,1)S(1)}, bf16[4,64,1536]{2,1,0:T(8,128)(2,1)S(1)}, u32[]{:S(2)}, u32[]{:S(2)}) collective-permute-start(bf16[4,64,1536]{2,1,0:T(8,128)(2,1)S(1)} %band.1), channel_id=1, source_target_pairs={{0,32},{32,64},{64,96},{96,128},{128,160},{160,192},{192,224},{1,3... | collective-permute-start | bytes 2359304 | tf_op jit(solution)/shard_map/ppermute | solution.py:379
  26.1 14.5 %collective-permute-done.3.below = bf16[4,64,1536]{2,1,0:T(8,128)(2,1)S(1)} collective-permute-done((bf16[4,64,1536]{2,1,0:T(8,128)(2,1)S(1)}, bf16[4,64,1536]{2,1,0:T(8,128)(2,1)S(1)}, u32[]{:S(2)}, u32[]{:S(2)}) %collective-permute-start.3) | collective-permute-done | bytes 786464 | tf_op jit(solution)/shard_map/ppermute | solution.py:379
  41.5 4.0 %forward.1 = (bf16[8,64,1024]{2,1,0:T(8,128)(2,1)S(1)}, bf16[8,32,1024]{2,1,0:T(8,128)(2,1)S(1)}, bf16[8,16,1024]{2,1,0:T(8,128)(2,1)S(1)}, bf16[4,16,512]{2,1,0...) custom-call(bf16[4,64,1536]{2,1,0:T(8,128)(2,1)S(1)} %collective-per, ...), custom_call_target="tpu_custom_call" | custom-call | flops 1000000 | bytes 7021568 | tf_op jit(solution)/shard_map/forward/pallas_call | solution.py:34
  45.5 5.6 %collective-permute-start.4 = (bf16[4,16,1664]{2,1,0:T(8,128)(2,1)S(1)}, bf16[4,16,1664]{2,1,0:T(8,128)(2,1)S(1)}, u32[]{:S(2)}, u32[]{:S(2)}) collective-permute-start(bf16[4,16,1664]{2,1,0:T(8,128)(2,1)S(1)} %get-tuple-element.65), channel_id=1, source_target_pairs={{0,2},{2,4},{4,6},{6,8},{8,10},{10,12},{12,14},{14,16},{16,18},{18... | collective-permute-start | bytes 638984 | tf_op jit(solution)/shard_map/ppermute | solution.py:379
  51.1 1.3 collective-permute-start.5
  52.4 1.5 %collective-permute-done.4.before = bf16[4,16,1664]{2,1,0:T(8,128)(2,1)S(1)} collective-permute-done((bf16[4,16,1664]{2,1,0:T(8,128)(2,1)S(1)}, bf16[4,16,1664]{2,1,0:T(8,128)(2,1)S(1)}, u32[]{:S(2)}, u32[]{:S(2)}) %collective-permute-start.4) | collective-permute-done | bytes 213024 | tf_op jit(solution)/shard_map/ppermute | solution.py:379
  53.9 5.3 %collective-permute-done.5.after = bf16[4,16,1664]{2,1,0:T(8,128)(2,1)S(1)} collective-permute-done((bf16[4,16,1664]{2,1,0:T(8,128)(2,1)S(1)}, bf16[4,16,1664]{2,1,0:T(8,128)(2,1)S(1)}, u32[]{:S(2)}, u32[]{:S(2)}) %collective-permute-start.5) | collective-permute-done | bytes 213024 | tf_op jit(solution)/shard_map/ppermute | solution.py:379
  59.3 4.1 %collective-permute-start.6 = (bf16[16,16640]{1,0:T(8,128)(2,1)S(1)}, bf16[16,16640]{1,0:T(8,128)(2,1)S(1)}, u32[]{:S(2)}, u32[]{:S(2)}) collective-permute-start(bf16[16,16640]{1,0:T(8,128)(2,1)S(1)} %get-tuple-element.68), channel_id=1, source_target_pairs={{0,32},{32,64},{64,96},{96,128},{128,160},{160,192},{192,224},{1,3... | collective-permute-start | bytes 1597448 | tf_op jit(solution)/shard_map/ppermute | solution.py:379
  63.4 1.3 collective-permute-start.7
  64.7 1.2 merge.4
  65.9 5.8 %collective-permute-done.6.above = bf16[16,16640]{1,0:T(8,128)(2,1)S(1)} collective-permute-done((bf16[16,16640]{1,0:T(8,128)(2,1)S(1)}, bf16[16,16640]{1,0:T(8,128)(2,1)S(1)}, u32[]{:S(2)}, u32[]{:S(2)}) %collective-permute-start.6) | collective-permute-done | bytes 532512 | tf_op jit(solution)/shard_map/ppermute | solution.py:379
  71.7 3.9 %collective-permute-done.7.below = bf16[16,16640]{1,0:T(8,128)(2,1)S(1)} collective-permute-done((bf16[16,16640]{1,0:T(8,128)(2,1)S(1)}, bf16[16,16640]{1,0:T(8,128)(2,1)S(1)}, u32[]{:S(2)}, u32[]{:S(2)}) %collective-permute-start.7) | collective-permute-done | bytes 532512 | tf_op jit(solution)/shard_map/ppermute | solution.py:379
  75.5 4.9 %backward.1 = (bf16[12,48,1536]{2,1,0:T(8,128)(2,1)S(1)}, bf16[12,48,1536]{2,1,0:T(8,128)(2,1)S(1)}, bf16[12,48,1536]{2,1,0:T(8,128)(2,1)S(1)}, bf16[12,48,1536]...) custom-call(bf16[16,16640]{1,0:T(8,128)(2,1)S(1)} %collective-permute-done.6.above, ...), custom_call_target="tpu_custom_call" | custom-call | flops 1000000 | bytes 13274112 | tf_op jit(solution)/shard_map/backward/pallas_call | solution.py:34
  80.5 4.4 %collective-permute-start.8 = (bf16[1024,128]{1,0:T(8,128)(2,1)S(1)}, bf16[1024,128]{1,0:T(8,128)(2,1)S(1)}, u32[]{:S(2)}, u32[]{:S(2)}) collective-permute-start(bf16[1024,128]{1,0:T(8,128)(2,1)S(1)} %get-tuple-element.85), channel_id=1, source_target_pairs={{0,1},{1,0},{2,3},{3,2},{4,5},{5,4},{6,7},{7,6},{8,9},{9,8},{10,11... | collective-permute-start | bytes 786440 | tf_op jit(solution)/shard_map/ppermute | solution.py:456
  84.9 1.2 collective-permute-done.8.came
  86.1 32.4 %all_to_all.10 = bf16[128,8,128]{2,1,0:T(8,128)(2,1)S(1)} all-to-all(bf16[128,8,128]{2,1,0:T(8,128)(2,1)S(1)} %bitcast.38), channel_id=1, replica_groups=mesh['gx'=8,'row'=16,'rep'=2] {'gx','row'}, dimensions={0} | all-to-all | bytes 524288 | tf_op jit(solution)/shard_map/all_to_all | solution.py:457
  118.7 20.1 %all_to_all.11 = bf16[128,8,128]{2,1,0:T(8,128)(2,1)S(1)} all-to-all(bf16[128,8,128]{2,1,0:T(8,128)(2,1)S(1)} %bitcast.37), channel_id=1, replica_groups=mesh['gx'=8,'row'=16,'rep'=2] {'gx','row'}, dimensions={0} | all-to-all | bytes 524288 | tf_op jit(solution)/shard_map/all_to_all | solution.py:459
  138.7 3.5 %collective-permute-start.9 = (bf16[1024,128]{1,0:T(8,128)(2,1)S(1)}, bf16[1024,128]{1,0:T(8,128)(2,1)S(1)}, u32[]{:S(2)}, u32[]{:S(2)}) collective-permute-start(bf16[1024,128]{1,0:T(8,128)(2,1)S(1)} %bitcast.34), channel_id=1, source_target_pairs={{0,1},{1,0},{2,3},{3,2},{4,5},{5,4},{6,7},{7,6},{8,9},{9,8},{10,11... | collective-permute-start | bytes 786440 | tf_op jit(solution)/shard_map/ppermute | solution.py:461
  142.2 2.2 %input_gradient.1 = f32[1024,128]{1,0:T(8,128)} custom-call(bf16[12,48,1536]{2,1,0:T(8,128)(2,1)S(1)} %get-tuple-element.78.spread_0, bf16[12,48,1536]{2,1,0:T(8,128)(2,1)S(1)} %get-tuple-element.79.spread_1, bf16[12,48,1536]{2,1,0:T(8,128)(2,1)S(1)} %get-tuple-element.80.spread_2, bf16[12,48,1536]{2,1,0:T(8,128)(2,1)S(1)} %get-tuple-element.81.spread_3, ...), custom_call_target="tpu_custom_call" | custom-call | flops 300000000 | bytes 8430592 | tf_op jit(solution)/shard_map/input_gradient/pallas_call | solution.py:34
  (27 shorter events, 3.9 us)
Async XLA Ops:
  0.6 24.8 %copy-start = (bf16[1,64,4,4,128]{4,3,2,1,0:T(4,128)(2,1)S(1)}, bf16[1,64,4,4,128]{4,3,2,1,0:T(4,128)(2,1)}, u32[]{:S(2)}) copy-start(bf16[1,64,4,4,128]{4,3,2,1,0:T(4,128)(2,1)} %param.10) | copy-start | bytes 786436
  0.7 1.0 copy-start.1
  1.6 23.8 %copy-start.2 = (bf16[16,27,64]{2,0,1:T(8,128)(2,1)S(1)}, bf16[16,27,64]{2,0,1:T(8,128)(2,1)}, u32[]{:S(2)}) copy-start(bf16[16,27,64]{2,0,1:T(8,128)(2,1)} %param.11) | copy-start | bytes 165892
  1.7 23.8 %copy-start.3 = (bf16[16,27,80]{2,0,1:T(8,128)(2,1)S(1)}, bf16[16,27,80]{2,0,1:T(8,128)(2,1)}, u32[]{:S(2)}) copy-start(bf16[16,27,80]{2,0,1:T(8,128)(2,1)} %param.12) | copy-start | bytes 207364
  1.7 23.8 %copy-start.4 = (bf16[16,27,96]{2,0,1:T(8,128)(2,1)S(1)}, bf16[16,27,96]{2,0,1:T(8,128)(2,1)}, u32[]{:S(2)}) copy-start(bf16[16,27,96]{2,0,1:T(8,128)(2,1)} %param.13) | copy-start | bytes 248836
  1.7 23.8 %copy-start.5 = (bf16[16,27,112]{2,0,1:T(8,128)(2,1)S(1)}, bf16[16,27,112]{2,0,1:T(8,128)(2,1)}, u32[]{:S(2)}) copy-start(bf16[16,27,112]{2,0,1:T(8,128)(2,1)} %param.14) | copy-start | bytes 290308
  1.7 23.9 %copy-start.6 = (bf16[64,128]{1,0:T(8,128)(2,1)S(1)}, bf16[64,128]{1,0:T(8,128)(2,1)}, u32[]{:S(2)}) copy-start(bf16[64,128]{1,0:T(8,128)(2,1)} %merge.5) | copy-start | bytes 49156
  1.7 23.9 %copy-start.7 = (bf16[4,16]{1,0:T(4,128)(2,1)S(1)}, bf16[4,16]{1,0:T(4,128)(2,1)}, u32[]{:S(2)}) copy-start(bf16[4,16]{1,0:T(4,128)(2,1)} %layer_bias.1) | copy-start | bytes 388
  1.7 23.9 %copy-start.8 = (bf16[64]{0:T(256)(128)(2,1)S(1)}, bf16[64]{0:T(256)(128)(2,1)}, u32[]{:S(2)}) copy-start(bf16[64]{0:T(256)(128)(2,1)} %param.17) | copy-start | bytes 388
  1.9 9.4 %collective-permute-start.1 = (bf16[4,64,512]{2,1,0:T(8,128)(2,1)S(1)}, bf16[4,64,512]{2,1,0:T(8,128)(2,1)S(1)}, u32[]{:S(2)}, u32[]{:S(2)}) collective-permute-start(bf16[4,64,512]{2,1,0:T(8,128)(2,1)S(1)} %pack.1.own), channel_id=1, source_target_pairs={{2,0},{4,2},{6,4},{8,6},{10,8},{12,10},{14,12},{16,14},{18,16},{20... | collective-permute-start | bytes 786440 | tf_op jit(solution)/shard_map/ppermute | solution.py:379
  3.2 16.9 %collective-permute-start = (bf16[4,64,512]{2,1,0:T(8,128)(2,1)S(1)}, bf16[4,64,512]{2,1,0:T(8,128)(2,1)S(1)}, u32[]{:S(2)}, u32[]{:S(2)}) collective-permute-start(bf16[4,64,512]{2,1,0:T(8,128)(2,1)S(1)} %pack.1.own), channel_id=1, source_target_pairs={{0,2},{2,4},{4,6},{6,8},{8,10},{10,12},{12,14},{14,16},{16,18},{18... | collective-permute-start | bytes 786440 | tf_op jit(solution)/shard_map/ppermute | solution.py:379
  20.1 20.5 %collective-permute-start.3 = (bf16[4,64,1536]{2,1,0:T(8,128)(2,1)S(1)}, bf16[4,64,1536]{2,1,0:T(8,128)(2,1)S(1)}, u32[]{:S(2)}, u32[]{:S(2)}) collective-permute-start(bf16[4,64,1536]{2,1,0:T(8,128)(2,1)S(1)} %band.1), channel_id=1, source_target_pairs={{32,0},{64,32},{96,64},{128,96},{160,128},{192,160},{224,192},{33,... | collective-permute-start | bytes 2359304 | tf_op jit(solution)/shard_map/ppermute | solution.py:379
  21.4 20.1 %collective-permute-start.2 = (bf16[4,64,1536]{2,1,0:T(8,128)(2,1)S(1)}, bf16[4,64,1536]{2,1,0:T(8,128)(2,1)S(1)}, u32[]{:S(2)}, u32[]{:S(2)}) collective-permute-start(bf16[4,64,1536]{2,1,0:T(8,128)(2,1)S(1)} %band.1), channel_id=1, source_target_pairs={{0,32},{32,64},{64,96},{96,128},{128,160},{160,192},{192,224},{1,3... | collective-permute-start | bytes 2359304 | tf_op jit(solution)/shard_map/ppermute | solution.py:379
  45.5 8.4 %collective-permute-start.4 = (bf16[4,16,1664]{2,1,0:T(8,128)(2,1)S(1)}, bf16[4,16,1664]{2,1,0:T(8,128)(2,1)S(1)}, u32[]{:S(2)}, u32[]{:S(2)}) collective-permute-start(bf16[4,16,1664]{2,1,0:T(8,128)(2,1)S(1)} %get-tuple-element.65), channel_id=1, source_target_pairs={{0,2},{2,4},{4,6},{6,8},{8,10},{10,12},{12,14},{14,16},{16,18},{18... | collective-permute-start | bytes 638984 | tf_op jit(solution)/shard_map/ppermute | solution.py:379
  51.1 8.1 %collective-permute-start.5 = (bf16[4,16,1664]{2,1,0:T(8,128)(2,1)S(1)}, bf16[4,16,1664]{2,1,0:T(8,128)(2,1)S(1)}, u32[]{:S(2)}, u32[]{:S(2)}) collective-permute-start(bf16[4,16,1664]{2,1,0:T(8,128)(2,1)S(1)} %get-tuple-element.67), channel_id=1, source_target_pairs={{2,0},{4,2},{6,4},{8,6},{10,8},{12,10},{14,12},{16,14},{18,16},{20... | collective-permute-start | bytes 638984 | tf_op jit(solution)/shard_map/ppermute | solution.py:379
  59.3 12.4 %collective-permute-start.6 = (bf16[16,16640]{1,0:T(8,128)(2,1)S(1)}, bf16[16,16640]{1,0:T(8,128)(2,1)S(1)}, u32[]{:S(2)}, u32[]{:S(2)}) collective-permute-start(bf16[16,16640]{1,0:T(8,128)(2,1)S(1)} %get-tuple-element.68), channel_id=1, source_target_pairs={{0,32},{32,64},{64,96},{96,128},{128,160},{160,192},{192,224},{1,3... | collective-permute-start | bytes 1597448 | tf_op jit(solution)/shard_map/ppermute | solution.py:379
  63.4 12.1 %collective-permute-start.7 = (bf16[16,16640]{1,0:T(8,128)(2,1)S(1)}, bf16[16,16640]{1,0:T(8,128)(2,1)S(1)}, u32[]{:S(2)}, u32[]{:S(2)}) collective-permute-start(bf16[16,16640]{1,0:T(8,128)(2,1)S(1)} %get-tuple-element.69), channel_id=1, source_target_pairs={{32,0},{64,32},{96,64},{128,96},{160,128},{192,160},{224,192},{33,... | collective-permute-start | bytes 1597448 | tf_op jit(solution)/shard_map/ppermute | solution.py:379
  80.5 5.6 %collective-permute-start.8 = (bf16[1024,128]{1,0:T(8,128)(2,1)S(1)}, bf16[1024,128]{1,0:T(8,128)(2,1)S(1)}, u32[]{:S(2)}, u32[]{:S(2)}) collective-permute-start(bf16[1024,128]{1,0:T(8,128)(2,1)S(1)} %get-tuple-element.85), channel_id=1, source_target_pairs={{0,1},{1,0},{2,3},{3,2},{4,5},{5,4},{6,7},{7,6},{8,9},{9,8},{10,11... | collective-permute-start | bytes 786440 | tf_op jit(solution)/shard_map/ppermute | solution.py:456
  138.7 5.7 %collective-permute-start.9 = (bf16[1024,128]{1,0:T(8,128)(2,1)S(1)}, bf16[1024,128]{1,0:T(8,128)(2,1)S(1)}, u32[]{:S(2)}, u32[]{:S(2)}) collective-permute-start(bf16[1024,128]{1,0:T(8,128)(2,1)S(1)} %bitcast.34), channel_id=1, source_target_pairs={{0,1},{1,0},{2,3},{3,2},{4,5},{5,4},{6,7},{7,6},{8,9},{9,8},{10,11... | collective-permute-start | bytes 786440 | tf_op jit(solution)/shard_map/ppermute | solution.py:461

commit v7 on v6

--- a/solution.py
+++ b/solution.py
@@ -15,9 +15,7 @@
 H = 2
 N = B + 2 * H
 MID = slice(H * Z, (H + B) * Z)
-WIDTHS = (4, 3, 3, 2, 1)
-Y_AT = tuple(Z * sum(WIDTHS[:u]) for u in range(6))
-X_AT = tuple(Z * sum(w * (B + 2 * w) for w in WIDTHS[:u]) for u in range(6))
+EARLY, LATE = (3, 2, 1), (4, 3)
 RING = slice((H - 1) * Z, (H + B + 1) * Z)
 GROUP = 128
 ROWS = 8
@@ -49,16 +47,18 @@
 
 
 def from_left(v, keep):
-    return jnp.where(keep, pltpu.roll(v, 1, 1), 0.0)
+    parts = [pltpu.roll(v[:, k * Z : (k + 1) * Z], 1, 1) for k in range(v.shape[1] // Z)]
+    return jnp.where(keep, jnp.concatenate(parts, axis=1), jnp.zeros_like(v))
 
 
 def from_right(v, keep):
-    return jnp.where(keep, pltpu.roll(v, v.shape[1] - 1, 1), 0.0)
+    parts = [pltpu.roll(v[:, k * Z : (k + 1) * Z], Z - 1, 1) for k in range(v.shape[1] // Z)]
+    return jnp.where(keep, jnp.concatenate(parts, axis=1), jnp.zeros_like(v))
 
 
 def spread(v):
     not_first, not_last = lane_moves(*v.shape)
-    return jnp.concatenate([from_right(v, not_last), v, from_left(v, not_first)], axis=0).astype(BF16)
+    return jnp.concatenate([from_right(v, not_last), v, from_left(v, not_first)], axis=0)
 
 
 def inside(x, y, blocks):
@@ -97,26 +97,29 @@
 
 
 def kernel_gradient(own, sources):
-    gap = jnp.zeros((48, Z), BF16)
-
-    def shifted(rows):
-        return [jnp.concatenate([gap] * b + [rows] + [gap] * (2 - b), axis=1) for b in range(3)]
-
     lhs = jnp.concatenate(
-        [
-            jnp.concatenate([part for layer in own for part in shifted(layer[i])], axis=0)
-            for i in range(B)
-        ],
-        axis=1,
+        [jnp.concatenate([layer[i] for layer in own], axis=0) for i in range(B)], axis=1
     )
     for a in range(3):
-        rhs = jnp.concatenate(
-            [jnp.concatenate([s[H + i + a - 1, :, RING] for s in sources], axis=0) for i in range(B)],
-            axis=1,
+        taps = [
+            jnp.concatenate(
+                [
+                    jnp.concatenate(
+                        [s[H + i + a - 1, :, pl.ds((H + b - 1) * Z, B * Z)] for s in sources], axis=0
+                    )
+                    for i in range(B)
+                ],
+                axis=1,
+            )
+            for b in range(3)
+        ]
+        q = taps[0].shape[0]
+        got = lax.dot_general(
+            lhs, jnp.concatenate(taps, axis=0), (((1,), (1,)), ((), ())), preferred_element_type=F32
         )
-        got = lax.dot_general(lhs, rhs, (((1,), (1,)), ((), ())), preferred_element_type=F32)
-        gap_lanes = jnp.zeros((got.shape[0], Z - got.shape[1]), F32)
-        yield a, jnp.concatenate([got, gap_lanes], axis=1)
+        gap = jnp.zeros((got.shape[0], Z - q), F32)
+        for b in range(3):
+            yield 3 * a + b, jnp.concatenate([got[:, q * b : q * (b + 1)], gap], axis=1)
 
 
 def own_cells(spread_ref):
@@ -130,18 +133,32 @@
     )
 
 
-def ring_row(parts, u, f):
+def y_at(widths, u):
+    return Z * sum(widths[:u])
+
+
+def x_at(widths, u):
+    return Z * sum(w * (B + 2 * w) for w in widths[:u])
+
+
+def ring_row(parts, widths, u, f):
     above, below, before, own, after = parts
-    w = WIDTHS[u]
+    w = widths[u]
     if B <= f < 2 * B:
-        side = slice(Y_AT[u], Y_AT[u + 1])
+        side = slice(y_at(widths, u), y_at(widths, u + 1))
         i = f - B
         return jnp.concatenate(
             [before[i, :, side], own[i, 16 * u : 16 * (u + 1)], after[i, :, side]], axis=1
         )
     ref, r = (above, f - B + w) if f < B else (below, f - 2 * B)
-    at = X_AT[u] + r * (B + 2 * w) * Z
+    at = x_at(widths, u) + r * (B + 2 * w) * Z
     return ref[:, at : at + (B + 2 * w) * Z]
+
+
+def put(widths, i, ready, own, left, right):
+    own[i] = jnp.concatenate(ready, axis=0)
+    left[i] = jnp.concatenate([v[:, : w * Z] for v, w in zip(ready, widths)], axis=1)
+    right[i] = jnp.concatenate([v[:, (B - w) * Z :] for v, w in zip(ready, widths)], axis=1)
 
 
 def wide_sum(blocks):
@@ -165,19 +182,19 @@
         out_ref[:, :, k * B * Z : (k + 1) * B * Z] = ref[...]
 
 
-def edges_kernel(before, own, after, top, bottom):
-    for u, w in enumerate(WIDTHS):
+def edges_kernel(widths, before, own, after, top, bottom):
+    for u, w in enumerate(widths):
         parts = (top, bottom, before, own, after)
         for r in range(w):
-            at = X_AT[u] + r * (B + 2 * w) * Z
+            at = x_at(widths, u) + r * (B + 2 * w) * Z
             lanes = slice(at, at + (B + 2 * w) * Z)
-            top[:, lanes] = ring_row(parts, u, B + r)
-            bottom[:, lanes] = ring_row(parts, u, 2 * B - w + r)
+            top[:, lanes] = ring_row(parts, widths, u, B + r)
+            bottom[:, lanes] = ring_row(parts, widths, u, 2 * B - w + r)
 
 
 def prepare_kernel(
     cot_ref, merge, layer_bias, merging_bias, k0, k1, k2, k3,
-    base, carried, merge_grad, bias, merge_bias, w0, w1, w2, w3, t0, t1, t2, t3, wide,
+    base, carried, merge_grad, bias, merge_bias, w0, w1, w2, w3, t0, t1, t2, t3, own, left, right, wide,
 ):
     for k in range(4):
         column = as_column(layer_bias[k : k + 1].astype(F32))
@@ -199,6 +216,8 @@
         back = jnp.dot(merge_t, grad, preferred_element_type=F32)
         base[i] = cot + back[:64]
         carried[i] = back[64:]
+        ready = [back[64 + 16 * k : 80 + 16 * k].astype(BF16) for k in (2, 1, 0)]
+        put(EARLY, i, ready, own, left, right)
 
 
 def forward_kernel(
@@ -237,12 +256,8 @@
         value, slope = activate(pre)
         hidden_3[i] = value.astype(BF16)
         grad = (carried[i, 48:64] * slope).astype(BF16)
-        own_3[i] = spread(grad.astype(F32))
-        rest = [slope_2[i]] + [carried[i, 16 * k : 16 * (k + 1)] for k in (2, 1, 0)]
-        ready = [grad] + [value.astype(BF16) for value in rest]
-        own[i] = jnp.concatenate(ready, axis=0)
-        left[i] = jnp.concatenate([v[:, : w * Z] for v, w in zip(ready, WIDTHS)], axis=1)
-        right[i] = jnp.concatenate([v[:, (B - w) * Z :] for v, w in zip(ready, WIDTHS)], axis=1)
+        own_3[i] = spread(grad)
+        put(LATE, i, [grad, slope_2[i].astype(BF16)], own, left, right)
 
 
 def merge_kernel(
@@ -267,20 +282,22 @@
     grad_merge[64:128] = wide_sum([merge_grad[i] for i in range(B)])
     own = [own_3[i] for i in range(B)]
     grad_merge[128:144] = cell_sum(own)
-    for a, got in kernel_gradient([own], [frame, hidden_01, hidden_2]):
-        grad_3[144 * a : 144 * (a + 1)] = got
+    for t, got in kernel_gradient([own], [frame, hidden_01, hidden_2]):
+        grad_3[48 * t : 48 * (t + 1)] = got
 
 
 def backward_kernel(
-    above, below, before, own, after, t1, t2, t3, slope_0, slope_1, slope_2, carried,
+    above, below, before, own, after, c_above, c_below, c_before, c_own, c_after,
+    t1, t2, t3, slope_0, slope_1, slope_2, carried,
     frame, hidden_01, grad_3, grad_merge,
     spread_0, spread_1, spread_2, spread_3, kept, sent, sums,
 ):
-    parts = (above, below, before, own, after)
+    late = (above, below, before, own, after)
+    early = (c_above, c_below, c_before, c_own, c_after)
     spreads = (spread_0, spread_1, spread_2, spread_3)
     turned_refs = (None, t1, t2, t3)
     for f in range(3 * B):
-        spread_3[f] = spread(ring_row(parts, 0, f).astype(F32))
+        spread_3[f] = spread(ring_row(late, LATE, 0, f))
     for k in (2, 1, 0):
         reach = k + 1
         lanes = slice((B - reach) * Z, (2 * B + reach) * Z)
@@ -289,14 +306,14 @@
         for f in range(B - reach, 2 * B + reach):
             i = f - B
             here = 0 <= i < B
-            got = ring_row(parts, 4 - k, f).astype(F32)
+            got = ring_row(early, EARLY, 2 - k, f).astype(F32)
             if here:
                 exact = carried[i, 16 * k : 16 * (k + 1)]
                 got = jnp.concatenate([got[:, : middle.start], exact, got[:, middle.stop :]], axis=1)
             for m in range(k + 1, 4):
                 got = got + back_row(turned_refs[m], channels, spreads[m], f, lanes)
             if k == 2:
-                slope = ring_row(parts, 1, f).astype(F32)
+                slope = ring_row(late, LATE, 1, f).astype(F32)
                 if here:
                     slope = jnp.concatenate(
                         [slope[:, : middle.start], slope_2[i], slope[:, middle.stop :]], axis=1
@@ -304,12 +321,12 @@
             else:
                 slope = (slope_0, slope_1)[k][i + reach]
             grad = (got * slope).astype(BF16)
-            spreads[k][f, :, lanes] = spread(grad.astype(F32))
+            spreads[k][f, :, lanes] = spread(grad)
     owns = [own_cells(ref) for ref in spreads[:3]]
-    for a, got in kernel_gradient(owns, [frame, hidden_01]):
+    for t, got in kernel_gradient(owns, [frame, hidden_01]):
         for k in range(3):
-            at = 432 * k + 144 * a
-            sums[at : at + 144] = got[144 * k : 144 * (k + 1)]
+            at = 432 * k + 48 * t
+            sums[at : at + 48] = got[48 * k : 48 * (k + 1)]
     sums[1296:1728] = grad_3[...]
     sums[1728:1856] = grad_merge[0:128]
     for k in range(3):
@@ -377,6 +394,12 @@
 def neighbours(low, high, axis):
     up = [(i, i + 1) for i in range(lax.axis_size(axis) - 1)]
     return lax.ppermute(high, axis, up), lax.ppermute(low, axis, [(j, i) for i, j in up])
+
+
+def edges(widths, before, own, after):
+    edge = shape((16, x_at(widths, len(widths))), BF16)
+    kernel = functools.partial(edges_kernel, widths)
+    return call(kernel, [edge, edge], [before, own, after], name="edges")
 
 
 def body(samples, cotangent, kernel_0, kernel_1, kernel_2, kernel_3, layer_bias, merging_weight, merging_bias):
@@ -393,12 +416,14 @@
         [wide],
         name="pack",
     )
-    base, carried, merge_grad, bias, merge_bias, w0, w1, w2, w3, t0, t1, t2, t3 = call(
+    base, carried, merge_grad, bias, merge_bias, w0, w1, w2, w3, t0, t1, t2, t3, c_own, c_left, c_right = call(
         prepare_kernel,
         [shape((B, 64, B * Z), F32)] * 2
         + [shape((B, 64, B * Z), BF16), columns, columns]
         + [shape((144, 3 * k.shape[2]), BF16) for k in kernels]
-        + [shape((3, k.shape[2], 144), BF16) for k in kernels],
+        + [shape((3, k.shape[2], 144), BF16) for k in kernels]
+        + [shape((B, 48, B * Z), BF16)]
+        + [shape((B, 16, y_at(EARLY, 3)), BF16)] * 2,
         [cotangent.reshape(1024, Z), merging_weight, layer_bias, merging_bias.reshape(1, 64)] + flat,
         [wide],
         flops=40_000_000,
@@ -407,7 +432,10 @@
     before, after = neighbours(own, own, "row")
     (band,) = call(band_kernel, [shape((B, 64, 3 * B * Z), BF16)], [before, own, after], name="band")
     above, below = neighbours(band, band, "gx")
-    side = shape((B, 16, Y_AT[5]), BF16)
+    c_before, c_after = neighbours(c_left, c_right, "row")
+    above, below, c_before, c_after = lax.optimization_barrier((above, below, c_before, c_after))
+    c_top, c_bottom = edges(EARLY, c_before, c_own, c_after)
+    side = shape((B, 16, y_at(LATE, 2)), BF16)
     (
         frame, hidden_01, hidden_2, hidden_3,
         slope_0, slope_1, slope_2, own_3, own, left, right,
@@ -422,7 +450,7 @@
             shape((B + 4, 16, (B + 4) * Z), F32),
             shape((B, 16, B * Z), F32),
             shape((B, 48, B * Z), BF16),
-            shape((B, 80, B * Z), BF16),
+            shape((B, 32, B * Z), BF16),
             side,
             side,
         ],
@@ -431,8 +459,10 @@
         name="forward",
     )
     before, after = neighbours(left, right, "row")
-    edge = shape((16, X_AT[5]), BF16)
-    top, bottom = call(edges_kernel, [edge, edge], [before, own, after], name="edges")
+    c_top, c_bottom, _ = lax.optimization_barrier((c_top, c_bottom, left))
+    c_above, c_below = neighbours(c_top, c_bottom, "gx")
+    before, after, c_above, c_below = lax.optimization_barrier((before, after, c_above, c_below))
+    top, bottom = edges(LATE, before, own, after)
     above, below = neighbours(top, bottom, "gx")
     output, grad_3, grad_merge = call(
         merge_kernel,
@@ -445,7 +475,7 @@
     *spreads, kept, sent = call(
         backward_kernel,
         spreads + [shape((HALF, Z), F32), shape((HALF, Z), BF16)],
-        [above, below, before, own, after, t1, t2, t3, slope_0, slope_1, slope_2, carried]
+        [above, below, before, own, after, c_above, c_below, c_before, c_own, c_after, t1, t2, t3, slope_0, slope_1, slope_2, carried]
         + [frame, hidden_01, grad_3, grad_merge],
         [pltpu.VMEM((2 * HALF, Z), F32)],
         name="backward",

time: 146 us -> 149 us (1.021)
  starting transfers between devices: 33.1 us -> 38.4 us
  blocking collectives: 52.5 us -> 49.1 us
  waiting for transfers between devices: 43.5 us -> 45.3 us
    ppermute x4 -> x6, waiting for transfers between devices: 16.8 us -> 29.5 us  [neighbours(): lax.ppermute(high, axis, up)]
    ppermute x4 -> x6, waiting for transfers between devices: 25.5 us -> 14.7 us  [neighbours(): lax.ppermute(low, axis, [(j, i) for i, j in up])]
    ppermute x4 -> x6, starting transfers between devices: 20.1 us -> 24 us  [neighbours(): lax.ppermute(high, axis, up)]
    all_to_all x1, blocking collectives: 32.4 us -> 29 us  [body(): lax.all_to_all(paired.reshape(GROUP, ROWS, Z), axes, 0, 0, tiled=True)]
    ppermute x4 -> x6, starting transfers between devices: 5.17 us -> 7.75 us  [neighbours(): lax.ppermute(low, axis, [(j, i) for i, j in up])]
    pallas_call x11 -> x12, Pallas kernels: 14.4 us -> 13.7 us  [call(): pl.pallas_call(kernel, out_shape=list(outs), in_specs=[pl.BlockSpec(memor...]
  transfers between devices with their start and end apart: 10 -> 14, of which waited for: 9 -> 9; matrix products, arithmetic and copies ran while one was open for 0% -> 0% of each run, Pallas kernels for 3% -> 3%
where the time goes in v7:
time: 149 us; the launch traced here: 148 us
  blocking collectives  49.1 us (33%)
  waiting for transfers between devices  45.3 us (30%)
  starting transfers between devices  38.4 us (26%)
  Pallas kernels  13.7 us (9%)
    ppermute x6, waiting for transfers between devices, neighbours(): lax.ppermute(high, axis, up)  29.5 us
    all_to_all x1, blocking collectives, body(): lax.all_to_all(paired.reshape(GROUP, ROWS, Z), axes, 0, 0, tiled=True)  29 us
    ppermute x6, starting transfers between devices, neighbours(): lax.ppermute(high, axis, up)  24 us
    all_to_all x1, blocking collectives, body(): lax.all_to_all(added.reshape(GROUP, ROWS, Z), axes, 0, 0, tiled=True)  20.1 us
    ppermute x6, waiting for transfers between devices, neighbours(): lax.ppermute(low, axis, [(j, i) for i, j in up])  14.7 us
    pallas_call x12, Pallas kernels, call(): pl.pallas_call(kernel, out_shape=list(outs), in_specs=[pl.BlockSpec(memor...  13.7 us
    ppermute x6, starting transfers between devices, neighbours(): lax.ppermute(low, axis, [(j, i) for i, j in up])  7.75 us
    ppermute x1, starting transfers between devices, body(): others = lax.ppermute(totals, 'rep', swap)  3.47 us
  transfers between devices with their start and end apart: 14, of which 9 were waited for; matrix products, arithmetic and copies ran while one was open for 0% of the time, Pallas kernels for 3%

profile of v7, /device:TPU:1, one launch (start us, length us, event | category | flops | bytes accessed | tf_op | source)
XLA Modules:
  0.0 148.4 jit_solution(16907409950060515276)
XLA Ops:
  1.9 1.3 collective-permute-start.1
  3.2 6.3 %collective-permute-start = (bf16[4,64,512]{2,1,0:T(8,128)(2,1)S(1)}, bf16[4,64,512]{2,1,0:T(8,128)(2,1)S(1)}, u32[]{:S(2)}, u32[]{:S(2)}) collective-permute-start(bf16[4,64,512]{2,1,0:T(8,128)(2,1)S(1)} %pack.1.own), channel_id=1, source_target_pairs={{0,2},{2,4},{4,6},{6,8},{8,10},{10,12},{12,14},{14,16},{16,18},{18... | collective-permute-start | bytes 786440 | tf_op jit(solution)/shard_map/ppermute | solution.py:396
  9.5 1.8 %collective-permute-done.1.after = bf16[4,64,512]{2,1,0:T(8,128)(2,1)S(1)} collective-permute-done((bf16[4,64,512]{2,1,0:T(8,128)(2,1)S(1)}, bf16[4,64,512]{2,1,0:T(8,128)(2,1)S(1)}, u32[]{:S(2)}, u32[]{:S(2)}) %collective-permute-start.1) | collective-permute-done | bytes 262176 | tf_op jit(solution)/shard_map/ppermute | solution.py:396
  11.3 8.8 %collective-permute-done.before = bf16[4,64,512]{2,1,0:T(8,128)(2,1)S(1)} collective-permute-done((bf16[4,64,512]{2,1,0:T(8,128)(2,1)S(1)}, bf16[4,64,512]{2,1,0:T(8,128)(2,1)S(1)}, u32[]{:S(2)}, u32[]{:S(2)}) %collective-permute-start) | collective-permute-done | bytes 262176 | tf_op jit(solution)/shard_map/ppermute | solution.py:396
  20.1 1.3 collective-permute-start.3
  21.4 4.0 %collective-permute-start.2 = (bf16[4,64,1536]{2,1,0:T(8,128)(2,1)S(1)}, bf16[4,64,1536]{2,1,0:T(8,128)(2,1)S(1)}, u32[]{:S(2)}, u32[]{:S(2)}) collective-permute-start(bf16[4,64,1536]{2,1,0:T(8,128)(2,1)S(1)} %band.1), channel_id=1, source_target_pairs={{0,32},{32,64},{64,96},{96,128},{128,160},{160,192},{192,224},{1,3... | collective-permute-start | bytes 2359304 | tf_op jit(solution)/shard_map/ppermute | solution.py:396
  26.1 5.6 %collective-permute-start.4 = (bf16[4,16,768]{2,1,0:T(8,128)(2,1)S(1)}, bf16[4,16,768]{2,1,0:T(8,128)(2,1)S(1)}, u32[]{:S(2)}, u32[]{:S(2)}) collective-permute-start(bf16[4,16,768]{2,1,0:T(8,128)(2,1)S(1)} %get-tuple-element.66), channel_id=1, source_target_pairs={{0,2},{2,4},{4,6},{6,8},{8,10},{10,12},{12,14},{14,16},{16,18},{18... | collective-permute-start | bytes 294920 | tf_op jit(solution)/shard_map/ppermute | solution.py:396
  33.0 18.1 %collective-permute-done.4.before.c_before = bf16[4,16,768]{2,1,0:T(8,128)(2,1)S(1)} collective-permute-done((bf16[4,16,768]{2,1,0:T(8,128)(2,1)S(1)}, bf16[4,16,768]{2,1,0:T(8,128)(2,1)S(1)}, u32[]{:S(2)}, u32[]{:S(2)}) %collective-permute-start.4) | collective-permute-done | bytes 98336 | tf_op jit(solution)/shard_map/ppermute | solution.py:396
  51.2 2.3 %collective-permute-done.5.after.c_after = bf16[4,16,768]{2,1,0:T(8,128)(2,1)S(1)} collective-permute-done((bf16[4,16,768]{2,1,0:T(8,128)(2,1)S(1)}, bf16[4,16,768]{2,1,0:T(8,128)(2,1)S(1)}, u32[]{:S(2)}, u32[]{:S(2)}) %collective-permute-start.5) | collective-permute-done | bytes 98336 | tf_op jit(solution)/shard_map/ppermute | solution.py:396
  53.5 3.8 %forward.1 = (bf16[8,64,1024]{2,1,0:T(8,128)(2,1)S(1)}, bf16[8,32,1024]{2,1,0:T(8,128)(2,1)S(1)}, bf16[8,16,1024]{2,1,0:T(8,128)(2,1)S(1)}, bf16[4,16,512]{2,1,0...) custom-call(bf16[4,64,1536]{2,1,0:T(8,128)(2,1)S(1)} %collective-per, ...), custom_call_target="tpu_custom_call" | custom-call | flops 1000000 | bytes 6628352 | tf_op jit(solution)/shard_map/forward/pallas_call | solution.py:32
  57.4 1.3 collective-permute-start.8
  60.0 3.3 %collective-permute-start.6 = (bf16[4,16,896]{2,1,0:T(8,128)(2,1)S(1)}, bf16[4,16,896]{2,1,0:T(8,128)(2,1)S(1)}, u32[]{:S(2)}, u32[]{:S(2)}) collective-permute-start(bf16[4,16,896]{2,1,0:T(8,128)(2,1)S(1)} %get-tuple-element.84), channel_id=1, source_target_pairs={{0,2},{2,4},{4,6},{6,8},{8,10},{10,12},{12,14},{14,16},{16,18},{18... | collective-permute-start | bytes 344072 | tf_op jit(solution)/shard_map/ppermute | solution.py:396
  63.3 1.3 collective-permute-start.7
  65.3 6.7 %collective-permute-done.7.after = bf16[4,16,896]{2,1,0:T(8,128)(2,1)S(1)} collective-permute-done((bf16[4,16,896]{2,1,0:T(8,128)(2,1)S(1)}, bf16[4,16,896]{2,1,0:T(8,128)(2,1)S(1)}, u32[]{:S(2)}, u32[]{:S(2)}) %collective-permute-start.7) | collective-permute-done | bytes 114720 | tf_op jit(solution)/shard_map/ppermute | solution.py:396
  72.0 3.4 %collective-permute-start.10 = (bf16[16,9984]{1,0:T(8,128)(2,1)S(1)}, bf16[16,9984]{1,0:T(8,128)(2,1)S(1)}, u32[]{:S(2)}, u32[]{:S(2)}) collective-permute-start(bf16[16,9984]{1,0:T(8,128)(2,1)S(1)} %get-tuple-element.96), channel_id=1, source_target_pairs={{0,32},{32,64},{64,96},{96,128},{128,160},{160,192},{192,224},{1,3... | collective-permute-start | bytes 958472 | tf_op jit(solution)/shard_map/ppermute | solution.py:396
  76.7 1.7 %merge.4 = (f32[1024,128]{1,0:T(8,128)}, f32[432,128]{1,0:T(8,128)S(1)}, f32[144,128]{1,0:T(8,128)S(1)}) custom-call(bf16[8,64,1024]{2,1,0:T(8,128)(2,1)S(1)} %get-tuple-element.76.frame, bf16[8,32,1024]{2,1,0:T(8,128)(2,1)S(1)} %get-tuple-element.77.hidden_01, bf16[8,16,1024]{2,1,0:T(8,128)(2,1)S(1)} %get-tuple-element.78.hidden_2, ...), custom_call_target="tpu_custom_call" | custom-call | flops 100000000 | bytes 3227648 | tf_op jit(solution)/shard_map/merge/pallas_call | solution.py:32
  78.4 1.9 %collective-permute-done.10.above = bf16[16,9984]{1,0:T(8,128)(2,1)S(1)} collective-permute-done((bf16[16,9984]{1,0:T(8,128)(2,1)S(1)}, bf16[16,9984]{1,0:T(8,128)(2,1)S(1)}, u32[]{:S(2)}, u32[]{:S(2)}) %collective-permute-start.10) | collective-permute-done | bytes 319520 | tf_op jit(solution)/shard_map/ppermute | solution.py:396
  80.3 3.9 %collective-permute-done.11.below = bf16[16,9984]{1,0:T(8,128)(2,1)S(1)} collective-permute-done((bf16[16,9984]{1,0:T(8,128)(2,1)S(1)}, bf16[16,9984]{1,0:T(8,128)(2,1)S(1)}, u32[]{:S(2)}, u32[]{:S(2)}) %collective-permute-start.11) | collective-permute-done | bytes 319520 | tf_op jit(solution)/shard_map/ppermute | solution.py:396
  84.1 3.9 %backward.1 = (bf16[12,48,1536]{2,1,0:T(8,128)(2,1)S(1)}, bf16[12,48,1536]{2,1,0:T(8,128)(2,1)S(1)}, bf16[12,48,1536]{2,1,0:T(8,128)(2,1)S(1)}, bf16[12,48,1536]...) custom-call(bf16[16,9984]{1,0:T(8,128)(2,1)S(1)} %collective-permute-done.10.above, ...), custom_call_target="tpu_custom_call" | custom-call | flops 1000000 | bytes 13274112 | tf_op jit(solution)/shard_map/backward/pallas_call | solution.py:32
  88.1 3.2 %collective-permute-start.12 = (bf16[1024,128]{1,0:T(8,128)(2,1)S(1)}, bf16[1024,128]{1,0:T(8,128)(2,1)S(1)}, u32[]{:S(2)}, u32[]{:S(2)}) collective-permute-start(bf16[1024,128]{1,0:T(8,128)(2,1)S(1)} %get-tuple-element.115), channel_id=1, source_target_pairs={{0,1},{1,0},{2,3},{3,2},{4,5},{5,4},{6,7},{7,6},{8,9},{9,8},{10,11... | collective-permute-start | bytes 786440 | tf_op jit(solution)/shard_map/ppermute | solution.py:486
  92.5 29.0 %all_to_all.10 = bf16[128,8,128]{2,1,0:T(8,128)(2,1)S(1)} all-to-all(bf16[128,8,128]{2,1,0:T(8,128)(2,1)S(1)} %bitcast.38), channel_id=1, replica_groups=mesh['gx'=8,'row'=16,'rep'=2] {'gx','row'}, dimensions={0} | all-to-all | bytes 524288 | tf_op jit(solution)/shard_map/all_to_all | solution.py:487
  121.6 20.1 %all_to_all.11 = bf16[128,8,128]{2,1,0:T(8,128)(2,1)S(1)} all-to-all(bf16[128,8,128]{2,1,0:T(8,128)(2,1)S(1)} %bitcast.37), channel_id=1, replica_groups=mesh['gx'=8,'row'=16,'rep'=2] {'gx','row'}, dimensions={0} | all-to-all | bytes 524288 | tf_op jit(solution)/shard_map/all_to_all | solution.py:489
  141.7 3.5 %collective-permute-start.13 = (bf16[1024,128]{1,0:T(8,128)(2,1)S(1)}, bf16[1024,128]{1,0:T(8,128)(2,1)S(1)}, u32[]{:S(2)}, u32[]{:S(2)}) collective-permute-start(bf16[1024,128]{1,0:T(8,128)(2,1)S(1)} %bitcast.34), channel_id=1, source_target_pairs={{0,1},{1,0},{2,3},{3,2},{4,5},{5,4},{6,7},{7,6},{8,9},{9,8},{10,11... | collective-permute-start | bytes 786440 | tf_op jit(solution)/shard_map/ppermute | solution.py:491
  145.2 2.2 %input_gradient.1 = f32[1024,128]{1,0:T(8,128)} custom-call(bf16[12,48,1536]{2,1,0:T(8,128)(2,1)S(1)} %get-tuple-element.108.spread_0, bf16[12,48,1536]{2,1,0:T(8,128)(2,1)S(1)} %get-tuple-element.109.spread_1, bf16[12,48,1536]{2,1,0:T(8,128)(2,1)S(1)} %get-tuple-element.110.spread_2, bf16[12,48,1536]{2,1,0:T(8,128)(2,1)S(1)} %get-tuple-element.111.spread_3, ...), custom_call_target="tpu_custom_call" | custom-call | flops 300000000 | bytes 8430592 | tf_op jit(solution)/shard_map/input_gradient/pallas_call | solution.py:32
  (36 shorter events, 8.8 us)
Async XLA Ops:
  0.6 24.8 %copy-start = (bf16[1,64,4,4,128]{4,3,2,1,0:T(4,128)(2,1)S(1)}, bf16[1,64,4,4,128]{4,3,2,1,0:T(4,128)(2,1)}, u32[]{:S(2)}) copy-start(bf16[1,64,4,4,128]{4,3,2,1,0:T(4,128)(2,1)} %param.10) | copy-start | bytes 786436
  0.7 1.0 copy-start.1
  1.6 23.8 %copy-start.2 = (bf16[16,27,64]{2,0,1:T(8,128)(2,1)S(1)}, bf16[16,27,64]{2,0,1:T(8,128)(2,1)}, u32[]{:S(2)}) copy-start(bf16[16,27,64]{2,0,1:T(8,128)(2,1)} %param.11) | copy-start | bytes 165892
  1.7 23.8 %copy-start.3 = (bf16[16,27,80]{2,0,1:T(8,128)(2,1)S(1)}, bf16[16,27,80]{2,0,1:T(8,128)(2,1)}, u32[]{:S(2)}) copy-start(bf16[16,27,80]{2,0,1:T(8,128)(2,1)} %param.12) | copy-start | bytes 207364
  1.7 23.8 %copy-start.4 = (bf16[16,27,96]{2,0,1:T(8,128)(2,1)S(1)}, bf16[16,27,96]{2,0,1:T(8,128)(2,1)}, u32[]{:S(2)}) copy-start(bf16[16,27,96]{2,0,1:T(8,128)(2,1)} %param.13) | copy-start | bytes 248836
  1.7 23.8 %copy-start.5 = (bf16[16,27,112]{2,0,1:T(8,128)(2,1)S(1)}, bf16[16,27,112]{2,0,1:T(8,128)(2,1)}, u32[]{:S(2)}) copy-start(bf16[16,27,112]{2,0,1:T(8,128)(2,1)} %param.14) | copy-start | bytes 290308
  1.7 23.9 %copy-start.6 = (bf16[64,128]{1,0:T(8,128)(2,1)S(1)}, bf16[64,128]{1,0:T(8,128)(2,1)}, u32[]{:S(2)}) copy-start(bf16[64,128]{1,0:T(8,128)(2,1)} %merge.5) | copy-start | bytes 49156
  1.7 23.9 %copy-start.7 = (bf16[4,16]{1,0:T(4,128)(2,1)S(1)}, bf16[4,16]{1,0:T(4,128)(2,1)}, u32[]{:S(2)}) copy-start(bf16[4,16]{1,0:T(4,128)(2,1)} %layer_bias.1) | copy-start | bytes 388
  1.7 23.9 %copy-start.8 = (bf16[64]{0:T(256)(128)(2,1)S(1)}, bf16[64]{0:T(256)(128)(2,1)}, u32[]{:S(2)}) copy-start(bf16[64]{0:T(256)(128)(2,1)} %param.17) | copy-start | bytes 388
  1.9 9.4 %collective-permute-start.1 = (bf16[4,64,512]{2,1,0:T(8,128)(2,1)S(1)}, bf16[4,64,512]{2,1,0:T(8,128)(2,1)S(1)}, u32[]{:S(2)}, u32[]{:S(2)}) collective-permute-start(bf16[4,64,512]{2,1,0:T(8,128)(2,1)S(1)} %pack.1.own), channel_id=1, source_target_pairs={{2,0},{4,2},{6,4},{8,6},{10,8},{12,10},{14,12},{16,14},{18,16},{20... | collective-permute-start | bytes 786440 | tf_op jit(solution)/shard_map/ppermute | solution.py:396
  3.2 16.9 %collective-permute-start = (bf16[4,64,512]{2,1,0:T(8,128)(2,1)S(1)}, bf16[4,64,512]{2,1,0:T(8,128)(2,1)S(1)}, u32[]{:S(2)}, u32[]{:S(2)}) collective-permute-start(bf16[4,64,512]{2,1,0:T(8,128)(2,1)S(1)} %pack.1.own), channel_id=1, source_target_pairs={{0,2},{2,4},{4,6},{6,8},{8,10},{10,12},{12,14},{14,16},{16,18},{18... | collective-permute-start | bytes 786440 | tf_op jit(solution)/shard_map/ppermute | solution.py:396
  20.1 33.4 %collective-permute-start.3 = (bf16[4,64,1536]{2,1,0:T(8,128)(2,1)S(1)}, bf16[4,64,1536]{2,1,0:T(8,128)(2,1)S(1)}, u32[]{:S(2)}, u32[]{:S(2)}) collective-permute-start(bf16[4,64,1536]{2,1,0:T(8,128)(2,1)S(1)} %band.1), channel_id=1, source_target_pairs={{32,0},{64,32},{96,64},{128,96},{160,128},{192,160},{224,192},{33,... | collective-permute-start | bytes 2359304 | tf_op jit(solution)/shard_map/ppermute | solution.py:396
  21.4 32.1 %collective-permute-start.2 = (bf16[4,64,1536]{2,1,0:T(8,128)(2,1)S(1)}, bf16[4,64,1536]{2,1,0:T(8,128)(2,1)S(1)}, u32[]{:S(2)}, u32[]{:S(2)}) collective-permute-start(bf16[4,64,1536]{2,1,0:T(8,128)(2,1)S(1)} %band.1), channel_id=1, source_target_pairs={{0,32},{32,64},{64,96},{96,128},{128,160},{160,192},{192,224},{1,3... | collective-permute-start | bytes 2359304 | tf_op jit(solution)/shard_map/ppermute | solution.py:396
  26.1 25.1 %collective-permute-start.4 = (bf16[4,16,768]{2,1,0:T(8,128)(2,1)S(1)}, bf16[4,16,768]{2,1,0:T(8,128)(2,1)S(1)}, u32[]{:S(2)}, u32[]{:S(2)}) collective-permute-start(bf16[4,16,768]{2,1,0:T(8,128)(2,1)S(1)} %get-tuple-element.66), channel_id=1, source_target_pairs={{0,2},{2,4},{4,6},{6,8},{8,10},{10,12},{12,14},{14,16},{16,18},{18... | collective-permute-start | bytes 294920 | tf_op jit(solution)/shard_map/ppermute | solution.py:396
  31.7 21.8 %collective-permute-start.5 = (bf16[4,16,768]{2,1,0:T(8,128)(2,1)S(1)}, bf16[4,16,768]{2,1,0:T(8,128)(2,1)S(1)}, u32[]{:S(2)}, u32[]{:S(2)}) collective-permute-start(bf16[4,16,768]{2,1,0:T(8,128)(2,1)S(1)} %get-tuple-element.67), channel_id=1, source_target_pairs={{2,0},{4,2},{6,4},{8,6},{10,8},{12,10},{14,12},{16,14},{18,16},{20... | collective-permute-start | bytes 294920 | tf_op jit(solution)/shard_map/ppermute | solution.py:396
  57.4 14.6 %collective-permute-start.8 = (bf16[16,6656]{1,0:T(8,128)(2,1)S(1)}, bf16[16,6656]{1,0:T(8,128)(2,1)S(1)}, u32[]{:S(2)}, u32[]{:S(2)}) collective-permute-start(bf16[16,6656]{1,0:T(8,128)(2,1)S(1)} %get-tuple-element.91), channel_id=1, source_target_pairs={{0,32},{32,64},{64,96},{96,128},{128,160},{160,192},{192,224},{1,3... | collective-permute-start | bytes 638984 | tf_op jit(solution)/shard_map/ppermute | solution.py:396
  58.7 13.3 %collective-permute-start.9 = (bf16[16,6656]{1,0:T(8,128)(2,1)S(1)}, bf16[16,6656]{1,0:T(8,128)(2,1)S(1)}, u32[]{:S(2)}, u32[]{:S(2)}) collective-permute-start(bf16[16,6656]{1,0:T(8,128)(2,1)S(1)} %get-tuple-element.92), channel_id=1, source_target_pairs={{32,0},{64,32},{96,64},{128,96},{160,128},{192,160},{224,192},{33,... | collective-permute-start | bytes 638984 | tf_op jit(solution)/shard_map/ppermute | solution.py:396
  60.0 5.3 %collective-permute-start.6 = (bf16[4,16,896]{2,1,0:T(8,128)(2,1)S(1)}, bf16[4,16,896]{2,1,0:T(8,128)(2,1)S(1)}, u32[]{:S(2)}, u32[]{:S(2)}) collective-permute-start(bf16[4,16,896]{2,1,0:T(8,128)(2,1)S(1)} %get-tuple-element.84), channel_id=1, source_target_pairs={{0,2},{2,4},{4,6},{6,8},{8,10},{10,12},{12,14},{14,16},{16,18},{18... | collective-permute-start | bytes 344072 | tf_op jit(solution)/shard_map/ppermute | solution.py:396
  63.3 8.6 %collective-permute-start.7 = (bf16[4,16,896]{2,1,0:T(8,128)(2,1)S(1)}, bf16[4,16,896]{2,1,0:T(8,128)(2,1)S(1)}, u32[]{:S(2)}, u32[]{:S(2)}) collective-permute-start(bf16[4,16,896]{2,1,0:T(8,128)(2,1)S(1)} %get-tuple-element.85), channel_id=1, source_target_pairs={{2,0},{4,2},{6,4},{8,6},{10,8},{12,10},{14,12},{16,14},{18,16},{20... | collective-permute-start | bytes 344072 | tf_op jit(solution)/shard_map/ppermute | solution.py:396
  72.0 8.3 %collective-permute-start.10 = (bf16[16,9984]{1,0:T(8,128)(2,1)S(1)}, bf16[16,9984]{1,0:T(8,128)(2,1)S(1)}, u32[]{:S(2)}, u32[]{:S(2)}) collective-permute-start(bf16[16,9984]{1,0:T(8,128)(2,1)S(1)} %get-tuple-element.96), channel_id=1, source_target_pairs={{0,32},{32,64},{64,96},{96,128},{128,160},{160,192},{192,224},{1,3... | collective-permute-start | bytes 958472 | tf_op jit(solution)/shard_map/ppermute | solution.py:396
  75.4 8.7 %collective-permute-start.11 = (bf16[16,9984]{1,0:T(8,128)(2,1)S(1)}, bf16[16,9984]{1,0:T(8,128)(2,1)S(1)}, u32[]{:S(2)}, u32[]{:S(2)}) collective-permute-start(bf16[16,9984]{1,0:T(8,128)(2,1)S(1)} %get-tuple-element.97), channel_id=1, source_target_pairs={{32,0},{64,32},{96,64},{128,96},{160,128},{192,160},{224,192},{33,... | collective-permute-start | bytes 958472 | tf_op jit(solution)/shard_map/ppermute | solution.py:396
  88.1 4.4 %collective-permute-start.12 = (bf16[1024,128]{1,0:T(8,128)(2,1)S(1)}, bf16[1024,128]{1,0:T(8,128)(2,1)S(1)}, u32[]{:S(2)}, u32[]{:S(2)}) collective-permute-start(bf16[1024,128]{1,0:T(8,128)(2,1)S(1)} %get-tuple-element.115), channel_id=1, source_target_pairs={{0,1},{1,0},{2,3},{3,2},{4,5},{5,4},{6,7},{7,6},{8,9},{9,8},{10,11... | collective-permute-start | bytes 786440 | tf_op jit(solution)/shard_map/ppermute | solution.py:486
  141.7 5.7 %collective-permute-start.13 = (bf16[1024,128]{1,0:T(8,128)(2,1)S(1)}, bf16[1024,128]{1,0:T(8,128)(2,1)S(1)}, u32[]{:S(2)}, u32[]{:S(2)}) collective-permute-start(bf16[1024,128]{1,0:T(8,128)(2,1)S(1)} %bitcast.34), channel_id=1, source_target_pairs={{0,1},{1,0},{2,3},{3,2},{4,5},{5,4},{6,7},{7,6},{8,9},{9,8},{10,11... | collective-permute-start | bytes 786440 | tf_op jit(solution)/shard_map/ppermute | solution.py:491

commit v8 on v7

--- a/solution.py
+++ b/solution.py
@@ -182,14 +182,17 @@
         out_ref[:, :, k * B * Z : (k + 1) * B * Z] = ref[...]
 
 
-def edges_kernel(widths, before, own, after, top, bottom):
-    for u, w in enumerate(widths):
-        parts = (top, bottom, before, own, after)
-        for r in range(w):
-            at = x_at(widths, u) + r * (B + 2 * w) * Z
-            lanes = slice(at, at + (B + 2 * w) * Z)
-            top[:, lanes] = ring_row(parts, widths, u, B + r)
-            bottom[:, lanes] = ring_row(parts, widths, u, 2 * B - w + r)
+def edges_kernel(c_before, c_own, c_after, before, own, after, top, bottom):
+    first = 0
+    for widths, *y_parts in ((EARLY, c_before, c_own, c_after), (LATE, before, own, after)):
+        parts = (None, None, *y_parts)
+        for u, w in enumerate(widths):
+            for r in range(w):
+                at = first + x_at(widths, u) + r * (B + 2 * w) * Z
+                lanes = slice(at, at + (B + 2 * w) * Z)
+                top[:, lanes] = ring_row(parts, widths, u, B + r)
+                bottom[:, lanes] = ring_row(parts, widths, u, 2 * B - w + r)
+        first += x_at(widths, len(widths))
 
 
 def prepare_kernel(
@@ -287,13 +290,14 @@
 
 
 def backward_kernel(
-    above, below, before, own, after, c_above, c_below, c_before, c_own, c_after,
+    above, below, before, own, after, c_before, c_own, c_after,
     t1, t2, t3, slope_0, slope_1, slope_2, carried,
     frame, hidden_01, grad_3, grad_merge,
     spread_0, spread_1, spread_2, spread_3, kept, sent, sums,
 ):
-    late = (above, below, before, own, after)
-    early = (c_above, c_below, c_before, c_own, c_after)
+    cut = x_at(EARLY, 3)
+    early = (above.at[:, :cut], below.at[:, :cut], c_before, c_own, c_after)
+    late = (above.at[:, cut:], below.at[:, cut:], before, own, after)
     spreads = (spread_0, spread_1, spread_2, spread_3)
     turned_refs = (None, t1, t2, t3)
     for f in range(3 * B):
@@ -396,12 +400,6 @@
     return lax.ppermute(high, axis, up), lax.ppermute(low, axis, [(j, i) for i, j in up])
 
 
-def edges(widths, before, own, after):
-    edge = shape((16, x_at(widths, len(widths))), BF16)
-    kernel = functools.partial(edges_kernel, widths)
-    return call(kernel, [edge, edge], [before, own, after], name="edges")
-
-
 def body(samples, cotangent, kernel_0, kernel_1, kernel_2, kernel_3, layer_bias, merging_weight, merging_bias):
     kernels = (kernel_0, kernel_1, kernel_2, kernel_3)
     cells = B * B * Z * lax.axis_size("gx") * lax.axis_size("row") * lax.axis_size("rep")
@@ -434,7 +432,6 @@
     above, below = neighbours(band, band, "gx")
     c_before, c_after = neighbours(c_left, c_right, "row")
     above, below, c_before, c_after = lax.optimization_barrier((above, below, c_before, c_after))
-    c_top, c_bottom = edges(EARLY, c_before, c_own, c_after)
     side = shape((B, 16, y_at(LATE, 2)), BF16)
     (
         frame, hidden_01, hidden_2, hidden_3,
@@ -459,10 +456,13 @@
         name="forward",
     )
     before, after = neighbours(left, right, "row")
-    c_top, c_bottom, _ = lax.optimization_barrier((c_top, c_bottom, left))
-    c_above, c_below = neighbours(c_top, c_bottom, "gx")
-    before, after, c_above, c_below = lax.optimization_barrier((before, after, c_above, c_below))
-    top, bottom = edges(LATE, before, own, after)
+    edge = shape((16, x_at(EARLY, 3) + x_at(LATE, 2)), BF16)
+    top, bottom = call(
+        edges_kernel,
+        [edge, edge],
+        [c_before, c_own, c_after, before, own, after],
+        name="edges",
+    )
     above, below = neighbours(top, bottom, "gx")
     output, grad_3, grad_merge = call(
         merge_kernel,
@@ -475,7 +475,7 @@
     *spreads, kept, sent = call(
         backward_kernel,
         spreads + [shape((HALF, Z), F32), shape((HALF, Z), BF16)],
-        [above, below, before, own, after, c_above, c_below, c_before, c_own, c_after, t1, t2, t3, slope_0, slope_1, slope_2, carried]
+        [above, below, before, own, after, c_before, c_own, c_after, t1, t2, t3, slope_0, slope_1, slope_2, carried]
         + [frame, hidden_01, grad_3, grad_merge],
         [pltpu.VMEM((2 * HALF, Z), F32)],
         name="backward",

time: 149 us -> 149 us (level)
  starting transfers between devices: 38.4 us -> 32.8 us
  waiting for transfers between devices: 45.3 us -> 50.8 us
    ppermute x6 -> x5, waiting for transfers between devices: 29.5 us -> 34.9 us  [neighbours(): lax.ppermute(high, axis, up)]
    ppermute x6 -> x5, starting transfers between devices: 24 us -> 20.6 us  [neighbours(): lax.ppermute(high, axis, up)]
    ppermute x6 -> x5, starting transfers between devices: 7.75 us -> 6.46 us  [neighbours(): lax.ppermute(low, axis, [(j, i) for i, j in up])]
    pallas_call x12 -> x11, Pallas kernels: 13.7 us -> 13.7 us  [call(): pl.pallas_call(kernel, out_shape=list(outs), in_specs=[pl.BlockSpec(memor...]
    ppermute x6 -> x5, waiting for transfers between devices: 14.7 us -> 14.7 us  [neighbours(): lax.ppermute(low, axis, [(j, i) for i, j in up])]
  transfers between devices with their start and end apart: 14 -> 12, of which waited for: 9 -> 9; matrix products, arithmetic and copies ran while one was open for 0% -> 0% of each run, Pallas kernels for 3% -> 3%
where the time goes in v8:
time: 149 us; the launch traced here: 148 us
  waiting for transfers between devices  50.8 us (34%)
  blocking collectives  49.4 us (33%)
  starting transfers between devices  32.8 us (22%)
  Pallas kernels  13.7 us (9%)
    ppermute x5, waiting for transfers between devices, neighbours(): lax.ppermute(high, axis, up)  34.9 us
    all_to_all x1, blocking collectives, body(): lax.all_to_all(paired.reshape(GROUP, ROWS, Z), axes, 0, 0, tiled=True)  29.3 us
    ppermute x5, starting transfers between devices, neighbours(): lax.ppermute(high, axis, up)  20.6 us
    all_to_all x1, blocking collectives, body(): lax.all_to_all(added.reshape(GROUP, ROWS, Z), axes, 0, 0, tiled=True)  20.1 us
    ppermute x5, waiting for transfers between devices, neighbours(): lax.ppermute(low, axis, [(j, i) for i, j in up])  14.7 us
    pallas_call x11, Pallas kernels, call(): pl.pallas_call(kernel, out_shape=list(outs), in_specs=[pl.BlockSpec(memor...  13.7 us
    ppermute x5, starting transfers between devices, neighbours(): lax.ppermute(low, axis, [(j, i) for i, j in up])  6.46 us
    ppermute x1, starting transfers between devices, body(): others = lax.ppermute(totals, 'rep', swap)  3.47 us
  transfers between devices with their start and end apart: 12, of which 9 were waited for; matrix products, arithmetic and copies ran while one was open for 0% of the time, Pallas kernels for 3%

profile of v8, /device:TPU:1, one launch (start us, length us, event | category | flops | bytes accessed | tf_op | source)
XLA Modules:
  0.0 148.5 jit_solution(12025640129747540737)
XLA Ops:
  1.9 1.3 collective-permute-start.1
  3.2 6.3 %collective-permute-start = (bf16[4,64,512]{2,1,0:T(8,128)(2,1)S(1)}, bf16[4,64,512]{2,1,0:T(8,128)(2,1)S(1)}, u32[]{:S(2)}, u32[]{:S(2)}) collective-permute-start(bf16[4,64,512]{2,1,0:T(8,128)(2,1)S(1)} %pack.1.own), channel_id=1, source_target_pairs={{0,2},{2,4},{4,6},{6,8},{8,10},{10,12},{12,14},{14,16},{16,18},{18... | collective-permute-start | bytes 786440 | tf_op jit(solution)/shard_map/ppermute | solution.py:400
  9.5 1.8 %collective-permute-done.1.after = bf16[4,64,512]{2,1,0:T(8,128)(2,1)S(1)} collective-permute-done((bf16[4,64,512]{2,1,0:T(8,128)(2,1)S(1)}, bf16[4,64,512]{2,1,0:T(8,128)(2,1)S(1)}, u32[]{:S(2)}, u32[]{:S(2)}) %collective-permute-start.1) | collective-permute-done | bytes 262176 | tf_op jit(solution)/shard_map/ppermute | solution.py:400
  11.3 8.8 %collective-permute-done.before = bf16[4,64,512]{2,1,0:T(8,128)(2,1)S(1)} collective-permute-done((bf16[4,64,512]{2,1,0:T(8,128)(2,1)S(1)}, bf16[4,64,512]{2,1,0:T(8,128)(2,1)S(1)}, u32[]{:S(2)}, u32[]{:S(2)}) %collective-permute-start) | collective-permute-done | bytes 262176 | tf_op jit(solution)/shard_map/ppermute | solution.py:400
  20.1 1.3 collective-permute-start.3
  21.4 4.0 %collective-permute-start.2 = (bf16[4,64,1536]{2,1,0:T(8,128)(2,1)S(1)}, bf16[4,64,1536]{2,1,0:T(8,128)(2,1)S(1)}, u32[]{:S(2)}, u32[]{:S(2)}) collective-permute-start(bf16[4,64,1536]{2,1,0:T(8,128)(2,1)S(1)} %band.1), channel_id=1, source_target_pairs={{0,32},{32,64},{64,96},{96,128},{128,160},{160,192},{192,224},{1,3... | collective-permute-start | bytes 2359304 | tf_op jit(solution)/shard_map/ppermute | solution.py:400
  26.1 5.6 %collective-permute-start.4 = (bf16[4,16,768]{2,1,0:T(8,128)(2,1)S(1)}, bf16[4,16,768]{2,1,0:T(8,128)(2,1)S(1)}, u32[]{:S(2)}, u32[]{:S(2)}) collective-permute-start(bf16[4,16,768]{2,1,0:T(8,128)(2,1)S(1)} %get-tuple-element.58), channel_id=1, source_target_pairs={{0,2},{2,4},{4,6},{6,8},{8,10},{10,12},{12,14},{14,16},{16,18},{18... | collective-permute-start | bytes 294920 | tf_op jit(solution)/shard_map/ppermute | solution.py:400
  31.7 1.3 collective-permute-start.5
  33.0 18.1 %collective-permute-done.4.c_before = bf16[4,16,768]{2,1,0:T(8,128)(2,1)S(1)} collective-permute-done((bf16[4,16,768]{2,1,0:T(8,128)(2,1)S(1)}, bf16[4,16,768]{2,1,0:T(8,128)(2,1)S(1)}, u32[]{:S(2)}, u32[]{:S(2)}) %collective-permute-start.4) | collective-permute-done | bytes 98336 | tf_op jit(solution)/shard_map/ppermute | solution.py:400
  51.2 2.3 %collective-permute-done.5.c_after = bf16[4,16,768]{2,1,0:T(8,128)(2,1)S(1)} collective-permute-done((bf16[4,16,768]{2,1,0:T(8,128)(2,1)S(1)}, bf16[4,16,768]{2,1,0:T(8,128)(2,1)S(1)}, u32[]{:S(2)}, u32[]{:S(2)}) %collective-permute-start.5) | collective-permute-done | bytes 98336 | tf_op jit(solution)/shard_map/ppermute | solution.py:400
  53.5 3.8 %forward.1 = (bf16[8,64,1024]{2,1,0:T(8,128)(2,1)S(1)}, bf16[8,32,1024]{2,1,0:T(8,128)(2,1)S(1)}, bf16[8,16,1024]{2,1,0:T(8,128)(2,1)S(1)}, bf16[4,16,512]{2,1,0...) custom-call(bf16[4,64,1536]{2,1,0:T(8,128)(2,1)S(1)} %collective-per, ...), custom_call_target="tpu_custom_call" | custom-call | flops 1000000 | bytes 6628352 | tf_op jit(solution)/shard_map/forward/pallas_call | solution.py:32
  57.3 3.3 %collective-permute-start.6 = (bf16[4,16,896]{2,1,0:T(8,128)(2,1)S(1)}, bf16[4,16,896]{2,1,0:T(8,128)(2,1)S(1)}, u32[]{:S(2)}, u32[]{:S(2)}) collective-permute-start(bf16[4,16,896]{2,1,0:T(8,128)(2,1)S(1)} %get-tuple-element.79), channel_id=1, source_target_pairs={{0,2},{2,4},{4,6},{6,8},{8,10},{10,12},{12,14},{14,16},{16,18},{18... | collective-permute-start | bytes 344072 | tf_op jit(solution)/shard_map/ppermute | solution.py:400
  60.6 1.3 collective-permute-start.7
  62.6 6.7 %collective-permute-done.7.after = bf16[4,16,896]{2,1,0:T(8,128)(2,1)S(1)} collective-permute-done((bf16[4,16,896]{2,1,0:T(8,128)(2,1)S(1)}, bf16[4,16,896]{2,1,0:T(8,128)(2,1)S(1)}, u32[]{:S(2)}, u32[]{:S(2)}) %collective-permute-start.7) | collective-permute-done | bytes 114720 | tf_op jit(solution)/shard_map/ppermute | solution.py:400
  69.3 1.3 collective-permute-start.8
  72.0 1.7 %merge.4 = (f32[1024,128]{1,0:T(8,128)}, f32[432,128]{1,0:T(8,128)S(1)}, f32[144,128]{1,0:T(8,128)S(1)}) custom-call(bf16[8,64,1024]{2,1,0:T(8,128)(2,1)S(1)} %get-tuple-element.68.frame, bf16[8,32,1024]{2,1,0:T(8,128)(2,1)S(1)} %get-tuple-element.69.hidden_01, bf16[8,16,1024]{2,1,0:T(8,128)(2,1)S(1)} %get-tuple-element.70.hidden_2, ...), custom_call_target="tpu_custom_call" | custom-call | flops 100000000 | bytes 3227648 | tf_op jit(solution)/shard_map/merge/pallas_call | solution.py:32
  73.6 7.3 %collective-permute-done.8.above = bf16[16,16640]{1,0:T(8,128)(2,1)S(1)} collective-permute-done((bf16[16,16640]{1,0:T(8,128)(2,1)S(1)}, bf16[16,16640]{1,0:T(8,128)(2,1)S(1)}, u32[]{:S(2)}, u32[]{:S(2)}) %collective-permute-start.8) | collective-permute-done | bytes 532512 | tf_op jit(solution)/shard_map/ppermute | solution.py:400
  80.9 3.9 %collective-permute-done.9.below = bf16[16,16640]{1,0:T(8,128)(2,1)S(1)} collective-permute-done((bf16[16,16640]{1,0:T(8,128)(2,1)S(1)}, bf16[16,16640]{1,0:T(8,128)(2,1)S(1)}, u32[]{:S(2)}, u32[]{:S(2)}) %collective-permute-start.9) | collective-permute-done | bytes 532512 | tf_op jit(solution)/shard_map/ppermute | solution.py:400
  84.8 3.9 %backward.1 = (bf16[12,48,1536]{2,1,0:T(8,128)(2,1)S(1)}, bf16[12,48,1536]{2,1,0:T(8,128)(2,1)S(1)}, bf16[12,48,1536]{2,1,0:T(8,128)(2,1)S(1)}, bf16[12,48,1536]...) custom-call(bf16[16,16640]{1,0:T(8,128)(2,1)S(1)} %collective-permute-done.8.above, ...), custom_call_target="tpu_custom_call" | custom-call | flops 1000000 | bytes 13274112 | tf_op jit(solution)/shard_map/backward/pallas_call | solution.py:32
  88.7 2.4 %collective-permute-start.10 = (bf16[1024,128]{1,0:T(8,128)(2,1)S(1)}, bf16[1024,128]{1,0:T(8,128)(2,1)S(1)}, u32[]{:S(2)}, u32[]{:S(2)}) collective-permute-start(bf16[1024,128]{1,0:T(8,128)(2,1)S(1)} %get-tuple-element.99), channel_id=1, source_target_pairs={{0,1},{1,0},{2,3},{3,2},{4,5},{5,4},{6,7},{7,6},{8,9},{9,8},{10,11... | collective-permute-start | bytes 786440 | tf_op jit(solution)/shard_map/ppermute | solution.py:486
  92.3 29.3 %all_to_all.10 = bf16[128,8,128]{2,1,0:T(8,128)(2,1)S(1)} all-to-all(bf16[128,8,128]{2,1,0:T(8,128)(2,1)S(1)} %bitcast.38), channel_id=1, replica_groups=mesh['gx'=8,'row'=16,'rep'=2] {'gx','row'}, dimensions={0} | all-to-all | bytes 524288 | tf_op jit(solution)/shard_map/all_to_all | solution.py:487
  121.7 20.1 %all_to_all.11 = bf16[128,8,128]{2,1,0:T(8,128)(2,1)S(1)} all-to-all(bf16[128,8,128]{2,1,0:T(8,128)(2,1)S(1)} %bitcast.37), channel_id=1, replica_groups=mesh['gx'=8,'row'=16,'rep'=2] {'gx','row'}, dimensions={0} | all-to-all | bytes 524288 | tf_op jit(solution)/shard_map/all_to_all | solution.py:489
  141.8 3.5 %collective-permute-start.11 = (bf16[1024,128]{1,0:T(8,128)(2,1)S(1)}, bf16[1024,128]{1,0:T(8,128)(2,1)S(1)}, u32[]{:S(2)}, u32[]{:S(2)}) collective-permute-start(bf16[1024,128]{1,0:T(8,128)(2,1)S(1)} %bitcast.34), channel_id=1, source_target_pairs={{0,1},{1,0},{2,3},{3,2},{4,5},{5,4},{6,7},{7,6},{8,9},{9,8},{10,11... | collective-permute-start | bytes 786440 | tf_op jit(solution)/shard_map/ppermute | solution.py:491
  145.3 2.2 %input_gradient.1 = f32[1024,128]{1,0:T(8,128)} custom-call(bf16[12,48,1536]{2,1,0:T(8,128)(2,1)S(1)} %get-tuple-element.92.spread_0, bf16[12,48,1536]{2,1,0:T(8,128)(2,1)S(1)} %get-tuple-element.93.spread_1, bf16[12,48,1536]{2,1,0:T(8,128)(2,1)S(1)} %get-tuple-element.94.spread_2, bf16[12,48,1536]{2,1,0:T(8,128)(2,1)S(1)} %get-tuple-element.95.spread_3, ...), custom_call_target="tpu_custom_call" | custom-call | flops 300000000 | bytes 8430592 | tf_op jit(solution)/shard_map/input_gradient/pallas_call | solution.py:32
  (31 shorter events, 6.2 us)
Async XLA Ops:
  0.6 24.8 %copy-start = (bf16[1,64,4,4,128]{4,3,2,1,0:T(4,128)(2,1)S(1)}, bf16[1,64,4,4,128]{4,3,2,1,0:T(4,128)(2,1)}, u32[]{:S(2)}) copy-start(bf16[1,64,4,4,128]{4,3,2,1,0:T(4,128)(2,1)} %param.10) | copy-start | bytes 786436
  0.7 1.0 copy-start.1
  1.6 23.8 %copy-start.2 = (bf16[16,27,64]{2,0,1:T(8,128)(2,1)S(1)}, bf16[16,27,64]{2,0,1:T(8,128)(2,1)}, u32[]{:S(2)}) copy-start(bf16[16,27,64]{2,0,1:T(8,128)(2,1)} %param.11) | copy-start | bytes 165892
  1.7 23.8 %copy-start.3 = (bf16[16,27,80]{2,0,1:T(8,128)(2,1)S(1)}, bf16[16,27,80]{2,0,1:T(8,128)(2,1)}, u32[]{:S(2)}) copy-start(bf16[16,27,80]{2,0,1:T(8,128)(2,1)} %param.12) | copy-start | bytes 207364
  1.7 23.8 %copy-start.4 = (bf16[16,27,96]{2,0,1:T(8,128)(2,1)S(1)}, bf16[16,27,96]{2,0,1:T(8,128)(2,1)}, u32[]{:S(2)}) copy-start(bf16[16,27,96]{2,0,1:T(8,128)(2,1)} %param.13) | copy-start | bytes 248836
  1.7 23.8 %copy-start.5 = (bf16[16,27,112]{2,0,1:T(8,128)(2,1)S(1)}, bf16[16,27,112]{2,0,1:T(8,128)(2,1)}, u32[]{:S(2)}) copy-start(bf16[16,27,112]{2,0,1:T(8,128)(2,1)} %param.14) | copy-start | bytes 290308
  1.7 23.9 %copy-start.6 = (bf16[64,128]{1,0:T(8,128)(2,1)S(1)}, bf16[64,128]{1,0:T(8,128)(2,1)}, u32[]{:S(2)}) copy-start(bf16[64,128]{1,0:T(8,128)(2,1)} %merge.5) | copy-start | bytes 49156
  1.7 23.9 %copy-start.7 = (bf16[4,16]{1,0:T(4,128)(2,1)S(1)}, bf16[4,16]{1,0:T(4,128)(2,1)}, u32[]{:S(2)}) copy-start(bf16[4,16]{1,0:T(4,128)(2,1)} %layer_bias.1) | copy-start | bytes 388
  1.7 23.9 %copy-start.8 = (bf16[64]{0:T(256)(128)(2,1)S(1)}, bf16[64]{0:T(256)(128)(2,1)}, u32[]{:S(2)}) copy-start(bf16[64]{0:T(256)(128)(2,1)} %param.17) | copy-start | bytes 388
  1.9 9.4 %collective-permute-start.1 = (bf16[4,64,512]{2,1,0:T(8,128)(2,1)S(1)}, bf16[4,64,512]{2,1,0:T(8,128)(2,1)S(1)}, u32[]{:S(2)}, u32[]{:S(2)}) collective-permute-start(bf16[4,64,512]{2,1,0:T(8,128)(2,1)S(1)} %pack.1.own), channel_id=1, source_target_pairs={{2,0},{4,2},{6,4},{8,6},{10,8},{12,10},{14,12},{16,14},{18,16},{20... | collective-permute-start | bytes 786440 | tf_op jit(solution)/shard_map/ppermute | solution.py:400
  3.2 16.9 %collective-permute-start = (bf16[4,64,512]{2,1,0:T(8,128)(2,1)S(1)}, bf16[4,64,512]{2,1,0:T(8,128)(2,1)S(1)}, u32[]{:S(2)}, u32[]{:S(2)}) collective-permute-start(bf16[4,64,512]{2,1,0:T(8,128)(2,1)S(1)} %pack.1.own), channel_id=1, source_target_pairs={{0,2},{2,4},{4,6},{6,8},{8,10},{10,12},{12,14},{14,16},{16,18},{18... | collective-permute-start | bytes 786440 | tf_op jit(solution)/shard_map/ppermute | solution.py:400
  20.1 33.4 %collective-permute-start.3 = (bf16[4,64,1536]{2,1,0:T(8,128)(2,1)S(1)}, bf16[4,64,1536]{2,1,0:T(8,128)(2,1)S(1)}, u32[]{:S(2)}, u32[]{:S(2)}) collective-permute-start(bf16[4,64,1536]{2,1,0:T(8,128)(2,1)S(1)} %band.1), channel_id=1, source_target_pairs={{32,0},{64,32},{96,64},{128,96},{160,128},{192,160},{224,192},{33,... | collective-permute-start | bytes 2359304 | tf_op jit(solution)/shard_map/ppermute | solution.py:400
  21.4 32.1 %collective-permute-start.2 = (bf16[4,64,1536]{2,1,0:T(8,128)(2,1)S(1)}, bf16[4,64,1536]{2,1,0:T(8,128)(2,1)S(1)}, u32[]{:S(2)}, u32[]{:S(2)}) collective-permute-start(bf16[4,64,1536]{2,1,0:T(8,128)(2,1)S(1)} %band.1), channel_id=1, source_target_pairs={{0,32},{32,64},{64,96},{96,128},{128,160},{160,192},{192,224},{1,3... | collective-permute-start | bytes 2359304 | tf_op jit(solution)/shard_map/ppermute | solution.py:400
  26.1 25.1 %collective-permute-start.4 = (bf16[4,16,768]{2,1,0:T(8,128)(2,1)S(1)}, bf16[4,16,768]{2,1,0:T(8,128)(2,1)S(1)}, u32[]{:S(2)}, u32[]{:S(2)}) collective-permute-start(bf16[4,16,768]{2,1,0:T(8,128)(2,1)S(1)} %get-tuple-element.58), channel_id=1, source_target_pairs={{0,2},{2,4},{4,6},{6,8},{8,10},{10,12},{12,14},{14,16},{16,18},{18... | collective-permute-start | bytes 294920 | tf_op jit(solution)/shard_map/ppermute | solution.py:400
  31.7 21.8 %collective-permute-start.5 = (bf16[4,16,768]{2,1,0:T(8,128)(2,1)S(1)}, bf16[4,16,768]{2,1,0:T(8,128)(2,1)S(1)}, u32[]{:S(2)}, u32[]{:S(2)}) collective-permute-start(bf16[4,16,768]{2,1,0:T(8,128)(2,1)S(1)} %get-tuple-element.59), channel_id=1, source_target_pairs={{2,0},{4,2},{6,4},{8,6},{10,8},{12,10},{14,12},{16,14},{18,16},{20... | collective-permute-start | bytes 294920 | tf_op jit(solution)/shard_map/ppermute | solution.py:400
  57.3 5.3 %collective-permute-start.6 = (bf16[4,16,896]{2,1,0:T(8,128)(2,1)S(1)}, bf16[4,16,896]{2,1,0:T(8,128)(2,1)S(1)}, u32[]{:S(2)}, u32[]{:S(2)}) collective-permute-start(bf16[4,16,896]{2,1,0:T(8,128)(2,1)S(1)} %get-tuple-element.79), channel_id=1, source_target_pairs={{0,2},{2,4},{4,6},{6,8},{8,10},{10,12},{12,14},{14,16},{16,18},{18... | collective-permute-start | bytes 344072 | tf_op jit(solution)/shard_map/ppermute | solution.py:400
  60.6 8.6 %collective-permute-start.7 = (bf16[4,16,896]{2,1,0:T(8,128)(2,1)S(1)}, bf16[4,16,896]{2,1,0:T(8,128)(2,1)S(1)}, u32[]{:S(2)}, u32[]{:S(2)}) collective-permute-start(bf16[4,16,896]{2,1,0:T(8,128)(2,1)S(1)} %get-tuple-element.81), channel_id=1, source_target_pairs={{2,0},{4,2},{6,4},{8,6},{10,8},{12,10},{14,12},{16,14},{18,16},{20... | collective-permute-start | bytes 344072 | tf_op jit(solution)/shard_map/ppermute | solution.py:400
  69.3 11.6 %collective-permute-start.8 = (bf16[16,16640]{1,0:T(8,128)(2,1)S(1)}, bf16[16,16640]{1,0:T(8,128)(2,1)S(1)}, u32[]{:S(2)}, u32[]{:S(2)}) collective-permute-start(bf16[16,16640]{1,0:T(8,128)(2,1)S(1)} %get-tuple-element.82), channel_id=1, source_target_pairs={{0,32},{32,64},{64,96},{96,128},{128,160},{160,192},{192,224},{1,3... | collective-permute-start | bytes 1597448 | tf_op jit(solution)/shard_map/ppermute | solution.py:400
  70.7 14.1 %collective-permute-start.9 = (bf16[16,16640]{1,0:T(8,128)(2,1)S(1)}, bf16[16,16640]{1,0:T(8,128)(2,1)S(1)}, u32[]{:S(2)}, u32[]{:S(2)}) collective-permute-start(bf16[16,16640]{1,0:T(8,128)(2,1)S(1)} %get-tuple-element.83), channel_id=1, source_target_pairs={{32,0},{64,32},{96,64},{128,96},{160,128},{192,160},{224,192},{33,... | collective-permute-start | bytes 1597448 | tf_op jit(solution)/shard_map/ppermute | solution.py:400
  88.7 3.5 %collective-permute-start.10 = (bf16[1024,128]{1,0:T(8,128)(2,1)S(1)}, bf16[1024,128]{1,0:T(8,128)(2,1)S(1)}, u32[]{:S(2)}, u32[]{:S(2)}) collective-permute-start(bf16[1024,128]{1,0:T(8,128)(2,1)S(1)} %get-tuple-element.99), channel_id=1, source_target_pairs={{0,1},{1,0},{2,3},{3,2},{4,5},{5,4},{6,7},{7,6},{8,9},{9,8},{10,11... | collective-permute-start | bytes 786440 | tf_op jit(solution)/shard_map/ppermute | solution.py:486
  141.8 5.7 %collective-permute-start.11 = (bf16[1024,128]{1,0:T(8,128)(2,1)S(1)}, bf16[1024,128]{1,0:T(8,128)(2,1)S(1)}, u32[]{:S(2)}, u32[]{:S(2)}) collective-permute-start(bf16[1024,128]{1,0:T(8,128)(2,1)S(1)} %bitcast.34), channel_id=1, source_target_pairs={{0,1},{1,0},{2,3},{3,2},{4,5},{5,4},{6,7},{7,6},{8,9},{9,8},{10,11... | collective-permute-start | bytes 786440 | tf_op jit(solution)/shard_map/ppermute | solution.py:491

commit v9 on v6

--- a/solution.py
+++ b/solution.py
@@ -49,16 +49,18 @@
 
 
 def from_left(v, keep):
-    return jnp.where(keep, pltpu.roll(v, 1, 1), 0.0)
+    parts = [pltpu.roll(v[:, k * Z : (k + 1) * Z], 1, 1) for k in range(v.shape[1] // Z)]
+    return jnp.where(keep, jnp.concatenate(parts, axis=1), jnp.zeros_like(v))
 
 
 def from_right(v, keep):
-    return jnp.where(keep, pltpu.roll(v, v.shape[1] - 1, 1), 0.0)
+    parts = [pltpu.roll(v[:, k * Z : (k + 1) * Z], Z - 1, 1) for k in range(v.shape[1] // Z)]
+    return jnp.where(keep, jnp.concatenate(parts, axis=1), jnp.zeros_like(v))
 
 
 def spread(v):
     not_first, not_last = lane_moves(*v.shape)
-    return jnp.concatenate([from_right(v, not_last), v, from_left(v, not_first)], axis=0).astype(BF16)
+    return jnp.concatenate([from_right(v, not_last), v, from_left(v, not_first)], axis=0)
 
 
 def inside(x, y, blocks):
@@ -97,26 +99,29 @@
 
 
 def kernel_gradient(own, sources):
-    gap = jnp.zeros((48, Z), BF16)
-
-    def shifted(rows):
-        return [jnp.concatenate([gap] * b + [rows] + [gap] * (2 - b), axis=1) for b in range(3)]
-
     lhs = jnp.concatenate(
-        [
-            jnp.concatenate([part for layer in own for part in shifted(layer[i])], axis=0)
-            for i in range(B)
-        ],
-        axis=1,
+        [jnp.concatenate([layer[i] for layer in own], axis=0) for i in range(B)], axis=1
     )
     for a in range(3):
-        rhs = jnp.concatenate(
-            [jnp.concatenate([s[H + i + a - 1, :, RING] for s in sources], axis=0) for i in range(B)],
-            axis=1,
+        taps = [
+            jnp.concatenate(
+                [
+                    jnp.concatenate(
+                        [s[H + i + a - 1, :, pl.ds((H + b - 1) * Z, B * Z)] for s in sources], axis=0
+                    )
+                    for i in range(B)
+                ],
+                axis=1,
+            )
+            for b in range(3)
+        ]
+        q = taps[0].shape[0]
+        got = lax.dot_general(
+            lhs, jnp.concatenate(taps, axis=0), (((1,), (1,)), ((), ())), preferred_element_type=F32
         )
-        got = lax.dot_general(lhs, rhs, (((1,), (1,)), ((), ())), preferred_element_type=F32)
-        gap_lanes = jnp.zeros((got.shape[0], Z - got.shape[1]), F32)
-        yield a, jnp.concatenate([got, gap_lanes], axis=1)
+        gap = jnp.zeros((got.shape[0], Z - q), F32)
+        for b in range(3):
+            yield 3 * a + b, jnp.concatenate([got[:, q * b : q * (b + 1)], gap], axis=1)
 
 
 def own_cells(spread_ref):
@@ -237,7 +242,7 @@
         value, slope = activate(pre)
         hidden_3[i] = value.astype(BF16)
         grad = (carried[i, 48:64] * slope).astype(BF16)
-        own_3[i] = spread(grad.astype(F32))
+        own_3[i] = spread(grad)
         rest = [slope_2[i]] + [carried[i, 16 * k : 16 * (k + 1)] for k in (2, 1, 0)]
         ready = [grad] + [value.astype(BF16) for value in rest]
         own[i] = jnp.concatenate(ready, axis=0)
@@ -267,8 +272,8 @@
     grad_merge[64:128] = wide_sum([merge_grad[i] for i in range(B)])
     own = [own_3[i] for i in range(B)]
     grad_merge[128:144] = cell_sum(own)
-    for a, got in kernel_gradient([own], [frame, hidden_01, hidden_2]):
-        grad_3[144 * a : 144 * (a + 1)] = got
+    for t, got in kernel_gradient([own], [frame, hidden_01, hidden_2]):
+        grad_3[48 * t : 48 * (t + 1)] = got
 
 
 def backward_kernel(
@@ -280,7 +285,7 @@
     spreads = (spread_0, spread_1, spread_2, spread_3)
     turned_refs = (None, t1, t2, t3)
     for f in range(3 * B):
-        spread_3[f] = spread(ring_row(parts, 0, f).astype(F32))
+        spread_3[f] = spread(ring_row(parts, 0, f))
     for k in (2, 1, 0):
         reach = k + 1
         lanes = slice((B - reach) * Z, (2 * B + reach) * Z)
@@ -304,12 +309,12 @@
             else:
                 slope = (slope_0, slope_1)[k][i + reach]
             grad = (got * slope).astype(BF16)
-            spreads[k][f, :, lanes] = spread(grad.astype(F32))
+            spreads[k][f, :, lanes] = spread(grad)
     owns = [own_cells(ref) for ref in spreads[:3]]
-    for a, got in kernel_gradient(owns, [frame, hidden_01]):
+    for t, got in kernel_gradient(owns, [frame, hidden_01]):
         for k in range(3):
-            at = 432 * k + 144 * a
-            sums[at : at + 144] = got[144 * k : 144 * (k + 1)]
+            at = 432 * k + 48 * t
+            sums[at : at + 48] = got[48 * k : 48 * (k + 1)]
     sums[1296:1728] = grad_3[...]
     sums[1728:1856] = grad_merge[0:128]
     for k in range(3):

time: 146 us -> 145 us (level)
  no operation moved by 1% of the time
where the time goes in v9:
time: 145 us; the launch traced here: 144 us
  blocking collectives  52.5 us (36%)
  waiting for transfers between devices  43.1 us (30%)
  starting transfers between devices  33.1 us (23%)
  Pallas kernels  13.7 us (9%)
    all_to_all x1, blocking collectives, body(): lax.all_to_all(paired.reshape(GROUP, ROWS, Z), axes, 0, 0, tiled=True)  32.4 us
    ppermute x4, waiting for transfers between devices, neighbours(): lax.ppermute(low, axis, [(j, i) for i, j in up])  25.5 us
    ppermute x4, starting transfers between devices, neighbours(): lax.ppermute(high, axis, up)  20.1 us
    all_to_all x1, blocking collectives, body(): lax.all_to_all(added.reshape(GROUP, ROWS, Z), axes, 0, 0, tiled=True)  20.1 us
    ppermute x4, waiting for transfers between devices, neighbours(): lax.ppermute(high, axis, up)  16.4 us
    pallas_call x11, Pallas kernels, call(): pl.pallas_call(kernel, out_shape=list(outs), in_specs=[pl.BlockSpec(memor...  13.7 us
    ppermute x4, starting transfers between devices, neighbours(): lax.ppermute(low, axis, [(j, i) for i, j in up])  5.17 us
    ppermute x1, starting transfers between devices, body(): lax.ppermute(sent, 'rep', swap)  4.4 us
  transfers between devices with their start and end apart: 10, of which 9 were waited for; matrix products, arithmetic and copies ran while one was open for 0% of the time, Pallas kernels for 3%

profile of v9, /device:TPU:1, one launch (start us, length us, event | category | flops | bytes accessed | tf_op | source)
XLA Modules:
  0.0 144.2 jit_solution(16891620644339080555)
XLA Ops:
  1.9 1.3 collective-permute-start.1
  3.2 6.3 %collective-permute-start = (bf16[4,64,512]{2,1,0:T(8,128)(2,1)S(1)}, bf16[4,64,512]{2,1,0:T(8,128)(2,1)S(1)}, u32[]{:S(2)}, u32[]{:S(2)}) collective-permute-start(bf16[4,64,512]{2,1,0:T(8,128)(2,1)S(1)} %pack.1.own), channel_id=1, source_target_pairs={{0,2},{2,4},{4,6},{6,8},{8,10},{10,12},{12,14},{14,16},{16,18},{18... | collective-permute-start | bytes 786440 | tf_op jit(solution)/shard_map/ppermute | solution.py:384
  9.5 1.8 %collective-permute-done.1.after = bf16[4,64,512]{2,1,0:T(8,128)(2,1)S(1)} collective-permute-done((bf16[4,64,512]{2,1,0:T(8,128)(2,1)S(1)}, bf16[4,64,512]{2,1,0:T(8,128)(2,1)S(1)}, u32[]{:S(2)}, u32[]{:S(2)}) %collective-permute-start.1) | collective-permute-done | bytes 262176 | tf_op jit(solution)/shard_map/ppermute | solution.py:384
  11.3 8.8 %collective-permute-done.before = bf16[4,64,512]{2,1,0:T(8,128)(2,1)S(1)} collective-permute-done((bf16[4,64,512]{2,1,0:T(8,128)(2,1)S(1)}, bf16[4,64,512]{2,1,0:T(8,128)(2,1)S(1)}, u32[]{:S(2)}, u32[]{:S(2)}) %collective-permute-start) | collective-permute-done | bytes 262176 | tf_op jit(solution)/shard_map/ppermute | solution.py:384
  20.1 1.3 collective-permute-start.3
  21.4 4.0 %collective-permute-start.2 = (bf16[4,64,1536]{2,1,0:T(8,128)(2,1)S(1)}, bf16[4,64,1536]{2,1,0:T(8,128)(2,1)S(1)}, u32[]{:S(2)}, u32[]{:S(2)}) collective-permute-start(bf16[4,64,1536]{2,1,0:T(8,128)(2,1)S(1)} %band.1), channel_id=1, source_target_pairs={{0,32},{32,64},{64,96},{96,128},{128,160},{160,192},{192,224},{1,3... | collective-permute-start | bytes 2359304 | tf_op jit(solution)/shard_map/ppermute | solution.py:384
  26.1 14.5 %collective-permute-done.3.below = bf16[4,64,1536]{2,1,0:T(8,128)(2,1)S(1)} collective-permute-done((bf16[4,64,1536]{2,1,0:T(8,128)(2,1)S(1)}, bf16[4,64,1536]{2,1,0:T(8,128)(2,1)S(1)}, u32[]{:S(2)}, u32[]{:S(2)}) %collective-permute-start.3) | collective-permute-done | bytes 786464 | tf_op jit(solution)/shard_map/ppermute | solution.py:384
  41.5 3.8 %forward.1 = (bf16[8,64,1024]{2,1,0:T(8,128)(2,1)S(1)}, bf16[8,32,1024]{2,1,0:T(8,128)(2,1)S(1)}, bf16[8,16,1024]{2,1,0:T(8,128)(2,1)S(1)}, bf16[4,16,512]{2,1,0...) custom-call(bf16[4,64,1536]{2,1,0:T(8,128)(2,1)S(1)} %collective-per, ...), custom_call_target="tpu_custom_call" | custom-call | flops 1000000 | bytes 7021568 | tf_op jit(solution)/shard_map/forward/pallas_call | solution.py:34
  45.3 5.6 %collective-permute-start.4 = (bf16[4,16,1664]{2,1,0:T(8,128)(2,1)S(1)}, bf16[4,16,1664]{2,1,0:T(8,128)(2,1)S(1)}, u32[]{:S(2)}, u32[]{:S(2)}) collective-permute-start(bf16[4,16,1664]{2,1,0:T(8,128)(2,1)S(1)} %get-tuple-element.65), channel_id=1, source_target_pairs={{0,2},{2,4},{4,6},{6,8},{8,10},{10,12},{12,14},{14,16},{16,18},{18... | collective-permute-start | bytes 638984 | tf_op jit(solution)/shard_map/ppermute | solution.py:384
  50.9 1.3 collective-permute-start.5
  52.2 1.5 %collective-permute-done.4.before = bf16[4,16,1664]{2,1,0:T(8,128)(2,1)S(1)} collective-permute-done((bf16[4,16,1664]{2,1,0:T(8,128)(2,1)S(1)}, bf16[4,16,1664]{2,1,0:T(8,128)(2,1)S(1)}, u32[]{:S(2)}, u32[]{:S(2)}) %collective-permute-start.4) | collective-permute-done | bytes 213024 | tf_op jit(solution)/shard_map/ppermute | solution.py:384
  53.7 5.3 %collective-permute-done.5.after = bf16[4,16,1664]{2,1,0:T(8,128)(2,1)S(1)} collective-permute-done((bf16[4,16,1664]{2,1,0:T(8,128)(2,1)S(1)}, bf16[4,16,1664]{2,1,0:T(8,128)(2,1)S(1)}, u32[]{:S(2)}, u32[]{:S(2)}) %collective-permute-start.5) | collective-permute-done | bytes 213024 | tf_op jit(solution)/shard_map/ppermute | solution.py:384
  59.1 4.1 %collective-permute-start.6 = (bf16[16,16640]{1,0:T(8,128)(2,1)S(1)}, bf16[16,16640]{1,0:T(8,128)(2,1)S(1)}, u32[]{:S(2)}, u32[]{:S(2)}) collective-permute-start(bf16[16,16640]{1,0:T(8,128)(2,1)S(1)} %get-tuple-element.68), channel_id=1, source_target_pairs={{0,32},{32,64},{64,96},{96,128},{128,160},{160,192},{192,224},{1,3... | collective-permute-start | bytes 1597448 | tf_op jit(solution)/shard_map/ppermute | solution.py:384
  63.2 1.3 collective-permute-start.7
  64.5 1.7 %merge.4 = (f32[1024,128]{1,0:T(8,128)}, f32[432,128]{1,0:T(8,128)S(1)}, f32[144,128]{1,0:T(8,128)S(1)}) custom-call(bf16[8,64,1024]{2,1,0:T(8,128)(2,1)S(1)} %get-tuple-element.57.frame, bf16[8,32,1024]{2,1,0:T(8,128)(2,1)S(1)} %get-tuple-element.58.hidden_01, bf16[8,16,1024]{2,1,0:T(8,128)(2,1)S(1)} %get-tuple-element.59.hidden_2, ...), custom_call_target="tpu_custom_call" | custom-call | flops 100000000 | bytes 3227648 | tf_op jit(solution)/shard_map/merge/pallas_call | solution.py:34
  66.2 5.3 %collective-permute-done.6.above = bf16[16,16640]{1,0:T(8,128)(2,1)S(1)} collective-permute-done((bf16[16,16640]{1,0:T(8,128)(2,1)S(1)}, bf16[16,16640]{1,0:T(8,128)(2,1)S(1)}, u32[]{:S(2)}, u32[]{:S(2)}) %collective-permute-start.6) | collective-permute-done | bytes 532512 | tf_op jit(solution)/shard_map/ppermute | solution.py:384
  71.5 3.9 %collective-permute-done.7.below = bf16[16,16640]{1,0:T(8,128)(2,1)S(1)} collective-permute-done((bf16[16,16640]{1,0:T(8,128)(2,1)S(1)}, bf16[16,16640]{1,0:T(8,128)(2,1)S(1)}, u32[]{:S(2)}, u32[]{:S(2)}) %collective-permute-start.7) | collective-permute-done | bytes 532512 | tf_op jit(solution)/shard_map/ppermute | solution.py:384
  75.4 3.9 %backward.1 = (bf16[12,48,1536]{2,1,0:T(8,128)(2,1)S(1)}, bf16[12,48,1536]{2,1,0:T(8,128)(2,1)S(1)}, bf16[12,48,1536]{2,1,0:T(8,128)(2,1)S(1)}, bf16[12,48,1536]...) custom-call(bf16[16,16640]{1,0:T(8,128)(2,1)S(1)} %collective-permute-done.6.above, ...), custom_call_target="tpu_custom_call" | custom-call | flops 1000000 | bytes 13274112 | tf_op jit(solution)/shard_map/backward/pallas_call | solution.py:34
  79.3 4.4 %collective-permute-start.8 = (bf16[1024,128]{1,0:T(8,128)(2,1)S(1)}, bf16[1024,128]{1,0:T(8,128)(2,1)S(1)}, u32[]{:S(2)}, u32[]{:S(2)}) collective-permute-start(bf16[1024,128]{1,0:T(8,128)(2,1)S(1)} %get-tuple-element.85), channel_id=1, source_target_pairs={{0,1},{1,0},{2,3},{3,2},{4,5},{5,4},{6,7},{7,6},{8,9},{9,8},{10,11... | collective-permute-start | bytes 786440 | tf_op jit(solution)/shard_map/ppermute | solution.py:461
  83.7 1.2 collective-permute-done.8.came
  84.9 32.4 %all_to_all.10 = bf16[128,8,128]{2,1,0:T(8,128)(2,1)S(1)} all-to-all(bf16[128,8,128]{2,1,0:T(8,128)(2,1)S(1)} %bitcast.38), channel_id=1, replica_groups=mesh['gx'=8,'row'=16,'rep'=2] {'gx','row'}, dimensions={0} | all-to-all | bytes 524288 | tf_op jit(solution)/shard_map/all_to_all | solution.py:462
  117.5 20.1 %all_to_all.11 = bf16[128,8,128]{2,1,0:T(8,128)(2,1)S(1)} all-to-all(bf16[128,8,128]{2,1,0:T(8,128)(2,1)S(1)} %bitcast.37), channel_id=1, replica_groups=mesh['gx'=8,'row'=16,'rep'=2] {'gx','row'}, dimensions={0} | all-to-all | bytes 524288 | tf_op jit(solution)/shard_map/all_to_all | solution.py:464
  137.5 3.5 %collective-permute-start.9 = (bf16[1024,128]{1,0:T(8,128)(2,1)S(1)}, bf16[1024,128]{1,0:T(8,128)(2,1)S(1)}, u32[]{:S(2)}, u32[]{:S(2)}) collective-permute-start(bf16[1024,128]{1,0:T(8,128)(2,1)S(1)} %bitcast.34), channel_id=1, source_target_pairs={{0,1},{1,0},{2,3},{3,2},{4,5},{5,4},{6,7},{7,6},{8,9},{9,8},{10,11... | collective-permute-start | bytes 786440 | tf_op jit(solution)/shard_map/ppermute | solution.py:466
  141.0 2.2 %input_gradient.1 = f32[1024,128]{1,0:T(8,128)} custom-call(bf16[12,48,1536]{2,1,0:T(8,128)(2,1)S(1)} %get-tuple-element.78.spread_0, bf16[12,48,1536]{2,1,0:T(8,128)(2,1)S(1)} %get-tuple-element.79.spread_1, bf16[12,48,1536]{2,1,0:T(8,128)(2,1)S(1)} %get-tuple-element.80.spread_2, bf16[12,48,1536]{2,1,0:T(8,128)(2,1)S(1)} %get-tuple-element.81.spread_3, ...), custom_call_target="tpu_custom_call" | custom-call | flops 300000000 | bytes 8430592 | tf_op jit(solution)/shard_map/input_gradient/pallas_call | solution.py:34
  (27 shorter events, 3.9 us)
Async XLA Ops:
  0.6 24.8 %copy-start = (bf16[1,64,4,4,128]{4,3,2,1,0:T(4,128)(2,1)S(1)}, bf16[1,64,4,4,128]{4,3,2,1,0:T(4,128)(2,1)}, u32[]{:S(2)}) copy-start(bf16[1,64,4,4,128]{4,3,2,1,0:T(4,128)(2,1)} %param.10) | copy-start | bytes 786436
  0.7 1.0 copy-start.1
  1.6 23.8 %copy-start.2 = (bf16[16,27,64]{2,0,1:T(8,128)(2,1)S(1)}, bf16[16,27,64]{2,0,1:T(8,128)(2,1)}, u32[]{:S(2)}) copy-start(bf16[16,27,64]{2,0,1:T(8,128)(2,1)} %param.11) | copy-start | bytes 165892
  1.7 23.8 %copy-start.3 = (bf16[16,27,80]{2,0,1:T(8,128)(2,1)S(1)}, bf16[16,27,80]{2,0,1:T(8,128)(2,1)}, u32[]{:S(2)}) copy-start(bf16[16,27,80]{2,0,1:T(8,128)(2,1)} %param.12) | copy-start | bytes 207364
  1.7 23.8 %copy-start.4 = (bf16[16,27,96]{2,0,1:T(8,128)(2,1)S(1)}, bf16[16,27,96]{2,0,1:T(8,128)(2,1)}, u32[]{:S(2)}) copy-start(bf16[16,27,96]{2,0,1:T(8,128)(2,1)} %param.13) | copy-start | bytes 248836
  1.7 23.8 %copy-start.5 = (bf16[16,27,112]{2,0,1:T(8,128)(2,1)S(1)}, bf16[16,27,112]{2,0,1:T(8,128)(2,1)}, u32[]{:S(2)}) copy-start(bf16[16,27,112]{2,0,1:T(8,128)(2,1)} %param.14) | copy-start | bytes 290308
  1.7 23.9 %copy-start.6 = (bf16[64,128]{1,0:T(8,128)(2,1)S(1)}, bf16[64,128]{1,0:T(8,128)(2,1)}, u32[]{:S(2)}) copy-start(bf16[64,128]{1,0:T(8,128)(2,1)} %merge.5) | copy-start | bytes 49156
  1.7 23.9 %copy-start.7 = (bf16[4,16]{1,0:T(4,128)(2,1)S(1)}, bf16[4,16]{1,0:T(4,128)(2,1)}, u32[]{:S(2)}) copy-start(bf16[4,16]{1,0:T(4,128)(2,1)} %layer_bias.1) | copy-start | bytes 388
  1.7 23.9 %copy-start.8 = (bf16[64]{0:T(256)(128)(2,1)S(1)}, bf16[64]{0:T(256)(128)(2,1)}, u32[]{:S(2)}) copy-start(bf16[64]{0:T(256)(128)(2,1)} %param.17) | copy-start | bytes 388
  1.9 9.4 %collective-permute-start.1 = (bf16[4,64,512]{2,1,0:T(8,128)(2,1)S(1)}, bf16[4,64,512]{2,1,0:T(8,128)(2,1)S(1)}, u32[]{:S(2)}, u32[]{:S(2)}) collective-permute-start(bf16[4,64,512]{2,1,0:T(8,128)(2,1)S(1)} %pack.1.own), channel_id=1, source_target_pairs={{2,0},{4,2},{6,4},{8,6},{10,8},{12,10},{14,12},{16,14},{18,16},{20... | collective-permute-start | bytes 786440 | tf_op jit(solution)/shard_map/ppermute | solution.py:384
  3.2 16.9 %collective-permute-start = (bf16[4,64,512]{2,1,0:T(8,128)(2,1)S(1)}, bf16[4,64,512]{2,1,0:T(8,128)(2,1)S(1)}, u32[]{:S(2)}, u32[]{:S(2)}) collective-permute-start(bf16[4,64,512]{2,1,0:T(8,128)(2,1)S(1)} %pack.1.own), channel_id=1, source_target_pairs={{0,2},{2,4},{4,6},{6,8},{8,10},{10,12},{12,14},{14,16},{16,18},{18... | collective-permute-start | bytes 786440 | tf_op jit(solution)/shard_map/ppermute | solution.py:384
  20.1 20.5 %collective-permute-start.3 = (bf16[4,64,1536]{2,1,0:T(8,128)(2,1)S(1)}, bf16[4,64,1536]{2,1,0:T(8,128)(2,1)S(1)}, u32[]{:S(2)}, u32[]{:S(2)}) collective-permute-start(bf16[4,64,1536]{2,1,0:T(8,128)(2,1)S(1)} %band.1), channel_id=1, source_target_pairs={{32,0},{64,32},{96,64},{128,96},{160,128},{192,160},{224,192},{33,... | collective-permute-start | bytes 2359304 | tf_op jit(solution)/shard_map/ppermute | solution.py:384
  21.4 20.1 %collective-permute-start.2 = (bf16[4,64,1536]{2,1,0:T(8,128)(2,1)S(1)}, bf16[4,64,1536]{2,1,0:T(8,128)(2,1)S(1)}, u32[]{:S(2)}, u32[]{:S(2)}) collective-permute-start(bf16[4,64,1536]{2,1,0:T(8,128)(2,1)S(1)} %band.1), channel_id=1, source_target_pairs={{0,32},{32,64},{64,96},{96,128},{128,160},{160,192},{192,224},{1,3... | collective-permute-start | bytes 2359304 | tf_op jit(solution)/shard_map/ppermute | solution.py:384
  45.3 8.4 %collective-permute-start.4 = (bf16[4,16,1664]{2,1,0:T(8,128)(2,1)S(1)}, bf16[4,16,1664]{2,1,0:T(8,128)(2,1)S(1)}, u32[]{:S(2)}, u32[]{:S(2)}) collective-permute-start(bf16[4,16,1664]{2,1,0:T(8,128)(2,1)S(1)} %get-tuple-element.65), channel_id=1, source_target_pairs={{0,2},{2,4},{4,6},{6,8},{8,10},{10,12},{12,14},{14,16},{16,18},{18... | collective-permute-start | bytes 638984 | tf_op jit(solution)/shard_map/ppermute | solution.py:384
  50.9 8.1 %collective-permute-start.5 = (bf16[4,16,1664]{2,1,0:T(8,128)(2,1)S(1)}, bf16[4,16,1664]{2,1,0:T(8,128)(2,1)S(1)}, u32[]{:S(2)}, u32[]{:S(2)}) collective-permute-start(bf16[4,16,1664]{2,1,0:T(8,128)(2,1)S(1)} %get-tuple-element.67), channel_id=1, source_target_pairs={{2,0},{4,2},{6,4},{8,6},{10,8},{12,10},{14,12},{16,14},{18,16},{20... | collective-permute-start | bytes 638984 | tf_op jit(solution)/shard_map/ppermute | solution.py:384
  59.1 12.4 %collective-permute-start.6 = (bf16[16,16640]{1,0:T(8,128)(2,1)S(1)}, bf16[16,16640]{1,0:T(8,128)(2,1)S(1)}, u32[]{:S(2)}, u32[]{:S(2)}) collective-permute-start(bf16[16,16640]{1,0:T(8,128)(2,1)S(1)} %get-tuple-element.68), channel_id=1, source_target_pairs={{0,32},{32,64},{64,96},{96,128},{128,160},{160,192},{192,224},{1,3... | collective-permute-start | bytes 1597448 | tf_op jit(solution)/shard_map/ppermute | solution.py:384
  63.2 12.1 %collective-permute-start.7 = (bf16[16,16640]{1,0:T(8,128)(2,1)S(1)}, bf16[16,16640]{1,0:T(8,128)(2,1)S(1)}, u32[]{:S(2)}, u32[]{:S(2)}) collective-permute-start(bf16[16,16640]{1,0:T(8,128)(2,1)S(1)} %get-tuple-element.69), channel_id=1, source_target_pairs={{32,0},{64,32},{96,64},{128,96},{160,128},{192,160},{224,192},{33,... | collective-permute-start | bytes 1597448 | tf_op jit(solution)/shard_map/ppermute | solution.py:384
  79.3 5.6 %collective-permute-start.8 = (bf16[1024,128]{1,0:T(8,128)(2,1)S(1)}, bf16[1024,128]{1,0:T(8,128)(2,1)S(1)}, u32[]{:S(2)}, u32[]{:S(2)}) collective-permute-start(bf16[1024,128]{1,0:T(8,128)(2,1)S(1)} %get-tuple-element.85), channel_id=1, source_target_pairs={{0,1},{1,0},{2,3},{3,2},{4,5},{5,4},{6,7},{7,6},{8,9},{9,8},{10,11... | collective-permute-start | bytes 786440 | tf_op jit(solution)/shard_map/ppermute | solution.py:461
  137.5 5.7 %collective-permute-start.9 = (bf16[1024,128]{1,0:T(8,128)(2,1)S(1)}, bf16[1024,128]{1,0:T(8,128)(2,1)S(1)}, u32[]{:S(2)}, u32[]{:S(2)}) collective-permute-start(bf16[1024,128]{1,0:T(8,128)(2,1)S(1)} %bitcast.34), channel_id=1, source_target_pairs={{0,1},{1,0},{2,3},{3,2},{4,5},{5,4},{6,7},{7,6},{8,9},{9,8},{10,11... | collective-permute-start | bytes 786440 | tf_op jit(solution)/shard_map/ppermute | solution.py:466

commit v10 on v9

--- a/solution.py
+++ b/solution.py
@@ -326,11 +326,19 @@
     sent[...] = sums[pl.ds(other, HALF), :].astype(BF16)
 
 
-def last_kernel(spread_0, spread_1, spread_2, spread_3, t0, t1, t2, t3, base, out_ref):
+def pulled(i, refs, turned_refs):
+    lanes = slice(B * Z, 2 * B * Z)
+    return sum(back_row(t, slice(0, 64), ref, B + i, lanes) for ref, t in zip(refs, turned_refs))
+
+
+def half_kernel(spread_2, spread_3, t2, t3, base, out_ref):
     for i in range(B):
-        out = base[i]
-        for ref, turned_ref in zip((spread_0, spread_1, spread_2, spread_3), (t0, t1, t2, t3)):
-            out = out + back_row(turned_ref, slice(0, 64), ref, B + i, slice(B * Z, 2 * B * Z))
+        out_ref[i] = base[i] + pulled(i, (spread_2, spread_3), (t2, t3))
+
+
+def last_kernel(spread_0, spread_1, t0, t1, base, out_ref):
+    for i in range(B):
+        out = base[i] + pulled(i, (spread_0, spread_1), (t0, t1))
         for j in range(B):
             out_ref[pl.ds(B * i + j, 64, stride=B * B), :] = out[:, j * Z : (j + 1) * Z]
 
@@ -458,7 +466,15 @@
     axes = ("gx", "row")
     swap = [(0, 1), (1, 0)]
     half_sum = shape((HALF, Z), BF16)
-    (paired,) = call(pair_kernel, [half_sum], [kept, lax.ppermute(sent, "rep", swap)], name="pair")
+    (part,) = call(
+        half_kernel,
+        [shape((B, 64, B * Z), F32)],
+        spreads[2:] + [t2, t3, base],
+        flops=150_000_000,
+        name="input_gradient_3_2",
+    )
+    came, part = lax.optimization_barrier((lax.ppermute(sent, "rep", swap), part))
+    (paired,) = call(pair_kernel, [half_sum], [kept, came], name="pair")
     spread_sums = lax.all_to_all(paired.reshape(GROUP, ROWS, Z), axes, 0, 0, tiled=True)
     (added,) = call(add_kernel, [half_sum], [spread_sums.reshape(HALF, Z)], name="add")
     totals = lax.all_to_all(added.reshape(GROUP, ROWS, Z), axes, 0, 0, tiled=True)
@@ -467,7 +483,7 @@
     (grad_input,) = call(
         last_kernel,
         [shape((1024, Z), F32)],
-        spreads + [t0, t1, t2, t3, base],
+        spreads[:2] + [t0, t1, part],
         flops=300_000_000,
         name="input_gradient",
     )

time: 145 us -> 144 us (level)
    pallas_call x11 -> x12, Pallas kernels: 13.7 us -> 13.9 us  [call(): pl.pallas_call(kernel, out_shape=list(outs), in_specs=[pl.BlockSpec(memor...]
where the time goes in v10:
time: 144 us
  blocking collectives  52.7 us (37%)
  waiting for transfers between devices  42.3 us (29%)
  starting transfers between devices  33.1 us (23%)
  Pallas kernels  13.9 us (10%)
    all_to_all x1, blocking collectives, body(): lax.all_to_all(paired.reshape(GROUP, ROWS, Z), axes, 0, 0, tiled=True)  32.6 us
    ppermute x4, waiting for transfers between devices, neighbours(): lax.ppermute(low, axis, [(j, i) for i, j in up])  25.5 us
    ppermute x4, starting transfers between devices, neighbours(): lax.ppermute(high, axis, up)  20.1 us
    all_to_all x1, blocking collectives, body(): lax.all_to_all(added.reshape(GROUP, ROWS, Z), axes, 0, 0, tiled=True)  20.1 us
    ppermute x4, waiting for transfers between devices, neighbours(): lax.ppermute(high, axis, up)  16.4 us
    pallas_call x12, Pallas kernels, call(): pl.pallas_call(kernel, out_shape=list(outs), in_specs=[pl.BlockSpec(memor...  13.9 us
    ppermute x4, starting transfers between devices, neighbours(): lax.ppermute(low, axis, [(j, i) for i, j in up])  5.17 us
    ppermute x1, starting transfers between devices, body(): lax.ppermute(sent, 'rep', swap)  4.39 us
  transfers between devices with their start and end apart: 10, of which 9 were waited for; matrix products, arithmetic and copies ran while one was open for 0% of the time, Pallas kernels for 3%

profile of v10, /device:TPU:1, one launch (start us, length us, event | category | flops | bytes accessed | tf_op | source)
XLA Modules:
  0.0 143.8 jit_solution(12405151565099124538)
XLA Ops:
  1.9 1.3 collective-permute-start.1
  3.2 6.3 %collective-permute-start = (bf16[4,64,512]{2,1,0:T(8,128)(2,1)S(1)}, bf16[4,64,512]{2,1,0:T(8,128)(2,1)S(1)}, u32[]{:S(2)}, u32[]{:S(2)}) collective-permute-start(bf16[4,64,512]{2,1,0:T(8,128)(2,1)S(1)} %pack.1.own), channel_id=1, source_target_pairs={{0,2},{2,4},{4,6},{6,8},{8,10},{10,12},{12,14},{14,16},{16,18},{18... | collective-permute-start | bytes 786440 | tf_op jit(solution)/shard_map/ppermute | solution.py:392
  9.5 1.8 %collective-permute-done.1.after = bf16[4,64,512]{2,1,0:T(8,128)(2,1)S(1)} collective-permute-done((bf16[4,64,512]{2,1,0:T(8,128)(2,1)S(1)}, bf16[4,64,512]{2,1,0:T(8,128)(2,1)S(1)}, u32[]{:S(2)}, u32[]{:S(2)}) %collective-permute-start.1) | collective-permute-done | bytes 262176 | tf_op jit(solution)/shard_map/ppermute | solution.py:392
  11.3 8.8 %collective-permute-done.before = bf16[4,64,512]{2,1,0:T(8,128)(2,1)S(1)} collective-permute-done((bf16[4,64,512]{2,1,0:T(8,128)(2,1)S(1)}, bf16[4,64,512]{2,1,0:T(8,128)(2,1)S(1)}, u32[]{:S(2)}, u32[]{:S(2)}) %collective-permute-start) | collective-permute-done | bytes 262176 | tf_op jit(solution)/shard_map/ppermute | solution.py:392
  20.1 1.3 collective-permute-start.3
  21.4 4.0 %collective-permute-start.2 = (bf16[4,64,1536]{2,1,0:T(8,128)(2,1)S(1)}, bf16[4,64,1536]{2,1,0:T(8,128)(2,1)S(1)}, u32[]{:S(2)}, u32[]{:S(2)}) collective-permute-start(bf16[4,64,1536]{2,1,0:T(8,128)(2,1)S(1)} %band.1), channel_id=1, source_target_pairs={{0,32},{32,64},{64,96},{96,128},{128,160},{160,192},{192,224},{1,3... | collective-permute-start | bytes 2359304 | tf_op jit(solution)/shard_map/ppermute | solution.py:392
  26.1 14.5 %collective-permute-done.3.below = bf16[4,64,1536]{2,1,0:T(8,128)(2,1)S(1)} collective-permute-done((bf16[4,64,1536]{2,1,0:T(8,128)(2,1)S(1)}, bf16[4,64,1536]{2,1,0:T(8,128)(2,1)S(1)}, u32[]{:S(2)}, u32[]{:S(2)}) %collective-permute-start.3) | collective-permute-done | bytes 786464 | tf_op jit(solution)/shard_map/ppermute | solution.py:392
  41.5 3.8 %forward.1 = (bf16[8,64,1024]{2,1,0:T(8,128)(2,1)S(1)}, bf16[8,32,1024]{2,1,0:T(8,128)(2,1)S(1)}, bf16[8,16,1024]{2,1,0:T(8,128)(2,1)S(1)}, bf16[4,16,512]{2,1,0...) custom-call(bf16[4,64,1536]{2,1,0:T(8,128)(2,1)S(1)} %collective-per, ...), custom_call_target="tpu_custom_call" | custom-call | flops 1000000 | bytes 7021568 | tf_op jit(solution)/shard_map/forward/pallas_call | solution.py:34
  45.3 5.6 %collective-permute-start.4 = (bf16[4,16,1664]{2,1,0:T(8,128)(2,1)S(1)}, bf16[4,16,1664]{2,1,0:T(8,128)(2,1)S(1)}, u32[]{:S(2)}, u32[]{:S(2)}) collective-permute-start(bf16[4,16,1664]{2,1,0:T(8,128)(2,1)S(1)} %get-tuple-element.67), channel_id=1, source_target_pairs={{0,2},{2,4},{4,6},{6,8},{8,10},{10,12},{12,14},{14,16},{16,18},{18... | collective-permute-start | bytes 638984 | tf_op jit(solution)/shard_map/ppermute | solution.py:392
  50.9 1.3 collective-permute-start.5
  52.2 1.5 %collective-permute-done.4.before = bf16[4,16,1664]{2,1,0:T(8,128)(2,1)S(1)} collective-permute-done((bf16[4,16,1664]{2,1,0:T(8,128)(2,1)S(1)}, bf16[4,16,1664]{2,1,0:T(8,128)(2,1)S(1)}, u32[]{:S(2)}, u32[]{:S(2)}) %collective-permute-start.4) | collective-permute-done | bytes 213024 | tf_op jit(solution)/shard_map/ppermute | solution.py:392
  53.7 5.3 %collective-permute-done.5.after = bf16[4,16,1664]{2,1,0:T(8,128)(2,1)S(1)} collective-permute-done((bf16[4,16,1664]{2,1,0:T(8,128)(2,1)S(1)}, bf16[4,16,1664]{2,1,0:T(8,128)(2,1)S(1)}, u32[]{:S(2)}, u32[]{:S(2)}) %collective-permute-start.5) | collective-permute-done | bytes 213024 | tf_op jit(solution)/shard_map/ppermute | solution.py:392
  59.1 4.1 %collective-permute-start.6 = (bf16[16,16640]{1,0:T(8,128)(2,1)S(1)}, bf16[16,16640]{1,0:T(8,128)(2,1)S(1)}, u32[]{:S(2)}, u32[]{:S(2)}) collective-permute-start(bf16[16,16640]{1,0:T(8,128)(2,1)S(1)} %get-tuple-element.70), channel_id=1, source_target_pairs={{0,32},{32,64},{64,96},{96,128},{128,160},{160,192},{192,224},{1,3... | collective-permute-start | bytes 1597448 | tf_op jit(solution)/shard_map/ppermute | solution.py:392
  63.2 1.3 collective-permute-start.7
  64.5 1.7 %merge.4 = (f32[1024,128]{1,0:T(8,128)}, f32[432,128]{1,0:T(8,128)S(1)}, f32[144,128]{1,0:T(8,128)S(1)}) custom-call(bf16[8,64,1024]{2,1,0:T(8,128)(2,1)S(1)} %get-tuple-element.59.frame, bf16[8,32,1024]{2,1,0:T(8,128)(2,1)S(1)} %get-tuple-element.60.hidden_01, bf16[8,16,1024]{2,1,0:T(8,128)(2,1)S(1)} %get-tuple-element.61.hidden_2, ...), custom_call_target="tpu_custom_call" | custom-call | flops 100000000 | bytes 3227648 | tf_op jit(solution)/shard_map/merge/pallas_call | solution.py:34
  66.2 5.3 %collective-permute-done.6.above = bf16[16,16640]{1,0:T(8,128)(2,1)S(1)} collective-permute-done((bf16[16,16640]{1,0:T(8,128)(2,1)S(1)}, bf16[16,16640]{1,0:T(8,128)(2,1)S(1)}, u32[]{:S(2)}, u32[]{:S(2)}) %collective-permute-start.6) | collective-permute-done | bytes 532512 | tf_op jit(solution)/shard_map/ppermute | solution.py:392
  71.5 3.9 %collective-permute-done.7.below = bf16[16,16640]{1,0:T(8,128)(2,1)S(1)} collective-permute-done((bf16[16,16640]{1,0:T(8,128)(2,1)S(1)}, bf16[16,16640]{1,0:T(8,128)(2,1)S(1)}, u32[]{:S(2)}, u32[]{:S(2)}) %collective-permute-start.7) | collective-permute-done | bytes 532512 | tf_op jit(solution)/shard_map/ppermute | solution.py:392
  75.4 3.9 %backward.1 = (bf16[12,48,1536]{2,1,0:T(8,128)(2,1)S(1)}, bf16[12,48,1536]{2,1,0:T(8,128)(2,1)S(1)}, bf16[12,48,1536]{2,1,0:T(8,128)(2,1)S(1)}, bf16[12,48,1536]...) custom-call(bf16[16,16640]{1,0:T(8,128)(2,1)S(1)} %collective-permute-done.6.above, ...), custom_call_target="tpu_custom_call" | custom-call | flops 1000000 | bytes 13274112 | tf_op jit(solution)/shard_map/backward/pallas_call | solution.py:34
  79.3 4.4 %collective-permute-start.8 = (bf16[1024,128]{1,0:T(8,128)(2,1)S(1)}, bf16[1024,128]{1,0:T(8,128)(2,1)S(1)}, u32[]{:S(2)}, u32[]{:S(2)}) collective-permute-start(bf16[1024,128]{1,0:T(8,128)(2,1)S(1)} %get-tuple-element.83), channel_id=1, source_target_pairs={{0,1},{1,0},{2,3},{3,2},{4,5},{5,4},{6,7},{7,6},{8,9},{9,8},{10,11... | collective-permute-start | bytes 786440 | tf_op jit(solution)/shard_map/ppermute | solution.py:476
  84.9 32.6 %all_to_all.10 = bf16[128,8,128]{2,1,0:T(8,128)(2,1)S(1)} all-to-all(bf16[128,8,128]{2,1,0:T(8,128)(2,1)S(1)} %bitcast.38), channel_id=1, replica_groups=mesh['gx'=8,'row'=16,'rep'=2] {'gx','row'}, dimensions={0} | all-to-all | bytes 524288 | tf_op jit(solution)/shard_map/all_to_all | solution.py:478
  117.6 20.1 %all_to_all.11 = bf16[128,8,128]{2,1,0:T(8,128)(2,1)S(1)} all-to-all(bf16[128,8,128]{2,1,0:T(8,128)(2,1)S(1)} %bitcast.37), channel_id=1, replica_groups=mesh['gx'=8,'row'=16,'rep'=2] {'gx','row'}, dimensions={0} | all-to-all | bytes 524288 | tf_op jit(solution)/shard_map/all_to_all | solution.py:480
  137.7 3.5 %collective-permute-start.9 = (bf16[1024,128]{1,0:T(8,128)(2,1)S(1)}, bf16[1024,128]{1,0:T(8,128)(2,1)S(1)}, u32[]{:S(2)}, u32[]{:S(2)}) collective-permute-start(bf16[1024,128]{1,0:T(8,128)(2,1)S(1)} %bitcast.34), channel_id=1, source_target_pairs={{0,1},{1,0},{2,3},{3,2},{4,5},{5,4},{6,7},{7,6},{8,9},{9,8},{10,11... | collective-permute-start | bytes 786440 | tf_op jit(solution)/shard_map/ppermute | solution.py:482
  141.2 1.6 %input_gradient.1 = f32[1024,128]{1,0:T(8,128)} custom-call(bf16[12,48,1536]{2,1,0:T(8,128)(2,1)S(1)} %get-tuple-element.80.spread_0, bf16[12,48,1536]{2,1,0:T(8,128)(2,1)S(1)} %get-tuple-element.81.spread_1, bf16[3,64,144]{2,1,0:T(8,128)(2,1)S(1)} %get-tuple-element.82.t0, bf16[3,80,144]{2,1,0:T(8,128)(2,1)S(1)} %get-tuple-element.72.t1, ...), custom_call_target="tpu_custom_call" | custom-call | flops 300000000 | bytes 4711936 | tf_op jit(solution)/shard_map/input_gradient/pallas_call | solution.py:34
  142.8 1.0 unpack.1
  (28 shorter events, 4.1 us)
Async XLA Ops:
  0.6 24.8 %copy-start = (bf16[1,64,4,4,128]{4,3,2,1,0:T(4,128)(2,1)S(1)}, bf16[1,64,4,4,128]{4,3,2,1,0:T(4,128)(2,1)}, u32[]{:S(2)}) copy-start(bf16[1,64,4,4,128]{4,3,2,1,0:T(4,128)(2,1)} %param.10) | copy-start | bytes 786436
  0.7 1.0 copy-start.1
  1.6 23.8 %copy-start.2 = (bf16[16,27,64]{2,0,1:T(8,128)(2,1)S(1)}, bf16[16,27,64]{2,0,1:T(8,128)(2,1)}, u32[]{:S(2)}) copy-start(bf16[16,27,64]{2,0,1:T(8,128)(2,1)} %param.11) | copy-start | bytes 165892
  1.7 23.8 %copy-start.3 = (bf16[16,27,80]{2,0,1:T(8,128)(2,1)S(1)}, bf16[16,27,80]{2,0,1:T(8,128)(2,1)}, u32[]{:S(2)}) copy-start(bf16[16,27,80]{2,0,1:T(8,128)(2,1)} %param.12) | copy-start | bytes 207364
  1.7 23.8 %copy-start.4 = (bf16[16,27,96]{2,0,1:T(8,128)(2,1)S(1)}, bf16[16,27,96]{2,0,1:T(8,128)(2,1)}, u32[]{:S(2)}) copy-start(bf16[16,27,96]{2,0,1:T(8,128)(2,1)} %param.13) | copy-start | bytes 248836
  1.7 23.8 %copy-start.5 = (bf16[16,27,112]{2,0,1:T(8,128)(2,1)S(1)}, bf16[16,27,112]{2,0,1:T(8,128)(2,1)}, u32[]{:S(2)}) copy-start(bf16[16,27,112]{2,0,1:T(8,128)(2,1)} %param.14) | copy-start | bytes 290308
  1.7 23.9 %copy-start.6 = (bf16[64,128]{1,0:T(8,128)(2,1)S(1)}, bf16[64,128]{1,0:T(8,128)(2,1)}, u32[]{:S(2)}) copy-start(bf16[64,128]{1,0:T(8,128)(2,1)} %merge.5) | copy-start | bytes 49156
  1.7 23.9 %copy-start.7 = (bf16[4,16]{1,0:T(4,128)(2,1)S(1)}, bf16[4,16]{1,0:T(4,128)(2,1)}, u32[]{:S(2)}) copy-start(bf16[4,16]{1,0:T(4,128)(2,1)} %layer_bias.1) | copy-start | bytes 388
  1.7 23.9 %copy-start.8 = (bf16[64]{0:T(256)(128)(2,1)S(1)}, bf16[64]{0:T(256)(128)(2,1)}, u32[]{:S(2)}) copy-start(bf16[64]{0:T(256)(128)(2,1)} %param.17) | copy-start | bytes 388
  1.9 9.4 %collective-permute-start.1 = (bf16[4,64,512]{2,1,0:T(8,128)(2,1)S(1)}, bf16[4,64,512]{2,1,0:T(8,128)(2,1)S(1)}, u32[]{:S(2)}, u32[]{:S(2)}) collective-permute-start(bf16[4,64,512]{2,1,0:T(8,128)(2,1)S(1)} %pack.1.own), channel_id=1, source_target_pairs={{2,0},{4,2},{6,4},{8,6},{10,8},{12,10},{14,12},{16,14},{18,16},{20... | collective-permute-start | bytes 786440 | tf_op jit(solution)/shard_map/ppermute | solution.py:392
  3.2 16.9 %collective-permute-start = (bf16[4,64,512]{2,1,0:T(8,128)(2,1)S(1)}, bf16[4,64,512]{2,1,0:T(8,128)(2,1)S(1)}, u32[]{:S(2)}, u32[]{:S(2)}) collective-permute-start(bf16[4,64,512]{2,1,0:T(8,128)(2,1)S(1)} %pack.1.own), channel_id=1, source_target_pairs={{0,2},{2,4},{4,6},{6,8},{8,10},{10,12},{12,14},{14,16},{16,18},{18... | collective-permute-start | bytes 786440 | tf_op jit(solution)/shard_map/ppermute | solution.py:392
  20.1 20.5 %collective-permute-start.3 = (bf16[4,64,1536]{2,1,0:T(8,128)(2,1)S(1)}, bf16[4,64,1536]{2,1,0:T(8,128)(2,1)S(1)}, u32[]{:S(2)}, u32[]{:S(2)}) collective-permute-start(bf16[4,64,1536]{2,1,0:T(8,128)(2,1)S(1)} %band.1), channel_id=1, source_target_pairs={{32,0},{64,32},{96,64},{128,96},{160,128},{192,160},{224,192},{33,... | collective-permute-start | bytes 2359304 | tf_op jit(solution)/shard_map/ppermute | solution.py:392
  21.4 20.1 %collective-permute-start.2 = (bf16[4,64,1536]{2,1,0:T(8,128)(2,1)S(1)}, bf16[4,64,1536]{2,1,0:T(8,128)(2,1)S(1)}, u32[]{:S(2)}, u32[]{:S(2)}) collective-permute-start(bf16[4,64,1536]{2,1,0:T(8,128)(2,1)S(1)} %band.1), channel_id=1, source_target_pairs={{0,32},{32,64},{64,96},{96,128},{128,160},{160,192},{192,224},{1,3... | collective-permute-start | bytes 2359304 | tf_op jit(solution)/shard_map/ppermute | solution.py:392
  45.3 8.4 %collective-permute-start.4 = (bf16[4,16,1664]{2,1,0:T(8,128)(2,1)S(1)}, bf16[4,16,1664]{2,1,0:T(8,128)(2,1)S(1)}, u32[]{:S(2)}, u32[]{:S(2)}) collective-permute-start(bf16[4,16,1664]{2,1,0:T(8,128)(2,1)S(1)} %get-tuple-element.67), channel_id=1, source_target_pairs={{0,2},{2,4},{4,6},{6,8},{8,10},{10,12},{12,14},{14,16},{16,18},{18... | collective-permute-start | bytes 638984 | tf_op jit(solution)/shard_map/ppermute | solution.py:392
  50.9 8.1 %collective-permute-start.5 = (bf16[4,16,1664]{2,1,0:T(8,128)(2,1)S(1)}, bf16[4,16,1664]{2,1,0:T(8,128)(2,1)S(1)}, u32[]{:S(2)}, u32[]{:S(2)}) collective-permute-start(bf16[4,16,1664]{2,1,0:T(8,128)(2,1)S(1)} %get-tuple-element.69), channel_id=1, source_target_pairs={{2,0},{4,2},{6,4},{8,6},{10,8},{12,10},{14,12},{16,14},{18,16},{20... | collective-permute-start | bytes 638984 | tf_op jit(solution)/shard_map/ppermute | solution.py:392
  59.1 12.4 %collective-permute-start.6 = (bf16[16,16640]{1,0:T(8,128)(2,1)S(1)}, bf16[16,16640]{1,0:T(8,128)(2,1)S(1)}, u32[]{:S(2)}, u32[]{:S(2)}) collective-permute-start(bf16[16,16640]{1,0:T(8,128)(2,1)S(1)} %get-tuple-element.70), channel_id=1, source_target_pairs={{0,32},{32,64},{64,96},{96,128},{128,160},{160,192},{192,224},{1,3... | collective-permute-start | bytes 1597448 | tf_op jit(solution)/shard_map/ppermute | solution.py:392
  63.2 12.1 %collective-permute-start.7 = (bf16[16,16640]{1,0:T(8,128)(2,1)S(1)}, bf16[16,16640]{1,0:T(8,128)(2,1)S(1)}, u32[]{:S(2)}, u32[]{:S(2)}) collective-permute-start(bf16[16,16640]{1,0:T(8,128)(2,1)S(1)} %get-tuple-element.71), channel_id=1, source_target_pairs={{32,0},{64,32},{96,64},{128,96},{160,128},{192,160},{224,192},{33,... | collective-permute-start | bytes 1597448 | tf_op jit(solution)/shard_map/ppermute | solution.py:392
  79.3 5.6 %collective-permute-start.8 = (bf16[1024,128]{1,0:T(8,128)(2,1)S(1)}, bf16[1024,128]{1,0:T(8,128)(2,1)S(1)}, u32[]{:S(2)}, u32[]{:S(2)}) collective-permute-start(bf16[1024,128]{1,0:T(8,128)(2,1)S(1)} %get-tuple-element.83), channel_id=1, source_target_pairs={{0,1},{1,0},{2,3},{3,2},{4,5},{5,4},{6,7},{7,6},{8,9},{9,8},{10,11... | collective-permute-start | bytes 786440 | tf_op jit(solution)/shard_map/ppermute | solution.py:476
  137.7 5.1 %collective-permute-start.9 = (bf16[1024,128]{1,0:T(8,128)(2,1)S(1)}, bf16[1024,128]{1,0:T(8,128)(2,1)S(1)}, u32[]{:S(2)}, u32[]{:S(2)}) collective-permute-start(bf16[1024,128]{1,0:T(8,128)(2,1)S(1)} %bitcast.34), channel_id=1, source_target_pairs={{0,1},{1,0},{2,3},{3,2},{4,5},{5,4},{6,7},{7,6},{8,9},{9,8},{10,11... | collective-permute-start | bytes 786440 | tf_op jit(solution)/shard_map/ppermute | solution.py:482
